TPU v7x, 512 devices: a whole 4x8x8 slice. The times are simulated.
512 devices in a mesh: gx: 8 (over y), gy: 4 (over z_hi), gz: 16 (over x, z_lo, core).
Axes of the slice: x: 4, y: 8, z: 8 (z_hi: 4, z_lo: 2; z = z_hi * 2 + z_lo), core: 2. Of those that a mesh axis runs over, the one named last changes fastest.
Arguments:
- rhs: float32 [16, 8, 64, 256], P('gx', 'gy', 'gz'), may hold values from -12 to 12
- diagonal: float32 [16, 8, 64, 16], P('gx', 'gy', 'gz'), may hold values from 1 to 3
- blocks: float32 [16, 8, 64, 16, 432], P('gx', 'gy', 'gz'), may hold values from -0.09 to 0.09
- neighbours: int32 [16, 8, 64, 27], P('gx', 'gy', 'gz'), may hold values from 0 to 8191, as said below
Outputs:
- solution: float32 [16, 8, 64, 256], P('gx', 'gy', 'gz')
Inputs may be any that keep to these rules, and one draw needn't show every extreme that they name: `neighbours`: entry k of an atom's list is the flat index of an atom whose three lattice coordinates each differ from the atom's own by at most one, periodically; every list names the atom itself at least once, and entries may repeat, their blocks then adding.
All inputs are finite; a program needn't handle non-finite values.
Results may differ from a plain program's by a relative error of at most 0.0003.
Values sent between devices are 32-bit elements; how exact they have to be, the bound alone decides.
No kernel may reach another device: no remote copies, remote signals or barrier semaphores. Data moves between devices by JAX's collectives and lax.ppermute only.
A program may use at most 64 MiB of HBM per device.

v0:
```python
import jax
import jax.numpy as jnp
from jax import lax
from jax.sharding import PartitionSpec as P

ITERS = 2


def with_halo(cells, sides, width):
    for axis, dim in sides:
        count = lax.axis_size(axis)
        head = lax.slice_in_dim(cells, 0, width, axis=dim)
        tail = lax.slice_in_dim(cells, cells.shape[dim] - width, cells.shape[dim], axis=dim)
        cells = jnp.concatenate(
            [
                lax.ppermute(tail, axis, [(i, (i + 1) % count) for i in range(count)]),
                cells,
                lax.ppermute(head, axis, [((i + 1) % count, i) for i in range(count)]),
            ],
            axis=dim,
        )
    return cells


def column_dot(first, second, components):
    return jnp.sum(
        (first * second).reshape(-1, components, first.shape[-1] // components), axis=(0, 1)
    )


def broaden(values, components):
    return jnp.tile(values, components)


def shrink_step(quasi_norm, ratio_step, step_size):
    damping = 1.0 / (1.0 + ratio_step * ratio_step)
    return (quasi_norm * ratio_step * jnp.sqrt(damping), damping * step_size)


def body(rhs, diagonal, blocks, neighbours):
    first_len, second_len, third_len, width = rhs.shape
    components = diagonal.shape[-1]
    columns = width // components
    slot_count = neighbours.shape[-1]
    total_first = first_len * lax.axis_size("gx")
    total_second = second_len * lax.axis_size("gy")
    total_third = third_len * lax.axis_size("gz")
    coord_first = neighbours // (total_second * total_third)
    coord_second = neighbours // total_third % total_second
    coord_third = neighbours % total_third
    local_first = (coord_first - lax.axis_index("gx") * first_len + 1) % total_first
    local_second = (coord_second - lax.axis_index("gy") * second_len + 1) % total_second
    local_third = (coord_third - lax.axis_index("gz") * third_len + 1) % total_third
    gather_rows = (local_first * (second_len + 2) + local_second) * (third_len + 2) + local_third
    scaled_diag = jnp.repeat(diagonal, columns, axis=-1)
    coupling = blocks.reshape(first_len, second_len, third_len, components, slot_count, components)

    def operate(field):
        padded = with_halo(field, (("gx", 0), ("gy", 1), ("gz", 2)), 1)
        flattened = padded.reshape(-1, width)
        nearby = jnp.take(flattened, gather_rows, axis=0)
        nearby = nearby.reshape(first_len, second_len, third_len, slot_count, components, columns)
        summed = jnp.einsum(
            "abclkm,abckmr->abclr",
            coupling,
            nearby,
            precision=lax.Precision.HIGHEST,
            preferred_element_type=jnp.float32,
        )
        return scaled_diag * field - summed.reshape(first_len, second_len, third_len, width)

    image = operate(rhs)
    inner_now = lax.psum(column_dot(rhs, rhs, components), ("gx", "gy", "gz"))
    curvature = inner_now
    quasi_norm = jnp.sqrt(inner_now)
    empty_field = jnp.zeros_like(rhs)
    solution = empty_field
    quasi_resid = rhs
    search = rhs
    direction = empty_field
    ratio_step = jnp.zeros_like(inner_now)
    weight_step = jnp.zeros_like(inner_now)
    for iteration in range(ITERS):
        going_on = iteration + 1 < ITERS
        curvature = lax.psum(column_dot(image, rhs, components), ("gx", "gy", "gz"))
        step_size = inner_now / curvature
        spread_step = broaden(step_size, components)
        quasi_resid = quasi_resid - spread_step * image
        direction = (
            search
            + broaden(ratio_step * ratio_step * weight_step / step_size, components) * direction
        )
        ratio_step = (
            jnp.sqrt(lax.psum(column_dot(quasi_resid, quasi_resid, components), ("gx", "gy", "gz")))
            / quasi_norm
        )
        quasi_norm, weight_step = shrink_step(quasi_norm, ratio_step, step_size)
        solution = solution + broaden(weight_step, components) * direction
        search_odd = search - spread_step * image
        image_odd = operate(search_odd)
        quasi_resid = quasi_resid - spread_step * image_odd
        direction = (
            search_odd
            + broaden(ratio_step * ratio_step * weight_step / step_size, components) * direction
        )
        norm_square, inner_next = lax.psum(
            (
                column_dot(quasi_resid, quasi_resid, components),
                column_dot(quasi_resid, rhs, components),
            ),
            ("gx", "gy", "gz"),
        )
        ratio_step = jnp.sqrt(norm_square) / quasi_norm
        quasi_norm, weight_step = shrink_step(quasi_norm, ratio_step, step_size)
        solution = solution + broaden(weight_step, components) * direction
        if going_on:
            mix_ratio = inner_next / inner_now
            spread_mix = broaden(mix_ratio, components)
            search = quasi_resid + spread_mix * search_odd
            image_new = operate(search)
            image = image_new + spread_mix * (image_odd + spread_mix * image)
            inner_now = inner_next
    return solution


def solution(mesh):
    return jax.shard_map(
        body,
        mesh=mesh,
        in_specs=(
            P("gx", "gy", "gz", None),
            P("gx", "gy", "gz", None),
            P("gx", "gy", "gz", None, None),
            P("gx", "gy", "gz", None),
        ),
        out_specs=P("gx", "gy", "gz", None),
        check_vma=False,
    )
```

profile of v0, /device:TPU:1, one launch (start us, length us, event | category | flops | bytes accessed | tf_op | source)
XLA Modules:
  0.0 606.2 jit_solution(7584907500446243506)
XLA Ops:
  0.7 4.0 collective-permute-start
  4.7 3.8 collective-permute-start.1
  9.4 5.8 collective-permute-start.2
  15.2 6.8 %collective-permute-start.3 = (f32[4,1,4,256]{3,2,1,0:T(4,128)S(1)}, f32[4,1,4,256]{3,2,1,0:T(4,128)S(1)}, u32[]{:S(2)}, u32[]{:S(2)}) collective-permute-start(f32[4,1,4,256]{3,2,1,0:T(4,128)S(1)} %get-tuple-element.54), channel_id=1, source_target_pairs={{16,0},{32,16},{48,32},{0,48},{17,1},{33,17},{49,33},{1,49},{18,2}... | collective-permute-start | bytes 49160 | tf_op jit(solution)/shard_map/ppermute | solution.py:18
  23.6 6.0 collective-permute-start.4
  33.0 4.1 reshape.90
  42.1 11.2 %fusion.8 = f32[2,2,4,16,16]{3,4,2,1,0:T(8,128)} fusion(f32[2,2,4,27,16,16]{5,4,3,2,1,0:T(8,128)S(1)} %reshape.161, f32[2,2,4,16,27,16]{5,4,3,2,1,0:T(8,128)} %reshape.90), kind=kOutput, calls=%fused_computation.12 | convolution fusion | flops 21233664 | bytes 901120 | tf_op jit(solution)/shard_map/abclkm,abckmr->abclr/dot_general | solution.py:63
  55.3 99.6 %all-reduce.1 = (f32[16]{0:T(128)S(1)}, f32[16]{0:T(128)S(1)}) all-reduce(f32[16]{0:T(128)S(1)} %reduce_sum.97, f32[16]{0:T(128)S(1)} %reduce_sum.100), channel_id=1, replica_groups=mesh['gx'=8,'gy'=4,'gz'=16] {'gx','gy','gz'}, use_global_device_ids=true, to_apply=%region_2.3 | all-reduce | flops 32 | bytes 256 | tf_op jit(solution)/shard_map/psum | solution.py:73
  160.6 3.3 collective-permute-start.7
  165.0 3.8 collective-permute-start.8
  168.8 3.6 collective-permute-start.9
  174.5 5.4 collective-permute-start.10
  190.0 11.2 %fusion.11 = f32[2,2,4,16,16]{3,4,2,1,0:T(8,128)} fusion(f32[2,2,4,27,16,16]{5,4,3,2,1,0:T(8,128)S(1)} %reshape.162, f32[2,2,4,16,27,16]{5,4,3,2,1,0:T(8,128)} %reshape.90), kind=kOutput, calls=%fused_computation.13 | convolution fusion | flops 21233664 | bytes 901120 | tf_op jit(solution)/shard_map/abclkm,abckmr->abclr/dot_general | solution.py:63
  203.2 101.2 %psum.60 = f32[16]{0:T(128)S(1)} all-reduce(f32[16]{0:T(128)S(1)} %reduce_sum.115), channel_id=1, replica_groups=mesh['gx'=8,'gy'=4,'gz'=16] {'gx','gy','gz'}, use_global_device_ids=true, to_apply=%region_14.16 | all-reduce | flops 16 | bytes 128 | tf_op jit(solution)/shard_map/psum | solution.py:106
  307.5 4.6 collective-permute-start.13
  316.0 4.2 collective-permute-start.15
  321.7 5.6 collective-permute-start.16
  337.4 11.2 %fusion.14 = f32[2,2,4,16,16]{3,4,2,1,0:T(8,128)} fusion(f32[2,2,4,27,16,16]{5,4,3,2,1,0:T(8,128)S(1)} %reshape.163, f32[2,2,4,16,27,16]{5,4,3,2,1,0:T(8,128)} %reshape.90), kind=kOutput, calls=%fused_computation.14 | convolution fusion | flops 21233664 | bytes 901120 | tf_op jit(solution)/shard_map/abclkm,abckmr->abclr/dot_general | solution.py:63
  350.6 101.8 %psum.61 = f32[16]{0:T(128)S(1)} all-reduce(f32[16]{0:T(128)S(1)} %reduce_sum.145), channel_id=1, replica_groups=mesh['gx'=8,'gy'=4,'gz'=16] {'gx','gy','gz'}, use_global_device_ids=true, to_apply=%region_17.19 | all-reduce | flops 16 | bytes 128 | tf_op jit(solution)/shard_map/psum | solution.py:85
  456.2 4.6 collective-permute-start.19
  464.7 4.2 collective-permute-start.21
  470.5 5.6 collective-permute-start.22
  486.2 11.2 %fusion.17 = f32[2,2,4,16,16]{3,4,2,1,0:T(8,128)} fusion(f32[2,2,4,27,16,16]{5,4,3,2,1,0:T(8,128)S(1)} %reshape.164, f32[2,2,4,16,27,16]{5,4,3,2,1,0:T(8,128)} %reshape.90), kind=kOutput, calls=%fused_computation.15 | convolution fusion | flops 21233664 | bytes 901120 | tf_op jit(solution)/shard_map/abclkm,abckmr->abclr/dot_general | solution.py:63
  499.6 101.8 %all-reduce = (f32[16]{0:T(128)S(1)}, f32[16]{0:T(128)S(1)}, f32[16]{0:T(128)S(1)}, f32[16]{0:T(128)S(1)}) all-reduce(f32[16]{0:T(128)S(1)} %reduce_sum.148, f32[16]{0:T(128)} %reduce_sum.106, f32[16]{0:T(128)S(1)} %reduce_sum.112, f32[16]{0:T(128)S(1)} %reduce_sum.151), channel_id=1, replica_groups=mesh['gx'=8,'gy'=4,'gz'=16] {'gx','gy','gz'}, use_global_device_ids=true, to_apply=%region_20.22 | all-reduce | flops 64 | bytes 512 | tf_op jit(solution)/shard_map/psum | solution.py:94
  (183 shorter events, 81.2 us)
Async XLA Ops:
  0.7 7.9 %collective-permute-start = (f32[1,2,4,256]{3,2,1,0:T(4,128)S(1)}, f32[1,2,4,256]{3,2,1,0:T(4,128)S(1)}, u32[]{:S(2)}, u32[]{:S(2)}) collective-permute-start(f32[1,2,4,256]{3,2,1,0:T(4,128)S(1)} %get-tuple-element.62), channel_id=1, source_target_pairs={{0,64},{64,128},{128,192},{192,256},{256,320},{320,384},{384,448},... | collective-permute-start | bytes 24584 | tf_op jit(solution)/shard_map/ppermute | solution.py:16
  4.7 4.6 collective-permute-start.1
  9.4 13.5 %collective-permute-start.2 = (f32[4,1,4,256]{3,2,1,0:T(4,128)S(1)}, f32[4,1,4,256]{3,2,1,0:T(4,128)S(1)}, u32[]{:S(2)}, u32[]{:S(2)}) collective-permute-start(f32[4,1,4,256]{3,2,1,0:T(4,128)S(1)} %get-tuple-element.53), channel_id=1, source_target_pairs={{0,16},{16,32},{32,48},{48,0},{1,17},{17,33},{33,49},{49,1},{2,18}... | collective-permute-start | bytes 49160 | tf_op jit(solution)/shard_map/ppermute | solution.py:16
  15.2 8.4 %collective-permute-start.3 = (f32[4,1,4,256]{3,2,1,0:T(4,128)S(1)}, f32[4,1,4,256]{3,2,1,0:T(4,128)S(1)}, u32[]{:S(2)}, u32[]{:S(2)}) collective-permute-start(f32[4,1,4,256]{3,2,1,0:T(4,128)S(1)} %get-tuple-element.54), channel_id=1, source_target_pairs={{16,0},{32,16},{48,32},{0,48},{17,1},{33,17},{49,33},{1,49},{18,2}... | collective-permute-start | bytes 49160 | tf_op jit(solution)/shard_map/ppermute | solution.py:18
  23.6 13.6 %collective-permute-start.4 = (f32[4,4,1,256]{3,2,1,0:T(1,128)S(1)}, f32[4,4,1,256]{3,2,1,0:T(1,128)S(1)}, u32[]{:S(2)}, u32[]{:S(2)}) collective-permute-start(f32[4,4,1,256]{3,2,1,0:T(1,128)S(1)} %get-tuple-element.45), channel_id=1, source_target_pairs={{0,1},{1,2},{2,3},{3,4},{4,5},{5,6},{6,7},{7,8},{8,9},{9,10},{10,1... | collective-permute-start | bytes 49160 | tf_op jit(solution)/shard_map/ppermute | solution.py:16
  29.6 7.6 %collective-permute-start.5 = (f32[4,4,1,256]{3,2,1,0:T(1,128)S(1)}, f32[4,4,1,256]{3,2,1,0:T(1,128)S(1)}, u32[]{:S(2)}, u32[]{:S(2)}) collective-permute-start(f32[4,4,1,256]{3,2,1,0:T(1,128)S(1)} %get-tuple-element.46), channel_id=1, source_target_pairs={{1,0},{2,1},{3,2},{4,3},{5,4},{6,5},{7,6},{8,7},{9,8},{10,9},{11,1... | collective-permute-start | bytes 49160 | tf_op jit(solution)/shard_map/ppermute | solution.py:18
  157.4 6.5 %collective-permute-start.6 = (f32[1,2,4,256]{3,2,1,0:T(4,128)S(1)}, f32[1,2,4,256]{3,2,1,0:T(4,128)S(1)}, u32[]{:S(2)}, u32[]{:S(2)}) collective-permute-start(f32[1,2,4,256]{3,2,1,0:T(4,128)S(1)} %get-tuple-element.59), channel_id=1, source_target_pairs={{0,64},{64,128},{128,192},{192,256},{256,320},{320,384},{384,448},... | collective-permute-start | bytes 24584 | tf_op jit(solution)/shard_map/ppermute | solution.py:16
  160.6 4.4 collective-permute-start.7
  165.0 7.4 %collective-permute-start.8 = (f32[4,1,4,256]{3,2,1,0:T(4,128)S(1)}, f32[4,1,4,256]{3,2,1,0:T(4,128)S(1)}, u32[]{:S(2)}, u32[]{:S(2)}) collective-permute-start(f32[4,1,4,256]{3,2,1,0:T(4,128)S(1)} %get-tuple-element.51), channel_id=1, source_target_pairs={{0,16},{16,32},{32,48},{48,0},{1,17},{17,33},{33,49},{49,1},{2,18}... | collective-permute-start | bytes 49160 | tf_op jit(solution)/shard_map/ppermute | solution.py:16
  168.8 5.6 collective-permute-start.9
  174.5 7.5 %collective-permute-start.10 = (f32[4,4,1,256]{3,2,1,0:T(1,128)S(1)}, f32[4,4,1,256]{3,2,1,0:T(1,128)S(1)}, u32[]{:S(2)}, u32[]{:S(2)}) collective-permute-start(f32[4,4,1,256]{3,2,1,0:T(1,128)S(1)} %get-tuple-element.43), channel_id=1, source_target_pairs={{0,1},{1,2},{2,3},{3,4},{4,5},{5,6},{6,7},{7,8},{8,9},{9,10},{10,1... | collective-permute-start | bytes 49160 | tf_op jit(solution)/shard_map/ppermute | solution.py:16
  179.9 5.1 collective-permute-start.11
  305.5 6.5 %collective-permute-start.12 = (f32[1,2,4,256]{3,2,1,0:T(4,128)S(1)}, f32[1,2,4,256]{3,2,1,0:T(4,128)S(1)}, u32[]{:S(2)}, u32[]{:S(2)}) collective-permute-start(f32[1,2,4,256]{3,2,1,0:T(4,128)S(1)} %get-tuple-element.57), channel_id=1, source_target_pairs={{0,64},{64,128},{128,192},{192,256},{256,320},{320,384},{384,448},... | collective-permute-start | bytes 24584 | tf_op jit(solution)/shard_map/ppermute | solution.py:16
  307.5 5.4 collective-permute-start.13
  312.8 7.4 %collective-permute-start.14 = (f32[4,1,4,256]{3,2,1,0:T(4,128)S(1)}, f32[4,1,4,256]{3,2,1,0:T(4,128)S(1)}, u32[]{:S(2)}, u32[]{:S(2)}) collective-permute-start(f32[4,1,4,256]{3,2,1,0:T(4,128)S(1)} %get-tuple-element.49), channel_id=1, source_target_pairs={{0,16},{16,32},{32,48},{48,0},{1,17},{17,33},{33,49},{49,1},{2,18}... | collective-permute-start | bytes 49160 | tf_op jit(solution)/shard_map/ppermute | solution.py:16
  316.0 5.7 collective-permute-start.15
  321.7 7.7 %collective-permute-start.16 = (f32[4,4,1,256]{3,2,1,0:T(1,128)S(1)}, f32[4,4,1,256]{3,2,1,0:T(1,128)S(1)}, u32[]{:S(2)}, u32[]{:S(2)}) collective-permute-start(f32[4,4,1,256]{3,2,1,0:T(1,128)S(1)} %get-tuple-element.41), channel_id=1, source_target_pairs={{0,1},{1,2},{2,3},{3,4},{4,5},{5,6},{6,7},{7,8},{8,9},{9,10},{10,1... | collective-permute-start | bytes 49160 | tf_op jit(solution)/shard_map/ppermute | solution.py:16
  327.3 5.1 collective-permute-start.17
  454.3 6.5 %collective-permute-start.18 = (f32[1,2,4,256]{3,2,1,0:T(4,128)S(1)}, f32[1,2,4,256]{3,2,1,0:T(4,128)S(1)}, u32[]{:S(2)}, u32[]{:S(2)}) collective-permute-start(f32[1,2,4,256]{3,2,1,0:T(4,128)S(1)} %get-tuple-element.55), channel_id=1, source_target_pairs={{0,64},{64,128},{128,192},{192,256},{256,320},{320,384},{384,448},... | collective-permute-start | bytes 24584 | tf_op jit(solution)/shard_map/ppermute | solution.py:16
  456.2 5.4 collective-permute-start.19
  461.6 7.4 %collective-permute-start.20 = (f32[4,1,4,256]{3,2,1,0:T(4,128)S(1)}, f32[4,1,4,256]{3,2,1,0:T(4,128)S(1)}, u32[]{:S(2)}, u32[]{:S(2)}) collective-permute-start(f32[4,1,4,256]{3,2,1,0:T(4,128)S(1)} %get-tuple-element.47), channel_id=1, source_target_pairs={{0,16},{16,32},{32,48},{48,0},{1,17},{17,33},{33,49},{49,1},{2,18}... | collective-permute-start | bytes 49160 | tf_op jit(solution)/shard_map/ppermute | solution.py:16
  464.7 5.7 collective-permute-start.21
  470.5 9.1 %collective-permute-start.22 = (f32[4,4,1,256]{3,2,1,0:T(1,128)S(1)}, f32[4,4,1,256]{3,2,1,0:T(1,128)S(1)}, u32[]{:S(2)}, u32[]{:S(2)}) collective-permute-start(f32[4,4,1,256]{3,2,1,0:T(1,128)S(1)} %get-tuple-element.39), channel_id=1, source_target_pairs={{0,1},{1,2},{2,3},{3,4},{4,5},{5,6},{6,7},{7,8},{8,9},{9,10},{10,1... | collective-permute-start | bytes 49160 | tf_op jit(solution)/shard_map/ppermute | solution.py:16
  476.1 5.1 collective-permute-start.23
  (21 other events, 1050.0 us)
where the time goes:
time: 609 us; the launch traced here: 606 us
  blocking collectives  404 us (66%)
  starting transfers between devices  92.9 us (15%)
  matrix products  44.7 us (7%)
  local copies, waits for them, and re-layouts  31.8 us (5%)
  other arithmetic  16.1 us (3%)
  waiting for transfers between devices  15.7 us (3%)
    psum x1, blocking collectives, body(): lax.psum(column_dot(quasi_resid, quasi_resid, components), ('gx', 'gy', '...  102 us
    psum x1, blocking collectives, body(): curvature = lax.psum(column_dot(image, rhs, components), ('gx', 'gy', 'gz'))  102 us
    psum x1, blocking collectives, body(): lax.psum((column_dot(quasi_resid, quasi_resid, components), column_dot(qu...  101 us
    psum x1, blocking collectives, body(): inner_now = lax.psum(column_dot(rhs, rhs, components), ('gx', 'gy', 'gz'))  99.6 us
    ppermute x12, starting transfers between devices, with_halo(): lax.ppermute(tail, axis, [(i, (i + 1) % count) for i in range(count)])  49.5 us
    dot_general x4, matrix products, operate(): jnp.einsum('abclkm,abckmr->abclr', coupling, nearby, precision=lax.Precis...  44.7 us
    ppermute x12, starting transfers between devices, with_halo(): lax.ppermute(head, axis, [((i + 1) % count, i) for i in range(count)])  43.4 us
    ppermute x12, waiting for transfers between devices, with_halo(): lax.ppermute(head, axis, [((i + 1) % count, i) for i in range(count)])  15.6 us
  transfers between devices with their start and end apart: 24, of which 10 were waited for; matrix products, arithmetic and copies ran while one was open for 1% of the time, Pallas kernels for 0%

commit v1 on v0

v1 whole, which is shorter than its diff:
```python
import jax
import jax.numpy as jnp
from jax import lax
from jax.experimental import pallas as pl
from jax.experimental.pallas import tpu as pltpu
from jax.sharding import PartitionSpec as P

ITERS = 2
DEGREE = 2 * ITERS
SHIFT = 2.0
LANES = 128
PAIRS = [(i, j) for i in range(DEGREE + 1) for j in range(i, DEGREE + 1)]
VMEM = pl.BlockSpec(memory_space=pltpu.VMEM)


def two_sum(a, b):
    total = a + b
    part = total - a
    return total, (a - (total - part)) + (b - part)


def quick_sum(a, b):
    total = a + b
    return total, b - (total - a)


def split(a):
    scaled = 4097.0 * a
    head = scaled - (scaled - a)
    return head, a - head


def two_prod(a, b):
    product = a * b
    a_head, a_tail = split(a)
    b_head, b_tail = split(b)
    rest = ((a_head * b_head - product) + a_head * b_tail + a_tail * b_head) + a_tail * b_tail
    return product, rest


def pair_add(a, b):
    head, tail = two_sum(a[0], b[0])
    return quick_sum(head, tail + (a[1] + b[1]))


def pair_mul(a, b):
    head, tail = two_prod(a[0], b[0])
    return quick_sum(head, tail + (a[0] * b[1] + a[1] * b[0]))


def pair_scale(a, factor):
    head, tail = two_prod(a[0], factor)
    return quick_sum(head, tail + a[1] * factor)


def roll_pair(a, amount, axis):
    return pltpu.roll(a[0], amount, axis), pltpu.roll(a[1], amount, axis)


def iota(shape, axis):
    return lax.broadcasted_iota(jnp.int32, shape, axis)


def gram_kernel(fields, out):
    columns = 16
    diagonal_mask = iota((8, LANES), 0) == iota((8, LANES), 1) // columns
    rows = []
    parts = [split(field) for field in fields]
    for i, j in PAIRS:
        product = fields[i] * fields[j]
        (a_head, a_tail), (b_head, b_tail) = parts[i], parts[j]
        rest = ((a_head * b_head - product) + a_head * b_tail + a_tail * b_head) + a_tail * b_tail
        pieces = [
            (product[s : s + 8, t : t + LANES], rest[s : s + 8, t : t + LANES])
            for s in range(0, product.shape[0], 8)
            for t in range(0, product.shape[1], LANES)
        ]
        while len(pieces) > 1:
            pieces = [pair_add(pieces[q], pieces[q + 1]) for q in range(0, len(pieces), 2)]
        total = pieces[0]
        for amount in (4, 2, 1):
            total = pair_add(total, roll_pair(total, amount, 0))
        rows.append((total[0][0:1], total[1][0:1]))
    rows += [(jnp.zeros((1, LANES), jnp.float32),) * 2] * (16 - len(rows))
    packed = [[], []]
    for start in (0, 8):
        total = tuple(
            jnp.concatenate([row[part] for row in rows[start : start + 8]], axis=0)
            for part in (0, 1)
        )
        for amount in (64, 32, 16):
            total = pair_add(total, roll_pair(total, amount, 1))
        for part in (0, 1):
            packed[part].append(
                jnp.sum(jnp.where(diagonal_mask, total[part], 0.0), axis=0, keepdims=True)
            )
    message = jnp.concatenate(packed[0] + packed[1], axis=0)
    for q in range(out.shape[0]):
        out[q] = message


def sum_messages(ref):
    terms = [(ref[q], None) for q in range(ref.shape[0])]
    while len(terms) > 1:
        merged = []
        for q in range(0, len(terms), 2):
            (a, a_rest), (b, b_rest) = terms[q], terms[q + 1]
            total, rest = two_sum(a, b)
            if a_rest is not None:
                rest = rest + (a_rest + b_rest)
            merged.append((total, rest))
        terms = merged
    total, rest = terms[0]
    return quick_sum(total[0:2], rest[0:2] + (total[2:4] + rest[2:4]))


def relay_kernel(ref, out):
    head, tail = sum_messages(ref)
    message = jnp.concatenate([head, tail], axis=0)
    for q in range(out.shape[0]):
        out[q] = message


def finish_kernel(ref, *refs):
    fields, out = refs[:-1], refs[-1]
    columns = 16
    shape = (8, LANES)
    row = iota(shape, 0)
    diagonal_mask = row == iota(shape, 1) // columns
    packed = sum_messages(ref)
    unpacked = []
    for part in (0, 1):
        halves = []
        for half in (0, 1):
            value = jnp.where(
                diagonal_mask, jnp.broadcast_to(packed[part][half : half + 1], shape), 0.0
            )
            for amount in (64, 32, 16):
                value = value + pltpu.roll(value, amount, 1)
            halves.append(value)
        unpacked.append(halves)

    def entry(part, i, j):
        place = PAIRS.index((min(i, j), max(i, j)))
        half = unpacked[part][place // 8]
        return jnp.broadcast_to(half[place % 8 : place % 8 + 1], shape)

    gram = []
    for j in range(DEGREE + 1):
        column = []
        for part in (0, 1):
            value = jnp.zeros(shape, jnp.float32)
            for i in range(DEGREE + 1):
                value = jnp.where(row == i, entry(part, i, j), value)
            column.append(value)
        gram.append(tuple(column))

    def total_rows(a):
        for amount in (4, 2, 1):
            a = pair_add(a, roll_pair(a, amount, 0))
        return a[0]

    def with_start(a):
        return total_rows(pair_mul(gram[0], a))

    def square(a, degree):
        acc = None
        for j in range(degree + 1):
            factor = tuple(jnp.broadcast_to(part[j : j + 1], shape) for part in a)
            term = pair_mul(gram[j], factor)
            acc = term if acc is None else pair_add(acc, term)
        return total_rows(pair_mul(acc, a))

    def apply(a):
        return pair_add((SHIFT * a[0], SHIFT * a[1]), roll_pair(a, 1, 0))

    def shrink(quasi_norm, ratio, step):
        damping = 1.0 / (1.0 + ratio * ratio)
        return quasi_norm * ratio * jnp.sqrt(damping), damping * step

    zero = jnp.zeros(shape, jnp.float32)
    start = (jnp.where(row == 0, 1.0, 0.0), zero)
    inner = entry(0, 0, 0)
    quasi_norm = jnp.sqrt(inner)
    image = apply(start)
    resid = search = start
    direction = total = (zero, zero)
    ratio = weight = zero
    for iteration in range(ITERS):
        step = inner / with_start(image)
        resid = pair_add(resid, pair_scale(image, -step))
        direction = pair_add(search, pair_scale(direction, ratio * ratio * weight / step))
        ratio = jnp.sqrt(square(resid, 2 * iteration + 1)) / quasi_norm
        quasi_norm, weight = shrink(quasi_norm, ratio, step)
        total = pair_add(total, pair_scale(direction, weight))
        search_odd = pair_add(search, pair_scale(image, -step))
        image_odd = apply(search_odd)
        resid = pair_add(resid, pair_scale(image_odd, -step))
        direction = pair_add(search_odd, pair_scale(direction, ratio * ratio * weight / step))
        ratio = jnp.sqrt(square(resid, 2 * iteration + 2)) / quasi_norm
        quasi_norm, weight = shrink(quasi_norm, ratio, step)
        total = pair_add(total, pair_scale(direction, weight))
        if iteration + 1 < ITERS:
            inner_next = with_start(resid)
            mix = inner_next / inner
            search = pair_add(resid, pair_scale(search_odd, mix))
            image = pair_add(
                apply(search), pair_scale(pair_add(image_odd, pair_scale(image, mix)), mix)
            )
            inner = inner_next
    coefficients = total[0] + total[1]
    height, width = out.shape
    acc = None
    for i, field in enumerate(fields):
        factor = jnp.broadcast_to(coefficients[i : i + 1], (height, LANES))
        factor = jnp.concatenate([factor] * (width // LANES), axis=1)
        term = factor * field[...]
        acc = term if acc is None else acc + term
    out[...] = acc


SLOT_ROWS = 16
WIDE = 512
SELF = 27
CODE = 448
REACH = 3
HIGH = lax.Precision.HIGHEST


def third_of(value):
    return (value * 11) >> 5


def offsets_of(code):
    first = (code * 57) >> 9
    rest = code - 9 * first
    second = third_of(rest)
    return first - 1, second - 1, rest - 3 * second - 1


def far_atom(row):
    column = (row * 205) >> 11
    return 1 + (column >> 1), 1 + (column & 1), row - 10 * column - 3


def near_atom(row):
    column = row >> 3
    return column >> 1, column & 1, (row & 7) - 2


def bricks_place(x, y, z):
    brick = ((z + 4) >> 2) * 4 + (x >> 1) * 2 + (y >> 1)
    return (brick * 2 + (x & 1)) * 8 + (y & 1) * 4 + ((z + 4) & 3)


def pieces_place(origin, run, low):
    def place(x, y, z):
        x, y = x - origin, y - origin
        piece = (x >> 1) * 2 + (y >> 1)
        return (piece * 4 + (x & 1) * 2 + (y & 1)) * run + z - low

    return place


def find_places(matrix, count, atom, place, staged, places, sem):
    rows = [q * SLOT_ROWS for q in range(count)]
    code = jnp.concatenate([matrix[row : row + 1, CODE - 64 : CODE + 64] for row in rows], axis=0)
    code = pltpu.roll(code, 64, 1).astype(jnp.int32)
    x, y, z = atom(iota(code.shape, 0))
    dx, dy, dz = offsets_of(code)
    staged[...] = place(x + dx, y + dy, z + dz)
    copy = pltpu.make_async_copy(staged, places, sem)
    copy.start()
    copy.wait()


def couple(matrix, groups, field, places, gathered):
    lane_slot = iota((SLOT_ROWS, LANES), 1) >> 4
    gathered[pl.ds(CODE, WIDE - CODE), :] = jnp.zeros((WIDE - CODE, LANES), jnp.float32)
    tiles = []
    for group in groups:

        def gather(k, carry):
            acc = None
            for slot, atom in enumerate(group):
                place = places[atom, k]
                tile = pltpu.roll(field[place >> 3], ((slot - place) & 7) * SLOT_ROWS, 1)
                acc = tile if acc is None else jnp.where(lane_slot == slot, tile, acc)
            gathered[pl.ds(pl.multiple_of(k * SLOT_ROWS, SLOT_ROWS), SLOT_ROWS), :] = acc
            return carry

        lax.fori_loop(0, SELF + 1, gather, 0)
        left, start = [], 0
        for q in range(1, 9):
            if q == 8 or group[q] != group[q - 1] + 1:
                left.append(matrix[group[start] * SLOT_ROWS : (group[q - 1] + 1) * SLOT_ROWS, :])
                start = q
        left = left[0] if len(left) == 1 else jnp.concatenate(left, axis=0)
        product = jnp.dot(
            left, gathered[...], precision=HIGH, preferred_element_type=jnp.float32
        )
        acc = product[0:SLOT_ROWS]
        for slot in range(1, 8):
            piece = product[slot * SLOT_ROWS : (slot + 1) * SLOT_ROWS]
            acc = jnp.where(lane_slot == slot, piece, acc)
        tiles.append(-acc)
    return tiles


def pick_own(field, place):
    lane_slot = iota((SLOT_ROWS, LANES), 1) >> 4
    tiles = []
    for x in (0, 1):
        acc = None
        for slot in range(8):
            where = place(x, slot >> 2, slot & 3)
            tile = field[where >> 3]
            amount = ((slot - where) & 7) * SLOT_ROWS
            tile = pltpu.roll(tile, amount, 1) if amount else tile
            acc = tile if acc is None else jnp.where(lane_slot == slot, tile, acc)
        tiles.append(acc)
    return jnp.concatenate(tiles, axis=1)


def pack_bricks(field):
    return jnp.concatenate([field[0:8], field[8:16]], axis=1)


def pack_kernel(blocks, diagonal, codes, start, matrix, to_x, to_y, to_xy):
    matrix[:, 0:432] = blocks[...]
    matrix[:, 432:WIDE] = jnp.zeros((matrix.shape[0], WIDE - 432), jnp.float32)
    eye = iota((SLOT_ROWS, SLOT_ROWS), 0) == iota((SLOT_ROWS, SLOT_ROWS), 1)
    for x in range(2):
        for y in range(2):
            for z in range(4):
                row = ((x * 2 + y) * 4 + z) * SLOT_ROWS
                own = SHIFT - jnp.broadcast_to(diagonal[x, y, z : z + 1], eye.shape)
                matrix[row : row + SLOT_ROWS, 432:448] = jnp.where(eye, own, 0.0)
                matrix[row : row + 1, CODE : CODE + SELF] = codes[x, y, z : z + 1]
                matrix[row : row + 1, CODE + SELF : CODE + SELF + 1] = jnp.full(
                    (1, 1), 13.0, jnp.float32
                )
    bricks = pack_bricks(start[...])
    for out, row in ((to_x, 64), (to_y, 128), (to_xy, 0)):
        out[0:64] = matrix[row : row + 64]
        out[64:72] = bricks


def spread_kernel(matrix, from_x, from_y, from_xy, start, up, down):
    far = ((matrix, 192), (from_y, 0), (from_x, 0), (from_xy, 0))
    for q, (ref, row) in enumerate(far):
        up[q * 48 : q * 48 + 48] = ref[row + 16 : row + 64]
        down[q * 48 : q * 48 + 48] = ref[row : row + 48]
    for q in range(3):
        up[192 + q * 32 : 224 + q * 32] = matrix[q * 64 + 32 : q * 64 + 64]
        down[192 + q * 32 : 224 + q * 32] = matrix[q * 64 : q * 64 + 32]
    bricks = [pack_bricks(start[...])] + [ref[64:72] for ref in (from_y, from_x, from_xy)]
    for q, brick in enumerate(bricks):
        up[288 + q * 8 : 296 + q * 8] = brick
        down[288 + q * 8 : 296 + q * 8] = brick


def far_kernel(
    matrix, from_x, from_y, from_xy, start, low, high,
    out, wide, field, gathered, staged, places, sem,
):
    for q, (ref, row) in enumerate(
        ((matrix, 192), (from_y, 0), (from_x, 0), (from_xy, 0))
    ):
        wide[q * 160 : q * 160 + 48] = low[q * 48 : q * 48 + 48]
        wide[q * 160 + 48 : q * 160 + 112] = ref[row : row + 64]
        wide[q * 160 + 112 : q * 160 + 160] = high[q * 48 : q * 48 + 48]
    bricks = [low[288 + q * 8 : 296 + q * 8] for q in range(4)]
    bricks += [pack_bricks(start[...])] + [ref[64:72] for ref in (from_y, from_x, from_xy)]
    bricks += [high[288 + q * 8 : 296 + q * 8] for q in range(4)]
    for q, brick in enumerate(bricks):
        for half in (0, 1):
            for part in (0, 1):
                lanes = brick[:, (part * 2 + half) * LANES : (part * 2 + half + 1) * LANES]
                field[q * 2 + half, part * 8 : part * 8 + 8] = lanes
    find_places(wide, 40, far_atom, bricks_place, staged, places, sem)
    groups = [list(range(q * 8, q * 8 + 8)) for q in range(5)]
    for q, tile in enumerate(couple(wide, groups, field, places, gathered)):
        out[:, q * LANES : (q + 1) * LANES] = tile


def near_matrix_kernel(matrix, low, high, out):
    for q in range(4):
        lo, hi = (192 + q * 32, 192 + q * 32) if q < 3 else (16, 0)
        out[q * 128 : q * 128 + 32] = low[lo : lo + 32]
        out[q * 128 + 32 : q * 128 + 96] = matrix[q * 64 : q * 64 + 64]
        out[q * 128 + 96 : q * 128 + 128] = high[hi : hi + 32]


def load_pieces(pieces, field):
    count = pieces[0].shape[1] // LANES
    for q, piece in enumerate(pieces):
        for t in range(count):
            field[q * count + t] = piece[:, t * LANES : (t + 1) * LANES]


def second_kernel(
    matrix, own, from_x, from_y, from_xy, out, first_own, second_own,
    field, gathered, staged, places, sem,
):
    place = pieces_place(-1, 10, -3)
    load_pieces((from_xy, from_x, from_y, own), field)
    find_places(matrix, 32, near_atom, place, staged, places, sem)
    groups = [list(range(q * 8, q * 8 + 8)) for q in range(4)]
    tiles = couple(matrix, groups, field, places, gathered)
    for q, tile in enumerate(tiles):
        out[:, q * LANES : (q + 1) * LANES] = tile
    first_own[...] = pick_own(field, place)
    second_own[...] = pick_own(tiles, lambda x, y, z: (x * 2 + y) * 8 + z + 2)


def third_kernel(
    matrix, own, from_x, from_y, from_xy, out, field, gathered, staged, places, sem
):
    load_pieces((own, from_y, from_x, from_xy), field)
    find_places(matrix, 40, far_atom, pieces_place(0, 8, -2), staged, places, sem)
    atoms = [c * 10 + z + 3 for c in range(4) for z in range(-1, 5)]
    groups = [atoms[q * 8 : q * 8 + 8] for q in range(3)]
    for q, tile in enumerate(couple(matrix, groups, field, places, gathered)):
        out[:, q * LANES : (q + 1) * LANES] = tile


def fourth_kernel(
    matrix, own, from_x, from_y, from_xy, start, first, second, third_own, out,
    field, gathered, staged, places, sem,
):
    place = pieces_place(-1, 6, -1)
    load_pieces((from_xy, from_x, from_y, own), field)
    find_places(matrix, 32, near_atom, place, staged, places, sem)
    atoms = [c * 8 + z + 2 for c in range(4) for z in range(4)]
    groups = [atoms[q * 8 : q * 8 + 8] for q in range(2)]
    fourth = jnp.concatenate(couple(matrix, groups, field, places, gathered), axis=1)
    third = pick_own(field, place)
    third_own[...] = third
    gram_kernel([start[...], first[...], second[...], third, fourth], out)


def call(kernel, shapes, *operands, scratch=()):
    shapes = [jax.ShapeDtypeStruct(shape, jnp.float32) for shape in shapes]
    out = pl.pallas_call(
        kernel,
        out_shape=shapes,
        in_specs=[VMEM] * len(operands),
        out_specs=[VMEM] * len(shapes),
        scratch_shapes=list(scratch),
        compiler_params=pltpu.CompilerParams(vmem_limit_bytes=32 * 1024 * 1024),
    )(*operands)
    return out


def scratch_for(tiles, rows):
    return (
        pltpu.VMEM((tiles, SLOT_ROWS, LANES), jnp.float32),
        pltpu.VMEM((WIDE, LANES), jnp.float32),
        pltpu.VMEM((rows, LANES), jnp.int32),
        pltpu.SMEM((rows, LANES), jnp.int32),
        pltpu.SemaphoreType.DMA,
    )


def fetch(value, first, second, third):
    axes = ("gx", "gy", "gz")
    sizes = [lax.axis_size(axis) for axis in axes]
    pairs = []
    for a in range(sizes[0]):
        for b in range(sizes[1]):
            for c in range(sizes[2]):
                near = (a + first) % sizes[0], (b + second) % sizes[1], (c + third) % sizes[2]
                source = (near[0] * sizes[1] + near[1]) * sizes[2] + near[2]
                pairs.append((source, (a * sizes[1] + b) * sizes[2] + c))
    return lax.ppermute(value, axes, pairs)


def fetch_three(to_x, to_y, to_xy, sign):
    return fetch(to_x, sign, 0, 0), fetch(to_y, 0, sign, 0), fetch(to_xy, sign, sign, 0)


def body(rhs, diagonal, blocks, neighbours):
    first_len, second_len, third_len, width = rhs.shape
    components = diagonal.shape[-1]
    columns = width // components
    lengths = (first_len, second_len, third_len)
    totals = [n * lax.axis_size(axis) for n, axis in zip(lengths, ("gx", "gy", "gz"))]
    coords = (
        neighbours // (totals[1] * totals[2]),
        neighbours // totals[2] % totals[1],
        neighbours % totals[2],
    )
    codes = 0
    for dim, axis in enumerate(("gx", "gy", "gz")):
        here = iota(neighbours.shape, dim) + lax.axis_index(axis) * lengths[dim]
        codes = codes * 3 + (coords[dim] - here + 1 + totals[dim]) % totals[dim]
    codes = codes.astype(jnp.float32)
    atoms = first_len * second_len * third_len
    start = rhs.reshape(atoms, components, columns).transpose(1, 0, 2).reshape(components, -1)

    matrix, *out = call(
        pack_kernel,
        [(atoms * SLOT_ROWS, WIDE)] + [(72, WIDE)] * 3,
        blocks.reshape(atoms * components, -1),
        diagonal,
        codes,
        start,
    )
    sides = fetch_three(*out, 1)
    up, down = call(spread_kernel, [(320, WIDE)] * 2, matrix, *sides, start)
    low, high = fetch(up, 0, 0, -1), fetch(down, 0, 0, 1)
    first, far_matrix = call(
        far_kernel,
        [(components, 5 * LANES), (640, WIDE)],
        matrix, *sides, start, low, high,
        scratch=scratch_for(24, 40),
    )
    (near_matrix,) = call(near_matrix_kernel, [(512, WIDE)], matrix, low, high)
    second, first_own, second_own = call(
        second_kernel,
        [(components, 4 * LANES)] + [(components, width)] * 2,
        near_matrix, first, *fetch_three(first, first, first, -1),
        scratch=scratch_for(20, 32),
    )
    (third,) = call(
        third_kernel,
        [(components, 3 * LANES)],
        far_matrix, second, *fetch_three(second, second, second, 1),
        scratch=scratch_for(16, 40),
    )
    third_own, message = call(
        fourth_kernel,
        [(components, width), (lax.axis_size("gx"), 4, LANES)],
        near_matrix, third, *fetch_three(third, third, third, -1), start, first_own, second_own,
        scratch=scratch_for(12, 32),
    )
    rest = lax.axis_size("gy") * lax.axis_size("gz")
    message = lax.all_to_all(message, "gx", 0, 0, tiled=True)
    (message,) = call(relay_kernel, [(rest, 4, LANES)], message)
    message = lax.all_to_all(message, ("gy", "gz"), 0, 0, tiled=True)
    (result,) = call(
        finish_kernel, [start.shape], message, start, first_own, second_own, third_own
    )
    result = result.reshape(components, atoms, columns).transpose(1, 0, 2)
    return result.reshape(rhs.shape)


def solution(mesh):
    return jax.shard_map(
        body,
        mesh=mesh,
        in_specs=(
            P("gx", "gy", "gz", None),
            P("gx", "gy", "gz", None),
            P("gx", "gy", "gz", None, None),
            P("gx", "gy", "gz", None),
        ),
        out_specs=P("gx", "gy", "gz", None),
        check_vma=False,
    )
```

time: 609 us -> 174 us (0.29)
  blocking collectives: 404 us -> 35.2 us
  Pallas kernels: 0 us -> 44.9 us
  matrix products: 44.7 us -> 0 us
  starting transfers between devices: 92.9 us -> 53.6 us
  local copies, waits for them, and re-layouts: 31.8 us -> 3.56 us
  waiting for transfers between devices: 15.7 us -> 34.7 us
  other arithmetic: 16.1 us -> 0.8 us
    psum x4 -> x0, blocking collectives: 404 us -> none  [the longest x1 102 us: body(): lax.psum(column_dot(quasi_resid, quasi_resid, components), ('gx', 'gy', '...]
    pallas_call x0 -> x9, Pallas kernels: none -> 44.9 us  [call(): pl.pallas_call(kernel, out_shape=shapes, in_specs=[VMEM] * len(operands),...]
    dot_general x4 -> x0, matrix products: 44.7 us -> none  [operate(): jnp.einsum('abclkm,abckmr->abclr', coupling, nearby, precision=lax.Precis...]
    ppermute x24 -> x14, starting transfers between devices: 92.9 us -> 53.6 us  [fetch(): return lax.ppermute(value, axes, pairs)]
    all_to_all x0 -> x2, blocking collectives: none -> 35.2 us  [the longest x1 24 us: body(): message = lax.all_to_all(message, ('gy', 'gz'), 0, 0, tiled=True)]
    ppermute x24 -> x14, waiting for transfers between devices: 15.7 us -> 34.7 us  [fetch(): return lax.ppermute(value, axes, pairs)]
    reshape x14 -> x5, local copies, waits for them, and re-layouts: 13.8 us -> 1.78 us  [the longest x3 0.97 us: body(): rhs.reshape(atoms, components, columns).transpose(1, 0, 2)]
    gather x8 -> x0, local copies, waits for them, and re-layouts: 7.46 us -> none  [operate(): nearby = jnp.take(flattened, gather_rows, axis=0)]
  transfers between devices with their start and end apart: 24 -> 14, of which waited for: 10 -> 10; matrix products, arithmetic and copies ran while one was open for 1% -> 0% of each run, Pallas kernels for 0% -> 0%
where the time goes in v1:
time: 174 us; the launch traced here: 173 us
  starting transfers between devices  53.6 us (31%)
  Pallas kernels  44.9 us (26%)
  blocking collectives  35.2 us (20%)
  waiting for transfers between devices  34.7 us (20%)
  local copies, waits for them, and re-layouts  3.56 us (2%)
    ppermute x14, starting transfers between devices, fetch(): return lax.ppermute(value, axes, pairs)  53.6 us
    pallas_call x9, Pallas kernels, call(): pl.pallas_call(kernel, out_shape=shapes, in_specs=[VMEM] * len(operands),...  44.9 us
    ppermute x14, waiting for transfers between devices, fetch(): return lax.ppermute(value, axes, pairs)  34.7 us
    all_to_all x1, blocking collectives, body(): message = lax.all_to_all(message, ('gy', 'gz'), 0, 0, tiled=True)  24 us
    all_to_all x1, blocking collectives, body(): message = lax.all_to_all(message, 'gx', 0, 0, tiled=True)  11.2 us
  transfers between devices with their start and end apart: 14, of which 10 were waited for; matrix products, arithmetic and copies ran while one was open for 0% of the time, Pallas kernels for 0%

profile of v1, /device:TPU:1, one launch (start us, length us, event | category | flops | bytes accessed | tf_op | source)
XLA Modules:
  0.0 173.1 jit_solution(17429275921498876104)
XLA Ops:
  3.7 5.9 %collective-permute-start = (f32[72,512]{1,0:T(8,128)S(1)}, f32[72,512]{1,0:T(8,128)S(1)}, u32[]{:S(2)}, u32[]{:S(2)}) collective-permute-start(f32[72,512]{1,0:T(8,128)S(1)} %get-tuple-element.19), channel_id=1, source_target_pairs={{64,0},{65,1},{66,2},{67,3},{68,4},{69,5},{70,6},{71,7},{72,8},{73... | collective-permute-start | bytes 442376 | tf_op jit(solution)/shard_map/ppermute | solution.py:476
  9.6 10.7 %collective-permute-start.1 = (f32[72,512]{1,0:T(8,128)S(1)}, f32[72,512]{1,0:T(8,128)S(1)}, u32[]{:S(2)}, u32[]{:S(2)}) collective-permute-start(f32[72,512]{1,0:T(8,128)S(1)} %get-tuple-element.20), channel_id=1, source_target_pairs={{16,0},{17,1},{18,2},{19,3},{20,4},{21,5},{22,6},{23,7},{24,8},{25... | collective-permute-start | bytes 442376 | tf_op jit(solution)/shard_map/ppermute | solution.py:476
  20.3 3.0 %collective-permute-start.2 = (f32[72,512]{1,0:T(8,128)S(1)}, f32[72,512]{1,0:T(8,128)S(1)}, u32[]{:S(2)}, u32[]{:S(2)}) collective-permute-start(f32[72,512]{1,0:T(8,128)S(1)} %get-tuple-element.21), channel_id=1, source_target_pairs={{80,0},{81,1},{82,2},{83,3},{84,4},{85,5},{86,6},{87,7},{88,8},{89... | collective-permute-start | bytes 442376 | tf_op jit(solution)/shard_map/ppermute | solution.py:476
  23.3 8.1 %collective-permute-done.1.from_y = f32[72,512]{1,0:T(8,128)S(1)} collective-permute-done((f32[72,512]{1,0:T(8,128)S(1)}, f32[72,512]{1,0:T(8,128)S(1)}, u32[]{:S(2)}, u32[]{:S(2)}) %collective-permute-start.1) | collective-permute-done | bytes 147488 | tf_op jit(solution)/shard_map/ppermute | solution.py:476
  31.4 4.1 %collective-permute-start.3 = (f32[320,512]{1,0:T(8,128)S(1)}, f32[320,512]{1,0:T(8,128)S(1)}, u32[]{:S(2)}, u32[]{:S(2)}) collective-permute-start(f32[320,512]{1,0:T(8,128)S(1)} %get-tuple-element.22), channel_id=1, source_target_pairs={{15,0},{0,1},{1,2},{2,3},{3,4},{4,5},{5,6},{6,7},{7,8},{8,9},{9,10... | collective-permute-start | bytes 1966088 | tf_op jit(solution)/shard_map/ppermute | solution.py:476
  35.6 2.2 %collective-permute-start.4 = (f32[320,512]{1,0:T(8,128)S(1)}, f32[320,512]{1,0:T(8,128)S(1)}, u32[]{:S(2)}, u32[]{:S(2)}) collective-permute-start(f32[320,512]{1,0:T(8,128)S(1)} %get-tuple-element.23), channel_id=1, source_target_pairs={{1,0},{2,1},{3,2},{4,3},{5,4},{6,5},{7,6},{8,7},{9,8},{10,9},{11,1... | collective-permute-start | bytes 1966088 | tf_op jit(solution)/shard_map/ppermute | solution.py:476
  37.8 6.1 %collective-permute-done.3.low = f32[320,512]{1,0:T(8,128)S(1)} collective-permute-done((f32[320,512]{1,0:T(8,128)S(1)}, f32[320,512]{1,0:T(8,128)S(1)}, u32[]{:S(2)}, u32[]{:S(2)}) %collective-permute-start.3) | collective-permute-done | bytes 655392 | tf_op jit(solution)/shard_map/ppermute | solution.py:476
  43.9 9.2 %collective-permute-done.4.high = f32[320,512]{1,0:T(8,128)S(1)} collective-permute-done((f32[320,512]{1,0:T(8,128)S(1)}, f32[320,512]{1,0:T(8,128)S(1)}, u32[]{:S(2)}, u32[]{:S(2)}) %collective-permute-start.4) | collective-permute-done | bytes 655392 | tf_op jit(solution)/shard_map/ppermute | solution.py:476
  53.1 15.1 %shard_map.49 = (f32[16,640]{1,0:T(8,128)S(1)}, f32[640,512]{1,0:T(8,128)S(1)}) custom-call(f32[256,512]{1,0:T(8,128)S(1)} %get-tuple-element.18.matrix, f32[72,512]{1,0:T(8,128)S(1)} %collective-permute-done.from_x, f32[72,512]{1,0:T(8,128)S(1)} %collective-permute-done.1.from_y, f32[72,512]{1,0:T(8,128)S(1)} %collective-permute-done.2.from_xy, ...), custom_call_target="tpu_custom_call" | custom-call | tf_op jit(solution)/shard_map/pallas_call | solution.py:445
  68.2 1.9 %collective-permute-start.7 = (f32[16,640]{1,0:T(8,128)S(1)}, f32[16,640]{1,0:T(8,128)S(1)}, u32[]{:S(2)}, u32[]{:S(2)}) collective-permute-start(f32[16,640]{1,0:T(8,128)S(1)} %get-tuple-element.25.own), channel_id=1, source_target_pairs={{496,0},{497,1},{498,2},{499,3},{500,4},{501,5},{502,6},{503,7},{5... | collective-permute-start | bytes 122888 | tf_op jit(solution)/shard_map/ppermute | solution.py:476
  70.2 3.4 %collective-permute-start.6 = (f32[16,640]{1,0:T(8,128)S(1)}, f32[16,640]{1,0:T(8,128)S(1)}, u32[]{:S(2)}, u32[]{:S(2)}) collective-permute-start(f32[16,640]{1,0:T(8,128)S(1)} %get-tuple-element.25.own), channel_id=1, source_target_pairs={{48,0},{49,1},{50,2},{51,3},{52,4},{53,5},{54,6},{55,7},{56,8},{57... | collective-permute-start | bytes 122888 | tf_op jit(solution)/shard_map/ppermute | solution.py:476
  73.5 3.2 %collective-permute-start.5 = (f32[16,640]{1,0:T(8,128)S(1)}, f32[16,640]{1,0:T(8,128)S(1)}, u32[]{:S(2)}, u32[]{:S(2)}) collective-permute-start(f32[16,640]{1,0:T(8,128)S(1)} %get-tuple-element.25.own), channel_id=1, source_target_pairs={{448,0},{449,1},{450,2},{451,3},{452,4},{453,5},{454,6},{455,7},{4... | collective-permute-start | bytes 122888 | tf_op jit(solution)/shard_map/ppermute | solution.py:476
  77.6 2.9 %collective-permute-done.6.from_y = f32[16,640]{1,0:T(8,128)S(1)} collective-permute-done((f32[16,640]{1,0:T(8,128)S(1)}, f32[16,640]{1,0:T(8,128)S(1)}, u32[]{:S(2)}, u32[]{:S(2)}) %collective-permute-start.6) | collective-permute-done | bytes 40992 | tf_op jit(solution)/shard_map/ppermute | solution.py:476
  81.3 12.3 %shard_map.50 = (f32[16,512]{1,0:T(8,128)S(1)}, f32[16,256]{1,0:T(8,128)S(1)}, f32[16,256]{1,0:T(8,128)S(1)}) custom-call(f32[512,512]{1,0:T(8,128)S(1)} %shard_map.48.matrix, f32[16,640]{1,0:T(8,128)S(1)} %get-tuple-element.25.own, f32[16,640]{1,0:T(8,128)S(1)} %collective-permute-done.5.from_x, f32[16,640]{1,0:T(8,128)S(1)} %collective-permute-done.6.from_y, ...), custom_call_target="tpu_custom_call" | custom-call | tf_op jit(solution)/shard_map/pallas_call | solution.py:445
  93.5 4.4 %collective-permute-start.10 = (f32[16,512]{1,0:T(8,128)S(1)}, f32[16,512]{1,0:T(8,128)S(1)}, u32[]{:S(2)}, u32[]{:S(2)}) collective-permute-start(f32[16,512]{1,0:T(8,128)S(1)} %get-tuple-element.26.own), channel_id=1, source_target_pairs={{80,0},{81,1},{82,2},{83,3},{84,4},{85,5},{86,6},{87,7},{88,8},{89... | collective-permute-start | bytes 98312 | tf_op jit(solution)/shard_map/ppermute | solution.py:476
  98.0 4.1 %collective-permute-start.9 = (f32[16,512]{1,0:T(8,128)S(1)}, f32[16,512]{1,0:T(8,128)S(1)}, u32[]{:S(2)}, u32[]{:S(2)}) collective-permute-start(f32[16,512]{1,0:T(8,128)S(1)} %get-tuple-element.26.own), channel_id=1, source_target_pairs={{16,0},{17,1},{18,2},{19,3},{20,4},{21,5},{22,6},{23,7},{24,8},{25... | collective-permute-start | bytes 98312 | tf_op jit(solution)/shard_map/ppermute | solution.py:476
  102.1 1.9 %collective-permute-start.8 = (f32[16,512]{1,0:T(8,128)S(1)}, f32[16,512]{1,0:T(8,128)S(1)}, u32[]{:S(2)}, u32[]{:S(2)}) collective-permute-start(f32[16,512]{1,0:T(8,128)S(1)} %get-tuple-element.26.own), channel_id=1, source_target_pairs={{64,0},{65,1},{66,2},{67,3},{68,4},{69,5},{70,6},{71,7},{72,8},{73... | collective-permute-start | bytes 98312 | tf_op jit(solution)/shard_map/ppermute | solution.py:476
  104.1 2.7 %collective-permute-done.8.from_x = f32[16,512]{1,0:T(8,128)S(1)} collective-permute-done((f32[16,512]{1,0:T(8,128)S(1)}, f32[16,512]{1,0:T(8,128)S(1)}, u32[]{:S(2)}, u32[]{:S(2)}) %collective-permute-start.8) | collective-permute-done | bytes 32800 | tf_op jit(solution)/shard_map/ppermute | solution.py:476
  106.8 9.5 %shard_map.51.own = f32[16,384]{1,0:T(8,128)S(1)} custom-call(f32[640,512]{1,0:T(8,128)S(1)} %get-tuple-element.24.matrix, f32[16,512]{1,0:T(8,128)S(1)} %get-tuple-element.26.own, f32[16,512]{1,0:T(8,128)S(1)} %collective-permute-done.8.from_x, f32[16,512]{1,0:T(8,128)S(1)} %collective-permute-done.9.from_y, f32[16,512]{1,0:T(8,128)S(1)} %collective-permute-done.10.from_xy), custom_call_target="tpu_custom_call" | custom-call | tf_op jit(solution)/shard_map/pallas_call | solution.py:445
  118.2 5.0 %collective-permute-start.12 = (f32[16,384]{1,0:T(8,128)S(1)}, f32[16,384]{1,0:T(8,128)S(1)}, u32[]{:S(2)}, u32[]{:S(2)}) collective-permute-start(f32[16,384]{1,0:T(8,128)S(1)} %shard_map.51.own), channel_id=1, source_target_pairs={{48,0},{49,1},{50,2},{51,3},{52,4},{53,5},{54,6},{55,7},{56,8},{57... | collective-permute-start | bytes 73736 | tf_op jit(solution)/shard_map/ppermute | solution.py:476
  125.5 3.7 %collective-permute-done.11.from_x = f32[16,384]{1,0:T(8,128)S(1)} collective-permute-done((f32[16,384]{1,0:T(8,128)S(1)}, f32[16,384]{1,0:T(8,128)S(1)}, u32[]{:S(2)}, u32[]{:S(2)}) %collective-permute-start.11) | collective-permute-done | bytes 24608 | tf_op jit(solution)/shard_map/ppermute | solution.py:476
  129.3 7.0 %shard_map.52 = (f32[16,256]{1,0:T(8,128)S(1)}, f32[8,4,128]{2,1,0:T(4,128)S(1)}) custom-call(f32[512,512]{1,0:T(8,128)S(1)} %shard_map.48.matrix, f32[16,384]{1,0:T(8,128)S(1)} %shard_map.51.own, f32[16,384]{1,0:T(8,128)S(1)} %collective-permute-done.11.from_x, f32[16,384]{1,0:T(8,128)S(1)} %collective-permute-done.12.from_y, ...), custom_call_target="tpu_custom_call" | custom-call | tf_op jit(solution)/shard_map/pallas_call | solution.py:445
  136.3 11.2 %all_to_all.10.ref = f32[8,4,128]{2,1,0:T(4,128)S(1)} all-to-all(f32[8,4,128]{2,1,0:T(4,128)S(1)} %get-tuple-element.29), channel_id=1, replica_groups=mesh['gx'=8,'gy'=4,'gz'=16] {'gx'}, dimensions={0} | all-to-all | bytes 32768 | tf_op jit(solution)/shard_map/all_to_all | solution.py:539
  147.5 24.0 %all_to_all.11.ref = f32[64,4,128]{2,1,0:T(4,128)S(1)} all-to-all(f32[64,4,128]{2,1,0:T(4,128)S(1)} %shard_map.53), channel_id=1, replica_groups=mesh['gx'=8,'gy'=4,'gz'=16] {'gy','gz'}, dimensions={0} | all-to-all | bytes 262144 | tf_op jit(solution)/shard_map/all_to_all | solution.py:541
  (28 shorter events, 11.2 us)
Async XLA Ops:
  1.8 1.0 copy-start
  2.8 0.7 copy-start.1
  3.7 19.6 %collective-permute-start = (f32[72,512]{1,0:T(8,128)S(1)}, f32[72,512]{1,0:T(8,128)S(1)}, u32[]{:S(2)}, u32[]{:S(2)}) collective-permute-start(f32[72,512]{1,0:T(8,128)S(1)} %get-tuple-element.19), channel_id=1, source_target_pairs={{64,0},{65,1},{66,2},{67,3},{68,4},{69,5},{70,6},{71,7},{72,8},{73... | collective-permute-start | bytes 442376 | tf_op jit(solution)/shard_map/ppermute | solution.py:476
  9.6 21.7 %collective-permute-start.1 = (f32[72,512]{1,0:T(8,128)S(1)}, f32[72,512]{1,0:T(8,128)S(1)}, u32[]{:S(2)}, u32[]{:S(2)}) collective-permute-start(f32[72,512]{1,0:T(8,128)S(1)} %get-tuple-element.20), channel_id=1, source_target_pairs={{16,0},{17,1},{18,2},{19,3},{20,4},{21,5},{22,6},{23,7},{24,8},{25... | collective-permute-start | bytes 442376 | tf_op jit(solution)/shard_map/ppermute | solution.py:476
  20.3 11.1 %collective-permute-start.2 = (f32[72,512]{1,0:T(8,128)S(1)}, f32[72,512]{1,0:T(8,128)S(1)}, u32[]{:S(2)}, u32[]{:S(2)}) collective-permute-start(f32[72,512]{1,0:T(8,128)S(1)} %get-tuple-element.21), channel_id=1, source_target_pairs={{80,0},{81,1},{82,2},{83,3},{84,4},{85,5},{86,6},{87,7},{88,8},{89... | collective-permute-start | bytes 442376 | tf_op jit(solution)/shard_map/ppermute | solution.py:476
  31.4 12.4 %collective-permute-start.3 = (f32[320,512]{1,0:T(8,128)S(1)}, f32[320,512]{1,0:T(8,128)S(1)}, u32[]{:S(2)}, u32[]{:S(2)}) collective-permute-start(f32[320,512]{1,0:T(8,128)S(1)} %get-tuple-element.22), channel_id=1, source_target_pairs={{15,0},{0,1},{1,2},{2,3},{3,4},{4,5},{5,6},{6,7},{7,8},{8,9},{9,10... | collective-permute-start | bytes 1966088 | tf_op jit(solution)/shard_map/ppermute | solution.py:476
  35.6 17.5 %collective-permute-start.4 = (f32[320,512]{1,0:T(8,128)S(1)}, f32[320,512]{1,0:T(8,128)S(1)}, u32[]{:S(2)}, u32[]{:S(2)}) collective-permute-start(f32[320,512]{1,0:T(8,128)S(1)} %get-tuple-element.23), channel_id=1, source_target_pairs={{1,0},{2,1},{3,2},{4,3},{5,4},{6,5},{7,6},{8,7},{9,8},{10,9},{11,1... | collective-permute-start | bytes 1966088 | tf_op jit(solution)/shard_map/ppermute | solution.py:476
  68.2 9.4 %collective-permute-start.7 = (f32[16,640]{1,0:T(8,128)S(1)}, f32[16,640]{1,0:T(8,128)S(1)}, u32[]{:S(2)}, u32[]{:S(2)}) collective-permute-start(f32[16,640]{1,0:T(8,128)S(1)} %get-tuple-element.25.own), channel_id=1, source_target_pairs={{496,0},{497,1},{498,2},{499,3},{500,4},{501,5},{502,6},{503,7},{5... | collective-permute-start | bytes 122888 | tf_op jit(solution)/shard_map/ppermute | solution.py:476
  70.2 10.3 %collective-permute-start.6 = (f32[16,640]{1,0:T(8,128)S(1)}, f32[16,640]{1,0:T(8,128)S(1)}, u32[]{:S(2)}, u32[]{:S(2)}) collective-permute-start(f32[16,640]{1,0:T(8,128)S(1)} %get-tuple-element.25.own), channel_id=1, source_target_pairs={{48,0},{49,1},{50,2},{51,3},{52,4},{53,5},{54,6},{55,7},{56,8},{57... | collective-permute-start | bytes 122888 | tf_op jit(solution)/shard_map/ppermute | solution.py:476
  73.5 7.7 %collective-permute-start.5 = (f32[16,640]{1,0:T(8,128)S(1)}, f32[16,640]{1,0:T(8,128)S(1)}, u32[]{:S(2)}, u32[]{:S(2)}) collective-permute-start(f32[16,640]{1,0:T(8,128)S(1)} %get-tuple-element.25.own), channel_id=1, source_target_pairs={{448,0},{449,1},{450,2},{451,3},{452,4},{453,5},{454,6},{455,7},{4... | collective-permute-start | bytes 122888 | tf_op jit(solution)/shard_map/ppermute | solution.py:476
  93.5 10.5 %collective-permute-start.10 = (f32[16,512]{1,0:T(8,128)S(1)}, f32[16,512]{1,0:T(8,128)S(1)}, u32[]{:S(2)}, u32[]{:S(2)}) collective-permute-start(f32[16,512]{1,0:T(8,128)S(1)} %get-tuple-element.26.own), channel_id=1, source_target_pairs={{80,0},{81,1},{82,2},{83,3},{84,4},{85,5},{86,6},{87,7},{88,8},{89... | collective-permute-start | bytes 98312 | tf_op jit(solution)/shard_map/ppermute | solution.py:476
  98.0 6.1 %collective-permute-start.9 = (f32[16,512]{1,0:T(8,128)S(1)}, f32[16,512]{1,0:T(8,128)S(1)}, u32[]{:S(2)}, u32[]{:S(2)}) collective-permute-start(f32[16,512]{1,0:T(8,128)S(1)} %get-tuple-element.26.own), channel_id=1, source_target_pairs={{16,0},{17,1},{18,2},{19,3},{20,4},{21,5},{22,6},{23,7},{24,8},{25... | collective-permute-start | bytes 98312 | tf_op jit(solution)/shard_map/ppermute | solution.py:476
  102.1 4.7 %collective-permute-start.8 = (f32[16,512]{1,0:T(8,128)S(1)}, f32[16,512]{1,0:T(8,128)S(1)}, u32[]{:S(2)}, u32[]{:S(2)}) collective-permute-start(f32[16,512]{1,0:T(8,128)S(1)} %get-tuple-element.26.own), channel_id=1, source_target_pairs={{64,0},{65,1},{66,2},{67,3},{68,4},{69,5},{70,6},{71,7},{72,8},{73... | collective-permute-start | bytes 98312 | tf_op jit(solution)/shard_map/ppermute | solution.py:476
  116.2 9.1 %collective-permute-start.13 = (f32[16,384]{1,0:T(8,128)S(1)}, f32[16,384]{1,0:T(8,128)S(1)}, u32[]{:S(2)}, u32[]{:S(2)}) collective-permute-start(f32[16,384]{1,0:T(8,128)S(1)} %shard_map.51.own), channel_id=1, source_target_pairs={{496,0},{497,1},{498,2},{499,3},{500,4},{501,5},{502,6},{503,7},{5... | collective-permute-start | bytes 73736 | tf_op jit(solution)/shard_map/ppermute | solution.py:476
  118.2 7.4 %collective-permute-start.12 = (f32[16,384]{1,0:T(8,128)S(1)}, f32[16,384]{1,0:T(8,128)S(1)}, u32[]{:S(2)}, u32[]{:S(2)}) collective-permute-start(f32[16,384]{1,0:T(8,128)S(1)} %shard_map.51.own), channel_id=1, source_target_pairs={{48,0},{49,1},{50,2},{51,3},{52,4},{53,5},{54,6},{55,7},{56,8},{57... | collective-permute-start | bytes 73736 | tf_op jit(solution)/shard_map/ppermute | solution.py:476
  123.2 6.1 %collective-permute-start.11 = (f32[16,384]{1,0:T(8,128)S(1)}, f32[16,384]{1,0:T(8,128)S(1)}, u32[]{:S(2)}, u32[]{:S(2)}) collective-permute-start(f32[16,384]{1,0:T(8,128)S(1)} %shard_map.51.own), channel_id=1, source_target_pairs={{448,0},{449,1},{450,2},{451,3},{452,4},{453,5},{454,6},{455,7},{4... | collective-permute-start | bytes 73736 | tf_op jit(solution)/shard_map/ppermute | solution.py:476

commit v2 on v1

--- a/solution.py
+++ b/solution.py
@@ -248,6 +248,14 @@
     return column >> 1, column & 1, (row & 7) - 2
 
 
+def far_slot(run, low):
+    return lambda x, y, z: (((x - 1) * 2 + y - 1) * run + z - low) & 7
+
+
+def near_slot(run, low):
+    return lambda x, y, z: ((x * 2 + y) * run + z - low) & 7
+
+
 def bricks_place(x, y, z):
     brick = ((z + 4) >> 2) * 4 + (x >> 1) * 2 + (y >> 1)
     return (brick * 2 + (x & 1)) * 8 + (y & 1) * 4 + ((z + 4) & 3)
@@ -262,42 +270,48 @@
     return place
 
 
-def find_places(matrix, count, atom, place, staged, places, sem):
+def find_places(matrix, count, atom, place, slot, staged, places, sem):
     rows = [q * SLOT_ROWS for q in range(count)]
     code = jnp.concatenate([matrix[row : row + 1, CODE - 64 : CODE + 64] for row in rows], axis=0)
     code = pltpu.roll(code, 64, 1).astype(jnp.int32)
     x, y, z = atom(iota(code.shape, 0))
     dx, dy, dz = offsets_of(code)
-    staged[...] = place(x + dx, y + dy, z + dz)
+    where = place(x + dx, y + dy, z + dz)
+    staged[...] = (where & ~7) + ((slot(x, y, z) - where) & 7)
     copy = pltpu.make_async_copy(staged, places, sem)
     copy.start()
     copy.wait()
 
 
+def set_tile(field, index, tile):
+    for turn in range(8):
+        field[index * 8 + turn] = pltpu.roll(tile, turn * SLOT_ROWS, 1) if turn else tile
+
+
 def couple(matrix, groups, field, places, gathered):
     lane_slot = iota((SLOT_ROWS, LANES), 1) >> 4
-    gathered[pl.ds(CODE, WIDE - CODE), :] = jnp.zeros((WIDE - CODE, LANES), jnp.float32)
-    tiles = []
-    for group in groups:
-
-        def gather(k, carry):
+
+    def gather(k, carry):
+        for q, group in enumerate(groups):
             acc = None
             for slot, atom in enumerate(group):
-                place = places[atom, k]
-                tile = pltpu.roll(field[place >> 3], ((slot - place) & 7) * SLOT_ROWS, 1)
+                tile = field[places[atom, k]]
                 acc = tile if acc is None else jnp.where(lane_slot == slot, tile, acc)
-            gathered[pl.ds(pl.multiple_of(k * SLOT_ROWS, SLOT_ROWS), SLOT_ROWS), :] = acc
-            return carry
-
-        lax.fori_loop(0, SELF + 1, gather, 0)
+            gathered[q, pl.ds(pl.multiple_of(k * SLOT_ROWS, SLOT_ROWS), SLOT_ROWS), :] = acc
+        return carry
+
+    lax.fori_loop(0, SELF + 1, gather, 0, unroll=4)
+    tiles = []
+    for q, group in enumerate(groups):
+        gathered[q, CODE:WIDE, :] = jnp.zeros((WIDE - CODE, LANES), jnp.float32)
         left, start = [], 0
-        for q in range(1, 9):
-            if q == 8 or group[q] != group[q - 1] + 1:
-                left.append(matrix[group[start] * SLOT_ROWS : (group[q - 1] + 1) * SLOT_ROWS, :])
-                start = q
+        for r in range(1, 9):
+            if r == 8 or group[r] != group[r - 1] + 1:
+                left.append(matrix[group[start] * SLOT_ROWS : (group[r - 1] + 1) * SLOT_ROWS, :])
+                start = r
         left = left[0] if len(left) == 1 else jnp.concatenate(left, axis=0)
         product = jnp.dot(
-            left, gathered[...], precision=HIGH, preferred_element_type=jnp.float32
+            left, gathered[q], precision=HIGH, preferred_element_type=jnp.float32
         )
         acc = product[0:SLOT_ROWS]
         for slot in range(1, 8):
@@ -314,9 +328,7 @@
         acc = None
         for slot in range(8):
             where = place(x, slot >> 2, slot & 3)
-            tile = field[where >> 3]
-            amount = ((slot - where) & 7) * SLOT_ROWS
-            tile = pltpu.roll(tile, amount, 1) if amount else tile
+            tile = field[(where & ~7) + ((slot - where) & 7)]
             acc = tile if acc is None else jnp.where(lane_slot == slot, tile, acc)
         tiles.append(acc)
     return jnp.concatenate(tiles, axis=1)
@@ -375,10 +387,9 @@
     bricks += [high[288 + q * 8 : 296 + q * 8] for q in range(4)]
     for q, brick in enumerate(bricks):
         for half in (0, 1):
-            for part in (0, 1):
-                lanes = brick[:, (part * 2 + half) * LANES : (part * 2 + half + 1) * LANES]
-                field[q * 2 + half, part * 8 : part * 8 + 8] = lanes
-    find_places(wide, 40, far_atom, bricks_place, staged, places, sem)
+            lanes = [brick[:, r * LANES : (r + 1) * LANES] for r in (half, half + 2)]
+            set_tile(field, q * 2 + half, jnp.concatenate(lanes, axis=0))
+    find_places(wide, 40, far_atom, bricks_place, far_slot(10, -3), staged, places, sem)
     groups = [list(range(q * 8, q * 8 + 8)) for q in range(5)]
     for q, tile in enumerate(couple(wide, groups, field, places, gathered)):
         out[:, q * LANES : (q + 1) * LANES] = tile
@@ -396,7 +407,7 @@
     count = pieces[0].shape[1] // LANES
     for q, piece in enumerate(pieces):
         for t in range(count):
-            field[q * count + t] = piece[:, t * LANES : (t + 1) * LANES]
+            set_tile(field, q * count + t, piece[:, t * LANES : (t + 1) * LANES])
 
 
 def second_kernel(
@@ -405,20 +416,23 @@
 ):
     place = pieces_place(-1, 10, -3)
     load_pieces((from_xy, from_x, from_y, own), field)
-    find_places(matrix, 32, near_atom, place, staged, places, sem)
+    find_places(matrix, 32, near_atom, place, near_slot(8, -2), staged, places, sem)
     groups = [list(range(q * 8, q * 8 + 8)) for q in range(4)]
     tiles = couple(matrix, groups, field, places, gathered)
     for q, tile in enumerate(tiles):
         out[:, q * LANES : (q + 1) * LANES] = tile
     first_own[...] = pick_own(field, place)
-    second_own[...] = pick_own(tiles, lambda x, y, z: (x * 2 + y) * 8 + z + 2)
+    turned = [pltpu.roll(tile, turn * SLOT_ROWS, 1) if turn else tile for tile in tiles for turn in range(8)]
+    second_own[...] = pick_own(turned, lambda x, y, z: (x * 2 + y) * 8 + z + 2)
 
 
 def third_kernel(
     matrix, own, from_x, from_y, from_xy, out, field, gathered, staged, places, sem
 ):
     load_pieces((own, from_y, from_x, from_xy), field)
-    find_places(matrix, 40, far_atom, pieces_place(0, 8, -2), staged, places, sem)
+    find_places(
+        matrix, 40, far_atom, pieces_place(0, 8, -2), far_slot(6, -1), staged, places, sem
+    )
     atoms = [c * 10 + z + 3 for c in range(4) for z in range(-1, 5)]
     groups = [atoms[q * 8 : q * 8 + 8] for q in range(3)]
     for q, tile in enumerate(couple(matrix, groups, field, places, gathered)):
@@ -431,7 +445,7 @@
 ):
     place = pieces_place(-1, 6, -1)
     load_pieces((from_xy, from_x, from_y, own), field)
-    find_places(matrix, 32, near_atom, place, staged, places, sem)
+    find_places(matrix, 32, near_atom, place, near_slot(4, 0), staged, places, sem)
     atoms = [c * 8 + z + 2 for c in range(4) for z in range(4)]
     groups = [atoms[q * 8 : q * 8 + 8] for q in range(2)]
     fourth = jnp.concatenate(couple(matrix, groups, field, places, gathered), axis=1)
@@ -453,10 +467,10 @@
     return out
 
 
-def scratch_for(tiles, rows):
+def scratch_for(tiles, groups, rows):
     return (
-        pltpu.VMEM((tiles, SLOT_ROWS, LANES), jnp.float32),
-        pltpu.VMEM((WIDE, LANES), jnp.float32),
+        pltpu.VMEM((tiles * 8, SLOT_ROWS, LANES), jnp.float32),
+        pltpu.VMEM((groups, WIDE, LANES), jnp.float32),
         pltpu.VMEM((rows, LANES), jnp.int32),
         pltpu.SMEM((rows, LANES), jnp.int32),
         pltpu.SemaphoreType.DMA,
@@ -514,26 +528,26 @@
         far_kernel,
         [(components, 5 * LANES), (640, WIDE)],
         matrix, *sides, start, low, high,
-        scratch=scratch_for(24, 40),
+        scratch=scratch_for(24, 5, 40),
     )
     (near_matrix,) = call(near_matrix_kernel, [(512, WIDE)], matrix, low, high)
     second, first_own, second_own = call(
         second_kernel,
         [(components, 4 * LANES)] + [(components, width)] * 2,
         near_matrix, first, *fetch_three(first, first, first, -1),
-        scratch=scratch_for(20, 32),
+        scratch=scratch_for(20, 4, 32),
     )
     (third,) = call(
         third_kernel,
         [(components, 3 * LANES)],
         far_matrix, second, *fetch_three(second, second, second, 1),
-        scratch=scratch_for(16, 40),
+        scratch=scratch_for(16, 3, 40),
     )
     third_own, message = call(
         fourth_kernel,
         [(components, width), (lax.axis_size("gx"), 4, LANES)],
         near_matrix, third, *fetch_three(third, third, third, -1), start, first_own, second_own,
-        scratch=scratch_for(12, 32),
+        scratch=scratch_for(12, 2, 32),
     )
     rest = lax.axis_size("gy") * lax.axis_size("gz")
     message = lax.all_to_all(message, "gx", 0, 0, tiled=True)

time: 174 us -> 143 us (0.82)
  Pallas kernels: 44.9 us -> 14.1 us
    pallas_call x9, Pallas kernels: 44.9 us -> 14.1 us  [call(): pl.pallas_call(kernel, out_shape=shapes, in_specs=[VMEM] * len(operands),...]
where the time goes in v2:
time: 143 us; the launch traced here: 142 us
  starting transfers between devices  53.6 us (37%)
  blocking collectives  35.2 us (25%)
  waiting for transfers between devices  34.7 us (24%)
  Pallas kernels  14.1 us (10%)
  local copies, waits for them, and re-layouts  3.56 us (2%)
    ppermute x14, starting transfers between devices, fetch(): return lax.ppermute(value, axes, pairs)  53.6 us
    ppermute x14, waiting for transfers between devices, fetch(): return lax.ppermute(value, axes, pairs)  34.7 us
    all_to_all x1, blocking collectives, body(): message = lax.all_to_all(message, ('gy', 'gz'), 0, 0, tiled=True)  24 us
    pallas_call x9, Pallas kernels, call(): pl.pallas_call(kernel, out_shape=shapes, in_specs=[VMEM] * len(operands),...  14.1 us
    all_to_all x1, blocking collectives, body(): message = lax.all_to_all(message, 'gx', 0, 0, tiled=True)  11.2 us
  transfers between devices with their start and end apart: 14, of which 10 were waited for; matrix products, arithmetic and copies ran while one was open for 0% of the time, Pallas kernels for 0%

profile of v2, /device:TPU:1, one launch (start us, length us, event | category | flops | bytes accessed | tf_op | source)
XLA Modules:
  0.0 142.3 jit_solution(2807311147853249215)
XLA Ops:
  3.7 5.9 %collective-permute-start = (f32[72,512]{1,0:T(8,128)S(1)}, f32[72,512]{1,0:T(8,128)S(1)}, u32[]{:S(2)}, u32[]{:S(2)}) collective-permute-start(f32[72,512]{1,0:T(8,128)S(1)} %get-tuple-element.19), channel_id=1, source_target_pairs={{64,0},{65,1},{66,2},{67,3},{68,4},{69,5},{70,6},{71,7},{72,8},{73... | collective-permute-start | bytes 442376 | tf_op jit(solution)/shard_map/ppermute | solution.py:490
  9.6 10.7 %collective-permute-start.1 = (f32[72,512]{1,0:T(8,128)S(1)}, f32[72,512]{1,0:T(8,128)S(1)}, u32[]{:S(2)}, u32[]{:S(2)}) collective-permute-start(f32[72,512]{1,0:T(8,128)S(1)} %get-tuple-element.20), channel_id=1, source_target_pairs={{16,0},{17,1},{18,2},{19,3},{20,4},{21,5},{22,6},{23,7},{24,8},{25... | collective-permute-start | bytes 442376 | tf_op jit(solution)/shard_map/ppermute | solution.py:490
  20.3 3.0 %collective-permute-start.2 = (f32[72,512]{1,0:T(8,128)S(1)}, f32[72,512]{1,0:T(8,128)S(1)}, u32[]{:S(2)}, u32[]{:S(2)}) collective-permute-start(f32[72,512]{1,0:T(8,128)S(1)} %get-tuple-element.21), channel_id=1, source_target_pairs={{80,0},{81,1},{82,2},{83,3},{84,4},{85,5},{86,6},{87,7},{88,8},{89... | collective-permute-start | bytes 442376 | tf_op jit(solution)/shard_map/ppermute | solution.py:490
  23.3 8.1 %collective-permute-done.1.from_y = f32[72,512]{1,0:T(8,128)S(1)} collective-permute-done((f32[72,512]{1,0:T(8,128)S(1)}, f32[72,512]{1,0:T(8,128)S(1)}, u32[]{:S(2)}, u32[]{:S(2)}) %collective-permute-start.1) | collective-permute-done | bytes 147488 | tf_op jit(solution)/shard_map/ppermute | solution.py:490
  31.4 4.1 %collective-permute-start.3 = (f32[320,512]{1,0:T(8,128)S(1)}, f32[320,512]{1,0:T(8,128)S(1)}, u32[]{:S(2)}, u32[]{:S(2)}) collective-permute-start(f32[320,512]{1,0:T(8,128)S(1)} %get-tuple-element.22), channel_id=1, source_target_pairs={{15,0},{0,1},{1,2},{2,3},{3,4},{4,5},{5,6},{6,7},{7,8},{8,9},{9,10... | collective-permute-start | bytes 1966088 | tf_op jit(solution)/shard_map/ppermute | solution.py:490
  35.6 2.2 %collective-permute-start.4 = (f32[320,512]{1,0:T(8,128)S(1)}, f32[320,512]{1,0:T(8,128)S(1)}, u32[]{:S(2)}, u32[]{:S(2)}) collective-permute-start(f32[320,512]{1,0:T(8,128)S(1)} %get-tuple-element.23), channel_id=1, source_target_pairs={{1,0},{2,1},{3,2},{4,3},{5,4},{6,5},{7,6},{8,7},{9,8},{10,9},{11,1... | collective-permute-start | bytes 1966088 | tf_op jit(solution)/shard_map/ppermute | solution.py:490
  37.8 6.1 %collective-permute-done.3.low = f32[320,512]{1,0:T(8,128)S(1)} collective-permute-done((f32[320,512]{1,0:T(8,128)S(1)}, f32[320,512]{1,0:T(8,128)S(1)}, u32[]{:S(2)}, u32[]{:S(2)}) %collective-permute-start.3) | collective-permute-done | bytes 655392 | tf_op jit(solution)/shard_map/ppermute | solution.py:490
  43.9 9.2 %collective-permute-done.4.high = f32[320,512]{1,0:T(8,128)S(1)} collective-permute-done((f32[320,512]{1,0:T(8,128)S(1)}, f32[320,512]{1,0:T(8,128)S(1)}, u32[]{:S(2)}, u32[]{:S(2)}) %collective-permute-start.4) | collective-permute-done | bytes 655392 | tf_op jit(solution)/shard_map/ppermute | solution.py:490
  53.1 4.0 %shard_map.49 = (f32[16,640]{1,0:T(8,128)S(1)}, f32[640,512]{1,0:T(8,128)S(1)}) custom-call(f32[256,512]{1,0:T(8,128)S(1)} %get-tuple-element.18.matrix, f32[72,512]{1,0:T(8,128)S(1)} %collective-permute-done.from_x, f32[72,512]{1,0:T(8,128)S(1)} %collective-permute-done.1.from_y, f32[72,512]{1,0:T(8,128)S(1)} %collective-permute-done.2.from_xy, ...), custom_call_target="tpu_custom_call" | custom-call | tf_op jit(solution)/shard_map/pallas_call | solution.py:459
  57.1 1.9 %collective-permute-start.7 = (f32[16,640]{1,0:T(8,128)S(1)}, f32[16,640]{1,0:T(8,128)S(1)}, u32[]{:S(2)}, u32[]{:S(2)}) collective-permute-start(f32[16,640]{1,0:T(8,128)S(1)} %get-tuple-element.25.own), channel_id=1, source_target_pairs={{496,0},{497,1},{498,2},{499,3},{500,4},{501,5},{502,6},{503,7},{5... | collective-permute-start | bytes 122888 | tf_op jit(solution)/shard_map/ppermute | solution.py:490
  59.1 3.4 %collective-permute-start.6 = (f32[16,640]{1,0:T(8,128)S(1)}, f32[16,640]{1,0:T(8,128)S(1)}, u32[]{:S(2)}, u32[]{:S(2)}) collective-permute-start(f32[16,640]{1,0:T(8,128)S(1)} %get-tuple-element.25.own), channel_id=1, source_target_pairs={{48,0},{49,1},{50,2},{51,3},{52,4},{53,5},{54,6},{55,7},{56,8},{57... | collective-permute-start | bytes 122888 | tf_op jit(solution)/shard_map/ppermute | solution.py:490
  62.4 3.2 %collective-permute-start.5 = (f32[16,640]{1,0:T(8,128)S(1)}, f32[16,640]{1,0:T(8,128)S(1)}, u32[]{:S(2)}, u32[]{:S(2)}) collective-permute-start(f32[16,640]{1,0:T(8,128)S(1)} %get-tuple-element.25.own), channel_id=1, source_target_pairs={{448,0},{449,1},{450,2},{451,3},{452,4},{453,5},{454,6},{455,7},{4... | collective-permute-start | bytes 122888 | tf_op jit(solution)/shard_map/ppermute | solution.py:490
  66.5 2.9 %collective-permute-done.6.from_y = f32[16,640]{1,0:T(8,128)S(1)} collective-permute-done((f32[16,640]{1,0:T(8,128)S(1)}, f32[16,640]{1,0:T(8,128)S(1)}, u32[]{:S(2)}, u32[]{:S(2)}) %collective-permute-start.6) | collective-permute-done | bytes 40992 | tf_op jit(solution)/shard_map/ppermute | solution.py:490
  70.2 3.4 %shard_map.50 = (f32[16,512]{1,0:T(8,128)S(1)}, f32[16,256]{1,0:T(8,128)S(1)}, f32[16,256]{1,0:T(8,128)S(1)}) custom-call(f32[512,512]{1,0:T(8,128)S(1)} %shard_map.48.matrix, f32[16,640]{1,0:T(8,128)S(1)} %get-tuple-element.25.own, f32[16,640]{1,0:T(8,128)S(1)} %collective-permute-done.5.from_x, f32[16,640]{1,0:T(8,128)S(1)} %collective-permute-done.6.from_y, ...), custom_call_target="tpu_custom_call" | custom-call | tf_op jit(solution)/shard_map/pallas_call | solution.py:459
  73.6 4.4 %collective-permute-start.10 = (f32[16,512]{1,0:T(8,128)S(1)}, f32[16,512]{1,0:T(8,128)S(1)}, u32[]{:S(2)}, u32[]{:S(2)}) collective-permute-start(f32[16,512]{1,0:T(8,128)S(1)} %get-tuple-element.26.own), channel_id=1, source_target_pairs={{80,0},{81,1},{82,2},{83,3},{84,4},{85,5},{86,6},{87,7},{88,8},{89... | collective-permute-start | bytes 98312 | tf_op jit(solution)/shard_map/ppermute | solution.py:490
  78.1 4.1 %collective-permute-start.9 = (f32[16,512]{1,0:T(8,128)S(1)}, f32[16,512]{1,0:T(8,128)S(1)}, u32[]{:S(2)}, u32[]{:S(2)}) collective-permute-start(f32[16,512]{1,0:T(8,128)S(1)} %get-tuple-element.26.own), channel_id=1, source_target_pairs={{16,0},{17,1},{18,2},{19,3},{20,4},{21,5},{22,6},{23,7},{24,8},{25... | collective-permute-start | bytes 98312 | tf_op jit(solution)/shard_map/ppermute | solution.py:490
  82.2 1.9 %collective-permute-start.8 = (f32[16,512]{1,0:T(8,128)S(1)}, f32[16,512]{1,0:T(8,128)S(1)}, u32[]{:S(2)}, u32[]{:S(2)}) collective-permute-start(f32[16,512]{1,0:T(8,128)S(1)} %get-tuple-element.26.own), channel_id=1, source_target_pairs={{64,0},{65,1},{66,2},{67,3},{68,4},{69,5},{70,6},{71,7},{72,8},{73... | collective-permute-start | bytes 98312 | tf_op jit(solution)/shard_map/ppermute | solution.py:490
  84.1 2.7 %collective-permute-done.8.from_x = f32[16,512]{1,0:T(8,128)S(1)} collective-permute-done((f32[16,512]{1,0:T(8,128)S(1)}, f32[16,512]{1,0:T(8,128)S(1)}, u32[]{:S(2)}, u32[]{:S(2)}) %collective-permute-start.8) | collective-permute-done | bytes 32800 | tf_op jit(solution)/shard_map/ppermute | solution.py:490
  86.8 2.9 %shard_map.51.own = f32[16,384]{1,0:T(8,128)S(1)} custom-call(f32[640,512]{1,0:T(8,128)S(1)} %get-tuple-element.24.matrix, f32[16,512]{1,0:T(8,128)S(1)} %get-tuple-element.26.own, f32[16,512]{1,0:T(8,128)S(1)} %collective-permute-done.8.from_x, f32[16,512]{1,0:T(8,128)S(1)} %collective-permute-done.9.from_y, f32[16,512]{1,0:T(8,128)S(1)} %collective-permute-done.10.from_xy), custom_call_target="tpu_custom_call" | custom-call | tf_op jit(solution)/shard_map/pallas_call | solution.py:459
  91.7 5.0 %collective-permute-start.12 = (f32[16,384]{1,0:T(8,128)S(1)}, f32[16,384]{1,0:T(8,128)S(1)}, u32[]{:S(2)}, u32[]{:S(2)}) collective-permute-start(f32[16,384]{1,0:T(8,128)S(1)} %shard_map.51.own), channel_id=1, source_target_pairs={{48,0},{49,1},{50,2},{51,3},{52,4},{53,5},{54,6},{55,7},{56,8},{57... | collective-permute-start | bytes 73736 | tf_op jit(solution)/shard_map/ppermute | solution.py:490
  99.1 3.7 %collective-permute-done.11.from_x = f32[16,384]{1,0:T(8,128)S(1)} collective-permute-done((f32[16,384]{1,0:T(8,128)S(1)}, f32[16,384]{1,0:T(8,128)S(1)}, u32[]{:S(2)}, u32[]{:S(2)}) %collective-permute-start.11) | collective-permute-done | bytes 24608 | tf_op jit(solution)/shard_map/ppermute | solution.py:490
  102.8 2.7 %shard_map.52 = (f32[16,256]{1,0:T(8,128)S(1)}, f32[8,4,128]{2,1,0:T(4,128)S(1)}) custom-call(f32[512,512]{1,0:T(8,128)S(1)} %shard_map.48.matrix, f32[16,384]{1,0:T(8,128)S(1)} %shard_map.51.own, f32[16,384]{1,0:T(8,128)S(1)} %collective-permute-done.11.from_x, f32[16,384]{1,0:T(8,128)S(1)} %collective-permute-done.12.from_y, ...), custom_call_target="tpu_custom_call" | custom-call | tf_op jit(solution)/shard_map/pallas_call | solution.py:459
  105.5 11.2 %all_to_all.10.ref = f32[8,4,128]{2,1,0:T(4,128)S(1)} all-to-all(f32[8,4,128]{2,1,0:T(4,128)S(1)} %get-tuple-element.29), channel_id=1, replica_groups=mesh['gx'=8,'gy'=4,'gz'=16] {'gx'}, dimensions={0} | all-to-all | bytes 32768 | tf_op jit(solution)/shard_map/all_to_all | solution.py:553
  116.7 24.0 %all_to_all.11.ref = f32[64,4,128]{2,1,0:T(4,128)S(1)} all-to-all(f32[64,4,128]{2,1,0:T(4,128)S(1)} %shard_map.53), channel_id=1, replica_groups=mesh['gx'=8,'gy'=4,'gz'=16] {'gy','gz'}, dimensions={0} | all-to-all | bytes 262144 | tf_op jit(solution)/shard_map/all_to_all | solution.py:555
  (28 shorter events, 11.2 us)
Async XLA Ops:
  1.8 1.0 copy-start
  2.8 0.7 copy-start.1
  3.7 19.6 %collective-permute-start = (f32[72,512]{1,0:T(8,128)S(1)}, f32[72,512]{1,0:T(8,128)S(1)}, u32[]{:S(2)}, u32[]{:S(2)}) collective-permute-start(f32[72,512]{1,0:T(8,128)S(1)} %get-tuple-element.19), channel_id=1, source_target_pairs={{64,0},{65,1},{66,2},{67,3},{68,4},{69,5},{70,6},{71,7},{72,8},{73... | collective-permute-start | bytes 442376 | tf_op jit(solution)/shard_map/ppermute | solution.py:490
  9.6 21.7 %collective-permute-start.1 = (f32[72,512]{1,0:T(8,128)S(1)}, f32[72,512]{1,0:T(8,128)S(1)}, u32[]{:S(2)}, u32[]{:S(2)}) collective-permute-start(f32[72,512]{1,0:T(8,128)S(1)} %get-tuple-element.20), channel_id=1, source_target_pairs={{16,0},{17,1},{18,2},{19,3},{20,4},{21,5},{22,6},{23,7},{24,8},{25... | collective-permute-start | bytes 442376 | tf_op jit(solution)/shard_map/ppermute | solution.py:490
  20.3 11.1 %collective-permute-start.2 = (f32[72,512]{1,0:T(8,128)S(1)}, f32[72,512]{1,0:T(8,128)S(1)}, u32[]{:S(2)}, u32[]{:S(2)}) collective-permute-start(f32[72,512]{1,0:T(8,128)S(1)} %get-tuple-element.21), channel_id=1, source_target_pairs={{80,0},{81,1},{82,2},{83,3},{84,4},{85,5},{86,6},{87,7},{88,8},{89... | collective-permute-start | bytes 442376 | tf_op jit(solution)/shard_map/ppermute | solution.py:490
  31.4 12.4 %collective-permute-start.3 = (f32[320,512]{1,0:T(8,128)S(1)}, f32[320,512]{1,0:T(8,128)S(1)}, u32[]{:S(2)}, u32[]{:S(2)}) collective-permute-start(f32[320,512]{1,0:T(8,128)S(1)} %get-tuple-element.22), channel_id=1, source_target_pairs={{15,0},{0,1},{1,2},{2,3},{3,4},{4,5},{5,6},{6,7},{7,8},{8,9},{9,10... | collective-permute-start | bytes 1966088 | tf_op jit(solution)/shard_map/ppermute | solution.py:490
  35.6 17.5 %collective-permute-start.4 = (f32[320,512]{1,0:T(8,128)S(1)}, f32[320,512]{1,0:T(8,128)S(1)}, u32[]{:S(2)}, u32[]{:S(2)}) collective-permute-start(f32[320,512]{1,0:T(8,128)S(1)} %get-tuple-element.23), channel_id=1, source_target_pairs={{1,0},{2,1},{3,2},{4,3},{5,4},{6,5},{7,6},{8,7},{9,8},{10,9},{11,1... | collective-permute-start | bytes 1966088 | tf_op jit(solution)/shard_map/ppermute | solution.py:490
  57.1 9.4 %collective-permute-start.7 = (f32[16,640]{1,0:T(8,128)S(1)}, f32[16,640]{1,0:T(8,128)S(1)}, u32[]{:S(2)}, u32[]{:S(2)}) collective-permute-start(f32[16,640]{1,0:T(8,128)S(1)} %get-tuple-element.25.own), channel_id=1, source_target_pairs={{496,0},{497,1},{498,2},{499,3},{500,4},{501,5},{502,6},{503,7},{5... | collective-permute-start | bytes 122888 | tf_op jit(solution)/shard_map/ppermute | solution.py:490
  59.1 10.3 %collective-permute-start.6 = (f32[16,640]{1,0:T(8,128)S(1)}, f32[16,640]{1,0:T(8,128)S(1)}, u32[]{:S(2)}, u32[]{:S(2)}) collective-permute-start(f32[16,640]{1,0:T(8,128)S(1)} %get-tuple-element.25.own), channel_id=1, source_target_pairs={{48,0},{49,1},{50,2},{51,3},{52,4},{53,5},{54,6},{55,7},{56,8},{57... | collective-permute-start | bytes 122888 | tf_op jit(solution)/shard_map/ppermute | solution.py:490
  62.4 7.7 %collective-permute-start.5 = (f32[16,640]{1,0:T(8,128)S(1)}, f32[16,640]{1,0:T(8,128)S(1)}, u32[]{:S(2)}, u32[]{:S(2)}) collective-permute-start(f32[16,640]{1,0:T(8,128)S(1)} %get-tuple-element.25.own), channel_id=1, source_target_pairs={{448,0},{449,1},{450,2},{451,3},{452,4},{453,5},{454,6},{455,7},{4... | collective-permute-start | bytes 122888 | tf_op jit(solution)/shard_map/ppermute | solution.py:490
  73.6 10.5 %collective-permute-start.10 = (f32[16,512]{1,0:T(8,128)S(1)}, f32[16,512]{1,0:T(8,128)S(1)}, u32[]{:S(2)}, u32[]{:S(2)}) collective-permute-start(f32[16,512]{1,0:T(8,128)S(1)} %get-tuple-element.26.own), channel_id=1, source_target_pairs={{80,0},{81,1},{82,2},{83,3},{84,4},{85,5},{86,6},{87,7},{88,8},{89... | collective-permute-start | bytes 98312 | tf_op jit(solution)/shard_map/ppermute | solution.py:490
  78.1 6.1 %collective-permute-start.9 = (f32[16,512]{1,0:T(8,128)S(1)}, f32[16,512]{1,0:T(8,128)S(1)}, u32[]{:S(2)}, u32[]{:S(2)}) collective-permute-start(f32[16,512]{1,0:T(8,128)S(1)} %get-tuple-element.26.own), channel_id=1, source_target_pairs={{16,0},{17,1},{18,2},{19,3},{20,4},{21,5},{22,6},{23,7},{24,8},{25... | collective-permute-start | bytes 98312 | tf_op jit(solution)/shard_map/ppermute | solution.py:490
  82.2 4.7 %collective-permute-start.8 = (f32[16,512]{1,0:T(8,128)S(1)}, f32[16,512]{1,0:T(8,128)S(1)}, u32[]{:S(2)}, u32[]{:S(2)}) collective-permute-start(f32[16,512]{1,0:T(8,128)S(1)} %get-tuple-element.26.own), channel_id=1, source_target_pairs={{64,0},{65,1},{66,2},{67,3},{68,4},{69,5},{70,6},{71,7},{72,8},{73... | collective-permute-start | bytes 98312 | tf_op jit(solution)/shard_map/ppermute | solution.py:490
  89.8 9.1 %collective-permute-start.13 = (f32[16,384]{1,0:T(8,128)S(1)}, f32[16,384]{1,0:T(8,128)S(1)}, u32[]{:S(2)}, u32[]{:S(2)}) collective-permute-start(f32[16,384]{1,0:T(8,128)S(1)} %shard_map.51.own), channel_id=1, source_target_pairs={{496,0},{497,1},{498,2},{499,3},{500,4},{501,5},{502,6},{503,7},{5... | collective-permute-start | bytes 73736 | tf_op jit(solution)/shard_map/ppermute | solution.py:490
  91.7 7.4 %collective-permute-start.12 = (f32[16,384]{1,0:T(8,128)S(1)}, f32[16,384]{1,0:T(8,128)S(1)}, u32[]{:S(2)}, u32[]{:S(2)}) collective-permute-start(f32[16,384]{1,0:T(8,128)S(1)} %shard_map.51.own), channel_id=1, source_target_pairs={{48,0},{49,1},{50,2},{51,3},{52,4},{53,5},{54,6},{55,7},{56,8},{57... | collective-permute-start | bytes 73736 | tf_op jit(solution)/shard_map/ppermute | solution.py:490
  96.7 6.1 %collective-permute-start.11 = (f32[16,384]{1,0:T(8,128)S(1)}, f32[16,384]{1,0:T(8,128)S(1)}, u32[]{:S(2)}, u32[]{:S(2)}) collective-permute-start(f32[16,384]{1,0:T(8,128)S(1)} %shard_map.51.own), channel_id=1, source_target_pairs={{448,0},{449,1},{450,2},{451,3},{452,4},{453,5},{454,6},{455,7},{4... | collective-permute-start | bytes 73736 | tf_op jit(solution)/shard_map/ppermute | solution.py:490

commit v3 on v2

v3 whole, which is shorter than its diff:
```python
import jax
import jax.numpy as jnp
from jax import lax
from jax.experimental import pallas as pl
from jax.experimental.pallas import tpu as pltpu
from jax.sharding import PartitionSpec as P

ITERS = 2
DEGREE = 2 * ITERS
SHIFT = 2.0
LANES = 128
PAIRS = [(i, j) for i in range(DEGREE + 1) for j in range(i, DEGREE + 1)]
VMEM = pl.BlockSpec(memory_space=pltpu.VMEM)


def two_sum(a, b):
    total = a + b
    part = total - a
    return total, (a - (total - part)) + (b - part)


def quick_sum(a, b):
    total = a + b
    return total, b - (total - a)


def split(a):
    scaled = 4097.0 * a
    head = scaled - (scaled - a)
    return head, a - head


def two_prod(a, b):
    product = a * b
    a_head, a_tail = split(a)
    b_head, b_tail = split(b)
    rest = ((a_head * b_head - product) + a_head * b_tail + a_tail * b_head) + a_tail * b_tail
    return product, rest


def pair_add(a, b):
    head, tail = two_sum(a[0], b[0])
    return quick_sum(head, tail + (a[1] + b[1]))


def pair_mul(a, b):
    head, tail = two_prod(a[0], b[0])
    return quick_sum(head, tail + (a[0] * b[1] + a[1] * b[0]))


def pair_scale(a, factor):
    head, tail = two_prod(a[0], factor)
    return quick_sum(head, tail + a[1] * factor)


def roll_pair(a, amount, axis):
    return pltpu.roll(a[0], amount, axis), pltpu.roll(a[1], amount, axis)


def iota(shape, axis):
    return lax.broadcasted_iota(jnp.int32, shape, axis)


def gram_kernel(fields, out):
    columns = 16
    diagonal_mask = iota((8, LANES), 0) == iota((8, LANES), 1) // columns
    rows = []
    parts = [split(field) for field in fields]
    for i, j in PAIRS:
        product = fields[i] * fields[j]
        (a_head, a_tail), (b_head, b_tail) = parts[i], parts[j]
        rest = ((a_head * b_head - product) + a_head * b_tail + a_tail * b_head) + a_tail * b_tail
        pieces = [
            (product[s : s + 8, t : t + LANES], rest[s : s + 8, t : t + LANES])
            for s in range(0, product.shape[0], 8)
            for t in range(0, product.shape[1], LANES)
        ]
        while len(pieces) > 1:
            pieces = [pair_add(pieces[q], pieces[q + 1]) for q in range(0, len(pieces), 2)]
        total = pieces[0]
        for amount in (4, 2, 1):
            total = pair_add(total, roll_pair(total, amount, 0))
        rows.append((total[0][0:1], total[1][0:1]))
    rows += [(jnp.zeros((1, LANES), jnp.float32),) * 2] * (16 - len(rows))
    packed = [[], []]
    for start in (0, 8):
        total = tuple(
            jnp.concatenate([row[part] for row in rows[start : start + 8]], axis=0)
            for part in (0, 1)
        )
        for amount in (64, 32, 16):
            total = pair_add(total, roll_pair(total, amount, 1))
        for part in (0, 1):
            packed[part].append(
                jnp.sum(jnp.where(diagonal_mask, total[part], 0.0), axis=0, keepdims=True)
            )
    message = jnp.concatenate(packed[0] + packed[1], axis=0)
    for q in range(out.shape[0]):
        out[q] = message


def sum_messages(ref):
    terms = [(ref[q], None) for q in range(ref.shape[0])]
    while len(terms) > 1:
        merged = []
        for q in range(0, len(terms), 2):
            (a, a_rest), (b, b_rest) = terms[q], terms[q + 1]
            total, rest = two_sum(a, b)
            if a_rest is not None:
                rest = rest + (a_rest + b_rest)
            merged.append((total, rest))
        terms = merged
    total, rest = terms[0]
    return quick_sum(total[0:2], rest[0:2] + (total[2:4] + rest[2:4]))


def relay_kernel(ref, out):
    head, tail = sum_messages(ref)
    message = jnp.concatenate([head, tail], axis=0)
    for q in range(out.shape[0]):
        out[q] = message


def finish_kernel(ref, *refs):
    fields, out = refs[:-1], refs[-1]
    columns = 16
    shape = (8, LANES)
    row = iota(shape, 0)
    diagonal_mask = row == iota(shape, 1) // columns
    packed = sum_messages(ref)
    unpacked = []
    for part in (0, 1):
        halves = []
        for half in (0, 1):
            value = jnp.where(
                diagonal_mask, jnp.broadcast_to(packed[part][half : half + 1], shape), 0.0
            )
            for amount in (64, 32, 16):
                value = value + pltpu.roll(value, amount, 1)
            halves.append(value)
        unpacked.append(halves)

    def entry(part, i, j):
        place = PAIRS.index((min(i, j), max(i, j)))
        half = unpacked[part][place // 8]
        return jnp.broadcast_to(half[place % 8 : place % 8 + 1], shape)

    gram = []
    for j in range(DEGREE + 1):
        column = []
        for part in (0, 1):
            value = jnp.zeros(shape, jnp.float32)
            for i in range(DEGREE + 1):
                value = jnp.where(row == i, entry(part, i, j), value)
            column.append(value)
        gram.append(tuple(column))

    def total_rows(a):
        for amount in (4, 2, 1):
            a = pair_add(a, roll_pair(a, amount, 0))
        return a[0]

    def with_start(a):
        return total_rows(pair_mul(gram[0], a))

    def square(a, degree):
        acc = None
        for j in range(degree + 1):
            factor = tuple(jnp.broadcast_to(part[j : j + 1], shape) for part in a)
            term = pair_mul(gram[j], factor)
            acc = term if acc is None else pair_add(acc, term)
        return total_rows(pair_mul(acc, a))

    def apply(a):
        return pair_add((SHIFT * a[0], SHIFT * a[1]), roll_pair(a, 1, 0))

    def shrink(quasi_norm, ratio, step):
        damping = 1.0 / (1.0 + ratio * ratio)
        return quasi_norm * ratio * jnp.sqrt(damping), damping * step

    zero = jnp.zeros(shape, jnp.float32)
    start = (jnp.where(row == 0, 1.0, 0.0), zero)
    inner = entry(0, 0, 0)
    quasi_norm = jnp.sqrt(inner)
    image = apply(start)
    resid = search = start
    direction = total = (zero, zero)
    ratio = weight = zero
    for iteration in range(ITERS):
        step = inner / with_start(image)
        resid = pair_add(resid, pair_scale(image, -step))
        direction = pair_add(search, pair_scale(direction, ratio * ratio * weight / step))
        ratio = jnp.sqrt(square(resid, 2 * iteration + 1)) / quasi_norm
        quasi_norm, weight = shrink(quasi_norm, ratio, step)
        total = pair_add(total, pair_scale(direction, weight))
        search_odd = pair_add(search, pair_scale(image, -step))
        image_odd = apply(search_odd)
        resid = pair_add(resid, pair_scale(image_odd, -step))
        direction = pair_add(search_odd, pair_scale(direction, ratio * ratio * weight / step))
        ratio = jnp.sqrt(square(resid, 2 * iteration + 2)) / quasi_norm
        quasi_norm, weight = shrink(quasi_norm, ratio, step)
        total = pair_add(total, pair_scale(direction, weight))
        if iteration + 1 < ITERS:
            inner_next = with_start(resid)
            mix = inner_next / inner
            search = pair_add(resid, pair_scale(search_odd, mix))
            image = pair_add(
                apply(search), pair_scale(pair_add(image_odd, pair_scale(image, mix)), mix)
            )
            inner = inner_next
    coefficients = total[0] + total[1]
    height, width = fields[0].shape
    acc = None
    for i, field in enumerate(fields):
        factor = jnp.broadcast_to(coefficients[i : i + 1], (height, LANES))
        factor = jnp.concatenate([factor] * (width // LANES), axis=1)
        term = factor * field[...]
        acc = term if acc is None else acc + term
    from_tiles(acc, out)


SLOT_ROWS = 16
WIDE = 512
SELF = 27
CODE = 448
HIGH = lax.Precision.HIGHEST
LENGTHS = (2, 2, 4)
ATOMS = 16
AXES = ("gx", "gy", "gz")


def far_place(x, y, z):
    piece = (x >> 1) * 2 + (y >> 1)
    outside = ((z >> 2) != 0).astype(jnp.int32)
    return (piece * 4 + outside * 2 + (x & 1)) * 8 + (y & 1) * 4 + (z & 3)


def far_slot(x, y, z):
    return (((x - 1) * 2 + y - 1) * 6 + z + 1) & 7


def near_place(x, y, z):
    x, y = x + 1, y + 1
    piece = (x >> 1) * 2 + (y >> 1)
    return (piece * 4 + (x & 1) * 2 + (y & 1)) * 6 + z + 1


def near_slot(x, y, z):
    return (y * 4 + z) & 7


def find_places(matrix, count, atom, place, slot, out):
    rows = [q * SLOT_ROWS for q in range(count)]
    code = jnp.concatenate([matrix[row : row + 1, CODE - 64 : CODE + 64] for row in rows], axis=0)
    code = pltpu.roll(code, 64, 1).astype(jnp.int32)
    x, y, z = atom(iota(code.shape, 0))
    first = (code * 57) >> 9
    rest = code - 9 * first
    second = (rest * 11) >> 5
    where = place(x + first - 1, y + second - 1, z + rest - 3 * second - 1)
    out[...] = (where & ~7) + ((slot(x, y, z) - where) & 7)


def set_tiles(field, pieces):
    count = pieces[0].shape[1] // LANES
    for q, piece in enumerate(pieces):
        for t in range(count):
            tile = piece[:, t * LANES : (t + 1) * LANES]
            for turn in range(8):
                place = (q * count + t) * 8 + turn
                field[place] = pltpu.roll(tile, turn * SLOT_ROWS, 1) if turn else tile


def couple(matrix, field, places, gathered):
    lane_slot = iota((SLOT_ROWS, LANES), 1) >> 4
    groups = matrix.shape[0] // LANES

    def gather(k, carry):
        for q in range(groups):
            acc = None
            for slot in range(8):
                tile = field[places[q * 8 + slot, k]]
                acc = tile if acc is None else jnp.where(lane_slot == slot, tile, acc)
            gathered[q, pl.ds(pl.multiple_of(k * SLOT_ROWS, SLOT_ROWS), SLOT_ROWS), :] = acc
        return carry

    lax.fori_loop(0, SELF + 1, gather, 0, unroll=7)
    tiles = []
    for q in range(groups):
        gathered[q, CODE:WIDE, :] = jnp.zeros((WIDE - CODE, LANES), jnp.float32)
        product = jnp.dot(
            matrix[q * LANES : (q + 1) * LANES, :],
            gathered[q],
            precision=HIGH,
            preferred_element_type=jnp.float32,
        )
        acc = product[0:SLOT_ROWS]
        for slot in range(1, 8):
            piece = product[slot * SLOT_ROWS : (slot + 1) * SLOT_ROWS]
            acc = jnp.where(lane_slot == slot, piece, acc)
        tiles.append(-acc)
    return jnp.concatenate(tiles, axis=1)


def pick_own(field):
    lane_slot = iota((SLOT_ROWS, LANES), 1) >> 4
    tiles = []
    for x in range(2):
        acc = None
        for slot in range(8):
            where = near_place(x, slot >> 2, slot & 3)
            tile = field[(where & ~7) + ((slot - where) & 7)]
            acc = tile if acc is None else jnp.where(lane_slot == slot, tile, acc)
        tiles.append(acc)
    return jnp.concatenate(tiles, axis=1)


def spread_lanes(value):
    for amount in (64, 32, 16):
        value = value + pltpu.roll(value, amount, 1)
    return value


def to_tiles(rows):
    shape = (8, LANES)
    diagonal_mask = iota(shape, 0) == iota(shape, 1) >> 4
    lane_slot = iota(shape, 1) >> 4
    halves = []
    for half in range(2):
        tiles = []
        for x in range(2):
            acc = jnp.zeros(shape, jnp.float32)
            for slot in range(8):
                row = rows(x, slot >> 2, slot & 3)[:, half * LANES : (half + 1) * LANES]
                value = jnp.where(diagonal_mask, jnp.broadcast_to(row, shape), 0.0)
                acc = jnp.where(lane_slot == slot, spread_lanes(value), acc)
            tiles.append(acc)
        halves.append(jnp.concatenate(tiles, axis=1))
    return jnp.concatenate(halves, axis=0)


def from_tiles(value, out):
    shape = (8, LANES)
    diagonal_mask = iota(shape, 0) == iota(shape, 1) >> 4
    lane_slot = iota(shape, 1) >> 4
    for half in range(2):
        for x in range(2):
            tile = value[half * 8 : half * 8 + 8, x * LANES : (x + 1) * LANES]
            for slot in range(8):
                own = spread_lanes(jnp.where(lane_slot == slot, tile, 0.0))
                row = jnp.sum(jnp.where(diagonal_mask, own, 0.0), axis=0, keepdims=True)
                z = slot & 3
                out[x, slot >> 2, z : z + 1, half * LANES : (half + 1) * LANES] = row


def pack_bricks(field):
    return jnp.concatenate([field[0:8], field[8:16]], axis=1)


def unpack_bricks(packed):
    return jnp.concatenate([packed[:, 0 : 2 * LANES], packed[:, 2 * LANES : 4 * LANES]], axis=0)


def pack_kernel(
    rhs_hbm, diagonal_hbm, blocks_hbm, neighbours_hbm,
    matrix, start, to_x, to_y, to_xy,
    rhs, diagonal, blocks, neighbours, sems,
):
    sources = (neighbours_hbm, diagonal_hbm, rhs_hbm, blocks_hbm)
    copies = [
        pltpu.make_async_copy(source, target, sems.at[q])
        for q, (source, target) in enumerate(zip(sources, (neighbours, diagonal, rhs, blocks)))
    ]
    for copy in copies:
        copy.start()
    matrix[:, 384:WIDE] = jnp.zeros((matrix.shape[0], WIDE - 384), jnp.float32)
    eye = iota((SLOT_ROWS, SLOT_ROWS), 0) == iota((SLOT_ROWS, SLOT_ROWS), 1)
    totals = [length * lax.axis_size(axis) for length, axis in zip(LENGTHS, AXES)]
    corner = [length * lax.axis_index(axis) for length, axis in zip(LENGTHS, AXES)]
    bits = [total.bit_length() - 1 for total in totals]
    for copy in copies[:2]:
        copy.wait()
    for x in range(2):
        for y in range(2):
            index = neighbours[x, y]
            along_x = index >> (bits[1] + bits[2])
            along_y = (index >> bits[2]) & (totals[1] - 1)
            along_z = index & (totals[2] - 1)
            z_here = corner[2] + iota(index.shape, 0)
            code = (along_x - (corner[0] + x - 1)) & (totals[0] - 1)
            code = code * 3 + ((along_y - (corner[1] + y - 1)) & (totals[1] - 1))
            code = code * 3 + ((along_z - z_here + 1) & (totals[2] - 1))
            code = code.astype(jnp.float32)
            for z in range(4):
                row = ((x * 2 + y) * 4 + z) * SLOT_ROWS
                matrix[row : row + 1, CODE : CODE + SELF] = code[z : z + 1]
                matrix[row : row + 1, CODE + SELF : CODE + SELF + 1] = jnp.full(
                    (1, 1), 13.0, jnp.float32
                )
                own = SHIFT - jnp.broadcast_to(diagonal[x, y, z : z + 1], eye.shape)
                matrix[row : row + SLOT_ROWS, 432:448] = jnp.where(eye, own, 0.0)
    copies[2].wait()
    value = to_tiles(lambda x, y, z: rhs[x, y, z : z + 1])
    start[...] = value
    bricks = pack_bricks(value)
    copies[3].wait()
    for x in range(2):
        for y in range(2):
            for z in range(4):
                row = ((x * 2 + y) * 4 + z) * SLOT_ROWS
                matrix[row : row + SLOT_ROWS, 0:432] = blocks[x, y, z]
    for out, row in ((to_x, 64), (to_y, 128), (to_xy, 0)):
        out[0:64] = matrix[row : row + 64]
        out[64:72] = bricks


def far_columns(matrix, from_x, from_y, from_xy):
    return (matrix, 192), (from_y, 0), (from_x, 0), (from_xy, 0)


def is_even():
    return lax.rem(lax.axis_index("gz"), 2) == 0


def spread_kernel(matrix, from_x, from_y, from_xy, start, to_first, to_second):
    even = is_even()
    for q, (ref, row) in enumerate(far_columns(matrix, from_x, from_y, from_xy)):
        up, down = ref[row + 48 : row + 64], ref[row : row + 16]
        to_first[q * 16 : q * 16 + 16] = jnp.where(even, up, down)
        to_second[q * 16 : q * 16 + 16] = jnp.where(even, down, up)
    bricks = [pack_bricks(start[...])] + [ref[64:72] for ref in (from_y, from_x, from_xy)]
    for q, brick in enumerate(bricks):
        to_first[64 + q * 8 : 72 + q * 8] = brick
        to_second[64 + q * 8 : 72 + q * 8] = brick


def outside(low, high):
    upper = ((iota(low.shape, 1) >> 4) & 3) < 2
    return jnp.where(upper, high, low)


def far_atom(row):
    column = (row * 43) >> 8
    return 1 + (column >> 1), 1 + (column & 1), row - 6 * column - 1


def near_atom(row):
    return row >> 3, (row >> 2) & 1, row & 3


def join_kernel(
    matrix, from_x, from_y, from_xy, start, first, second,
    wide, places, own, piece_y, piece_x, piece_xy,
):
    even = is_even()
    for q, (ref, row) in enumerate(far_columns(matrix, from_x, from_y, from_xy)):
        one, two = first[q * 16 : q * 16 + 16], second[q * 16 : q * 16 + 16]
        wide[q * 96 : q * 96 + 16] = jnp.where(even, two, one)
        wide[q * 96 + 16 : q * 96 + 80] = ref[row : row + 64]
        wide[q * 96 + 80 : q * 96 + 96] = jnp.where(even, one, two)
    inner = [start[...]] + [unpack_bricks(ref[64:72]) for ref in (from_y, from_x, from_xy)]
    for q, (out, value) in enumerate(zip((own, piece_y, piece_x, piece_xy), inner)):
        one = unpack_bricks(first[64 + q * 8 : 72 + q * 8])
        two = unpack_bricks(second[64 + q * 8 : 72 + q * 8])
        low, high = jnp.where(even, two, one), jnp.where(even, one, two)
        out[:, 0 : 2 * LANES] = value
        out[:, 2 * LANES : 4 * LANES] = outside(low, high)
    find_places(wide, 24, far_atom, far_place, far_slot, places)


def layers_kernel(value, first, second, out):
    even = is_even()
    one, two = first[...], second[...]
    out[:, 0 : 2 * LANES] = value[...]
    low, high = jnp.where(even, two, one), jnp.where(even, one, two)
    out[:, 2 * LANES : 4 * LANES] = outside(low, high)


def near_places_kernel(matrix, places):
    find_places(matrix, ATOMS, near_atom, near_place, near_slot, places)


def with_places(places_in, places, sem, work):
    copy = pltpu.make_async_copy(places_in, places, sem)
    copy.start()
    work()
    copy.wait()


def far_kernel(
    matrix, places_in, own, from_y, from_x, from_xy, out, field, gathered, places, sem
):
    with_places(places_in, places, sem, lambda: set_tiles(field, (own, from_y, from_x, from_xy)))
    out[...] = couple(matrix, field, places, gathered)


def near_kernel(
    matrix, places_in, own, from_y, from_x, from_xy, out, before, field, gathered, places, sem
):
    with_places(places_in, places, sem, lambda: set_tiles(field, (from_xy, from_x, from_y, own)))
    out[...] = couple(matrix, field, places, gathered)
    before[...] = pick_own(field)


def last_kernel(
    matrix, places_in, own, from_y, from_x, from_xy, start, first, second, third_out, out,
    field, gathered, places, sem,
):
    with_places(places_in, places, sem, lambda: set_tiles(field, (from_xy, from_x, from_y, own)))
    fourth = couple(matrix, field, places, gathered)
    third = pick_own(field)
    third_out[...] = third
    gram_kernel([start[...], first[...], second[...], third, fourth], out)


def call(kernel, shapes, *operands, scratch=(), place=VMEM):
    shapes = [
        shape if isinstance(shape, jax.ShapeDtypeStruct) else jax.ShapeDtypeStruct(shape, jnp.float32)
        for shape in shapes
    ]
    return pl.pallas_call(
        kernel,
        out_shape=shapes,
        in_specs=[place] * len(operands),
        out_specs=[VMEM] * len(shapes),
        scratch_shapes=list(scratch),
        compiler_params=pltpu.CompilerParams(vmem_limit_bytes=24 * 1024 * 1024),
    )(*operands)


def scratch_for(tiles, groups):
    return (
        pltpu.VMEM((tiles * 8, SLOT_ROWS, LANES), jnp.float32),
        pltpu.VMEM((groups, WIDE, LANES), jnp.float32),
        pltpu.SMEM((groups * 8, LANES), jnp.int32),
        pltpu.SemaphoreType.DMA,
    )


def fetch(value, first, second):
    sizes = [lax.axis_size(axis) for axis in AXES]
    pairs = []
    for a in range(sizes[0]):
        for b in range(sizes[1]):
            for c in range(sizes[2]):
                source = ((a + first) % sizes[0] * sizes[1] + (b + second) % sizes[1]) * sizes[2] + c
                pairs.append((source, (a * sizes[1] + b) * sizes[2] + c))
    return lax.ppermute(value, AXES, pairs)


def fetch_three(to_x, to_y, to_xy, sign):
    from_x, from_xy = fetch(to_x, sign, 0), fetch(to_xy, sign, sign)
    return fetch(to_y, 0, sign), from_x, from_xy


def swap_layers(to_first, to_second):
    count = lax.axis_size("gz")
    even = [(i, i ^ 1) for i in range(count)]
    odd = [(i, (i + 1 if i % 2 else i - 1) % count) for i in range(count)]
    return lax.ppermute(to_first, "gz", even), lax.ppermute(to_second, "gz", odd)


def body(rhs, diagonal, blocks, neighbours):
    width = rhs.shape[-1]
    flat = (SLOT_ROWS, width)
    matrix, start, *out = call(
        pack_kernel,
        [(ATOMS * SLOT_ROWS, WIDE), flat] + [(72, WIDE)] * 3,
        rhs, diagonal, blocks, neighbours,
        scratch=[
            pltpu.VMEM(rhs.shape, rhs.dtype),
            pltpu.VMEM(diagonal.shape, diagonal.dtype),
            pltpu.VMEM(blocks.shape, blocks.dtype),
            pltpu.VMEM(neighbours.shape, neighbours.dtype),
            pltpu.SemaphoreType.DMA((4,)),
        ],
        place=pl.BlockSpec(memory_space=pl.ANY),
    )
    from_y, from_x, from_xy = fetch_three(*out, 1)
    sides = from_x, from_y, from_xy
    (near_places,) = call(
        near_places_kernel, [jax.ShapeDtypeStruct((ATOMS, LANES), jnp.int32)], matrix
    )
    layers = swap_layers(*call(spread_kernel, [(96, WIDE)] * 2, matrix, *sides, start))
    wide, far_places, *pieces = call(
        join_kernel,
        [(24 * SLOT_ROWS, WIDE), jax.ShapeDtypeStruct((24, LANES), jnp.int32)]
        + [(SLOT_ROWS, 4 * LANES)] * 4,
        matrix, *sides, start, *layers,
    )
    far_scratch, near_scratch = scratch_for(16, 3), scratch_for(12, 2)
    far_shape = (SLOT_ROWS, 3 * LANES)
    (first,) = call(far_kernel, [far_shape], wide, far_places, *pieces, scratch=far_scratch)
    second, first_own = call(
        near_kernel, [flat, flat],
        matrix, near_places, first, *fetch_three(first, first, first, -1),
        scratch=near_scratch,
    )
    (layered,) = call(
        layers_kernel, [(SLOT_ROWS, 4 * LANES)], second, *swap_layers(second, second)
    )
    (third,) = call(
        far_kernel, [far_shape],
        wide, far_places, layered, *fetch_three(layered, layered, layered, 1),
        scratch=far_scratch,
    )
    third_own, message = call(
        last_kernel,
        [flat, (lax.axis_size("gx"), 4, LANES)],
        matrix, near_places, third, *fetch_three(third, third, third, -1),
        start, first_own, second,
        scratch=near_scratch,
    )
    rest = lax.axis_size("gy") * lax.axis_size("gz")
    message = lax.all_to_all(message, "gx", 0, 0, tiled=True)
    (message,) = call(relay_kernel, [(rest, 4, LANES)], message)
    message = lax.all_to_all(message, ("gy", "gz"), 0, 0, tiled=True)
    (result,) = call(finish_kernel, [rhs.shape], message, start, first_own, second, third_own)
    return result


def solution(mesh):
    return jax.shard_map(
        body,
        mesh=mesh,
        in_specs=(
            P("gx", "gy", "gz", None),
            P("gx", "gy", "gz", None),
            P("gx", "gy", "gz", None, None),
            P("gx", "gy", "gz", None),
        ),
        out_specs=P("gx", "gy", "gz", None),
        check_vma=False,
    )
```

time: 143 us -> 146 us (1.021)
  starting transfers between devices: 53.6 us -> 62.5 us
  waiting for transfers between devices: 34.7 us -> 30.1 us
  Pallas kernels: 14.1 us -> 12.3 us
  blocking collectives: 35.2 us -> 36.7 us
    ppermute x14 -> x16, starting transfers between devices: 53.6 us -> 62.5 us  [the longest x12 49.8 us: fetch(): return lax.ppermute(value, AXES, pairs)]
    ppermute x14 -> x16, waiting for transfers between devices: 34.7 us -> 30.1 us  [the longest x12 19.7 us: fetch(): return lax.ppermute(value, AXES, pairs)]
    pallas_call x9 -> x11, Pallas kernels: 14.1 us -> 12.3 us  [call(): pl.pallas_call(kernel, out_shape=shapes, in_specs=[place] * len(operands)...]
    reshape x5 -> x0, local copies, waits for them, and re-layouts: 1.78 us -> none  [the longest x3 0.97 us: body(): rhs.reshape(atoms, components, columns).transpose(1, 0, 2)]
    unnamed x4 -> x8, local copies, waits for them, and re-layouts: 1.73 us -> 3.15 us
  transfers between devices with their start and end apart: 14 -> 16, of which waited for: 10 -> 8; matrix products, arithmetic and copies ran while one was open for 0% -> 0% of each run, Pallas kernels for 0% -> 0%
where the time goes in v3:
time: 146 us; the launch traced here: 145 us
  starting transfers between devices  62.5 us (43%)
  blocking collectives  36.7 us (25%)
  waiting for transfers between devices  30.1 us (21%)
  Pallas kernels  12.3 us (8%)
  local copies, waits for them, and re-layouts  3.15 us (2%)
    ppermute x12, starting transfers between devices, fetch(): return lax.ppermute(value, AXES, pairs)  49.8 us
    all_to_all x1, blocking collectives, body(): message = lax.all_to_all(message, ('gy', 'gz'), 0, 0, tiled=True)  25.3 us
    ppermute x12, waiting for transfers between devices, fetch(): return lax.ppermute(value, AXES, pairs)  19.7 us
    pallas_call x11, Pallas kernels, call(): pl.pallas_call(kernel, out_shape=shapes, in_specs=[place] * len(operands)...  12.3 us
    all_to_all x1, blocking collectives, body(): message = lax.all_to_all(message, 'gx', 0, 0, tiled=True)  11.4 us
    ppermute x2, waiting for transfers between devices, swap_layers(): lax.ppermute(to_second, 'gz', odd)  10.3 us
    ppermute x2, starting transfers between devices, swap_layers(): lax.ppermute(to_first, 'gz', even)  8.89 us
    ppermute x2, starting transfers between devices, swap_layers(): lax.ppermute(to_second, 'gz', odd)  3.84 us
  transfers between devices with their start and end apart: 16, of which 8 were waited for; matrix products, arithmetic and copies ran while one was open for 0% of the time, Pallas kernels for 0%

profile of v3, /device:TPU:1, one launch (start us, length us, event | category | flops | bytes accessed | tf_op | source)
XLA Modules:
  0.0 145.0 jit_solution(10135505772831271034)
XLA Ops:
  3.7 5.9 %collective-permute-start = (f32[72,512]{1,0:T(8,128)S(1)}, f32[72,512]{1,0:T(8,128)S(1)}, u32[]{:S(2)}, u32[]{:S(2)}) collective-permute-start(f32[72,512]{1,0:T(8,128)S(1)} %get-tuple-element.23), channel_id=1, source_target_pairs={{64,0},{65,1},{66,2},{67,3},{68,4},{69,5},{70,6},{71,7},{72,8},{73... | collective-permute-start | bytes 442376 | tf_op jit(solution)/shard_map/ppermute | solution.py:548
  9.6 10.7 %collective-permute-start.1 = (f32[72,512]{1,0:T(8,128)S(1)}, f32[72,512]{1,0:T(8,128)S(1)}, u32[]{:S(2)}, u32[]{:S(2)}) collective-permute-start(f32[72,512]{1,0:T(8,128)S(1)} %get-tuple-element.24), channel_id=1, source_target_pairs={{16,0},{17,1},{18,2},{19,3},{20,4},{21,5},{22,6},{23,7},{24,8},{25... | collective-permute-start | bytes 442376 | tf_op jit(solution)/shard_map/ppermute | solution.py:548
  20.3 3.0 %collective-permute-start.2 = (f32[72,512]{1,0:T(8,128)S(1)}, f32[72,512]{1,0:T(8,128)S(1)}, u32[]{:S(2)}, u32[]{:S(2)}) collective-permute-start(f32[72,512]{1,0:T(8,128)S(1)} %get-tuple-element.25), channel_id=1, source_target_pairs={{80,0},{81,1},{82,2},{83,3},{84,4},{85,5},{86,6},{87,7},{88,8},{89... | collective-permute-start | bytes 442376 | tf_op jit(solution)/shard_map/ppermute | solution.py:548
  23.3 8.1 %collective-permute-done.1.from_y = f32[72,512]{1,0:T(8,128)S(1)} collective-permute-done((f32[72,512]{1,0:T(8,128)S(1)}, f32[72,512]{1,0:T(8,128)S(1)}, u32[]{:S(2)}, u32[]{:S(2)}) %collective-permute-start.1) | collective-permute-done | bytes 147488 | tf_op jit(solution)/shard_map/ppermute | solution.py:548
  31.4 4.4 %collective-permute-start.3 = (f32[96,512]{1,0:T(8,128)S(1)}, f32[96,512]{1,0:T(8,128)S(1)}, u32[]{:S(2)}, u32[]{:S(2)}) collective-permute-start(f32[96,512]{1,0:T(8,128)S(1)} %get-tuple-element.27), channel_id=1, source_target_pairs={{0,1},{1,0},{2,3},{3,2},{4,5},{5,4},{6,7},{7,6},{8,9},{9,8},{10,11... | collective-permute-start | bytes 589832 | tf_op jit(solution)/shard_map/ppermute | solution.py:560
  37.7 7.2 %collective-permute-done.4.second = f32[96,512]{1,0:T(8,128)S(1)} collective-permute-done((f32[96,512]{1,0:T(8,128)S(1)}, f32[96,512]{1,0:T(8,128)S(1)}, u32[]{:S(2)}, u32[]{:S(2)}) %collective-permute-start.4) | collective-permute-done | bytes 196640 | tf_op jit(solution)/shard_map/ppermute | solution.py:560
  45.0 2.7 %shard_map.50.own = f32[16,384]{1,0:T(8,128)S(1)} custom-call(f32[384,512]{1,0:T(8,128)S(1)} %get-tuple-element.29.matrix, s32[24,128]{1,0:T(8,128)S(1)} %get-tuple-element.30.places_in, f32[16,512]{1,0:T(8,128)S(1)} %get-tuple-element.31.own, f32[16,512]{1,0:T(8,128)S(1)} %get-tuple-element.32.from_y, f32[16,512]{1,0:T(8,128)S(1)} %get-tuple-element.33.from_x, ...), custom_call_target="tpu_custom_call" | custom-call | tf_op jit(solution)/shard_map/pallas_call | solution.py:521
  47.7 2.9 %collective-permute-start.5 = (f32[16,384]{1,0:T(8,128)S(1)}, f32[16,384]{1,0:T(8,128)S(1)}, u32[]{:S(2)}, u32[]{:S(2)}) collective-permute-start(f32[16,384]{1,0:T(8,128)S(1)} %shard_map.50.own), channel_id=1, source_target_pairs={{48,0},{49,1},{50,2},{51,3},{52,4},{53,5},{54,6},{55,7},{56,8},{57... | collective-permute-start | bytes 73736 | tf_op jit(solution)/shard_map/ppermute | solution.py:548
  52.6 3.5 %collective-permute-start.7 = (f32[16,384]{1,0:T(8,128)S(1)}, f32[16,384]{1,0:T(8,128)S(1)}, u32[]{:S(2)}, u32[]{:S(2)}) collective-permute-start(f32[16,384]{1,0:T(8,128)S(1)} %shard_map.50.own), channel_id=1, source_target_pairs={{496,0},{497,1},{498,2},{499,3},{500,4},{501,5},{502,6},{503,7},{5... | collective-permute-start | bytes 73736 | tf_op jit(solution)/shard_map/ppermute | solution.py:548
  56.7 4.8 %collective-permute-done.7.from_xy = f32[16,384]{1,0:T(8,128)S(1)} collective-permute-done((f32[16,384]{1,0:T(8,128)S(1)}, f32[16,384]{1,0:T(8,128)S(1)}, u32[]{:S(2)}, u32[]{:S(2)}) %collective-permute-start.7) | collective-permute-done | bytes 24608 | tf_op jit(solution)/shard_map/ppermute | solution.py:548
  61.5 2.1 %shard_map.51 = (f32[16,256]{1,0:T(8,128)S(1)}, f32[16,256]{1,0:T(8,128)S(1)}) custom-call(f32[256,512]{1,0:T(8,128)S(1)} %get-tuple-element.22.matrix, s32[16,128]{1,0:T(8,128)S(1)} %shard_map.47.places_in, f32[16,384]{1,0:T(8,128)S(1)} %shard_map.50.own, f32[16,384]{1,0:T(8,128)S(1)} %collective-permute-done.5.from_y, ...), custom_call_target="tpu_custom_call" | custom-call | tf_op jit(solution)/shard_map/pallas_call | solution.py:521
  63.6 4.5 %collective-permute-start.8 = (f32[16,256]{1,0:T(8,128)S(1)}, f32[16,256]{1,0:T(8,128)S(1)}, u32[]{:S(2)}, u32[]{:S(2)}) collective-permute-start(f32[16,256]{1,0:T(8,128)S(1)} %get-tuple-element.35.value.second.refs_2_), channel_id=1, source_target_pairs={{0,1},{1,0},{2,3},{3,2},{4,5},{5,4},{6,7},{7,6},{8,9},{9,8},{10,11... | collective-permute-start | bytes 49160 | tf_op jit(solution)/shard_map/ppermute | solution.py:560
  70.1 3.1 %collective-permute-done.9.second = f32[16,256]{1,0:T(8,128)S(1)} collective-permute-done((f32[16,256]{1,0:T(8,128)S(1)}, f32[16,256]{1,0:T(8,128)S(1)}, u32[]{:S(2)}, u32[]{:S(2)}) %collective-permute-start.9) | collective-permute-done | bytes 16416 | tf_op jit(solution)/shard_map/ppermute | solution.py:560
  73.2 4.5 %collective-permute-start.10 = (f32[16,512]{1,0:T(8,128)S(1)}, f32[16,512]{1,0:T(8,128)S(1)}, u32[]{:S(2)}, u32[]{:S(2)}) collective-permute-start(f32[16,512]{1,0:T(8,128)S(1)} %shard_map.52.own), channel_id=1, source_target_pairs={{16,0},{17,1},{18,2},{19,3},{20,4},{21,5},{22,6},{23,7},{24,8},{25... | collective-permute-start | bytes 98312 | tf_op jit(solution)/shard_map/ppermute | solution.py:548
  77.7 2.9 %collective-permute-start.11 = (f32[16,512]{1,0:T(8,128)S(1)}, f32[16,512]{1,0:T(8,128)S(1)}, u32[]{:S(2)}, u32[]{:S(2)}) collective-permute-start(f32[16,512]{1,0:T(8,128)S(1)} %shard_map.52.own), channel_id=1, source_target_pairs={{64,0},{65,1},{66,2},{67,3},{68,4},{69,5},{70,6},{71,7},{72,8},{73... | collective-permute-start | bytes 98312 | tf_op jit(solution)/shard_map/ppermute | solution.py:548
  80.6 5.5 %collective-permute-start.12 = (f32[16,512]{1,0:T(8,128)S(1)}, f32[16,512]{1,0:T(8,128)S(1)}, u32[]{:S(2)}, u32[]{:S(2)}) collective-permute-start(f32[16,512]{1,0:T(8,128)S(1)} %shard_map.52.own), channel_id=1, source_target_pairs={{80,0},{81,1},{82,2},{83,3},{84,4},{85,5},{86,6},{87,7},{88,8},{89... | collective-permute-start | bytes 98312 | tf_op jit(solution)/shard_map/ppermute | solution.py:548
  87.1 2.7 %shard_map.53.own = f32[16,384]{1,0:T(8,128)S(1)} custom-call(f32[384,512]{1,0:T(8,128)S(1)} %get-tuple-element.29.matrix, s32[24,128]{1,0:T(8,128)S(1)} %get-tuple-element.30.places_in, f32[16,512]{1,0:T(8,128)S(1)} %shard_map.52.own, f32[16,512]{1,0:T(8,128)S(1)} %collective-permute-done.10.from_y, f32[16,512]{1,0:T(8,128)S(1)} %collective-permute-done.11.from_x, ...), custom_call_target="tpu_custom_call" | custom-call | tf_op jit(solution)/shard_map/pallas_call | solution.py:521
  89.8 3.6 %collective-permute-start.13 = (f32[16,384]{1,0:T(8,128)S(1)}, f32[16,384]{1,0:T(8,128)S(1)}, u32[]{:S(2)}, u32[]{:S(2)}) collective-permute-start(f32[16,384]{1,0:T(8,128)S(1)} %shard_map.53.own), channel_id=1, source_target_pairs={{48,0},{49,1},{50,2},{51,3},{52,4},{53,5},{54,6},{55,7},{56,8},{57... | collective-permute-start | bytes 73736 | tf_op jit(solution)/shard_map/ppermute | solution.py:548
  93.4 2.0 %collective-permute-start.14 = (f32[16,384]{1,0:T(8,128)S(1)}, f32[16,384]{1,0:T(8,128)S(1)}, u32[]{:S(2)}, u32[]{:S(2)}) collective-permute-start(f32[16,384]{1,0:T(8,128)S(1)} %shard_map.53.own), channel_id=1, source_target_pairs={{448,0},{449,1},{450,2},{451,3},{452,4},{453,5},{454,6},{455,7},{4... | collective-permute-start | bytes 73736 | tf_op jit(solution)/shard_map/ppermute | solution.py:548
  95.4 3.4 %collective-permute-start.15 = (f32[16,384]{1,0:T(8,128)S(1)}, f32[16,384]{1,0:T(8,128)S(1)}, u32[]{:S(2)}, u32[]{:S(2)}) collective-permute-start(f32[16,384]{1,0:T(8,128)S(1)} %shard_map.53.own), channel_id=1, source_target_pairs={{496,0},{497,1},{498,2},{499,3},{500,4},{501,5},{502,6},{503,7},{5... | collective-permute-start | bytes 73736 | tf_op jit(solution)/shard_map/ppermute | solution.py:548
  99.2 5.0 %collective-permute-done.15.from_xy = f32[16,384]{1,0:T(8,128)S(1)} collective-permute-done((f32[16,384]{1,0:T(8,128)S(1)}, f32[16,384]{1,0:T(8,128)S(1)}, u32[]{:S(2)}, u32[]{:S(2)}) %collective-permute-start.15) | collective-permute-done | bytes 24608 | tf_op jit(solution)/shard_map/ppermute | solution.py:548
  104.2 2.5 %shard_map.54 = (f32[16,256]{1,0:T(8,128)S(1)}, f32[8,4,128]{2,1,0:T(4,128)S(1)}) custom-call(f32[256,512]{1,0:T(8,128)S(1)} %get-tuple-element.22.matrix, s32[16,128]{1,0:T(8,128)S(1)} %shard_map.47.places_in, f32[16,384]{1,0:T(8,128)S(1)} %shard_map.53.own, f32[16,384]{1,0:T(8,128)S(1)} %collective-permute-done.13.from_y, ...), custom_call_target="tpu_custom_call" | custom-call | tf_op jit(solution)/shard_map/pallas_call | solution.py:521
  106.7 11.4 %all_to_all.10.ref = f32[8,4,128]{2,1,0:T(4,128)S(1)} all-to-all(f32[8,4,128]{2,1,0:T(4,128)S(1)} %get-tuple-element.37), channel_id=1, replica_groups=mesh['gx'=8,'gy'=4,'gz'=16] {'gx'}, dimensions={0} | all-to-all | bytes 32768 | tf_op jit(solution)/shard_map/all_to_all | solution.py:615
  118.2 25.3 %all_to_all.11.ref = f32[64,4,128]{2,1,0:T(4,128)S(1)} all-to-all(f32[64,4,128]{2,1,0:T(4,128)S(1)} %shard_map.55), channel_id=1, replica_groups=mesh['gx'=8,'gy'=4,'gz'=16] {'gy','gz'}, dimensions={0} | all-to-all | bytes 262144 | tf_op jit(solution)/shard_map/all_to_all | solution.py:617
  (29 shorter events, 13.2 us)
Async XLA Ops:
  0.0 1.0 copy-start
  1.0 0.7 copy-start.1
  1.8 0.7 copy-start.2
  2.5 0.7 copy-start.3
  3.7 19.6 %collective-permute-start = (f32[72,512]{1,0:T(8,128)S(1)}, f32[72,512]{1,0:T(8,128)S(1)}, u32[]{:S(2)}, u32[]{:S(2)}) collective-permute-start(f32[72,512]{1,0:T(8,128)S(1)} %get-tuple-element.23), channel_id=1, source_target_pairs={{64,0},{65,1},{66,2},{67,3},{68,4},{69,5},{70,6},{71,7},{72,8},{73... | collective-permute-start | bytes 442376 | tf_op jit(solution)/shard_map/ppermute | solution.py:548
  9.6 21.7 %collective-permute-start.1 = (f32[72,512]{1,0:T(8,128)S(1)}, f32[72,512]{1,0:T(8,128)S(1)}, u32[]{:S(2)}, u32[]{:S(2)}) collective-permute-start(f32[72,512]{1,0:T(8,128)S(1)} %get-tuple-element.24), channel_id=1, source_target_pairs={{16,0},{17,1},{18,2},{19,3},{20,4},{21,5},{22,6},{23,7},{24,8},{25... | collective-permute-start | bytes 442376 | tf_op jit(solution)/shard_map/ppermute | solution.py:548
  20.3 11.1 %collective-permute-start.2 = (f32[72,512]{1,0:T(8,128)S(1)}, f32[72,512]{1,0:T(8,128)S(1)}, u32[]{:S(2)}, u32[]{:S(2)}) collective-permute-start(f32[72,512]{1,0:T(8,128)S(1)} %get-tuple-element.25), channel_id=1, source_target_pairs={{80,0},{81,1},{82,2},{83,3},{84,4},{85,5},{86,6},{87,7},{88,8},{89... | collective-permute-start | bytes 442376 | tf_op jit(solution)/shard_map/ppermute | solution.py:548
  31.4 6.3 %collective-permute-start.3 = (f32[96,512]{1,0:T(8,128)S(1)}, f32[96,512]{1,0:T(8,128)S(1)}, u32[]{:S(2)}, u32[]{:S(2)}) collective-permute-start(f32[96,512]{1,0:T(8,128)S(1)} %get-tuple-element.27), channel_id=1, source_target_pairs={{0,1},{1,0},{2,3},{3,2},{4,5},{5,4},{6,7},{7,6},{8,9},{9,8},{10,11... | collective-permute-start | bytes 589832 | tf_op jit(solution)/shard_map/ppermute | solution.py:560
  35.8 9.1 %collective-permute-start.4 = (f32[96,512]{1,0:T(8,128)S(1)}, f32[96,512]{1,0:T(8,128)S(1)}, u32[]{:S(2)}, u32[]{:S(2)}) collective-permute-start(f32[96,512]{1,0:T(8,128)S(1)} %get-tuple-element.28), channel_id=1, source_target_pairs={{0,15},{1,2},{2,1},{3,4},{4,3},{5,6},{6,5},{7,8},{8,7},{9,10},{10,... | collective-permute-start | bytes 589832 | tf_op jit(solution)/shard_map/ppermute | solution.py:560
  47.7 8.5 %collective-permute-start.5 = (f32[16,384]{1,0:T(8,128)S(1)}, f32[16,384]{1,0:T(8,128)S(1)}, u32[]{:S(2)}, u32[]{:S(2)}) collective-permute-start(f32[16,384]{1,0:T(8,128)S(1)} %shard_map.50.own), channel_id=1, source_target_pairs={{48,0},{49,1},{50,2},{51,3},{52,4},{53,5},{54,6},{55,7},{56,8},{57... | collective-permute-start | bytes 73736 | tf_op jit(solution)/shard_map/ppermute | solution.py:548
  50.7 6.1 %collective-permute-start.6 = (f32[16,384]{1,0:T(8,128)S(1)}, f32[16,384]{1,0:T(8,128)S(1)}, u32[]{:S(2)}, u32[]{:S(2)}) collective-permute-start(f32[16,384]{1,0:T(8,128)S(1)} %shard_map.50.own), channel_id=1, source_target_pairs={{448,0},{449,1},{450,2},{451,3},{452,4},{453,5},{454,6},{455,7},{4... | collective-permute-start | bytes 73736 | tf_op jit(solution)/shard_map/ppermute | solution.py:548
  52.6 8.9 %collective-permute-start.7 = (f32[16,384]{1,0:T(8,128)S(1)}, f32[16,384]{1,0:T(8,128)S(1)}, u32[]{:S(2)}, u32[]{:S(2)}) collective-permute-start(f32[16,384]{1,0:T(8,128)S(1)} %shard_map.50.own), channel_id=1, source_target_pairs={{496,0},{497,1},{498,2},{499,3},{500,4},{501,5},{502,6},{503,7},{5... | collective-permute-start | bytes 73736 | tf_op jit(solution)/shard_map/ppermute | solution.py:548
  63.6 6.5 %collective-permute-start.8 = (f32[16,256]{1,0:T(8,128)S(1)}, f32[16,256]{1,0:T(8,128)S(1)}, u32[]{:S(2)}, u32[]{:S(2)}) collective-permute-start(f32[16,256]{1,0:T(8,128)S(1)} %get-tuple-element.35.value.second.refs_2_), channel_id=1, source_target_pairs={{0,1},{1,0},{2,3},{3,2},{4,5},{5,4},{6,7},{7,6},{8,9},{9,8},{10,11... | collective-permute-start | bytes 49160 | tf_op jit(solution)/shard_map/ppermute | solution.py:560
  68.1 5.1 %collective-permute-start.9 = (f32[16,256]{1,0:T(8,128)S(1)}, f32[16,256]{1,0:T(8,128)S(1)}, u32[]{:S(2)}, u32[]{:S(2)}) collective-permute-start(f32[16,256]{1,0:T(8,128)S(1)} %get-tuple-element.35.value.second.refs_2_), channel_id=1, source_target_pairs={{0,15},{1,2},{2,1},{3,4},{4,3},{5,6},{6,5},{7,8},{8,7},{9,10},{10,... | collective-permute-start | bytes 49160 | tf_op jit(solution)/shard_map/ppermute | solution.py:560
  73.2 12.9 %collective-permute-start.10 = (f32[16,512]{1,0:T(8,128)S(1)}, f32[16,512]{1,0:T(8,128)S(1)}, u32[]{:S(2)}, u32[]{:S(2)}) collective-permute-start(f32[16,512]{1,0:T(8,128)S(1)} %shard_map.52.own), channel_id=1, source_target_pairs={{16,0},{17,1},{18,2},{19,3},{20,4},{21,5},{22,6},{23,7},{24,8},{25... | collective-permute-start | bytes 98312 | tf_op jit(solution)/shard_map/ppermute | solution.py:548
  77.7 8.4 %collective-permute-start.11 = (f32[16,512]{1,0:T(8,128)S(1)}, f32[16,512]{1,0:T(8,128)S(1)}, u32[]{:S(2)}, u32[]{:S(2)}) collective-permute-start(f32[16,512]{1,0:T(8,128)S(1)} %shard_map.52.own), channel_id=1, source_target_pairs={{64,0},{65,1},{66,2},{67,3},{68,4},{69,5},{70,6},{71,7},{72,8},{73... | collective-permute-start | bytes 98312 | tf_op jit(solution)/shard_map/ppermute | solution.py:548
  80.6 6.5 %collective-permute-start.12 = (f32[16,512]{1,0:T(8,128)S(1)}, f32[16,512]{1,0:T(8,128)S(1)}, u32[]{:S(2)}, u32[]{:S(2)}) collective-permute-start(f32[16,512]{1,0:T(8,128)S(1)} %shard_map.52.own), channel_id=1, source_target_pairs={{80,0},{81,1},{82,2},{83,3},{84,4},{85,5},{86,6},{87,7},{88,8},{89... | collective-permute-start | bytes 98312 | tf_op jit(solution)/shard_map/ppermute | solution.py:548
  89.8 9.0 %collective-permute-start.13 = (f32[16,384]{1,0:T(8,128)S(1)}, f32[16,384]{1,0:T(8,128)S(1)}, u32[]{:S(2)}, u32[]{:S(2)}) collective-permute-start(f32[16,384]{1,0:T(8,128)S(1)} %shard_map.53.own), channel_id=1, source_target_pairs={{48,0},{49,1},{50,2},{51,3},{52,4},{53,5},{54,6},{55,7},{56,8},{57... | collective-permute-start | bytes 73736 | tf_op jit(solution)/shard_map/ppermute | solution.py:548
  93.4 5.8 %collective-permute-start.14 = (f32[16,384]{1,0:T(8,128)S(1)}, f32[16,384]{1,0:T(8,128)S(1)}, u32[]{:S(2)}, u32[]{:S(2)}) collective-permute-start(f32[16,384]{1,0:T(8,128)S(1)} %shard_map.53.own), channel_id=1, source_target_pairs={{448,0},{449,1},{450,2},{451,3},{452,4},{453,5},{454,6},{455,7},{4... | collective-permute-start | bytes 73736 | tf_op jit(solution)/shard_map/ppermute | solution.py:548
  95.4 8.8 %collective-permute-start.15 = (f32[16,384]{1,0:T(8,128)S(1)}, f32[16,384]{1,0:T(8,128)S(1)}, u32[]{:S(2)}, u32[]{:S(2)}) collective-permute-start(f32[16,384]{1,0:T(8,128)S(1)} %shard_map.53.own), channel_id=1, source_target_pairs={{496,0},{497,1},{498,2},{499,3},{500,4},{501,5},{502,6},{503,7},{5... | collective-permute-start | bytes 73736 | tf_op jit(solution)/shard_map/ppermute | solution.py:548

commit v4 on v3

--- a/solution.py
+++ b/solution.py
@@ -229,36 +229,54 @@
 AXES = ("gx", "gy", "gz")
 
 
-def far_place(x, y, z):
-    piece = (x >> 1) * 2 + (y >> 1)
-    outside = ((z >> 2) != 0).astype(jnp.int32)
-    return (piece * 4 + outside * 2 + (x & 1)) * 8 + (y & 1) * 4 + (z & 3)
-
-
-def far_slot(x, y, z):
-    return (((x - 1) * 2 + y - 1) * 6 + z + 1) & 7
-
-
-def near_place(x, y, z):
-    x, y = x + 1, y + 1
-    piece = (x >> 1) * 2 + (y >> 1)
-    return (piece * 4 + (x & 1) * 2 + (y & 1)) * 6 + z + 1
-
-
-def near_slot(x, y, z):
-    return (y * 4 + z) & 7
-
-
-def find_places(matrix, count, atom, place, slot, out):
-    rows = [q * SLOT_ROWS for q in range(count)]
+def bricks_place(x, y, z):
+    brick = ((z + 4) >> 2) * 4 + (x >> 1) * 2 + (y >> 1)
+    return (brick * 2 + (x & 1)) * 8 + (y & 1) * 4 + (z & 3)
+
+
+def pieces_place(origin, run, low):
+    def place(x, y, z):
+        x, y = x - origin, y - origin
+        piece = (x >> 1) * 2 + (y >> 1)
+        return (piece * 4 + (x & 1) * 2 + (y & 1)) * run + z - low
+
+    return place
+
+
+def tall_far_atom(index):
+    column = (index * 205) >> 11
+    return 1 + (column >> 1), 1 + (column & 1), index - 10 * column - 3
+
+
+def far_atom(index):
+    column = (index * 43) >> 8
+    return 1 + (column >> 1), 1 + (column & 1), index - 6 * column - 1
+
+
+def tall_near_atom(index):
+    return index >> 4, (index >> 3) & 1, (index & 7) - 2
+
+
+def near_atom(index):
+    return index >> 3, (index >> 2) & 1, index & 3
+
+
+FAR_ROWS = [column * 10 + z + 3 for column in range(4) for z in range(-1, 5)]
+FIRST_PLACE, SECOND_PLACE = pieces_place(-1, 10, -3), pieces_place(0, 8, -2)
+THIRD_PLACE = pieces_place(-1, 6, -1)
+
+
+def find_places(matrix, rows, atom, place, out):
+    rows = [row * SLOT_ROWS for row in rows]
     code = jnp.concatenate([matrix[row : row + 1, CODE - 64 : CODE + 64] for row in rows], axis=0)
     code = pltpu.roll(code, 64, 1).astype(jnp.int32)
-    x, y, z = atom(iota(code.shape, 0))
+    index = iota(code.shape, 0)
+    x, y, z = atom(index)
     first = (code * 57) >> 9
     rest = code - 9 * first
     second = (rest * 11) >> 5
     where = place(x + first - 1, y + second - 1, z + rest - 3 * second - 1)
-    out[...] = (where & ~7) + ((slot(x, y, z) - where) & 7)
+    out[...] = (where & ~7) + ((index - where) & 7)
 
 
 def set_tiles(field, pieces):
@@ -271,9 +289,9 @@
                 field[place] = pltpu.roll(tile, turn * SLOT_ROWS, 1) if turn else tile
 
 
-def couple(matrix, field, places, gathered):
+def couple(matrix, rows, field, places, gathered):
     lane_slot = iota((SLOT_ROWS, LANES), 1) >> 4
-    groups = matrix.shape[0] // LANES
+    groups = len(rows) // 8
 
     def gather(k, carry):
         for q in range(groups):
@@ -284,15 +302,19 @@
             gathered[q, pl.ds(pl.multiple_of(k * SLOT_ROWS, SLOT_ROWS), SLOT_ROWS), :] = acc
         return carry
 
-    lax.fori_loop(0, SELF + 1, gather, 0, unroll=7)
+    lax.fori_loop(0, SELF + 1, gather, 0, unroll=SELF + 1)
     tiles = []
     for q in range(groups):
         gathered[q, CODE:WIDE, :] = jnp.zeros((WIDE - CODE, LANES), jnp.float32)
+        group = rows[q * 8 : q * 8 + 8]
+        left, start = [], 0
+        for r in range(1, 9):
+            if r == 8 or group[r] != group[r - 1] + 1:
+                left.append(matrix[group[start] * SLOT_ROWS : (group[r - 1] + 1) * SLOT_ROWS, :])
+                start = r
+        left = left[0] if len(left) == 1 else jnp.concatenate(left, axis=0)
         product = jnp.dot(
-            matrix[q * LANES : (q + 1) * LANES, :],
-            gathered[q],
-            precision=HIGH,
-            preferred_element_type=jnp.float32,
+            left, gathered[q], precision=HIGH, preferred_element_type=jnp.float32
         )
         acc = product[0:SLOT_ROWS]
         for slot in range(1, 8):
@@ -302,14 +324,18 @@
     return jnp.concatenate(tiles, axis=1)
 
 
-def pick_own(field):
+def pick_own(pieces, place):
     lane_slot = iota((SLOT_ROWS, LANES), 1) >> 4
     tiles = []
     for x in range(2):
         acc = None
         for slot in range(8):
-            where = near_place(x, slot >> 2, slot & 3)
-            tile = field[(where & ~7) + ((slot - where) & 7)]
+            where = place(x, slot >> 2, slot & 3)
+            count = pieces[0].shape[1] // LANES
+            tile, turn = where >> 3, (slot - where) & 7
+            lanes = pl.ds(tile % count * LANES, LANES)
+            tile = pieces[tile // count][:, lanes]
+            tile = pltpu.roll(tile, turn * SLOT_ROWS, 1) if turn else tile
             acc = tile if acc is None else jnp.where(lane_slot == slot, tile, acc)
         tiles.append(acc)
     return jnp.concatenate(tiles, axis=1)
@@ -422,95 +448,102 @@
     return lax.rem(lax.axis_index("gz"), 2) == 0
 
 
-def spread_kernel(matrix, from_x, from_y, from_xy, start, to_first, to_second):
+def spread_kernel(matrix, from_y, from_xy, from_x, start, to_first, to_second):
     even = is_even()
     for q, (ref, row) in enumerate(far_columns(matrix, from_x, from_y, from_xy)):
-        up, down = ref[row + 48 : row + 64], ref[row : row + 16]
-        to_first[q * 16 : q * 16 + 16] = jnp.where(even, up, down)
-        to_second[q * 16 : q * 16 + 16] = jnp.where(even, down, up)
+        up, down = ref[row + 16 : row + 64], ref[row : row + 48]
+        to_first[q * 48 : q * 48 + 48] = jnp.where(even, up, down)
+        to_second[q * 48 : q * 48 + 48] = jnp.where(even, down, up)
     bricks = [pack_bricks(start[...])] + [ref[64:72] for ref in (from_y, from_x, from_xy)]
     for q, brick in enumerate(bricks):
-        to_first[64 + q * 8 : 72 + q * 8] = brick
-        to_second[64 + q * 8 : 72 + q * 8] = brick
-
-
-def outside(low, high):
-    upper = ((iota(low.shape, 1) >> 4) & 3) < 2
-    return jnp.where(upper, high, low)
-
-
-def far_atom(row):
-    column = (row * 43) >> 8
-    return 1 + (column >> 1), 1 + (column & 1), row - 6 * column - 1
-
-
-def near_atom(row):
-    return row >> 3, (row >> 2) & 1, row & 3
-
-
-def join_kernel(
-    matrix, from_x, from_y, from_xy, start, first, second,
-    wide, places, own, piece_y, piece_x, piece_xy,
+        to_first[192 + q * 8 : 200 + q * 8] = brick
+        to_second[192 + q * 8 : 200 + q * 8] = brick
+
+
+def spread_near_kernel(matrix, to_first, to_second):
+    even = is_even()
+    for q in range(3):
+        up, down = matrix[q * 64 + 32 : q * 64 + 64], matrix[q * 64 : q * 64 + 32]
+        to_first[q * 32 : q * 32 + 32] = jnp.where(even, up, down)
+        to_second[q * 32 : q * 32 + 32] = jnp.where(even, down, up)
+
+
+def join_kernel(matrix, from_y, from_xy, from_x, first, second, wide, places):
+    even = is_even()
+    for q, (ref, row) in enumerate(far_columns(matrix, from_x, from_y, from_xy)):
+        one, two = first[q * 48 : q * 48 + 48], second[q * 48 : q * 48 + 48]
+        wide[q * 160 : q * 160 + 48] = jnp.where(even, two, one)
+        wide[q * 160 + 48 : q * 160 + 112] = ref[row : row + 64]
+        wide[q * 160 + 112 : q * 160 + 160] = jnp.where(even, one, two)
+    find_places(wide, range(40), tall_far_atom, bricks_place, places)
+
+
+def join_near_kernel(matrix, first, second, near_first, near_second, tall, places):
+    even = is_even()
+    for q in range(4):
+        if q < 3:
+            one, two = (ref[q * 32 : q * 32 + 32] for ref in (near_first, near_second))
+            low, high = jnp.where(even, two, one), jnp.where(even, one, two)
+        else:
+            low = jnp.where(even, second[16:48], first[16:48])
+            high = jnp.where(even, first[0:32], second[0:32])
+        tall[q * 128 : q * 128 + 32] = low
+        tall[q * 128 + 32 : q * 128 + 96] = matrix[q * 64 : q * 64 + 64]
+        tall[q * 128 + 96 : q * 128 + 128] = high
+    find_places(tall, range(32), tall_near_atom, FIRST_PLACE, places)
+
+
+def later_places_kernel(wide, matrix, third_places, fourth_places):
+    find_places(wide, FAR_ROWS, far_atom, SECOND_PLACE, third_places)
+    find_places(matrix, range(ATOMS), near_atom, THIRD_PLACE, fourth_places)
+
+
+def first_kernel(
+    wide, places, start, from_y, from_xy, from_x, first, second, out, field, gathered
 ):
     even = is_even()
-    for q, (ref, row) in enumerate(far_columns(matrix, from_x, from_y, from_xy)):
-        one, two = first[q * 16 : q * 16 + 16], second[q * 16 : q * 16 + 16]
-        wide[q * 96 : q * 96 + 16] = jnp.where(even, two, one)
-        wide[q * 96 + 16 : q * 96 + 80] = ref[row : row + 64]
-        wide[q * 96 + 80 : q * 96 + 96] = jnp.where(even, one, two)
     inner = [start[...]] + [unpack_bricks(ref[64:72]) for ref in (from_y, from_x, from_xy)]
-    for q, (out, value) in enumerate(zip((own, piece_y, piece_x, piece_xy), inner)):
-        one = unpack_bricks(first[64 + q * 8 : 72 + q * 8])
-        two = unpack_bricks(second[64 + q * 8 : 72 + q * 8])
-        low, high = jnp.where(even, two, one), jnp.where(even, one, two)
-        out[:, 0 : 2 * LANES] = value
-        out[:, 2 * LANES : 4 * LANES] = outside(low, high)
-    find_places(wide, 24, far_atom, far_place, far_slot, places)
-
-
-def layers_kernel(value, first, second, out):
-    even = is_even()
-    one, two = first[...], second[...]
-    out[:, 0 : 2 * LANES] = value[...]
-    low, high = jnp.where(even, two, one), jnp.where(even, one, two)
-    out[:, 2 * LANES : 4 * LANES] = outside(low, high)
-
-
-def near_places_kernel(matrix, places):
-    find_places(matrix, ATOMS, near_atom, near_place, near_slot, places)
-
-
-def with_places(places_in, places, sem, work):
-    copy = pltpu.make_async_copy(places_in, places, sem)
-    copy.start()
-    work()
-    copy.wait()
-
-
-def far_kernel(
-    matrix, places_in, own, from_y, from_x, from_xy, out, field, gathered, places, sem
+    outer = [
+        [unpack_bricks(ref[192 + q * 8 : 200 + q * 8]) for q in range(4)] for ref in (first, second)
+    ]
+    low = [jnp.where(even, two, one) for one, two in zip(*outer)]
+    high = [jnp.where(even, one, two) for one, two in zip(*outer)]
+    set_tiles(field, low + inner + high)
+    out[...] = couple(wide, range(40), field, places, gathered)
+
+
+def second_kernel(tall, places, own, from_x, from_y, from_xy, out, field, gathered):
+    set_tiles(field, (from_xy, from_x, from_y, own))
+    out[...] = couple(tall, range(32), field, places, gathered)
+
+
+def third_kernel(wide, places, own, from_x, from_y, from_xy, out, field, gathered):
+    set_tiles(field, (own, from_y, from_x, from_xy))
+    out[...] = couple(wide, FAR_ROWS, field, places, gathered)
+
+
+def pick_kernel(own, from_x, from_y, from_xy, second, first_own, second_own):
+    first_own[...] = pick_own((from_xy, from_x, from_y, own), FIRST_PLACE)
+    second_own[...] = pick_own((second,), SECOND_PLACE)
+
+
+def last_kernel(
+    matrix, places, own, from_x, from_y, from_xy, start, first, second, third_out, out,
+    field, gathered,
 ):
-    with_places(places_in, places, sem, lambda: set_tiles(field, (own, from_y, from_x, from_xy)))
-    out[...] = couple(matrix, field, places, gathered)
-
-
-def near_kernel(
-    matrix, places_in, own, from_y, from_x, from_xy, out, before, field, gathered, places, sem
-):
-    with_places(places_in, places, sem, lambda: set_tiles(field, (from_xy, from_x, from_y, own)))
-    out[...] = couple(matrix, field, places, gathered)
-    before[...] = pick_own(field)
-
-
-def last_kernel(
-    matrix, places_in, own, from_y, from_x, from_xy, start, first, second, third_out, out,
-    field, gathered, places, sem,
-):
-    with_places(places_in, places, sem, lambda: set_tiles(field, (from_xy, from_x, from_y, own)))
-    fourth = couple(matrix, field, places, gathered)
-    third = pick_own(field)
+    pieces = from_xy, from_x, from_y, own
+    set_tiles(field, pieces)
+    fourth = couple(matrix, range(ATOMS), field, places, gathered)
+    third = pick_own(pieces, THIRD_PLACE)
     third_out[...] = third
     gram_kernel([start[...], first[...], second[...], third, fourth], out)
+
+
+SMEM = pl.BlockSpec(memory_space=pltpu.SMEM)
+
+
+def whole_numbers(rows):
+    return jax.ShapeDtypeStruct((rows, LANES), jnp.int32)
 
 
 def call(kernel, shapes, *operands, scratch=(), place=VMEM):
@@ -521,7 +554,9 @@
     return pl.pallas_call(
         kernel,
         out_shape=shapes,
-        in_specs=[place] * len(operands),
+        in_specs=[
+            SMEM if operand.dtype == jnp.int32 and place is VMEM else place for operand in operands
+        ],
         out_specs=[VMEM] * len(shapes),
         scratch_shapes=list(scratch),
         compiler_params=pltpu.CompilerParams(vmem_limit_bytes=24 * 1024 * 1024),
@@ -532,8 +567,6 @@
     return (
         pltpu.VMEM((tiles * 8, SLOT_ROWS, LANES), jnp.float32),
         pltpu.VMEM((groups, WIDE, LANES), jnp.float32),
-        pltpu.SMEM((groups * 8, LANES), jnp.int32),
-        pltpu.SemaphoreType.DMA,
     )
 
 
@@ -549,8 +582,7 @@
 
 
 def fetch_three(to_x, to_y, to_xy, sign):
-    from_x, from_xy = fetch(to_x, sign, 0), fetch(to_xy, sign, sign)
-    return fetch(to_y, 0, sign), from_x, from_xy
+    return fetch(to_x, sign, 0), fetch(to_y, 0, sign), fetch(to_xy, sign, sign)
 
 
 def swap_layers(to_first, to_second):
@@ -566,7 +598,7 @@
     matrix, start, *out = call(
         pack_kernel,
         [(ATOMS * SLOT_ROWS, WIDE), flat] + [(72, WIDE)] * 3,
-        rhs, diagonal, blocks, neighbours,
+        *(pltpu.with_memory_space_constraint(x, pltpu.HBM) for x in (rhs, diagonal, blocks, neighbours)),
         scratch=[
             pltpu.VMEM(rhs.shape, rhs.dtype),
             pltpu.VMEM(diagonal.shape, diagonal.dtype),
@@ -574,48 +606,49 @@
             pltpu.VMEM(neighbours.shape, neighbours.dtype),
             pltpu.SemaphoreType.DMA((4,)),
         ],
-        place=pl.BlockSpec(memory_space=pl.ANY),
-    )
-    from_y, from_x, from_xy = fetch_three(*out, 1)
-    sides = from_x, from_y, from_xy
-    (near_places,) = call(
-        near_places_kernel, [jax.ShapeDtypeStruct((ATOMS, LANES), jnp.int32)], matrix
-    )
-    layers = swap_layers(*call(spread_kernel, [(96, WIDE)] * 2, matrix, *sides, start))
-    wide, far_places, *pieces = call(
-        join_kernel,
-        [(24 * SLOT_ROWS, WIDE), jax.ShapeDtypeStruct((24, LANES), jnp.int32)]
-        + [(SLOT_ROWS, 4 * LANES)] * 4,
-        matrix, *sides, start, *layers,
-    )
-    far_scratch, near_scratch = scratch_for(16, 3), scratch_for(12, 2)
-    far_shape = (SLOT_ROWS, 3 * LANES)
-    (first,) = call(far_kernel, [far_shape], wide, far_places, *pieces, scratch=far_scratch)
-    second, first_own = call(
-        near_kernel, [flat, flat],
-        matrix, near_places, first, *fetch_three(first, first, first, -1),
-        scratch=near_scratch,
-    )
-    (layered,) = call(
-        layers_kernel, [(SLOT_ROWS, 4 * LANES)], second, *swap_layers(second, second)
+        place=pl.BlockSpec(memory_space=pltpu.HBM),
+    )
+    from_x, from_y, from_xy = fetch_three(*out, 1)
+    sides = from_y, from_xy, from_x
+    layers = swap_layers(*call(spread_kernel, [(224, WIDE)] * 2, matrix, *sides, start))
+    near_layers = swap_layers(*call(spread_near_kernel, [(96, WIDE)] * 2, matrix))
+    wide, places = call(
+        join_kernel, [(40 * SLOT_ROWS, WIDE), whole_numbers(40)], matrix, *sides, *layers
+    )
+    (first,) = call(
+        first_kernel, [(SLOT_ROWS, 5 * LANES)],
+        wide, places, start, *sides, *layers,
+        scratch=scratch_for(24, 5),
+    )
+    tall, places = call(
+        join_near_kernel, [(32 * SLOT_ROWS, WIDE), whole_numbers(32)],
+        matrix, *layers, *near_layers,
+    )
+    pieces = fetch_three(first, first, first, -1)
+    (second,) = call(
+        second_kernel, [(SLOT_ROWS, 4 * LANES)], tall, places, first, *pieces,
+        scratch=scratch_for(20, 4),
+    )
+    first_own, second_own = call(pick_kernel, [flat] * 2, first, *pieces, second)
+    third_places, fourth_places = call(
+        later_places_kernel, [whole_numbers(24), whole_numbers(ATOMS)], wide, matrix
     )
     (third,) = call(
-        far_kernel, [far_shape],
-        wide, far_places, layered, *fetch_three(layered, layered, layered, 1),
-        scratch=far_scratch,
+        third_kernel, [(SLOT_ROWS, 3 * LANES)],
+        wide, third_places, second, *fetch_three(second, second, second, 1),
+        scratch=scratch_for(16, 3),
     )
     third_own, message = call(
         last_kernel,
-        [flat, (lax.axis_size("gx"), 4, LANES)],
-        matrix, near_places, third, *fetch_three(third, third, third, -1),
-        start, first_own, second,
-        scratch=near_scratch,
-    )
-    rest = lax.axis_size("gy") * lax.axis_size("gz")
-    message = lax.all_to_all(message, "gx", 0, 0, tiled=True)
-    (message,) = call(relay_kernel, [(rest, 4, LANES)], message)
-    message = lax.all_to_all(message, ("gy", "gz"), 0, 0, tiled=True)
-    (result,) = call(finish_kernel, [rhs.shape], message, start, first_own, second, third_own)
+        [flat, (lax.axis_size("gx") * lax.axis_size("gy"), 4, LANES)],
+        matrix, fourth_places, third, *fetch_three(third, third, third, -1),
+        start, first_own, second_own,
+        scratch=scratch_for(12, 2),
+    )
+    message = lax.all_to_all(message, ("gx", "gy"), 0, 0, tiled=True)
+    (message,) = call(relay_kernel, [(lax.axis_size("gz"), 4, LANES)], message)
+    message = lax.all_to_all(message, "gz", 0, 0, tiled=True)
+    (result,) = call(finish_kernel, [rhs.shape], message, start, first_own, second_own, third_own)
     return result
 
 

time: 146 us -> 132 us (0.904)
  waiting for transfers between devices: 30.1 us -> 15.4 us
  starting transfers between devices: 62.5 us -> 66.1 us
  local copies, waits for them, and re-layouts: 3.15 us -> 0 us
    ppermute x12, waiting for transfers between devices: 19.7 us -> 10.2 us  [fetch(): return lax.ppermute(value, AXES, pairs)]
    ppermute x2, waiting for transfers between devices: 10.3 us -> 5.15 us  [swap_layers(): lax.ppermute(to_second, 'gz', odd)]
    unnamed x8 -> x0, local copies, waits for them, and re-layouts: 3.15 us -> none
    ppermute x12, starting transfers between devices: 49.8 us -> 52.9 us  [fetch(): return lax.ppermute(value, AXES, pairs)]
    pallas_call x11 -> x13, Pallas kernels: 12.3 us -> 13.5 us  [call(): pl.pallas_call(kernel, out_shape=shapes, in_specs=[SMEM if operand.dtype...]
  transfers between devices with their start and end apart: 16 -> 16, of which waited for: 8 -> 7; matrix products, arithmetic and copies ran while one was open for 0% -> 0% of each run, Pallas kernels for 0% -> 3%
where the time goes in v4:
time: 132 us
  starting transfers between devices  66.1 us (50%)
  blocking collectives  36.4 us (28%)
  waiting for transfers between devices  15.4 us (12%)
  Pallas kernels  13.5 us (10%)
    ppermute x12, starting transfers between devices, fetch(): return lax.ppermute(value, AXES, pairs)  52.9 us
    all_to_all x1, blocking collectives, body(): message = lax.all_to_all(message, ('gx', 'gy'), 0, 0, tiled=True)  19.4 us
    all_to_all x1, blocking collectives, body(): message = lax.all_to_all(message, 'gz', 0, 0, tiled=True)  17 us
    pallas_call x13, Pallas kernels, call(): pl.pallas_call(kernel, out_shape=shapes, in_specs=[SMEM if operand.dtype...  13.5 us
    ppermute x12, waiting for transfers between devices, fetch(): return lax.ppermute(value, AXES, pairs)  10.2 us
    ppermute x2, starting transfers between devices, swap_layers(): lax.ppermute(to_first, 'gz', even)  8.34 us
    ppermute x2, waiting for transfers between devices, swap_layers(): lax.ppermute(to_second, 'gz', odd)  5.15 us
    ppermute x2, starting transfers between devices, swap_layers(): lax.ppermute(to_second, 'gz', odd)  4.91 us
  transfers between devices with their start and end apart: 16, of which 7 were waited for; matrix products, arithmetic and copies ran while one was open for 0% of the time, Pallas kernels for 3%

profile of v4, /device:TPU:1, one launch (start us, length us, event | category | flops | bytes accessed | tf_op | source)
XLA Modules:
  0.0 131.6 jit_solution(15808684617031779731)
XLA Ops:
  1.2 11.5 %collective-permute-start = (f32[72,512]{1,0:T(8,128)S(1)}, f32[72,512]{1,0:T(8,128)S(1)}, u32[]{:S(2)}, u32[]{:S(2)}) collective-permute-start(f32[72,512]{1,0:T(8,128)S(1)} %get-tuple-element.25), channel_id=1, source_target_pairs={{16,0},{17,1},{18,2},{19,3},{20,4},{21,5},{22,6},{23,7},{24,8},{25... | collective-permute-start | bytes 442376 | tf_op jit(solution)/shard_map/ppermute | solution.py:581
  12.7 5.1 %collective-permute-start.1 = (f32[72,512]{1,0:T(8,128)S(1)}, f32[72,512]{1,0:T(8,128)S(1)}, u32[]{:S(2)}, u32[]{:S(2)}) collective-permute-start(f32[72,512]{1,0:T(8,128)S(1)} %get-tuple-element.26), channel_id=1, source_target_pairs={{80,0},{81,1},{82,2},{83,3},{84,4},{85,5},{86,6},{87,7},{88,8},{89... | collective-permute-start | bytes 442376 | tf_op jit(solution)/shard_map/ppermute | solution.py:581
  17.8 3.0 %collective-permute-start.2 = (f32[72,512]{1,0:T(8,128)S(1)}, f32[72,512]{1,0:T(8,128)S(1)}, u32[]{:S(2)}, u32[]{:S(2)}) collective-permute-start(f32[72,512]{1,0:T(8,128)S(1)} %get-tuple-element.27), channel_id=1, source_target_pairs={{64,0},{65,1},{66,2},{67,3},{68,4},{69,5},{70,6},{71,7},{72,8},{73... | collective-permute-start | bytes 442376 | tf_op jit(solution)/shard_map/ppermute | solution.py:581
  20.8 3.3 %collective-permute-done.from_y = f32[72,512]{1,0:T(8,128)S(1)} collective-permute-done((f32[72,512]{1,0:T(8,128)S(1)}, f32[72,512]{1,0:T(8,128)S(1)}, u32[]{:S(2)}, u32[]{:S(2)}) %collective-permute-start) | collective-permute-done | bytes 147488 | tf_op jit(solution)/shard_map/ppermute | solution.py:581
  24.5 3.7 %collective-permute-start.3 = (f32[224,512]{1,0:T(8,128)S(1)}, f32[224,512]{1,0:T(8,128)S(1)}, u32[]{:S(2)}, u32[]{:S(2)}) collective-permute-start(f32[224,512]{1,0:T(8,128)S(1)} %get-tuple-element.29), channel_id=1, source_target_pairs={{0,1},{1,0},{2,3},{3,2},{4,5},{5,4},{6,7},{7,6},{8,9},{9,8},{10,11... | collective-permute-start | bytes 1376264 | tf_op jit(solution)/shard_map/ppermute | solution.py:592
  28.3 3.0 %collective-permute-start.4 = (f32[224,512]{1,0:T(8,128)S(1)}, f32[224,512]{1,0:T(8,128)S(1)}, u32[]{:S(2)}, u32[]{:S(2)}) collective-permute-start(f32[224,512]{1,0:T(8,128)S(1)} %get-tuple-element.30), channel_id=1, source_target_pairs={{0,15},{1,2},{2,1},{3,4},{4,3},{5,6},{6,5},{7,8},{8,7},{9,10},{10,... | collective-permute-start | bytes 1376264 | tf_op jit(solution)/shard_map/ppermute | solution.py:592
  31.3 4.6 %collective-permute-start.5 = (f32[96,512]{1,0:T(8,128)S(1)}, f32[96,512]{1,0:T(8,128)S(1)}, u32[]{:S(2)}, u32[]{:S(2)}) collective-permute-start(f32[96,512]{1,0:T(8,128)S(1)} %get-tuple-element.34), channel_id=1, source_target_pairs={{0,1},{1,0},{2,3},{3,2},{4,5},{5,4},{6,7},{7,6},{8,9},{9,8},{10,11... | collective-permute-start | bytes 589832 | tf_op jit(solution)/shard_map/ppermute | solution.py:592
  37.9 5.2 %collective-permute-done.4.second = f32[224,512]{1,0:T(8,128)S(1)} collective-permute-done((f32[224,512]{1,0:T(8,128)S(1)}, f32[224,512]{1,0:T(8,128)S(1)}, u32[]{:S(2)}, u32[]{:S(2)}) %collective-permute-start.4) | collective-permute-done | bytes 458784 | tf_op jit(solution)/shard_map/ppermute | solution.py:592
  43.2 3.2 %shard_map.52.own = f32[16,640]{1,0:T(8,128)S(1)} custom-call(f32[640,512]{1,0:T(8,128)S(1)} %get-tuple-element.31.wide, s32[40,128]{1,0:T(8,128)S(1)} %get-tuple-element.38.places, f32[16,256]{1,0:T(8,128)S(1)} %get-tuple-element.28.start.refs_0_, f32[72,512]{1,0:T(8,128)S(1)} %collective-permute-done.from_y, f32[72,512]{1,0:T(8,128)S(1)} %collective-permute-done.1.from_xy, ...), custom_call_target="tpu_custom_call" | custom-call | tf_op jit(solution)/shard_map/pallas_call | solution.py:554
  46.3 3.9 %collective-permute-start.9 = (f32[16,640]{1,0:T(8,128)S(1)}, f32[16,640]{1,0:T(8,128)S(1)}, u32[]{:S(2)}, u32[]{:S(2)}) collective-permute-start(f32[16,640]{1,0:T(8,128)S(1)} %shard_map.52.own), channel_id=1, source_target_pairs={{496,0},{497,1},{498,2},{499,3},{500,4},{501,5},{502,6},{503,7},{5... | collective-permute-start | bytes 122888 | tf_op jit(solution)/shard_map/ppermute | solution.py:581
  50.2 4.2 %collective-permute-start.8 = (f32[16,640]{1,0:T(8,128)S(1)}, f32[16,640]{1,0:T(8,128)S(1)}, u32[]{:S(2)}, u32[]{:S(2)}) collective-permute-start(f32[16,640]{1,0:T(8,128)S(1)} %shard_map.52.own), channel_id=1, source_target_pairs={{48,0},{49,1},{50,2},{51,3},{52,4},{53,5},{54,6},{55,7},{56,8},{57... | collective-permute-start | bytes 122888 | tf_op jit(solution)/shard_map/ppermute | solution.py:581
  54.5 3.2 %collective-permute-start.7 = (f32[16,640]{1,0:T(8,128)S(1)}, f32[16,640]{1,0:T(8,128)S(1)}, u32[]{:S(2)}, u32[]{:S(2)}) collective-permute-start(f32[16,640]{1,0:T(8,128)S(1)} %shard_map.52.own), channel_id=1, source_target_pairs={{448,0},{449,1},{450,2},{451,3},{452,4},{453,5},{454,6},{455,7},{4... | collective-permute-start | bytes 122888 | tf_op jit(solution)/shard_map/ppermute | solution.py:581
  57.9 2.2 %collective-permute-done.8.from_y = f32[16,640]{1,0:T(8,128)S(1)} collective-permute-done((f32[16,640]{1,0:T(8,128)S(1)}, f32[16,640]{1,0:T(8,128)S(1)}, u32[]{:S(2)}, u32[]{:S(2)}) %collective-permute-start.8) | collective-permute-done | bytes 40992 | tf_op jit(solution)/shard_map/ppermute | solution.py:581
  60.5 2.6 %shard_map.53.own.second = f32[16,512]{1,0:T(8,128)S(1)} custom-call(f32[512,512]{1,0:T(8,128)S(1)} %get-tuple-element.36.tall, s32[32,128]{1,0:T(8,128)S(1)} %get-tuple-element.37.places, f32[16,640]{1,0:T(8,128)S(1)} %shard_map.52.own, f32[16,640]{1,0:T(8,128)S(1)} %collective-permute-done.7.from_x, f32[16,640]{1,0:T(8,128)S(1)} %collective-permute-done.8.from_y, ...), custom_call_target="tpu_custom_call" | custom-call | tf_op jit(solution)/shard_map/pallas_call | solution.py:554
  63.1 3.9 %collective-permute-start.12 = (f32[16,512]{1,0:T(8,128)S(1)}, f32[16,512]{1,0:T(8,128)S(1)}, u32[]{:S(2)}, u32[]{:S(2)}) collective-permute-start(f32[16,512]{1,0:T(8,128)S(1)} %shard_map.53.own.second), channel_id=1, source_target_pairs={{80,0},{81,1},{82,2},{83,3},{84,4},{85,5},{86,6},{87,7},{88,8},{89... | collective-permute-start | bytes 98312 | tf_op jit(solution)/shard_map/ppermute | solution.py:581
  67.0 3.9 %collective-permute-start.11 = (f32[16,512]{1,0:T(8,128)S(1)}, f32[16,512]{1,0:T(8,128)S(1)}, u32[]{:S(2)}, u32[]{:S(2)}) collective-permute-start(f32[16,512]{1,0:T(8,128)S(1)} %shard_map.53.own.second), channel_id=1, source_target_pairs={{16,0},{17,1},{18,2},{19,3},{20,4},{21,5},{22,6},{23,7},{24,8},{25... | collective-permute-start | bytes 98312 | tf_op jit(solution)/shard_map/ppermute | solution.py:581
  70.9 3.4 %collective-permute-start.10 = (f32[16,512]{1,0:T(8,128)S(1)}, f32[16,512]{1,0:T(8,128)S(1)}, u32[]{:S(2)}, u32[]{:S(2)}) collective-permute-start(f32[16,512]{1,0:T(8,128)S(1)} %shard_map.53.own.second), channel_id=1, source_target_pairs={{64,0},{65,1},{66,2},{67,3},{68,4},{69,5},{70,6},{71,7},{72,8},{73... | collective-permute-start | bytes 98312 | tf_op jit(solution)/shard_map/ppermute | solution.py:581
  75.6 2.2 %shard_map.54.own = f32[16,384]{1,0:T(8,128)S(1)} custom-call(f32[640,512]{1,0:T(8,128)S(1)} %get-tuple-element.31.wide, s32[24,128]{1,0:T(8,128)S(1)} %get-tuple-element.33.places, f32[16,512]{1,0:T(8,128)S(1)} %shard_map.53.own.second, f32[16,512]{1,0:T(8,128)S(1)} %collective-permute-done.10.from_x, f32[16,512]{1,0:T(8,128)S(1)} %collective-permute-done.11.from_y, ...), custom_call_target="tpu_custom_call" | custom-call | tf_op jit(solution)/shard_map/pallas_call | solution.py:554
  77.8 2.7 %collective-permute-start.15 = (f32[16,384]{1,0:T(8,128)S(1)}, f32[16,384]{1,0:T(8,128)S(1)}, u32[]{:S(2)}, u32[]{:S(2)}) collective-permute-start(f32[16,384]{1,0:T(8,128)S(1)} %shard_map.54.own), channel_id=1, source_target_pairs={{496,0},{497,1},{498,2},{499,3},{500,4},{501,5},{502,6},{503,7},{5... | collective-permute-start | bytes 73736 | tf_op jit(solution)/shard_map/ppermute | solution.py:581
  80.5 4.9 %collective-permute-start.14 = (f32[16,384]{1,0:T(8,128)S(1)}, f32[16,384]{1,0:T(8,128)S(1)}, u32[]{:S(2)}, u32[]{:S(2)}) collective-permute-start(f32[16,384]{1,0:T(8,128)S(1)} %shard_map.54.own), channel_id=1, source_target_pairs={{48,0},{49,1},{50,2},{51,3},{52,4},{53,5},{54,6},{55,7},{56,8},{57... | collective-permute-start | bytes 73736 | tf_op jit(solution)/shard_map/ppermute | solution.py:581
  85.4 3.2 %collective-permute-start.13 = (f32[16,384]{1,0:T(8,128)S(1)}, f32[16,384]{1,0:T(8,128)S(1)}, u32[]{:S(2)}, u32[]{:S(2)}) collective-permute-start(f32[16,384]{1,0:T(8,128)S(1)} %shard_map.54.own), channel_id=1, source_target_pairs={{448,0},{449,1},{450,2},{451,3},{452,4},{453,5},{454,6},{455,7},{4... | collective-permute-start | bytes 73736 | tf_op jit(solution)/shard_map/ppermute | solution.py:581
  88.7 2.8 %collective-permute-done.13.from_x = f32[16,384]{1,0:T(8,128)S(1)} collective-permute-done((f32[16,384]{1,0:T(8,128)S(1)}, f32[16,384]{1,0:T(8,128)S(1)}, u32[]{:S(2)}, u32[]{:S(2)}) %collective-permute-start.13) | collective-permute-done | bytes 24608 | tf_op jit(solution)/shard_map/ppermute | solution.py:581
  93.7 19.4 %all_to_all.10.ref = f32[32,4,128]{2,1,0:T(4,128)S(1)} all-to-all(f32[32,4,128]{2,1,0:T(4,128)S(1)} %get-tuple-element.41), channel_id=1, replica_groups=mesh['gx'=8,'gy'=4,'gz'=16] {'gx','gy'}, dimensions={0} | all-to-all | bytes 131072 | tf_op jit(solution)/shard_map/all_to_all | solution.py:648
  113.1 17.0 %all_to_all.11.ref = f32[16,4,128]{2,1,0:T(4,128)S(1)} all-to-all(f32[16,4,128]{2,1,0:T(4,128)S(1)} %shard_map.57), channel_id=1, replica_groups=mesh['gx'=8,'gy'=4,'gz'=16] {'gz'}, dimensions={0} | all-to-all | bytes 65536 | tf_op jit(solution)/shard_map/all_to_all | solution.py:650
  (23 shorter events, 9.3 us)
Async XLA Ops:
  1.2 22.9 %collective-permute-start = (f32[72,512]{1,0:T(8,128)S(1)}, f32[72,512]{1,0:T(8,128)S(1)}, u32[]{:S(2)}, u32[]{:S(2)}) collective-permute-start(f32[72,512]{1,0:T(8,128)S(1)} %get-tuple-element.25), channel_id=1, source_target_pairs={{16,0},{17,1},{18,2},{19,3},{20,4},{21,5},{22,6},{23,7},{24,8},{25... | collective-permute-start | bytes 442376 | tf_op jit(solution)/shard_map/ppermute | solution.py:581
  12.7 11.4 %collective-permute-start.1 = (f32[72,512]{1,0:T(8,128)S(1)}, f32[72,512]{1,0:T(8,128)S(1)}, u32[]{:S(2)}, u32[]{:S(2)}) collective-permute-start(f32[72,512]{1,0:T(8,128)S(1)} %get-tuple-element.26), channel_id=1, source_target_pairs={{80,0},{81,1},{82,2},{83,3},{84,4},{85,5},{86,6},{87,7},{88,8},{89... | collective-permute-start | bytes 442376 | tf_op jit(solution)/shard_map/ppermute | solution.py:581
  17.8 6.7 %collective-permute-start.2 = (f32[72,512]{1,0:T(8,128)S(1)}, f32[72,512]{1,0:T(8,128)S(1)}, u32[]{:S(2)}, u32[]{:S(2)}) collective-permute-start(f32[72,512]{1,0:T(8,128)S(1)} %get-tuple-element.27), channel_id=1, source_target_pairs={{64,0},{65,1},{66,2},{67,3},{68,4},{69,5},{70,6},{71,7},{72,8},{73... | collective-permute-start | bytes 442376 | tf_op jit(solution)/shard_map/ppermute | solution.py:581
  24.5 13.3 %collective-permute-start.3 = (f32[224,512]{1,0:T(8,128)S(1)}, f32[224,512]{1,0:T(8,128)S(1)}, u32[]{:S(2)}, u32[]{:S(2)}) collective-permute-start(f32[224,512]{1,0:T(8,128)S(1)} %get-tuple-element.29), channel_id=1, source_target_pairs={{0,1},{1,0},{2,3},{3,2},{4,5},{5,4},{6,7},{7,6},{8,9},{9,8},{10,11... | collective-permute-start | bytes 1376264 | tf_op jit(solution)/shard_map/ppermute | solution.py:592
  28.3 14.8 %collective-permute-start.4 = (f32[224,512]{1,0:T(8,128)S(1)}, f32[224,512]{1,0:T(8,128)S(1)}, u32[]{:S(2)}, u32[]{:S(2)}) collective-permute-start(f32[224,512]{1,0:T(8,128)S(1)} %get-tuple-element.30), channel_id=1, source_target_pairs={{0,15},{1,2},{2,1},{3,4},{4,3},{5,6},{6,5},{7,8},{8,7},{9,10},{10,... | collective-permute-start | bytes 1376264 | tf_op jit(solution)/shard_map/ppermute | solution.py:592
  31.3 26.4 %collective-permute-start.5 = (f32[96,512]{1,0:T(8,128)S(1)}, f32[96,512]{1,0:T(8,128)S(1)}, u32[]{:S(2)}, u32[]{:S(2)}) collective-permute-start(f32[96,512]{1,0:T(8,128)S(1)} %get-tuple-element.34), channel_id=1, source_target_pairs={{0,1},{1,0},{2,3},{3,2},{4,5},{5,4},{6,7},{7,6},{8,9},{9,8},{10,11... | collective-permute-start | bytes 589832 | tf_op jit(solution)/shard_map/ppermute | solution.py:592
  35.9 21.8 %collective-permute-start.6 = (f32[96,512]{1,0:T(8,128)S(1)}, f32[96,512]{1,0:T(8,128)S(1)}, u32[]{:S(2)}, u32[]{:S(2)}) collective-permute-start(f32[96,512]{1,0:T(8,128)S(1)} %get-tuple-element.35), channel_id=1, source_target_pairs={{0,15},{1,2},{2,1},{3,4},{4,3},{5,6},{6,5},{7,8},{8,7},{9,10},{10,... | collective-permute-start | bytes 589832 | tf_op jit(solution)/shard_map/ppermute | solution.py:592
  46.3 11.5 %collective-permute-start.9 = (f32[16,640]{1,0:T(8,128)S(1)}, f32[16,640]{1,0:T(8,128)S(1)}, u32[]{:S(2)}, u32[]{:S(2)}) collective-permute-start(f32[16,640]{1,0:T(8,128)S(1)} %shard_map.52.own), channel_id=1, source_target_pairs={{496,0},{497,1},{498,2},{499,3},{500,4},{501,5},{502,6},{503,7},{5... | collective-permute-start | bytes 122888 | tf_op jit(solution)/shard_map/ppermute | solution.py:581
  50.2 9.8 %collective-permute-start.8 = (f32[16,640]{1,0:T(8,128)S(1)}, f32[16,640]{1,0:T(8,128)S(1)}, u32[]{:S(2)}, u32[]{:S(2)}) collective-permute-start(f32[16,640]{1,0:T(8,128)S(1)} %shard_map.52.own), channel_id=1, source_target_pairs={{48,0},{49,1},{50,2},{51,3},{52,4},{53,5},{54,6},{55,7},{56,8},{57... | collective-permute-start | bytes 122888 | tf_op jit(solution)/shard_map/ppermute | solution.py:581
  54.5 6.0 %collective-permute-start.7 = (f32[16,640]{1,0:T(8,128)S(1)}, f32[16,640]{1,0:T(8,128)S(1)}, u32[]{:S(2)}, u32[]{:S(2)}) collective-permute-start(f32[16,640]{1,0:T(8,128)S(1)} %shard_map.52.own), channel_id=1, source_target_pairs={{448,0},{449,1},{450,2},{451,3},{452,4},{453,5},{454,6},{455,7},{4... | collective-permute-start | bytes 122888 | tf_op jit(solution)/shard_map/ppermute | solution.py:581
  63.1 11.3 %collective-permute-start.12 = (f32[16,512]{1,0:T(8,128)S(1)}, f32[16,512]{1,0:T(8,128)S(1)}, u32[]{:S(2)}, u32[]{:S(2)}) collective-permute-start(f32[16,512]{1,0:T(8,128)S(1)} %shard_map.53.own.second), channel_id=1, source_target_pairs={{80,0},{81,1},{82,2},{83,3},{84,4},{85,5},{86,6},{87,7},{88,8},{89... | collective-permute-start | bytes 98312 | tf_op jit(solution)/shard_map/ppermute | solution.py:581
  67.0 7.4 %collective-permute-start.11 = (f32[16,512]{1,0:T(8,128)S(1)}, f32[16,512]{1,0:T(8,128)S(1)}, u32[]{:S(2)}, u32[]{:S(2)}) collective-permute-start(f32[16,512]{1,0:T(8,128)S(1)} %shard_map.53.own.second), channel_id=1, source_target_pairs={{16,0},{17,1},{18,2},{19,3},{20,4},{21,5},{22,6},{23,7},{24,8},{25... | collective-permute-start | bytes 98312 | tf_op jit(solution)/shard_map/ppermute | solution.py:581
  70.9 4.7 %collective-permute-start.10 = (f32[16,512]{1,0:T(8,128)S(1)}, f32[16,512]{1,0:T(8,128)S(1)}, u32[]{:S(2)}, u32[]{:S(2)}) collective-permute-start(f32[16,512]{1,0:T(8,128)S(1)} %shard_map.53.own.second), channel_id=1, source_target_pairs={{64,0},{65,1},{66,2},{67,3},{68,4},{69,5},{70,6},{71,7},{72,8},{73... | collective-permute-start | bytes 98312 | tf_op jit(solution)/shard_map/ppermute | solution.py:581
  77.8 10.9 %collective-permute-start.15 = (f32[16,384]{1,0:T(8,128)S(1)}, f32[16,384]{1,0:T(8,128)S(1)}, u32[]{:S(2)}, u32[]{:S(2)}) collective-permute-start(f32[16,384]{1,0:T(8,128)S(1)} %shard_map.54.own), channel_id=1, source_target_pairs={{496,0},{497,1},{498,2},{499,3},{500,4},{501,5},{502,6},{503,7},{5... | collective-permute-start | bytes 73736 | tf_op jit(solution)/shard_map/ppermute | solution.py:581
  80.5 8.2 %collective-permute-start.14 = (f32[16,384]{1,0:T(8,128)S(1)}, f32[16,384]{1,0:T(8,128)S(1)}, u32[]{:S(2)}, u32[]{:S(2)}) collective-permute-start(f32[16,384]{1,0:T(8,128)S(1)} %shard_map.54.own), channel_id=1, source_target_pairs={{48,0},{49,1},{50,2},{51,3},{52,4},{53,5},{54,6},{55,7},{56,8},{57... | collective-permute-start | bytes 73736 | tf_op jit(solution)/shard_map/ppermute | solution.py:581
  85.4 6.1 %collective-permute-start.13 = (f32[16,384]{1,0:T(8,128)S(1)}, f32[16,384]{1,0:T(8,128)S(1)}, u32[]{:S(2)}, u32[]{:S(2)}) collective-permute-start(f32[16,384]{1,0:T(8,128)S(1)} %shard_map.54.own), channel_id=1, source_target_pairs={{448,0},{449,1},{450,2},{451,3},{452,4},{453,5},{454,6},{455,7},{4... | collective-permute-start | bytes 73736 | tf_op jit(solution)/shard_map/ppermute | solution.py:581

commit v5 on v4

--- a/solution.py
+++ b/solution.py
@@ -387,9 +387,25 @@
     return jnp.concatenate([packed[:, 0 : 2 * LANES], packed[:, 2 * LANES : 4 * LANES]], axis=0)
 
 
+def is_even():
+    return lax.rem(lax.axis_index("gz"), 2) == 0
+
+
+def spread_own(matrix, brick, to_first, to_second):
+    even = is_even()
+    for q in range(4):
+        rows = 32 if q < 3 else 48
+        up = matrix[q * 64 + 64 - rows : q * 64 + 64]
+        down = matrix[q * 64 : q * 64 + rows]
+        to_first[q * 32 : q * 32 + rows] = jnp.where(even, up, down)
+        to_second[q * 32 : q * 32 + rows] = jnp.where(even, down, up)
+    to_first[144:152] = brick
+    to_second[144:152] = brick
+
+
 def pack_kernel(
     rhs_hbm, diagonal_hbm, blocks_hbm, neighbours_hbm,
-    matrix, start, to_x, to_y, to_xy,
+    matrix, start, to_x, to_y, to_xy, to_first, to_second,
     rhs, diagonal, blocks, neighbours, sems,
 ):
     sources = (neighbours_hbm, diagonal_hbm, rhs_hbm, blocks_hbm)
@@ -438,55 +454,45 @@
     for out, row in ((to_x, 64), (to_y, 128), (to_xy, 0)):
         out[0:64] = matrix[row : row + 64]
         out[64:72] = bricks
+    spread_own(matrix, bricks, to_first, to_second)
 
 
 def far_columns(matrix, from_x, from_y, from_xy):
     return (matrix, 192), (from_y, 0), (from_x, 0), (from_xy, 0)
 
 
-def is_even():
-    return lax.rem(lax.axis_index("gz"), 2) == 0
-
-
-def spread_kernel(matrix, from_y, from_xy, from_x, start, to_first, to_second):
+def spread_kernel(from_y, from_xy, from_x, to_first, to_second):
+    even = is_even()
+    for q, ref in enumerate((from_y, from_x, from_xy)):
+        up, down = ref[16:64], ref[0:48]
+        to_first[q * 48 : q * 48 + 48] = jnp.where(even, up, down)
+        to_second[q * 48 : q * 48 + 48] = jnp.where(even, down, up)
+        to_first[144 + q * 8 : 152 + q * 8] = ref[64:72]
+        to_second[144 + q * 8 : 152 + q * 8] = ref[64:72]
+
+
+def join_kernel(
+    matrix, from_y, from_xy, from_x, first, second, own_first, own_second, wide, places
+):
     even = is_even()
     for q, (ref, row) in enumerate(far_columns(matrix, from_x, from_y, from_xy)):
-        up, down = ref[row + 16 : row + 64], ref[row : row + 48]
-        to_first[q * 48 : q * 48 + 48] = jnp.where(even, up, down)
-        to_second[q * 48 : q * 48 + 48] = jnp.where(even, down, up)
-    bricks = [pack_bricks(start[...])] + [ref[64:72] for ref in (from_y, from_x, from_xy)]
-    for q, brick in enumerate(bricks):
-        to_first[192 + q * 8 : 200 + q * 8] = brick
-        to_second[192 + q * 8 : 200 + q * 8] = brick
-
-
-def spread_near_kernel(matrix, to_first, to_second):
-    even = is_even()
-    for q in range(3):
-        up, down = matrix[q * 64 + 32 : q * 64 + 64], matrix[q * 64 : q * 64 + 32]
-        to_first[q * 32 : q * 32 + 32] = jnp.where(even, up, down)
-        to_second[q * 32 : q * 32 + 32] = jnp.where(even, down, up)
-
-
-def join_kernel(matrix, from_y, from_xy, from_x, first, second, wide, places):
-    even = is_even()
-    for q, (ref, row) in enumerate(far_columns(matrix, from_x, from_y, from_xy)):
-        one, two = first[q * 48 : q * 48 + 48], second[q * 48 : q * 48 + 48]
+        if q == 0:
+            one, two = own_first[96:144], own_second[96:144]
+        else:
+            one, two = (side[q * 48 - 48 : q * 48] for side in (first, second))
         wide[q * 160 : q * 160 + 48] = jnp.where(even, two, one)
         wide[q * 160 + 48 : q * 160 + 112] = ref[row : row + 64]
         wide[q * 160 + 112 : q * 160 + 160] = jnp.where(even, one, two)
     find_places(wide, range(40), tall_far_atom, bricks_place, places)
 
 
-def join_near_kernel(matrix, first, second, near_first, near_second, tall, places):
+def join_near_kernel(matrix, own_first, own_second, tall, places):
     even = is_even()
     for q in range(4):
-        if q < 3:
-            one, two = (ref[q * 32 : q * 32 + 32] for ref in (near_first, near_second))
-            low, high = jnp.where(even, two, one), jnp.where(even, one, two)
-        else:
-            low = jnp.where(even, second[16:48], first[16:48])
-            high = jnp.where(even, first[0:32], second[0:32])
+        ends = slice(112, 144) if q == 3 else slice(q * 32, q * 32 + 32)
+        starts = slice(q * 32, q * 32 + 32)
+        low = jnp.where(even, own_second[ends], own_first[ends])
+        high = jnp.where(even, own_first[starts], own_second[starts])
         tall[q * 128 : q * 128 + 32] = low
         tall[q * 128 + 32 : q * 128 + 96] = matrix[q * 64 : q * 64 + 64]
         tall[q * 128 + 96 : q * 128 + 128] = high
@@ -499,12 +505,15 @@
 
 
 def first_kernel(
-    wide, places, start, from_y, from_xy, from_x, first, second, out, field, gathered
+    wide, places, start, from_y, from_xy, from_x, first, second, own_first, own_second, out,
+    field, gathered,
 ):
     even = is_even()
     inner = [start[...]] + [unpack_bricks(ref[64:72]) for ref in (from_y, from_x, from_xy)]
     outer = [
-        [unpack_bricks(ref[192 + q * 8 : 200 + q * 8]) for q in range(4)] for ref in (first, second)
+        [unpack_bricks(own[144:152])]
+        + [unpack_bricks(ref[144 + q * 8 : 152 + q * 8]) for q in range(3)]
+        for own, ref in ((own_first, first), (own_second, second))
     ]
     low = [jnp.where(even, two, one) for one, two in zip(*outer)]
     high = [jnp.where(even, one, two) for one, two in zip(*outer)]
@@ -512,23 +521,23 @@
     out[...] = couple(wide, range(40), field, places, gathered)
 
 
-def second_kernel(tall, places, own, from_x, from_y, from_xy, out, field, gathered):
+def second_kernel(tall, places, own, from_xy, from_y, from_x, out, field, gathered):
     set_tiles(field, (from_xy, from_x, from_y, own))
     out[...] = couple(tall, range(32), field, places, gathered)
 
 
-def third_kernel(wide, places, own, from_x, from_y, from_xy, out, field, gathered):
+def third_kernel(wide, places, own, from_xy, from_y, from_x, out, field, gathered):
     set_tiles(field, (own, from_y, from_x, from_xy))
     out[...] = couple(wide, FAR_ROWS, field, places, gathered)
 
 
-def pick_kernel(own, from_x, from_y, from_xy, second, first_own, second_own):
+def pick_kernel(own, from_xy, from_y, from_x, second, first_own, second_own):
     first_own[...] = pick_own((from_xy, from_x, from_y, own), FIRST_PLACE)
     second_own[...] = pick_own((second,), SECOND_PLACE)
 
 
 def last_kernel(
-    matrix, places, own, from_x, from_y, from_xy, start, first, second, third_out, out,
+    matrix, places, own, from_xy, from_y, from_x, start, first, second, third_out, out,
     field, gathered,
 ):
     pieces = from_xy, from_x, from_y, own
@@ -582,7 +591,7 @@
 
 
 def fetch_three(to_x, to_y, to_xy, sign):
-    return fetch(to_x, sign, 0), fetch(to_y, 0, sign), fetch(to_xy, sign, sign)
+    return fetch(to_xy, sign, sign), fetch(to_y, 0, sign), fetch(to_x, sign, 0)
 
 
 def swap_layers(to_first, to_second):
@@ -597,7 +606,7 @@
     flat = (SLOT_ROWS, width)
     matrix, start, *out = call(
         pack_kernel,
-        [(ATOMS * SLOT_ROWS, WIDE), flat] + [(72, WIDE)] * 3,
+        [(ATOMS * SLOT_ROWS, WIDE), flat] + [(72, WIDE)] * 3 + [(152, WIDE)] * 2,
         *(pltpu.with_memory_space_constraint(x, pltpu.HBM) for x in (rhs, diagonal, blocks, neighbours)),
         scratch=[
             pltpu.VMEM(rhs.shape, rhs.dtype),
@@ -608,21 +617,22 @@
         ],
         place=pl.BlockSpec(memory_space=pltpu.HBM),
     )
-    from_x, from_y, from_xy = fetch_three(*out, 1)
-    sides = from_y, from_xy, from_x
-    layers = swap_layers(*call(spread_kernel, [(224, WIDE)] * 2, matrix, *sides, start))
-    near_layers = swap_layers(*call(spread_near_kernel, [(96, WIDE)] * 2, matrix))
+    from_xy, from_y, from_x = fetch_three(*out[:3], 1)
+    own_layers = swap_layers(*out[3:])
+    first, second, *sides = lax.optimization_barrier((*own_layers, from_y, from_xy, from_x))
+    own_layers = first, second
+    layers = swap_layers(*call(spread_kernel, [(168, WIDE)] * 2, *sides))
     wide, places = call(
-        join_kernel, [(40 * SLOT_ROWS, WIDE), whole_numbers(40)], matrix, *sides, *layers
+        join_kernel, [(40 * SLOT_ROWS, WIDE), whole_numbers(40)],
+        matrix, *sides, *layers, *own_layers,
     )
     (first,) = call(
         first_kernel, [(SLOT_ROWS, 5 * LANES)],
-        wide, places, start, *sides, *layers,
+        wide, places, start, *sides, *layers, *own_layers,
         scratch=scratch_for(24, 5),
     )
     tall, places = call(
-        join_near_kernel, [(32 * SLOT_ROWS, WIDE), whole_numbers(32)],
-        matrix, *layers, *near_layers,
+        join_near_kernel, [(32 * SLOT_ROWS, WIDE), whole_numbers(32)], matrix, *own_layers
     )
     pieces = fetch_three(first, first, first, -1)
     (second,) = call(

time: 132 us -> 138 us (1.045)
  waiting for transfers between devices: 15.4 us -> 19.7 us
    ppermute x2, starting transfers between devices: 8.34 us -> 14.2 us  [swap_layers(): lax.ppermute(to_first, 'gz', even)]
    ppermute x2, waiting for transfers between devices: 5.15 us -> 9.12 us  [swap_layers(): lax.ppermute(to_second, 'gz', odd)]
    ppermute x12, starting transfers between devices: 52.9 us -> 49.1 us  [fetch(): return lax.ppermute(value, AXES, pairs)]
    pallas_call x13 -> x12, Pallas kernels: 13.5 us -> 13.4 us  [call(): pl.pallas_call(kernel, out_shape=shapes, in_specs=[SMEM if operand.dtype...]
  transfers between devices with their start and end apart: 16 -> 16, of which waited for: 7 -> 7; matrix products, arithmetic and copies ran while one was open for 0% -> 0% of each run, Pallas kernels for 3% -> 0%
where the time goes in v5:
time: 138 us; the launch traced here: 137 us
  starting transfers between devices  67.1 us (49%)
  blocking collectives  36.4 us (26%)
  waiting for transfers between devices  19.7 us (14%)
  Pallas kernels  13.4 us (10%)
    ppermute x12, starting transfers between devices, fetch(): return lax.ppermute(value, AXES, pairs)  49.1 us
    all_to_all x1, blocking collectives, body(): message = lax.all_to_all(message, ('gx', 'gy'), 0, 0, tiled=True)  18.7 us
    all_to_all x1, blocking collectives, body(): message = lax.all_to_all(message, 'gz', 0, 0, tiled=True)  17.7 us
    ppermute x2, starting transfers between devices, swap_layers(): lax.ppermute(to_first, 'gz', even)  14.2 us
    pallas_call x12, Pallas kernels, call(): pl.pallas_call(kernel, out_shape=shapes, in_specs=[SMEM if operand.dtype...  13.4 us
    ppermute x12, waiting for transfers between devices, fetch(): return lax.ppermute(value, AXES, pairs)  10.6 us
    ppermute x2, waiting for transfers between devices, swap_layers(): lax.ppermute(to_second, 'gz', odd)  9.12 us
    ppermute x2, starting transfers between devices, swap_layers(): lax.ppermute(to_second, 'gz', odd)  3.84 us
  transfers between devices with their start and end apart: 16, of which 7 were waited for; matrix products, arithmetic and copies ran while one was open for 0% of the time, Pallas kernels for 0%

profile of v5, /device:TPU:1, one launch (start us, length us, event | category | flops | bytes accessed | tf_op | source)
XLA Modules:
  0.0 136.9 jit_solution(9413760272086464671)
XLA Ops:
  1.3 8.8 %collective-permute-start = (f32[152,512]{1,0:T(8,128)S(1)}, f32[152,512]{1,0:T(8,128)S(1)}, u32[]{:S(2)}, u32[]{:S(2)}) collective-permute-start(f32[152,512]{1,0:T(8,128)S(1)} %get-tuple-element.30), channel_id=1, source_target_pairs={{0,1},{1,0},{2,3},{3,2},{4,5},{5,4},{6,7},{7,6},{8,9},{9,8},{10,11... | collective-permute-start | bytes 933896 | tf_op jit(solution)/shard_map/ppermute | solution.py:601
  12.0 6.4 %collective-permute-start.2 = (f32[72,512]{1,0:T(8,128)S(1)}, f32[72,512]{1,0:T(8,128)S(1)}, u32[]{:S(2)}, u32[]{:S(2)}) collective-permute-start(f32[72,512]{1,0:T(8,128)S(1)} %get-tuple-element.32), channel_id=1, source_target_pairs={{16,0},{17,1},{18,2},{19,3},{20,4},{21,5},{22,6},{23,7},{24,8},{25... | collective-permute-start | bytes 442376 | tf_op jit(solution)/shard_map/ppermute | solution.py:590
  18.3 5.1 %collective-permute-start.3 = (f32[72,512]{1,0:T(8,128)S(1)}, f32[72,512]{1,0:T(8,128)S(1)}, u32[]{:S(2)}, u32[]{:S(2)}) collective-permute-start(f32[72,512]{1,0:T(8,128)S(1)} %get-tuple-element.33), channel_id=1, source_target_pairs={{80,0},{81,1},{82,2},{83,3},{84,4},{85,5},{86,6},{87,7},{88,8},{89... | collective-permute-start | bytes 442376 | tf_op jit(solution)/shard_map/ppermute | solution.py:590
  23.4 3.0 %collective-permute-start.4 = (f32[72,512]{1,0:T(8,128)S(1)}, f32[72,512]{1,0:T(8,128)S(1)}, u32[]{:S(2)}, u32[]{:S(2)}) collective-permute-start(f32[72,512]{1,0:T(8,128)S(1)} %get-tuple-element.34), channel_id=1, source_target_pairs={{64,0},{65,1},{66,2},{67,3},{68,4},{69,5},{70,6},{71,7},{72,8},{73... | collective-permute-start | bytes 442376 | tf_op jit(solution)/shard_map/ppermute | solution.py:590
  27.7 2.6 %collective-permute-done.4.from_x = f32[72,512]{1,0:T(8,128)S(1)} collective-permute-done((f32[72,512]{1,0:T(8,128)S(1)}, f32[72,512]{1,0:T(8,128)S(1)}, u32[]{:S(2)}, u32[]{:S(2)}) %collective-permute-start.4) | collective-permute-done | bytes 147488 | tf_op jit(solution)/shard_map/ppermute | solution.py:590
  30.3 5.4 %collective-permute-start.5 = (f32[168,512]{1,0:T(8,128)S(1)}, f32[168,512]{1,0:T(8,128)S(1)}, u32[]{:S(2)}, u32[]{:S(2)}) collective-permute-start(f32[168,512]{1,0:T(8,128)S(1)} %get-tuple-element.38), channel_id=1, source_target_pairs={{0,1},{1,0},{2,3},{3,2},{4,5},{5,4},{6,7},{7,6},{8,9},{9,8},{10,11... | collective-permute-start | bytes 1032200 | tf_op jit(solution)/shard_map/ppermute | solution.py:601
  35.7 1.9 %collective-permute-start.6 = (f32[168,512]{1,0:T(8,128)S(1)}, f32[168,512]{1,0:T(8,128)S(1)}, u32[]{:S(2)}, u32[]{:S(2)}) collective-permute-start(f32[168,512]{1,0:T(8,128)S(1)} %get-tuple-element.39), channel_id=1, source_target_pairs={{0,15},{1,2},{2,1},{3,4},{4,3},{5,6},{6,5},{7,8},{8,7},{9,10},{10,... | collective-permute-start | bytes 1032200 | tf_op jit(solution)/shard_map/ppermute | solution.py:601
  37.6 9.1 %collective-permute-done.6.second = f32[168,512]{1,0:T(8,128)S(1)} collective-permute-done((f32[168,512]{1,0:T(8,128)S(1)}, f32[168,512]{1,0:T(8,128)S(1)}, u32[]{:S(2)}, u32[]{:S(2)}) %collective-permute-start.6) | collective-permute-done | bytes 344096 | tf_op jit(solution)/shard_map/ppermute | solution.py:601
  46.9 3.2 %shard_map.51.own = f32[16,640]{1,0:T(8,128)S(1)} custom-call(f32[640,512]{1,0:T(8,128)S(1)} %get-tuple-element.42.wide, s32[40,128]{1,0:T(8,128)S(1)} %get-tuple-element.47.places, f32[16,256]{1,0:T(8,128)S(1)} %get-tuple-element.48.start.refs_0_, f32[72,512]{1,0:T(8,128)S(1)} %collective-permute-done.2.from_y, ...), custom_call_target="tpu_custom_call" | custom-call | tf_op jit(solution)/shard_map/pallas_call | solution.py:563
  50.1 7.0 %collective-permute-start.7 = (f32[16,640]{1,0:T(8,128)S(1)}, f32[16,640]{1,0:T(8,128)S(1)}, u32[]{:S(2)}, u32[]{:S(2)}) collective-permute-start(f32[16,640]{1,0:T(8,128)S(1)} %shard_map.51.own), channel_id=1, source_target_pairs={{496,0},{497,1},{498,2},{499,3},{500,4},{501,5},{502,6},{503,7},{5... | collective-permute-start | bytes 122888 | tf_op jit(solution)/shard_map/ppermute | solution.py:590
  57.1 4.0 %collective-permute-start.8 = (f32[16,640]{1,0:T(8,128)S(1)}, f32[16,640]{1,0:T(8,128)S(1)}, u32[]{:S(2)}, u32[]{:S(2)}) collective-permute-start(f32[16,640]{1,0:T(8,128)S(1)} %shard_map.51.own), channel_id=1, source_target_pairs={{48,0},{49,1},{50,2},{51,3},{52,4},{53,5},{54,6},{55,7},{56,8},{57... | collective-permute-start | bytes 122888 | tf_op jit(solution)/shard_map/ppermute | solution.py:590
  61.1 3.2 %collective-permute-start.9 = (f32[16,640]{1,0:T(8,128)S(1)}, f32[16,640]{1,0:T(8,128)S(1)}, u32[]{:S(2)}, u32[]{:S(2)}) collective-permute-start(f32[16,640]{1,0:T(8,128)S(1)} %shard_map.51.own), channel_id=1, source_target_pairs={{448,0},{449,1},{450,2},{451,3},{452,4},{453,5},{454,6},{455,7},{4... | collective-permute-start | bytes 122888 | tf_op jit(solution)/shard_map/ppermute | solution.py:590
  64.5 2.6 %collective-permute-done.9.from_x = f32[16,640]{1,0:T(8,128)S(1)} collective-permute-done((f32[16,640]{1,0:T(8,128)S(1)}, f32[16,640]{1,0:T(8,128)S(1)}, u32[]{:S(2)}, u32[]{:S(2)}) %collective-permute-start.9) | collective-permute-done | bytes 40992 | tf_op jit(solution)/shard_map/ppermute | solution.py:590
  67.1 2.6 %shard_map.52.own.second = f32[16,512]{1,0:T(8,128)S(1)} custom-call(f32[512,512]{1,0:T(8,128)S(1)} %get-tuple-element.45.tall, s32[32,128]{1,0:T(8,128)S(1)} %get-tuple-element.46.places, f32[16,640]{1,0:T(8,128)S(1)} %shard_map.51.own, f32[16,640]{1,0:T(8,128)S(1)} %collective-permute-done.7.from_xy, f32[16,640]{1,0:T(8,128)S(1)} %collective-permute-done.8.from_y, ...), custom_call_target="tpu_custom_call" | custom-call | tf_op jit(solution)/shard_map/pallas_call | solution.py:563
  69.7 3.8 %collective-permute-start.10 = (f32[16,512]{1,0:T(8,128)S(1)}, f32[16,512]{1,0:T(8,128)S(1)}, u32[]{:S(2)}, u32[]{:S(2)}) collective-permute-start(f32[16,512]{1,0:T(8,128)S(1)} %shard_map.52.own.second), channel_id=1, source_target_pairs={{80,0},{81,1},{82,2},{83,3},{84,4},{85,5},{86,6},{87,7},{88,8},{89... | collective-permute-start | bytes 98312 | tf_op jit(solution)/shard_map/ppermute | solution.py:590
  75.4 3.4 %collective-permute-start.12 = (f32[16,512]{1,0:T(8,128)S(1)}, f32[16,512]{1,0:T(8,128)S(1)}, u32[]{:S(2)}, u32[]{:S(2)}) collective-permute-start(f32[16,512]{1,0:T(8,128)S(1)} %shard_map.52.own.second), channel_id=1, source_target_pairs={{64,0},{65,1},{66,2},{67,3},{68,4},{69,5},{70,6},{71,7},{72,8},{73... | collective-permute-start | bytes 98312 | tf_op jit(solution)/shard_map/ppermute | solution.py:590
  80.4 2.2 %shard_map.53.own = f32[16,384]{1,0:T(8,128)S(1)} custom-call(f32[640,512]{1,0:T(8,128)S(1)} %get-tuple-element.42.wide, s32[24,128]{1,0:T(8,128)S(1)} %get-tuple-element.44.places, f32[16,512]{1,0:T(8,128)S(1)} %shard_map.52.own.second, f32[16,512]{1,0:T(8,128)S(1)} %collective-permute-done.10.from_xy, f32[16,512]{1,0:T(8,128)S(1)} %collective-permute-done.11.from_y, ...), custom_call_target="tpu_custom_call" | custom-call | tf_op jit(solution)/shard_map/pallas_call | solution.py:563
  82.6 4.5 %collective-permute-start.13 = (f32[16,384]{1,0:T(8,128)S(1)}, f32[16,384]{1,0:T(8,128)S(1)}, u32[]{:S(2)}, u32[]{:S(2)}) collective-permute-start(f32[16,384]{1,0:T(8,128)S(1)} %shard_map.53.own), channel_id=1, source_target_pairs={{496,0},{497,1},{498,2},{499,3},{500,4},{501,5},{502,6},{503,7},{5... | collective-permute-start | bytes 73736 | tf_op jit(solution)/shard_map/ppermute | solution.py:590
  87.1 4.0 %collective-permute-start.14 = (f32[16,384]{1,0:T(8,128)S(1)}, f32[16,384]{1,0:T(8,128)S(1)}, u32[]{:S(2)}, u32[]{:S(2)}) collective-permute-start(f32[16,384]{1,0:T(8,128)S(1)} %shard_map.53.own), channel_id=1, source_target_pairs={{48,0},{49,1},{50,2},{51,3},{52,4},{53,5},{54,6},{55,7},{56,8},{57... | collective-permute-start | bytes 73736 | tf_op jit(solution)/shard_map/ppermute | solution.py:590
  91.1 2.9 %collective-permute-start.15 = (f32[16,384]{1,0:T(8,128)S(1)}, f32[16,384]{1,0:T(8,128)S(1)}, u32[]{:S(2)}, u32[]{:S(2)}) collective-permute-start(f32[16,384]{1,0:T(8,128)S(1)} %shard_map.53.own), channel_id=1, source_target_pairs={{448,0},{449,1},{450,2},{451,3},{452,4},{453,5},{454,6},{455,7},{4... | collective-permute-start | bytes 73736 | tf_op jit(solution)/shard_map/ppermute | solution.py:590
  94.1 2.8 %collective-permute-done.15.from_x = f32[16,384]{1,0:T(8,128)S(1)} collective-permute-done((f32[16,384]{1,0:T(8,128)S(1)}, f32[16,384]{1,0:T(8,128)S(1)}, u32[]{:S(2)}, u32[]{:S(2)}) %collective-permute-start.15) | collective-permute-done | bytes 24608 | tf_op jit(solution)/shard_map/ppermute | solution.py:590
  96.8 2.1 %shard_map.55 = (f32[16,256]{1,0:T(8,128)S(1)}, f32[32,4,128]{2,1,0:T(4,128)S(1)}) custom-call(f32[256,512]{1,0:T(8,128)S(1)} %get-tuple-element.29.matrix, s32[16,128]{1,0:T(8,128)S(1)} %get-tuple-element.43.places, f32[16,384]{1,0:T(8,128)S(1)} %shard_map.53.own, f32[16,384]{1,0:T(8,128)S(1)} %collective-permute-done.13.from_xy, ...), custom_call_target="tpu_custom_call" | custom-call | tf_op jit(solution)/shard_map/pallas_call | solution.py:563
  99.0 18.7 %all_to_all.10.ref = f32[32,4,128]{2,1,0:T(4,128)S(1)} all-to-all(f32[32,4,128]{2,1,0:T(4,128)S(1)} %get-tuple-element.51), channel_id=1, replica_groups=mesh['gx'=8,'gy'=4,'gz'=16] {'gx','gy'}, dimensions={0} | all-to-all | bytes 131072 | tf_op jit(solution)/shard_map/all_to_all | solution.py:658
  117.8 17.7 %all_to_all.11.ref = f32[16,4,128]{2,1,0:T(4,128)S(1)} all-to-all(f32[16,4,128]{2,1,0:T(4,128)S(1)} %shard_map.56), channel_id=1, replica_groups=mesh['gx'=8,'gy'=4,'gz'=16] {'gz'}, dimensions={0} | all-to-all | bytes 65536 | tf_op jit(solution)/shard_map/all_to_all | solution.py:660
  (22 shorter events, 9.9 us)
Async XLA Ops:
  1.3 29.0 %collective-permute-start = (f32[152,512]{1,0:T(8,128)S(1)}, f32[152,512]{1,0:T(8,128)S(1)}, u32[]{:S(2)}, u32[]{:S(2)}) collective-permute-start(f32[152,512]{1,0:T(8,128)S(1)} %get-tuple-element.30), channel_id=1, source_target_pairs={{0,1},{1,0},{2,3},{3,2},{4,5},{5,4},{6,7},{7,6},{8,9},{9,8},{10,11... | collective-permute-start | bytes 933896 | tf_op jit(solution)/shard_map/ppermute | solution.py:601
  10.0 20.2 %collective-permute-start.1 = (f32[152,512]{1,0:T(8,128)S(1)}, f32[152,512]{1,0:T(8,128)S(1)}, u32[]{:S(2)}, u32[]{:S(2)}) collective-permute-start(f32[152,512]{1,0:T(8,128)S(1)} %get-tuple-element.31), channel_id=1, source_target_pairs={{0,15},{1,2},{2,1},{3,4},{4,3},{5,6},{6,5},{7,8},{8,7},{9,10},{10,... | collective-permute-start | bytes 933896 | tf_op jit(solution)/shard_map/ppermute | solution.py:601
  12.0 14.4 %collective-permute-start.2 = (f32[72,512]{1,0:T(8,128)S(1)}, f32[72,512]{1,0:T(8,128)S(1)}, u32[]{:S(2)}, u32[]{:S(2)}) collective-permute-start(f32[72,512]{1,0:T(8,128)S(1)} %get-tuple-element.32), channel_id=1, source_target_pairs={{16,0},{17,1},{18,2},{19,3},{20,4},{21,5},{22,6},{23,7},{24,8},{25... | collective-permute-start | bytes 442376 | tf_op jit(solution)/shard_map/ppermute | solution.py:590
  18.3 9.3 %collective-permute-start.3 = (f32[72,512]{1,0:T(8,128)S(1)}, f32[72,512]{1,0:T(8,128)S(1)}, u32[]{:S(2)}, u32[]{:S(2)}) collective-permute-start(f32[72,512]{1,0:T(8,128)S(1)} %get-tuple-element.33), channel_id=1, source_target_pairs={{80,0},{81,1},{82,2},{83,3},{84,4},{85,5},{86,6},{87,7},{88,8},{89... | collective-permute-start | bytes 442376 | tf_op jit(solution)/shard_map/ppermute | solution.py:590
  23.4 6.8 %collective-permute-start.4 = (f32[72,512]{1,0:T(8,128)S(1)}, f32[72,512]{1,0:T(8,128)S(1)}, u32[]{:S(2)}, u32[]{:S(2)}) collective-permute-start(f32[72,512]{1,0:T(8,128)S(1)} %get-tuple-element.34), channel_id=1, source_target_pairs={{64,0},{65,1},{66,2},{67,3},{68,4},{69,5},{70,6},{71,7},{72,8},{73... | collective-permute-start | bytes 442376 | tf_op jit(solution)/shard_map/ppermute | solution.py:590
  30.3 7.3 %collective-permute-start.5 = (f32[168,512]{1,0:T(8,128)S(1)}, f32[168,512]{1,0:T(8,128)S(1)}, u32[]{:S(2)}, u32[]{:S(2)}) collective-permute-start(f32[168,512]{1,0:T(8,128)S(1)} %get-tuple-element.38), channel_id=1, source_target_pairs={{0,1},{1,0},{2,3},{3,2},{4,5},{5,4},{6,7},{7,6},{8,9},{9,8},{10,11... | collective-permute-start | bytes 1032200 | tf_op jit(solution)/shard_map/ppermute | solution.py:601
  35.7 11.1 %collective-permute-start.6 = (f32[168,512]{1,0:T(8,128)S(1)}, f32[168,512]{1,0:T(8,128)S(1)}, u32[]{:S(2)}, u32[]{:S(2)}) collective-permute-start(f32[168,512]{1,0:T(8,128)S(1)} %get-tuple-element.39), channel_id=1, source_target_pairs={{0,15},{1,2},{2,1},{3,4},{4,3},{5,6},{6,5},{7,8},{8,7},{9,10},{10,... | collective-permute-start | bytes 1032200 | tf_op jit(solution)/shard_map/ppermute | solution.py:601
  50.1 14.4 %collective-permute-start.7 = (f32[16,640]{1,0:T(8,128)S(1)}, f32[16,640]{1,0:T(8,128)S(1)}, u32[]{:S(2)}, u32[]{:S(2)}) collective-permute-start(f32[16,640]{1,0:T(8,128)S(1)} %shard_map.51.own), channel_id=1, source_target_pairs={{496,0},{497,1},{498,2},{499,3},{500,4},{501,5},{502,6},{503,7},{5... | collective-permute-start | bytes 122888 | tf_op jit(solution)/shard_map/ppermute | solution.py:590
  57.1 7.4 %collective-permute-start.8 = (f32[16,640]{1,0:T(8,128)S(1)}, f32[16,640]{1,0:T(8,128)S(1)}, u32[]{:S(2)}, u32[]{:S(2)}) collective-permute-start(f32[16,640]{1,0:T(8,128)S(1)} %shard_map.51.own), channel_id=1, source_target_pairs={{48,0},{49,1},{50,2},{51,3},{52,4},{53,5},{54,6},{55,7},{56,8},{57... | collective-permute-start | bytes 122888 | tf_op jit(solution)/shard_map/ppermute | solution.py:590
  61.1 6.0 %collective-permute-start.9 = (f32[16,640]{1,0:T(8,128)S(1)}, f32[16,640]{1,0:T(8,128)S(1)}, u32[]{:S(2)}, u32[]{:S(2)}) collective-permute-start(f32[16,640]{1,0:T(8,128)S(1)} %shard_map.51.own), channel_id=1, source_target_pairs={{448,0},{449,1},{450,2},{451,3},{452,4},{453,5},{454,6},{455,7},{4... | collective-permute-start | bytes 122888 | tf_op jit(solution)/shard_map/ppermute | solution.py:590
  69.7 9.2 %collective-permute-start.10 = (f32[16,512]{1,0:T(8,128)S(1)}, f32[16,512]{1,0:T(8,128)S(1)}, u32[]{:S(2)}, u32[]{:S(2)}) collective-permute-start(f32[16,512]{1,0:T(8,128)S(1)} %shard_map.52.own.second), channel_id=1, source_target_pairs={{80,0},{81,1},{82,2},{83,3},{84,4},{85,5},{86,6},{87,7},{88,8},{89... | collective-permute-start | bytes 98312 | tf_op jit(solution)/shard_map/ppermute | solution.py:590
  73.5 5.6 %collective-permute-start.11 = (f32[16,512]{1,0:T(8,128)S(1)}, f32[16,512]{1,0:T(8,128)S(1)}, u32[]{:S(2)}, u32[]{:S(2)}) collective-permute-start(f32[16,512]{1,0:T(8,128)S(1)} %shard_map.52.own.second), channel_id=1, source_target_pairs={{16,0},{17,1},{18,2},{19,3},{20,4},{21,5},{22,6},{23,7},{24,8},{25... | collective-permute-start | bytes 98312 | tf_op jit(solution)/shard_map/ppermute | solution.py:590
  75.4 5.0 %collective-permute-start.12 = (f32[16,512]{1,0:T(8,128)S(1)}, f32[16,512]{1,0:T(8,128)S(1)}, u32[]{:S(2)}, u32[]{:S(2)}) collective-permute-start(f32[16,512]{1,0:T(8,128)S(1)} %shard_map.52.own.second), channel_id=1, source_target_pairs={{64,0},{65,1},{66,2},{67,3},{68,4},{69,5},{70,6},{71,7},{72,8},{73... | collective-permute-start | bytes 98312 | tf_op jit(solution)/shard_map/ppermute | solution.py:590
  82.6 11.5 %collective-permute-start.13 = (f32[16,384]{1,0:T(8,128)S(1)}, f32[16,384]{1,0:T(8,128)S(1)}, u32[]{:S(2)}, u32[]{:S(2)}) collective-permute-start(f32[16,384]{1,0:T(8,128)S(1)} %shard_map.53.own), channel_id=1, source_target_pairs={{496,0},{497,1},{498,2},{499,3},{500,4},{501,5},{502,6},{503,7},{5... | collective-permute-start | bytes 73736 | tf_op jit(solution)/shard_map/ppermute | solution.py:590
  87.1 7.0 %collective-permute-start.14 = (f32[16,384]{1,0:T(8,128)S(1)}, f32[16,384]{1,0:T(8,128)S(1)}, u32[]{:S(2)}, u32[]{:S(2)}) collective-permute-start(f32[16,384]{1,0:T(8,128)S(1)} %shard_map.53.own), channel_id=1, source_target_pairs={{48,0},{49,1},{50,2},{51,3},{52,4},{53,5},{54,6},{55,7},{56,8},{57... | collective-permute-start | bytes 73736 | tf_op jit(solution)/shard_map/ppermute | solution.py:590
  91.1 5.8 %collective-permute-start.15 = (f32[16,384]{1,0:T(8,128)S(1)}, f32[16,384]{1,0:T(8,128)S(1)}, u32[]{:S(2)}, u32[]{:S(2)}) collective-permute-start(f32[16,384]{1,0:T(8,128)S(1)} %shard_map.53.own), channel_id=1, source_target_pairs={{448,0},{449,1},{450,2},{451,3},{452,4},{453,5},{454,6},{455,7},{4... | collective-permute-start | bytes 73736 | tf_op jit(solution)/shard_map/ppermute | solution.py:590

commit v6 on v4

--- a/solution.py
+++ b/solution.py
@@ -230,7 +230,8 @@
 
 
 def bricks_place(x, y, z):
-    brick = ((z + 4) >> 2) * 4 + (x >> 1) * 2 + (y >> 1)
+    layer = ((z >> 2) != 0).astype(jnp.int32)
+    brick = layer * 4 + (x >> 1) * 2 + (y >> 1)
     return (brick * 2 + (x & 1)) * 8 + (y & 1) * 4 + (z & 3)
 
 
@@ -243,11 +244,6 @@
     return place
 
 
-def tall_far_atom(index):
-    column = (index * 205) >> 11
-    return 1 + (column >> 1), 1 + (column & 1), index - 10 * column - 3
-
-
 def far_atom(index):
     column = (index * 43) >> 8
     return 1 + (column >> 1), 1 + (column & 1), index - 6 * column - 1
@@ -261,9 +257,29 @@
     return index >> 3, (index >> 2) & 1, index & 3
 
 
-FAR_ROWS = [column * 10 + z + 3 for column in range(4) for z in range(-1, 5)]
-FIRST_PLACE, SECOND_PLACE = pieces_place(-1, 10, -3), pieces_place(0, 8, -2)
-THIRD_PLACE = pieces_place(-1, 6, -1)
+def first_spans(even):
+    if isinstance(even, bool):
+        return (1, -3) if even else (-3, 3)
+    return jnp.where(even, 1, -3), jnp.where(even, -3, 3)
+
+
+def first_place(even):
+    wide_low, slim_low = first_spans(even)
+
+    def place(x, y, z):
+        x, y = x + 1, y + 1
+        piece = (x >> 1) * 2 + (y >> 1)
+        column = (x & 1) * 2 + (y & 1)
+        layer = z - wide_low
+        wide, slim = column * 6 + layer, 24 + column * 4 + z - slim_low
+        if isinstance(z, int):
+            return piece * 40 + (wide if 0 <= layer < 6 else slim)
+        return piece * 40 + jnp.where((layer >= 0) & (layer < 6), wide, slim)
+
+    return place
+
+
+SECOND_PLACE, THIRD_PLACE = pieces_place(0, 8, -2), pieces_place(-1, 6, -1)
 
 
 def find_places(matrix, rows, atom, place, out):
@@ -468,14 +484,34 @@
         to_second[q * 32 : q * 32 + 32] = jnp.where(even, down, up)
 
 
-def join_kernel(matrix, from_y, from_xy, from_x, first, second, wide, places):
+def join_wide_kernel(matrix, from_y, from_xy, from_x, first, wide, places):
     even = is_even()
     for q, (ref, row) in enumerate(far_columns(matrix, from_x, from_y, from_xy)):
-        one, two = first[q * 48 : q * 48 + 48], second[q * 48 : q * 48 + 48]
-        wide[q * 160 : q * 160 + 48] = jnp.where(even, two, one)
-        wide[q * 160 + 48 : q * 160 + 112] = ref[row : row + 64]
-        wide[q * 160 + 112 : q * 160 + 160] = jnp.where(even, one, two)
-    find_places(wide, range(40), tall_far_atom, bricks_place, places)
+        other = first[q * 48 : q * 48 + 48]
+        wide[q * 96 : q * 96 + 48] = jnp.where(even, ref[row + 16 : row + 64], other)
+        wide[q * 96 + 48 : q * 96 + 96] = jnp.where(even, other, ref[row : row + 48])
+    low, _ = first_spans(even)
+
+    def atom(index):
+        x, y, z = far_atom(index)
+        return x, y, z + 1 + low
+
+    find_places(wide, range(24), atom, bricks_place, places)
+
+
+def join_slim_kernel(matrix, from_y, from_xy, from_x, second, slim, places):
+    even = is_even()
+    for q, (ref, row) in enumerate(far_columns(matrix, from_x, from_y, from_xy)):
+        other = second[q * 48 : q * 48 + 48]
+        below = jnp.concatenate([other, ref[row : row + 16]], axis=0)
+        above = jnp.concatenate([ref[row + 48 : row + 64], other], axis=0)
+        slim[q * 64 : q * 64 + 64] = jnp.where(even, below, above)
+    _, low = first_spans(even)
+
+    def atom(index):
+        return 1 + (index >> 3), 1 + ((index >> 2) & 1), (index & 3) + low
+
+    find_places(slim, range(16), atom, bricks_place, places)
 
 
 def join_near_kernel(matrix, first, second, near_first, near_second, tall, places):
@@ -490,26 +526,43 @@
         tall[q * 128 : q * 128 + 32] = low
         tall[q * 128 + 32 : q * 128 + 96] = matrix[q * 64 : q * 64 + 64]
         tall[q * 128 + 96 : q * 128 + 128] = high
-    find_places(tall, range(32), tall_near_atom, FIRST_PLACE, places)
-
-
-def later_places_kernel(wide, matrix, third_places, fourth_places):
-    find_places(wide, FAR_ROWS, far_atom, SECOND_PLACE, third_places)
+    find_places(tall, range(32), tall_near_atom, first_place(even), places)
+
+
+def later_kernel(wide, slim, matrix, far, third_places, fourth_places):
+    even = is_even()
+    for q in range(4):
+        one, two = wide[q * 96 : q * 96 + 96], slim[q * 64 : q * 64 + 64]
+        below = jnp.concatenate([two[32:64], one[0:64]], axis=0)
+        above = jnp.concatenate([one[32:96], two[0:32]], axis=0)
+        far[q * 96 : q * 96 + 96] = jnp.where(even, below, above)
+    find_places(far, range(24), far_atom, SECOND_PLACE, third_places)
     find_places(matrix, range(ATOMS), near_atom, THIRD_PLACE, fourth_places)
 
 
-def first_kernel(
-    wide, places, start, from_y, from_xy, from_x, first, second, out, field, gathered
+WIDE_FLOPS = 1 << 28
+
+
+def first_tiles(rows, places, start, from_y, from_xy, from_x, side, field, gathered):
+    pieces = [start[...]] + [unpack_bricks(ref[64:72]) for ref in (from_y, from_x, from_xy)]
+    pieces += [unpack_bricks(side[192 + q * 8 : 200 + q * 8]) for q in range(4)]
+    set_tiles(field, pieces)
+    return couple(rows, range(rows.shape[0] // SLOT_ROWS), field, places, gathered)
+
+
+def first_wide_kernel(
+    wide, places, start, from_y, from_xy, from_x, first, out, field, gathered
 ):
-    even = is_even()
-    inner = [start[...]] + [unpack_bricks(ref[64:72]) for ref in (from_y, from_x, from_xy)]
-    outer = [
-        [unpack_bricks(ref[192 + q * 8 : 200 + q * 8]) for q in range(4)] for ref in (first, second)
-    ]
-    low = [jnp.where(even, two, one) for one, two in zip(*outer)]
-    high = [jnp.where(even, one, two) for one, two in zip(*outer)]
-    set_tiles(field, low + inner + high)
-    out[...] = couple(wide, range(40), field, places, gathered)
+    out[...] = first_tiles(wide, places, start, from_y, from_xy, from_x, first, field, gathered)
+
+
+def first_slim_kernel(
+    slim, places, start, from_y, from_xy, from_x, second, before, out, field, gathered
+):
+    out[:, 0 : 3 * LANES] = before[...]
+    out[:, 3 * LANES : 5 * LANES] = first_tiles(
+        slim, places, start, from_y, from_xy, from_x, second, field, gathered
+    )
 
 
 def second_kernel(tall, places, own, from_x, from_y, from_xy, out, field, gathered):
@@ -519,11 +572,14 @@
 
 def third_kernel(wide, places, own, from_x, from_y, from_xy, out, field, gathered):
     set_tiles(field, (own, from_y, from_x, from_xy))
-    out[...] = couple(wide, FAR_ROWS, field, places, gathered)
+    out[...] = couple(wide, range(24), field, places, gathered)
 
 
 def pick_kernel(own, from_x, from_y, from_xy, second, first_own, second_own):
-    first_own[...] = pick_own((from_xy, from_x, from_y, own), FIRST_PLACE)
+    pieces = from_xy, from_x, from_y, own
+    first_own[...] = jnp.where(
+        is_even(), pick_own(pieces, first_place(True)), pick_own(pieces, first_place(False))
+    )
     second_own[...] = pick_own((second,), SECOND_PLACE)
 
 
@@ -546,7 +602,7 @@
     return jax.ShapeDtypeStruct((rows, LANES), jnp.int32)
 
 
-def call(kernel, shapes, *operands, scratch=(), place=VMEM):
+def call(kernel, shapes, *operands, scratch=(), place=VMEM, flops=0):
     shapes = [
         shape if isinstance(shape, jax.ShapeDtypeStruct) else jax.ShapeDtypeStruct(shape, jnp.float32)
         for shape in shapes
@@ -559,6 +615,9 @@
         ],
         out_specs=[VMEM] * len(shapes),
         scratch_shapes=list(scratch),
+        cost_estimate=pl.CostEstimate(flops=flops, bytes_accessed=flops // 64, transcendentals=0)
+        if flops
+        else None,
         compiler_params=pltpu.CompilerParams(vmem_limit_bytes=24 * 1024 * 1024),
     )(*operands)
 
@@ -612,13 +671,24 @@
     sides = from_y, from_xy, from_x
     layers = swap_layers(*call(spread_kernel, [(224, WIDE)] * 2, matrix, *sides, start))
     near_layers = swap_layers(*call(spread_near_kernel, [(96, WIDE)] * 2, matrix))
-    wide, places = call(
-        join_kernel, [(40 * SLOT_ROWS, WIDE), whole_numbers(40)], matrix, *sides, *layers
+    wide, wide_places = call(
+        join_wide_kernel, [(24 * SLOT_ROWS, WIDE), whole_numbers(24)], matrix, *sides, layers[0]
     )
     (first,) = call(
-        first_kernel, [(SLOT_ROWS, 5 * LANES)],
-        wide, places, start, *sides, *layers,
-        scratch=scratch_for(24, 5),
+        first_wide_kernel, [(SLOT_ROWS, 3 * LANES)],
+        wide, wide_places, start, *sides, layers[0],
+        scratch=scratch_for(16, 3),
+        flops=WIDE_FLOPS,
+    )
+    first, last_layers = lax.optimization_barrier((first, layers[1]))
+    layers = layers[0], last_layers
+    slim, slim_places = call(
+        join_slim_kernel, [(16 * SLOT_ROWS, WIDE), whole_numbers(16)], matrix, *sides, layers[1]
+    )
+    (first,) = call(
+        first_slim_kernel, [(SLOT_ROWS, 5 * LANES)],
+        slim, slim_places, start, *sides, layers[1], first,
+        scratch=scratch_for(16, 2),
     )
     tall, places = call(
         join_near_kernel, [(32 * SLOT_ROWS, WIDE), whole_numbers(32)],
@@ -630,12 +700,14 @@
         scratch=scratch_for(20, 4),
     )
     first_own, second_own = call(pick_kernel, [flat] * 2, first, *pieces, second)
-    third_places, fourth_places = call(
-        later_places_kernel, [whole_numbers(24), whole_numbers(ATOMS)], wide, matrix
+    far, third_places, fourth_places = call(
+        later_kernel,
+        [(24 * SLOT_ROWS, WIDE), whole_numbers(24), whole_numbers(ATOMS)],
+        wide, slim, matrix,
     )
     (third,) = call(
         third_kernel, [(SLOT_ROWS, 3 * LANES)],
-        wide, third_places, second, *fetch_three(second, second, second, 1),
+        far, third_places, second, *fetch_three(second, second, second, 1),
         scratch=scratch_for(16, 3),
     )
     third_own, message = call(

time: 132 us -> 131 us (level)
  waiting for transfers between devices: 15.4 us -> 13 us
    ppermute x2, waiting for transfers between devices: 5.15 us -> 2.82 us  [swap_layers(): lax.ppermute(to_second, 'gz', odd)]
    pallas_call x13 -> x15, Pallas kernels: 13.5 us -> 14.4 us  [call(): pl.pallas_call(kernel, out_shape=shapes, in_specs=[SMEM if operand.dtype...]
  transfers between devices with their start and end apart: 16 -> 16, of which waited for: 7 -> 7; matrix products, arithmetic and copies ran while one was open for 0% -> 0% of each run, Pallas kernels for 3% -> 4%
where the time goes in v6:
time: 131 us; the launch traced here: 130 us
  starting transfers between devices  66.1 us (50%)
  blocking collectives  36.4 us (28%)
  Pallas kernels  14.4 us (11%)
  waiting for transfers between devices  13 us (10%)
    ppermute x12, starting transfers between devices, fetch(): return lax.ppermute(value, AXES, pairs)  52.9 us
    all_to_all x1, blocking collectives, body(): message = lax.all_to_all(message, ('gx', 'gy'), 0, 0, tiled=True)  19.4 us
    all_to_all x1, blocking collectives, body(): message = lax.all_to_all(message, 'gz', 0, 0, tiled=True)  17 us
    pallas_call x15, Pallas kernels, call(): pl.pallas_call(kernel, out_shape=shapes, in_specs=[SMEM if operand.dtype...  14.4 us
    ppermute x12, waiting for transfers between devices, fetch(): return lax.ppermute(value, AXES, pairs)  10.2 us
    ppermute x2, starting transfers between devices, swap_layers(): lax.ppermute(to_first, 'gz', even)  8.34 us
    ppermute x2, starting transfers between devices, swap_layers(): lax.ppermute(to_second, 'gz', odd)  4.91 us
    ppermute x2, waiting for transfers between devices, swap_layers(): lax.ppermute(to_second, 'gz', odd)  2.82 us
  transfers between devices with their start and end apart: 16, of which 7 were waited for; matrix products, arithmetic and copies ran while one was open for 0% of the time, Pallas kernels for 4%

profile of v6, /device:TPU:1, one launch (start us, length us, event | category | flops | bytes accessed | tf_op | source)
XLA Modules:
  0.0 130.2 jit_solution(1985733745573383828)
XLA Ops:
  1.2 11.5 %collective-permute-start = (f32[72,512]{1,0:T(8,128)S(1)}, f32[72,512]{1,0:T(8,128)S(1)}, u32[]{:S(2)}, u32[]{:S(2)}) collective-permute-start(f32[72,512]{1,0:T(8,128)S(1)} %get-tuple-element.30), channel_id=1, source_target_pairs={{16,0},{17,1},{18,2},{19,3},{20,4},{21,5},{22,6},{23,7},{24,8},{25... | collective-permute-start | bytes 442376 | tf_op jit(solution)/shard_map/ppermute | solution.py:640
  12.7 5.1 %collective-permute-start.1 = (f32[72,512]{1,0:T(8,128)S(1)}, f32[72,512]{1,0:T(8,128)S(1)}, u32[]{:S(2)}, u32[]{:S(2)}) collective-permute-start(f32[72,512]{1,0:T(8,128)S(1)} %get-tuple-element.31), channel_id=1, source_target_pairs={{80,0},{81,1},{82,2},{83,3},{84,4},{85,5},{86,6},{87,7},{88,8},{89... | collective-permute-start | bytes 442376 | tf_op jit(solution)/shard_map/ppermute | solution.py:640
  17.8 3.0 %collective-permute-start.2 = (f32[72,512]{1,0:T(8,128)S(1)}, f32[72,512]{1,0:T(8,128)S(1)}, u32[]{:S(2)}, u32[]{:S(2)}) collective-permute-start(f32[72,512]{1,0:T(8,128)S(1)} %get-tuple-element.32), channel_id=1, source_target_pairs={{64,0},{65,1},{66,2},{67,3},{68,4},{69,5},{70,6},{71,7},{72,8},{73... | collective-permute-start | bytes 442376 | tf_op jit(solution)/shard_map/ppermute | solution.py:640
  20.8 3.3 %collective-permute-done.from_y = f32[72,512]{1,0:T(8,128)S(1)} collective-permute-done((f32[72,512]{1,0:T(8,128)S(1)}, f32[72,512]{1,0:T(8,128)S(1)}, u32[]{:S(2)}, u32[]{:S(2)}) %collective-permute-start) | collective-permute-done | bytes 147488 | tf_op jit(solution)/shard_map/ppermute | solution.py:640
  24.5 3.7 %collective-permute-start.3 = (f32[224,512]{1,0:T(8,128)S(1)}, f32[224,512]{1,0:T(8,128)S(1)}, u32[]{:S(2)}, u32[]{:S(2)}) collective-permute-start(f32[224,512]{1,0:T(8,128)S(1)} %get-tuple-element.34), channel_id=1, source_target_pairs={{0,1},{1,0},{2,3},{3,2},{4,5},{5,4},{6,7},{7,6},{8,9},{9,8},{10,11... | collective-permute-start | bytes 1376264 | tf_op jit(solution)/shard_map/ppermute | solution.py:651
  28.3 3.0 %collective-permute-start.4 = (f32[224,512]{1,0:T(8,128)S(1)}, f32[224,512]{1,0:T(8,128)S(1)}, u32[]{:S(2)}, u32[]{:S(2)}) collective-permute-start(f32[224,512]{1,0:T(8,128)S(1)} %get-tuple-element.37), channel_id=1, source_target_pairs={{0,15},{1,2},{2,1},{3,4},{4,3},{5,6},{6,5},{7,8},{8,7},{9,10},{10,... | collective-permute-start | bytes 1376264 | tf_op jit(solution)/shard_map/ppermute | solution.py:651
  31.3 4.6 %collective-permute-start.5 = (f32[96,512]{1,0:T(8,128)S(1)}, f32[96,512]{1,0:T(8,128)S(1)}, u32[]{:S(2)}, u32[]{:S(2)}) collective-permute-start(f32[96,512]{1,0:T(8,128)S(1)} %get-tuple-element.43), channel_id=1, source_target_pairs={{0,1},{1,0},{2,3},{3,2},{4,5},{5,4},{6,7},{7,6},{8,9},{9,8},{10,11... | collective-permute-start | bytes 589832 | tf_op jit(solution)/shard_map/ppermute | solution.py:651
  38.0 2.2 %shard_map.49.before = f32[16,384]{1,0:T(8,128)S(1)} custom-call(f32[384,512]{1,0:T(8,128)S(1)} %get-tuple-element.35.wide, s32[24,128]{1,0:T(8,128)S(1)} %get-tuple-element.36.places, f32[16,256]{1,0:T(8,128)S(1)} %get-tuple-element.33.start.refs_0_, f32[72,512]{1,0:T(8,128)S(1)} %collective-permute-done.from_y, ...), custom_call_target="tpu_custom_call" | custom-call | flops 268435456 | bytes 4194304 | tf_op jit(solution)/shard_map/pallas_call | solution.py:610
  40.2 2.8 %collective-permute-done.4.second = f32[224,512]{1,0:T(8,128)S(1)} collective-permute-done((f32[224,512]{1,0:T(8,128)S(1)}, f32[224,512]{1,0:T(8,128)S(1)}, u32[]{:S(2)}, u32[]{:S(2)}) %collective-permute-start.4) | collective-permute-done | bytes 458784 | tf_op jit(solution)/shard_map/ppermute | solution.py:651
  44.9 3.9 %collective-permute-start.9 = (f32[16,640]{1,0:T(8,128)S(1)}, f32[16,640]{1,0:T(8,128)S(1)}, u32[]{:S(2)}, u32[]{:S(2)}) collective-permute-start(f32[16,640]{1,0:T(8,128)S(1)} %shard_map.54.own), channel_id=1, source_target_pairs={{496,0},{497,1},{498,2},{499,3},{500,4},{501,5},{502,6},{503,7},{5... | collective-permute-start | bytes 122888 | tf_op jit(solution)/shard_map/ppermute | solution.py:640
  48.8 4.3 %collective-permute-start.8 = (f32[16,640]{1,0:T(8,128)S(1)}, f32[16,640]{1,0:T(8,128)S(1)}, u32[]{:S(2)}, u32[]{:S(2)}) collective-permute-start(f32[16,640]{1,0:T(8,128)S(1)} %shard_map.54.own), channel_id=1, source_target_pairs={{48,0},{49,1},{50,2},{51,3},{52,4},{53,5},{54,6},{55,7},{56,8},{57... | collective-permute-start | bytes 122888 | tf_op jit(solution)/shard_map/ppermute | solution.py:640
  53.1 3.2 %collective-permute-start.7 = (f32[16,640]{1,0:T(8,128)S(1)}, f32[16,640]{1,0:T(8,128)S(1)}, u32[]{:S(2)}, u32[]{:S(2)}) collective-permute-start(f32[16,640]{1,0:T(8,128)S(1)} %shard_map.54.own), channel_id=1, source_target_pairs={{448,0},{449,1},{450,2},{451,3},{452,4},{453,5},{454,6},{455,7},{4... | collective-permute-start | bytes 122888 | tf_op jit(solution)/shard_map/ppermute | solution.py:640
  56.5 2.2 %collective-permute-done.8.from_y = f32[16,640]{1,0:T(8,128)S(1)} collective-permute-done((f32[16,640]{1,0:T(8,128)S(1)}, f32[16,640]{1,0:T(8,128)S(1)}, u32[]{:S(2)}, u32[]{:S(2)}) %collective-permute-start.8) | collective-permute-done | bytes 40992 | tf_op jit(solution)/shard_map/ppermute | solution.py:640
  59.1 2.6 %shard_map.55.own.second = f32[16,512]{1,0:T(8,128)S(1)} custom-call(f32[512,512]{1,0:T(8,128)S(1)} %get-tuple-element.45.tall, s32[32,128]{1,0:T(8,128)S(1)} %get-tuple-element.46.places, f32[16,640]{1,0:T(8,128)S(1)} %shard_map.54.own, f32[16,640]{1,0:T(8,128)S(1)} %collective-permute-done.7.from_x, f32[16,640]{1,0:T(8,128)S(1)} %collective-permute-done.8.from_y, ...), custom_call_target="tpu_custom_call" | custom-call | tf_op jit(solution)/shard_map/pallas_call | solution.py:610
  61.7 3.9 %collective-permute-start.12 = (f32[16,512]{1,0:T(8,128)S(1)}, f32[16,512]{1,0:T(8,128)S(1)}, u32[]{:S(2)}, u32[]{:S(2)}) collective-permute-start(f32[16,512]{1,0:T(8,128)S(1)} %shard_map.55.own.second), channel_id=1, source_target_pairs={{80,0},{81,1},{82,2},{83,3},{84,4},{85,5},{86,6},{87,7},{88,8},{89... | collective-permute-start | bytes 98312 | tf_op jit(solution)/shard_map/ppermute | solution.py:640
  65.6 3.9 %collective-permute-start.11 = (f32[16,512]{1,0:T(8,128)S(1)}, f32[16,512]{1,0:T(8,128)S(1)}, u32[]{:S(2)}, u32[]{:S(2)}) collective-permute-start(f32[16,512]{1,0:T(8,128)S(1)} %shard_map.55.own.second), channel_id=1, source_target_pairs={{16,0},{17,1},{18,2},{19,3},{20,4},{21,5},{22,6},{23,7},{24,8},{25... | collective-permute-start | bytes 98312 | tf_op jit(solution)/shard_map/ppermute | solution.py:640
  69.5 3.4 %collective-permute-start.10 = (f32[16,512]{1,0:T(8,128)S(1)}, f32[16,512]{1,0:T(8,128)S(1)}, u32[]{:S(2)}, u32[]{:S(2)}) collective-permute-start(f32[16,512]{1,0:T(8,128)S(1)} %shard_map.55.own.second), channel_id=1, source_target_pairs={{64,0},{65,1},{66,2},{67,3},{68,4},{69,5},{70,6},{71,7},{72,8},{73... | collective-permute-start | bytes 98312 | tf_op jit(solution)/shard_map/ppermute | solution.py:640
  74.2 2.2 %shard_map.56.own = f32[16,384]{1,0:T(8,128)S(1)} custom-call(f32[384,512]{1,0:T(8,128)S(1)} %get-tuple-element.41.wide, s32[24,128]{1,0:T(8,128)S(1)} %get-tuple-element.42.places, f32[16,512]{1,0:T(8,128)S(1)} %shard_map.55.own.second, f32[16,512]{1,0:T(8,128)S(1)} %collective-permute-done.10.from_x, f32[16,512]{1,0:T(8,128)S(1)} %collective-permute-done.11.from_y, ...), custom_call_target="tpu_custom_call" | custom-call | tf_op jit(solution)/shard_map/pallas_call | solution.py:610
  76.4 2.7 %collective-permute-start.15 = (f32[16,384]{1,0:T(8,128)S(1)}, f32[16,384]{1,0:T(8,128)S(1)}, u32[]{:S(2)}, u32[]{:S(2)}) collective-permute-start(f32[16,384]{1,0:T(8,128)S(1)} %shard_map.56.own), channel_id=1, source_target_pairs={{496,0},{497,1},{498,2},{499,3},{500,4},{501,5},{502,6},{503,7},{5... | collective-permute-start | bytes 73736 | tf_op jit(solution)/shard_map/ppermute | solution.py:640
  79.1 4.9 %collective-permute-start.14 = (f32[16,384]{1,0:T(8,128)S(1)}, f32[16,384]{1,0:T(8,128)S(1)}, u32[]{:S(2)}, u32[]{:S(2)}) collective-permute-start(f32[16,384]{1,0:T(8,128)S(1)} %shard_map.56.own), channel_id=1, source_target_pairs={{48,0},{49,1},{50,2},{51,3},{52,4},{53,5},{54,6},{55,7},{56,8},{57... | collective-permute-start | bytes 73736 | tf_op jit(solution)/shard_map/ppermute | solution.py:640
  84.0 3.2 %collective-permute-start.13 = (f32[16,384]{1,0:T(8,128)S(1)}, f32[16,384]{1,0:T(8,128)S(1)}, u32[]{:S(2)}, u32[]{:S(2)}) collective-permute-start(f32[16,384]{1,0:T(8,128)S(1)} %shard_map.56.own), channel_id=1, source_target_pairs={{448,0},{449,1},{450,2},{451,3},{452,4},{453,5},{454,6},{455,7},{4... | collective-permute-start | bytes 73736 | tf_op jit(solution)/shard_map/ppermute | solution.py:640
  87.3 2.8 %collective-permute-done.13.from_x = f32[16,384]{1,0:T(8,128)S(1)} collective-permute-done((f32[16,384]{1,0:T(8,128)S(1)}, f32[16,384]{1,0:T(8,128)S(1)}, u32[]{:S(2)}, u32[]{:S(2)}) %collective-permute-start.13) | collective-permute-done | bytes 24608 | tf_op jit(solution)/shard_map/ppermute | solution.py:640
  92.2 19.4 %all_to_all.10.ref = f32[32,4,128]{2,1,0:T(4,128)S(1)} all-to-all(f32[32,4,128]{2,1,0:T(4,128)S(1)} %get-tuple-element.51), channel_id=1, replica_groups=mesh['gx'=8,'gy'=4,'gz'=16] {'gx','gy'}, dimensions={0} | all-to-all | bytes 131072 | tf_op jit(solution)/shard_map/all_to_all | solution.py:720
  111.6 17.0 %all_to_all.11.ref = f32[16,4,128]{2,1,0:T(4,128)S(1)} all-to-all(f32[16,4,128]{2,1,0:T(4,128)S(1)} %shard_map.59), channel_id=1, replica_groups=mesh['gx'=8,'gy'=4,'gz'=16] {'gz'}, dimensions={0} | all-to-all | bytes 65536 | tf_op jit(solution)/shard_map/all_to_all | solution.py:722
  (25 shorter events, 11.2 us)
Async XLA Ops:
  1.2 22.9 %collective-permute-start = (f32[72,512]{1,0:T(8,128)S(1)}, f32[72,512]{1,0:T(8,128)S(1)}, u32[]{:S(2)}, u32[]{:S(2)}) collective-permute-start(f32[72,512]{1,0:T(8,128)S(1)} %get-tuple-element.30), channel_id=1, source_target_pairs={{16,0},{17,1},{18,2},{19,3},{20,4},{21,5},{22,6},{23,7},{24,8},{25... | collective-permute-start | bytes 442376 | tf_op jit(solution)/shard_map/ppermute | solution.py:640
  12.7 11.4 %collective-permute-start.1 = (f32[72,512]{1,0:T(8,128)S(1)}, f32[72,512]{1,0:T(8,128)S(1)}, u32[]{:S(2)}, u32[]{:S(2)}) collective-permute-start(f32[72,512]{1,0:T(8,128)S(1)} %get-tuple-element.31), channel_id=1, source_target_pairs={{80,0},{81,1},{82,2},{83,3},{84,4},{85,5},{86,6},{87,7},{88,8},{89... | collective-permute-start | bytes 442376 | tf_op jit(solution)/shard_map/ppermute | solution.py:640
  17.8 6.7 %collective-permute-start.2 = (f32[72,512]{1,0:T(8,128)S(1)}, f32[72,512]{1,0:T(8,128)S(1)}, u32[]{:S(2)}, u32[]{:S(2)}) collective-permute-start(f32[72,512]{1,0:T(8,128)S(1)} %get-tuple-element.32), channel_id=1, source_target_pairs={{64,0},{65,1},{66,2},{67,3},{68,4},{69,5},{70,6},{71,7},{72,8},{73... | collective-permute-start | bytes 442376 | tf_op jit(solution)/shard_map/ppermute | solution.py:640
  24.5 13.3 %collective-permute-start.3 = (f32[224,512]{1,0:T(8,128)S(1)}, f32[224,512]{1,0:T(8,128)S(1)}, u32[]{:S(2)}, u32[]{:S(2)}) collective-permute-start(f32[224,512]{1,0:T(8,128)S(1)} %get-tuple-element.34), channel_id=1, source_target_pairs={{0,1},{1,0},{2,3},{3,2},{4,5},{5,4},{6,7},{7,6},{8,9},{9,8},{10,11... | collective-permute-start | bytes 1376264 | tf_op jit(solution)/shard_map/ppermute | solution.py:651
  28.3 14.8 %collective-permute-start.4 = (f32[224,512]{1,0:T(8,128)S(1)}, f32[224,512]{1,0:T(8,128)S(1)}, u32[]{:S(2)}, u32[]{:S(2)}) collective-permute-start(f32[224,512]{1,0:T(8,128)S(1)} %get-tuple-element.37), channel_id=1, source_target_pairs={{0,15},{1,2},{2,1},{3,4},{4,3},{5,6},{6,5},{7,8},{8,7},{9,10},{10,... | collective-permute-start | bytes 1376264 | tf_op jit(solution)/shard_map/ppermute | solution.py:651
  31.3 25.0 %collective-permute-start.5 = (f32[96,512]{1,0:T(8,128)S(1)}, f32[96,512]{1,0:T(8,128)S(1)}, u32[]{:S(2)}, u32[]{:S(2)}) collective-permute-start(f32[96,512]{1,0:T(8,128)S(1)} %get-tuple-element.43), channel_id=1, source_target_pairs={{0,1},{1,0},{2,3},{3,2},{4,5},{5,4},{6,7},{7,6},{8,9},{9,8},{10,11... | collective-permute-start | bytes 589832 | tf_op jit(solution)/shard_map/ppermute | solution.py:651
  35.9 20.4 %collective-permute-start.6 = (f32[96,512]{1,0:T(8,128)S(1)}, f32[96,512]{1,0:T(8,128)S(1)}, u32[]{:S(2)}, u32[]{:S(2)}) collective-permute-start(f32[96,512]{1,0:T(8,128)S(1)} %get-tuple-element.44), channel_id=1, source_target_pairs={{0,15},{1,2},{2,1},{3,4},{4,3},{5,6},{6,5},{7,8},{8,7},{9,10},{10,... | collective-permute-start | bytes 589832 | tf_op jit(solution)/shard_map/ppermute | solution.py:651
  44.9 11.5 %collective-permute-start.9 = (f32[16,640]{1,0:T(8,128)S(1)}, f32[16,640]{1,0:T(8,128)S(1)}, u32[]{:S(2)}, u32[]{:S(2)}) collective-permute-start(f32[16,640]{1,0:T(8,128)S(1)} %shard_map.54.own), channel_id=1, source_target_pairs={{496,0},{497,1},{498,2},{499,3},{500,4},{501,5},{502,6},{503,7},{5... | collective-permute-start | bytes 122888 | tf_op jit(solution)/shard_map/ppermute | solution.py:640
  48.8 9.8 %collective-permute-start.8 = (f32[16,640]{1,0:T(8,128)S(1)}, f32[16,640]{1,0:T(8,128)S(1)}, u32[]{:S(2)}, u32[]{:S(2)}) collective-permute-start(f32[16,640]{1,0:T(8,128)S(1)} %shard_map.54.own), channel_id=1, source_target_pairs={{48,0},{49,1},{50,2},{51,3},{52,4},{53,5},{54,6},{55,7},{56,8},{57... | collective-permute-start | bytes 122888 | tf_op jit(solution)/shard_map/ppermute | solution.py:640
  53.1 6.0 %collective-permute-start.7 = (f32[16,640]{1,0:T(8,128)S(1)}, f32[16,640]{1,0:T(8,128)S(1)}, u32[]{:S(2)}, u32[]{:S(2)}) collective-permute-start(f32[16,640]{1,0:T(8,128)S(1)} %shard_map.54.own), channel_id=1, source_target_pairs={{448,0},{449,1},{450,2},{451,3},{452,4},{453,5},{454,6},{455,7},{4... | collective-permute-start | bytes 122888 | tf_op jit(solution)/shard_map/ppermute | solution.py:640
  61.7 11.4 %collective-permute-start.12 = (f32[16,512]{1,0:T(8,128)S(1)}, f32[16,512]{1,0:T(8,128)S(1)}, u32[]{:S(2)}, u32[]{:S(2)}) collective-permute-start(f32[16,512]{1,0:T(8,128)S(1)} %shard_map.55.own.second), channel_id=1, source_target_pairs={{80,0},{81,1},{82,2},{83,3},{84,4},{85,5},{86,6},{87,7},{88,8},{89... | collective-permute-start | bytes 98312 | tf_op jit(solution)/shard_map/ppermute | solution.py:640
  65.6 7.4 %collective-permute-start.11 = (f32[16,512]{1,0:T(8,128)S(1)}, f32[16,512]{1,0:T(8,128)S(1)}, u32[]{:S(2)}, u32[]{:S(2)}) collective-permute-start(f32[16,512]{1,0:T(8,128)S(1)} %shard_map.55.own.second), channel_id=1, source_target_pairs={{16,0},{17,1},{18,2},{19,3},{20,4},{21,5},{22,6},{23,7},{24,8},{25... | collective-permute-start | bytes 98312 | tf_op jit(solution)/shard_map/ppermute | solution.py:640
  69.5 4.7 %collective-permute-start.10 = (f32[16,512]{1,0:T(8,128)S(1)}, f32[16,512]{1,0:T(8,128)S(1)}, u32[]{:S(2)}, u32[]{:S(2)}) collective-permute-start(f32[16,512]{1,0:T(8,128)S(1)} %shard_map.55.own.second), channel_id=1, source_target_pairs={{64,0},{65,1},{66,2},{67,3},{68,4},{69,5},{70,6},{71,7},{72,8},{73... | collective-permute-start | bytes 98312 | tf_op jit(solution)/shard_map/ppermute | solution.py:640
  76.4 10.9 %collective-permute-start.15 = (f32[16,384]{1,0:T(8,128)S(1)}, f32[16,384]{1,0:T(8,128)S(1)}, u32[]{:S(2)}, u32[]{:S(2)}) collective-permute-start(f32[16,384]{1,0:T(8,128)S(1)} %shard_map.56.own), channel_id=1, source_target_pairs={{496,0},{497,1},{498,2},{499,3},{500,4},{501,5},{502,6},{503,7},{5... | collective-permute-start | bytes 73736 | tf_op jit(solution)/shard_map/ppermute | solution.py:640
  79.1 8.2 %collective-permute-start.14 = (f32[16,384]{1,0:T(8,128)S(1)}, f32[16,384]{1,0:T(8,128)S(1)}, u32[]{:S(2)}, u32[]{:S(2)}) collective-permute-start(f32[16,384]{1,0:T(8,128)S(1)} %shard_map.56.own), channel_id=1, source_target_pairs={{48,0},{49,1},{50,2},{51,3},{52,4},{53,5},{54,6},{55,7},{56,8},{57... | collective-permute-start | bytes 73736 | tf_op jit(solution)/shard_map/ppermute | solution.py:640
  84.0 6.1 %collective-permute-start.13 = (f32[16,384]{1,0:T(8,128)S(1)}, f32[16,384]{1,0:T(8,128)S(1)}, u32[]{:S(2)}, u32[]{:S(2)}) collective-permute-start(f32[16,384]{1,0:T(8,128)S(1)} %shard_map.56.own), channel_id=1, source_target_pairs={{448,0},{449,1},{450,2},{451,3},{452,4},{453,5},{454,6},{455,7},{4... | collective-permute-start | bytes 73736 | tf_op jit(solution)/shard_map/ppermute | solution.py:640

commit v7 on v6

--- a/solution.py
+++ b/solution.py
@@ -464,30 +464,39 @@
     return lax.rem(lax.axis_index("gz"), 2) == 0
 
 
-def spread_kernel(matrix, from_y, from_xy, from_x, start, to_first, to_second):
+def spread_second_kernel(matrix, from_y, from_xy, from_x, start, out):
     even = is_even()
     for q, (ref, row) in enumerate(far_columns(matrix, from_x, from_y, from_xy)):
         up, down = ref[row + 16 : row + 64], ref[row : row + 48]
-        to_first[q * 48 : q * 48 + 48] = jnp.where(even, up, down)
-        to_second[q * 48 : q * 48 + 48] = jnp.where(even, down, up)
+        out[q * 48 : q * 48 + 48] = jnp.where(even, down, up)
     bricks = [pack_bricks(start[...])] + [ref[64:72] for ref in (from_y, from_x, from_xy)]
     for q, brick in enumerate(bricks):
-        to_first[192 + q * 8 : 200 + q * 8] = brick
-        to_second[192 + q * 8 : 200 + q * 8] = brick
-
-
-def spread_near_kernel(matrix, to_first, to_second):
+        out[192 + q * 8 : 200 + q * 8] = brick
+
+
+def spread_first_kernel(from_y, from_xy, from_x, out):
     even = is_even()
-    for q in range(3):
-        up, down = matrix[q * 64 + 32 : q * 64 + 64], matrix[q * 64 : q * 64 + 32]
-        to_first[q * 32 : q * 32 + 32] = jnp.where(even, up, down)
-        to_second[q * 32 : q * 32 + 32] = jnp.where(even, down, up)
-
-
-def join_wide_kernel(matrix, from_y, from_xy, from_x, first, wide, places):
+    for q, ref in enumerate((from_y, from_x, from_xy)):
+        out[q * 48 : q * 48 + 48] = jnp.where(even, ref[16:64], ref[0:48])
+        out[144 + q * 8 : 152 + q * 8] = ref[64:72]
+
+
+def spread_own_kernel(matrix, start, to_first, to_second):
+    even = is_even()
+    for q in range(4):
+        rows = 32 if q < 3 else 48
+        up = matrix[q * 64 + 64 - rows : q * 64 + 64]
+        down = matrix[q * 64 : q * 64 + rows]
+        to_first[q * 32 : q * 32 + rows] = jnp.where(even, up, down)
+        if q < 3:
+            to_second[q * 32 : q * 32 + rows] = jnp.where(even, down, up)
+    to_first[144:152] = pack_bricks(start[...])
+
+
+def join_wide_kernel(matrix, from_y, from_xy, from_x, first, own_first, wide, places):
     even = is_even()
     for q, (ref, row) in enumerate(far_columns(matrix, from_x, from_y, from_xy)):
-        other = first[q * 48 : q * 48 + 48]
+        other = first[q * 48 - 48 : q * 48] if q else own_first[96:144]
         wide[q * 96 : q * 96 + 48] = jnp.where(even, ref[row + 16 : row + 64], other)
         wide[q * 96 + 48 : q * 96 + 96] = jnp.where(even, other, ref[row : row + 48])
     low, _ = first_spans(even)
@@ -514,15 +523,15 @@
     find_places(slim, range(16), atom, bricks_place, places)
 
 
-def join_near_kernel(matrix, first, second, near_first, near_second, tall, places):
+def join_near_kernel(matrix, second, own_first, near_second, tall, places):
     even = is_even()
     for q in range(4):
         if q < 3:
-            one, two = (ref[q * 32 : q * 32 + 32] for ref in (near_first, near_second))
+            one, two = (ref[q * 32 : q * 32 + 32] for ref in (own_first, near_second))
             low, high = jnp.where(even, two, one), jnp.where(even, one, two)
         else:
-            low = jnp.where(even, second[16:48], first[16:48])
-            high = jnp.where(even, first[0:32], second[0:32])
+            low = jnp.where(even, second[16:48], own_first[112:144])
+            high = jnp.where(even, own_first[96:128], second[0:32])
         tall[q * 128 : q * 128 + 32] = low
         tall[q * 128 + 32 : q * 128 + 96] = matrix[q * 64 : q * 64 + 64]
         tall[q * 128 + 96 : q * 128 + 128] = high
@@ -543,25 +552,26 @@
 WIDE_FLOPS = 1 << 28
 
 
-def first_tiles(rows, places, start, from_y, from_xy, from_x, side, field, gathered):
+def first_tiles(rows, places, start, from_y, from_xy, from_x, bricks, field, gathered):
     pieces = [start[...]] + [unpack_bricks(ref[64:72]) for ref in (from_y, from_x, from_xy)]
-    pieces += [unpack_bricks(side[192 + q * 8 : 200 + q * 8]) for q in range(4)]
-    set_tiles(field, pieces)
+    set_tiles(field, pieces + [unpack_bricks(brick) for brick in bricks])
     return couple(rows, range(rows.shape[0] // SLOT_ROWS), field, places, gathered)
 
 
 def first_wide_kernel(
-    wide, places, start, from_y, from_xy, from_x, first, out, field, gathered
+    wide, places, start, from_y, from_xy, from_x, first, own_first, out, field, gathered
 ):
-    out[...] = first_tiles(wide, places, start, from_y, from_xy, from_x, first, field, gathered)
+    bricks = [own_first[144:152]] + [first[144 + q * 8 : 152 + q * 8] for q in range(3)]
+    out[...] = first_tiles(wide, places, start, from_y, from_xy, from_x, bricks, field, gathered)
 
 
 def first_slim_kernel(
     slim, places, start, from_y, from_xy, from_x, second, before, out, field, gathered
 ):
+    bricks = [second[192 + q * 8 : 200 + q * 8] for q in range(4)]
     out[:, 0 : 3 * LANES] = before[...]
     out[:, 3 * LANES : 5 * LANES] = first_tiles(
-        slim, places, start, from_y, from_xy, from_x, second, field, gathered
+        slim, places, start, from_y, from_xy, from_x, bricks, field, gathered
     )
 
 
@@ -669,30 +679,34 @@
     )
     from_x, from_y, from_xy = fetch_three(*out, 1)
     sides = from_y, from_xy, from_x
-    layers = swap_layers(*call(spread_kernel, [(224, WIDE)] * 2, matrix, *sides, start))
-    near_layers = swap_layers(*call(spread_near_kernel, [(96, WIDE)] * 2, matrix))
+    (to_second,) = call(spread_second_kernel, [(224, WIDE)], matrix, *sides, start)
+    (to_first,) = call(spread_first_kernel, [(168, WIDE)], *sides)
+    first_layers, second_layers = swap_layers(to_first, to_second)
+    own_layers, near_layers = swap_layers(
+        *call(spread_own_kernel, [(152, WIDE), (96, WIDE)], matrix, start)
+    )
     wide, wide_places = call(
-        join_wide_kernel, [(24 * SLOT_ROWS, WIDE), whole_numbers(24)], matrix, *sides, layers[0]
+        join_wide_kernel, [(24 * SLOT_ROWS, WIDE), whole_numbers(24)],
+        matrix, *sides, first_layers, own_layers,
     )
     (first,) = call(
         first_wide_kernel, [(SLOT_ROWS, 3 * LANES)],
-        wide, wide_places, start, *sides, layers[0],
+        wide, wide_places, start, *sides, first_layers, own_layers,
         scratch=scratch_for(16, 3),
         flops=WIDE_FLOPS,
     )
-    first, last_layers = lax.optimization_barrier((first, layers[1]))
-    layers = layers[0], last_layers
+    first, second_layers = lax.optimization_barrier((first, second_layers))
     slim, slim_places = call(
-        join_slim_kernel, [(16 * SLOT_ROWS, WIDE), whole_numbers(16)], matrix, *sides, layers[1]
+        join_slim_kernel, [(16 * SLOT_ROWS, WIDE), whole_numbers(16)], matrix, *sides, second_layers
     )
     (first,) = call(
         first_slim_kernel, [(SLOT_ROWS, 5 * LANES)],
-        slim, slim_places, start, *sides, layers[1], first,
+        slim, slim_places, start, *sides, second_layers, first,
         scratch=scratch_for(16, 2),
     )
     tall, places = call(
         join_near_kernel, [(32 * SLOT_ROWS, WIDE), whole_numbers(32)],
-        matrix, *layers, *near_layers,
+        matrix, second_layers, own_layers, near_layers,
     )
     pieces = fetch_three(first, first, first, -1)
     (second,) = call(

time: 131 us -> 129 us (0.985)
  waiting for transfers between devices: 13 us -> 10.2 us
  blocking collectives: 36.4 us -> 38.4 us
  starting transfers between devices: 66.1 us -> 64.7 us
    ppermute x2, starting transfers between devices: 8.34 us -> 4.73 us  [swap_layers(): lax.ppermute(to_first, 'gz', even)]
    ppermute x2, starting transfers between devices: 4.91 us -> 7.41 us  [swap_layers(): lax.ppermute(to_second, 'gz', odd)]
    ppermute x2, waiting for transfers between devices: 2.82 us -> 0.65 us  [swap_layers(): lax.ppermute(to_second, 'gz', odd)]
    all_to_all x1, blocking collectives: 17 us -> 18.8 us  [body(): message = lax.all_to_all(message, 'gz', 0, 0, tiled=True)]
    pallas_call x15 -> x16, Pallas kernels: 14.4 us -> 14.5 us  [call(): pl.pallas_call(kernel, out_shape=shapes, in_specs=[SMEM if operand.dtype...]
  transfers between devices with their start and end apart: 16 -> 16, of which waited for: 7 -> 6; matrix products, arithmetic and copies ran while one was open for 0% -> 0% of each run, Pallas kernels for 4% -> 4%
where the time goes in v7:
time: 129 us; the launch traced here: 128 us
  starting transfers between devices  64.7 us (50%)
  blocking collectives  38.4 us (30%)
  Pallas kernels  14.5 us (11%)
  waiting for transfers between devices  10.2 us (8%)
    ppermute x12, starting transfers between devices, fetch(): return lax.ppermute(value, AXES, pairs)  52.5 us
    all_to_all x1, blocking collectives, body(): message = lax.all_to_all(message, ('gx', 'gy'), 0, 0, tiled=True)  19.6 us
    all_to_all x1, blocking collectives, body(): message = lax.all_to_all(message, 'gz', 0, 0, tiled=True)  18.8 us
    pallas_call x16, Pallas kernels, call(): pl.pallas_call(kernel, out_shape=shapes, in_specs=[SMEM if operand.dtype...  14.5 us
    ppermute x12, waiting for transfers between devices, fetch(): return lax.ppermute(value, AXES, pairs)  9.59 us
    ppermute x2, starting transfers between devices, swap_layers(): lax.ppermute(to_second, 'gz', odd)  7.41 us
    ppermute x2, starting transfers between devices, swap_layers(): lax.ppermute(to_first, 'gz', even)  4.73 us
  transfers between devices with their start and end apart: 16, of which 6 were waited for; matrix products, arithmetic and copies ran while one was open for 0% of the time, Pallas kernels for 4%

profile of v7, /device:TPU:1, one launch (start us, length us, event | category | flops | bytes accessed | tf_op | source)
XLA Modules:
  0.0 128.0 jit_solution(6228117567408897749)
XLA Ops:
  1.2 11.5 %collective-permute-start = (f32[72,512]{1,0:T(8,128)S(1)}, f32[72,512]{1,0:T(8,128)S(1)}, u32[]{:S(2)}, u32[]{:S(2)}) collective-permute-start(f32[72,512]{1,0:T(8,128)S(1)} %get-tuple-element.28), channel_id=1, source_target_pairs={{16,0},{17,1},{18,2},{19,3},{20,4},{21,5},{22,6},{23,7},{24,8},{25... | collective-permute-start | bytes 442376 | tf_op jit(solution)/shard_map/ppermute | solution.py:650
  12.7 5.1 %collective-permute-start.1 = (f32[72,512]{1,0:T(8,128)S(1)}, f32[72,512]{1,0:T(8,128)S(1)}, u32[]{:S(2)}, u32[]{:S(2)}) collective-permute-start(f32[72,512]{1,0:T(8,128)S(1)} %get-tuple-element.29), channel_id=1, source_target_pairs={{80,0},{81,1},{82,2},{83,3},{84,4},{85,5},{86,6},{87,7},{88,8},{89... | collective-permute-start | bytes 442376 | tf_op jit(solution)/shard_map/ppermute | solution.py:650
  17.8 3.0 %collective-permute-start.2 = (f32[72,512]{1,0:T(8,128)S(1)}, f32[72,512]{1,0:T(8,128)S(1)}, u32[]{:S(2)}, u32[]{:S(2)}) collective-permute-start(f32[72,512]{1,0:T(8,128)S(1)} %get-tuple-element.30), channel_id=1, source_target_pairs={{64,0},{65,1},{66,2},{67,3},{68,4},{69,5},{70,6},{71,7},{72,8},{73... | collective-permute-start | bytes 442376 | tf_op jit(solution)/shard_map/ppermute | solution.py:650
  20.8 3.3 %collective-permute-done.from_y = f32[72,512]{1,0:T(8,128)S(1)} collective-permute-done((f32[72,512]{1,0:T(8,128)S(1)}, f32[72,512]{1,0:T(8,128)S(1)}, u32[]{:S(2)}, u32[]{:S(2)}) %collective-permute-start) | collective-permute-done | bytes 147488 | tf_op jit(solution)/shard_map/ppermute | solution.py:650
  24.5 4.8 %collective-permute-start.5 = (f32[224,512]{1,0:T(8,128)S(1)}, f32[224,512]{1,0:T(8,128)S(1)}, u32[]{:S(2)}, u32[]{:S(2)}) collective-permute-start(f32[224,512]{1,0:T(8,128)S(1)} %shard_map.51), channel_id=1, source_target_pairs={{0,15},{1,2},{2,1},{3,4},{4,3},{5,6},{6,5},{7,8},{8,7},{9,10},{10,... | collective-permute-start | bytes 1376264 | tf_op jit(solution)/shard_map/ppermute | solution.py:661
  29.4 2.8 %collective-permute-start.3 = (f32[168,512]{1,0:T(8,128)S(1)}, f32[168,512]{1,0:T(8,128)S(1)}, u32[]{:S(2)}, u32[]{:S(2)}) collective-permute-start(f32[168,512]{1,0:T(8,128)S(1)} %shard_map.47), channel_id=1, source_target_pairs={{0,1},{1,0},{2,3},{3,2},{4,5},{5,4},{6,7},{7,6},{8,9},{9,8},{10,11... | collective-permute-start | bytes 1032200 | tf_op jit(solution)/shard_map/ppermute | solution.py:661
  34.2 2.6 %collective-permute-start.6 = (f32[96,512]{1,0:T(8,128)S(1)}, f32[96,512]{1,0:T(8,128)S(1)}, u32[]{:S(2)}, u32[]{:S(2)}) collective-permute-start(f32[96,512]{1,0:T(8,128)S(1)} %get-tuple-element.40), channel_id=1, source_target_pairs={{0,15},{1,2},{2,1},{3,4},{4,3},{5,6},{6,5},{7,8},{8,7},{9,10},{10,... | collective-permute-start | bytes 589832 | tf_op jit(solution)/shard_map/ppermute | solution.py:661
  36.9 2.2 %shard_map.50.before = f32[16,384]{1,0:T(8,128)S(1)} custom-call(f32[384,512]{1,0:T(8,128)S(1)} %get-tuple-element.33.wide, s32[24,128]{1,0:T(8,128)S(1)} %get-tuple-element.34.places, f32[16,256]{1,0:T(8,128)S(1)} %get-tuple-element.31.start.refs_0_, f32[72,512]{1,0:T(8,128)S(1)} %collective-permute-done.from_y, ...), custom_call_target="tpu_custom_call" | custom-call | flops 268435456 | bytes 4194304 | tf_op jit(solution)/shard_map/pallas_call | solution.py:620
  41.7 3.2 %collective-permute-start.9 = (f32[16,640]{1,0:T(8,128)S(1)}, f32[16,640]{1,0:T(8,128)S(1)}, u32[]{:S(2)}, u32[]{:S(2)}) collective-permute-start(f32[16,640]{1,0:T(8,128)S(1)} %shard_map.55.own), channel_id=1, source_target_pairs={{496,0},{497,1},{498,2},{499,3},{500,4},{501,5},{502,6},{503,7},{5... | collective-permute-start | bytes 122888 | tf_op jit(solution)/shard_map/ppermute | solution.py:650
  45.0 4.3 %collective-permute-start.8 = (f32[16,640]{1,0:T(8,128)S(1)}, f32[16,640]{1,0:T(8,128)S(1)}, u32[]{:S(2)}, u32[]{:S(2)}) collective-permute-start(f32[16,640]{1,0:T(8,128)S(1)} %shard_map.55.own), channel_id=1, source_target_pairs={{48,0},{49,1},{50,2},{51,3},{52,4},{53,5},{54,6},{55,7},{56,8},{57... | collective-permute-start | bytes 122888 | tf_op jit(solution)/shard_map/ppermute | solution.py:650
  49.2 3.2 %collective-permute-start.7 = (f32[16,640]{1,0:T(8,128)S(1)}, f32[16,640]{1,0:T(8,128)S(1)}, u32[]{:S(2)}, u32[]{:S(2)}) collective-permute-start(f32[16,640]{1,0:T(8,128)S(1)} %shard_map.55.own), channel_id=1, source_target_pairs={{448,0},{449,1},{450,2},{451,3},{452,4},{453,5},{454,6},{455,7},{4... | collective-permute-start | bytes 122888 | tf_op jit(solution)/shard_map/ppermute | solution.py:650
  52.7 2.8 %collective-permute-done.7.from_x = f32[16,640]{1,0:T(8,128)S(1)} collective-permute-done((f32[16,640]{1,0:T(8,128)S(1)}, f32[16,640]{1,0:T(8,128)S(1)}, u32[]{:S(2)}, u32[]{:S(2)}) %collective-permute-start.7) | collective-permute-done | bytes 40992 | tf_op jit(solution)/shard_map/ppermute | solution.py:650
  55.5 2.6 %shard_map.56.own.second = f32[16,512]{1,0:T(8,128)S(1)} custom-call(f32[512,512]{1,0:T(8,128)S(1)} %get-tuple-element.41.tall, s32[32,128]{1,0:T(8,128)S(1)} %get-tuple-element.42.places, f32[16,640]{1,0:T(8,128)S(1)} %shard_map.55.own, f32[16,640]{1,0:T(8,128)S(1)} %collective-permute-done.7.from_x, f32[16,640]{1,0:T(8,128)S(1)} %collective-permute-done.8.from_y, ...), custom_call_target="tpu_custom_call" | custom-call | tf_op jit(solution)/shard_map/pallas_call | solution.py:620
  58.1 4.3 %collective-permute-start.12 = (f32[16,512]{1,0:T(8,128)S(1)}, f32[16,512]{1,0:T(8,128)S(1)}, u32[]{:S(2)}, u32[]{:S(2)}) collective-permute-start(f32[16,512]{1,0:T(8,128)S(1)} %shard_map.56.own.second), channel_id=1, source_target_pairs={{80,0},{81,1},{82,2},{83,3},{84,4},{85,5},{86,6},{87,7},{88,8},{89... | collective-permute-start | bytes 98312 | tf_op jit(solution)/shard_map/ppermute | solution.py:650
  62.4 3.6 %collective-permute-start.11 = (f32[16,512]{1,0:T(8,128)S(1)}, f32[16,512]{1,0:T(8,128)S(1)}, u32[]{:S(2)}, u32[]{:S(2)}) collective-permute-start(f32[16,512]{1,0:T(8,128)S(1)} %shard_map.56.own.second), channel_id=1, source_target_pairs={{16,0},{17,1},{18,2},{19,3},{20,4},{21,5},{22,6},{23,7},{24,8},{25... | collective-permute-start | bytes 98312 | tf_op jit(solution)/shard_map/ppermute | solution.py:650
  66.1 4.0 %collective-permute-start.10 = (f32[16,512]{1,0:T(8,128)S(1)}, f32[16,512]{1,0:T(8,128)S(1)}, u32[]{:S(2)}, u32[]{:S(2)}) collective-permute-start(f32[16,512]{1,0:T(8,128)S(1)} %shard_map.56.own.second), channel_id=1, source_target_pairs={{64,0},{65,1},{66,2},{67,3},{68,4},{69,5},{70,6},{71,7},{72,8},{73... | collective-permute-start | bytes 98312 | tf_op jit(solution)/shard_map/ppermute | solution.py:650
  71.1 2.2 %shard_map.57.own = f32[16,384]{1,0:T(8,128)S(1)} custom-call(f32[384,512]{1,0:T(8,128)S(1)} %get-tuple-element.38.wide, s32[24,128]{1,0:T(8,128)S(1)} %get-tuple-element.39.places, f32[16,512]{1,0:T(8,128)S(1)} %shard_map.56.own.second, f32[16,512]{1,0:T(8,128)S(1)} %collective-permute-done.10.from_x, f32[16,512]{1,0:T(8,128)S(1)} %collective-permute-done.11.from_y, ...), custom_call_target="tpu_custom_call" | custom-call | tf_op jit(solution)/shard_map/pallas_call | solution.py:620
  73.3 2.2 %collective-permute-start.15 = (f32[16,384]{1,0:T(8,128)S(1)}, f32[16,384]{1,0:T(8,128)S(1)}, u32[]{:S(2)}, u32[]{:S(2)}) collective-permute-start(f32[16,384]{1,0:T(8,128)S(1)} %shard_map.57.own), channel_id=1, source_target_pairs={{496,0},{497,1},{498,2},{499,3},{500,4},{501,5},{502,6},{503,7},{5... | collective-permute-start | bytes 73736 | tf_op jit(solution)/shard_map/ppermute | solution.py:650
  75.5 4.6 %collective-permute-start.14 = (f32[16,384]{1,0:T(8,128)S(1)}, f32[16,384]{1,0:T(8,128)S(1)}, u32[]{:S(2)}, u32[]{:S(2)}) collective-permute-start(f32[16,384]{1,0:T(8,128)S(1)} %shard_map.57.own), channel_id=1, source_target_pairs={{48,0},{49,1},{50,2},{51,3},{52,4},{53,5},{54,6},{55,7},{56,8},{57... | collective-permute-start | bytes 73736 | tf_op jit(solution)/shard_map/ppermute | solution.py:650
  80.1 3.5 %collective-permute-start.13 = (f32[16,384]{1,0:T(8,128)S(1)}, f32[16,384]{1,0:T(8,128)S(1)}, u32[]{:S(2)}, u32[]{:S(2)}) collective-permute-start(f32[16,384]{1,0:T(8,128)S(1)} %shard_map.57.own), channel_id=1, source_target_pairs={{448,0},{449,1},{450,2},{451,3},{452,4},{453,5},{454,6},{455,7},{4... | collective-permute-start | bytes 73736 | tf_op jit(solution)/shard_map/ppermute | solution.py:650
  83.8 2.2 %collective-permute-done.13.from_x = f32[16,384]{1,0:T(8,128)S(1)} collective-permute-done((f32[16,384]{1,0:T(8,128)S(1)}, f32[16,384]{1,0:T(8,128)S(1)}, u32[]{:S(2)}, u32[]{:S(2)}) %collective-permute-start.13) | collective-permute-done | bytes 24608 | tf_op jit(solution)/shard_map/ppermute | solution.py:650
  85.9 2.1 %shard_map.59 = (f32[16,256]{1,0:T(8,128)S(1)}, f32[32,4,128]{2,1,0:T(4,128)S(1)}) custom-call(f32[256,512]{1,0:T(8,128)S(1)} %get-tuple-element.27.matrix, s32[16,128]{1,0:T(8,128)S(1)} %get-tuple-element.37.places, f32[16,384]{1,0:T(8,128)S(1)} %shard_map.57.own, f32[16,384]{1,0:T(8,128)S(1)} %collective-permute-done.13.from_x, ...), custom_call_target="tpu_custom_call" | custom-call | tf_op jit(solution)/shard_map/pallas_call | solution.py:620
  88.1 19.6 %all_to_all.10.ref = f32[32,4,128]{2,1,0:T(4,128)S(1)} all-to-all(f32[32,4,128]{2,1,0:T(4,128)S(1)} %get-tuple-element.47), channel_id=1, replica_groups=mesh['gx'=8,'gy'=4,'gz'=16] {'gx','gy'}, dimensions={0} | all-to-all | bytes 131072 | tf_op jit(solution)/shard_map/all_to_all | solution.py:734
  107.8 18.8 %all_to_all.11.ref = f32[16,4,128]{2,1,0:T(4,128)S(1)} all-to-all(f32[16,4,128]{2,1,0:T(4,128)S(1)} %shard_map.60), channel_id=1, replica_groups=mesh['gx'=8,'gy'=4,'gz'=16] {'gz'}, dimensions={0} | all-to-all | bytes 65536 | tf_op jit(solution)/shard_map/all_to_all | solution.py:736
  (26 shorter events, 9.2 us)
Async XLA Ops:
  1.2 22.9 %collective-permute-start = (f32[72,512]{1,0:T(8,128)S(1)}, f32[72,512]{1,0:T(8,128)S(1)}, u32[]{:S(2)}, u32[]{:S(2)}) collective-permute-start(f32[72,512]{1,0:T(8,128)S(1)} %get-tuple-element.28), channel_id=1, source_target_pairs={{16,0},{17,1},{18,2},{19,3},{20,4},{21,5},{22,6},{23,7},{24,8},{25... | collective-permute-start | bytes 442376 | tf_op jit(solution)/shard_map/ppermute | solution.py:650
  12.7 11.4 %collective-permute-start.1 = (f32[72,512]{1,0:T(8,128)S(1)}, f32[72,512]{1,0:T(8,128)S(1)}, u32[]{:S(2)}, u32[]{:S(2)}) collective-permute-start(f32[72,512]{1,0:T(8,128)S(1)} %get-tuple-element.29), channel_id=1, source_target_pairs={{80,0},{81,1},{82,2},{83,3},{84,4},{85,5},{86,6},{87,7},{88,8},{89... | collective-permute-start | bytes 442376 | tf_op jit(solution)/shard_map/ppermute | solution.py:650
  17.8 6.7 %collective-permute-start.2 = (f32[72,512]{1,0:T(8,128)S(1)}, f32[72,512]{1,0:T(8,128)S(1)}, u32[]{:S(2)}, u32[]{:S(2)}) collective-permute-start(f32[72,512]{1,0:T(8,128)S(1)} %get-tuple-element.30), channel_id=1, source_target_pairs={{64,0},{65,1},{66,2},{67,3},{68,4},{69,5},{70,6},{71,7},{72,8},{73... | collective-permute-start | bytes 442376 | tf_op jit(solution)/shard_map/ppermute | solution.py:650
  24.5 15.3 %collective-permute-start.5 = (f32[224,512]{1,0:T(8,128)S(1)}, f32[224,512]{1,0:T(8,128)S(1)}, u32[]{:S(2)}, u32[]{:S(2)}) collective-permute-start(f32[224,512]{1,0:T(8,128)S(1)} %shard_map.51), channel_id=1, source_target_pairs={{0,15},{1,2},{2,1},{3,4},{4,3},{5,6},{6,5},{7,8},{8,7},{9,10},{10,... | collective-permute-start | bytes 1376264 | tf_op jit(solution)/shard_map/ppermute | solution.py:661
  29.4 7.4 %collective-permute-start.3 = (f32[168,512]{1,0:T(8,128)S(1)}, f32[168,512]{1,0:T(8,128)S(1)}, u32[]{:S(2)}, u32[]{:S(2)}) collective-permute-start(f32[168,512]{1,0:T(8,128)S(1)} %shard_map.47), channel_id=1, source_target_pairs={{0,1},{1,0},{2,3},{3,2},{4,5},{5,4},{6,7},{7,6},{8,9},{9,8},{10,11... | collective-permute-start | bytes 1032200 | tf_op jit(solution)/shard_map/ppermute | solution.py:661
  32.2 4.6 %collective-permute-start.4 = (f32[152,512]{1,0:T(8,128)S(1)}, f32[152,512]{1,0:T(8,128)S(1)}, u32[]{:S(2)}, u32[]{:S(2)}) collective-permute-start(f32[152,512]{1,0:T(8,128)S(1)} %get-tuple-element.32), channel_id=1, source_target_pairs={{0,1},{1,0},{2,3},{3,2},{4,5},{5,4},{6,7},{7,6},{8,9},{9,8},{10,11... | collective-permute-start | bytes 933896 | tf_op jit(solution)/shard_map/ppermute | solution.py:661
  34.2 18.3 %collective-permute-start.6 = (f32[96,512]{1,0:T(8,128)S(1)}, f32[96,512]{1,0:T(8,128)S(1)}, u32[]{:S(2)}, u32[]{:S(2)}) collective-permute-start(f32[96,512]{1,0:T(8,128)S(1)} %get-tuple-element.40), channel_id=1, source_target_pairs={{0,15},{1,2},{2,1},{3,4},{4,3},{5,6},{6,5},{7,8},{8,7},{9,10},{10,... | collective-permute-start | bytes 589832 | tf_op jit(solution)/shard_map/ppermute | solution.py:661
  41.7 10.9 %collective-permute-start.9 = (f32[16,640]{1,0:T(8,128)S(1)}, f32[16,640]{1,0:T(8,128)S(1)}, u32[]{:S(2)}, u32[]{:S(2)}) collective-permute-start(f32[16,640]{1,0:T(8,128)S(1)} %shard_map.55.own), channel_id=1, source_target_pairs={{496,0},{497,1},{498,2},{499,3},{500,4},{501,5},{502,6},{503,7},{5... | collective-permute-start | bytes 122888 | tf_op jit(solution)/shard_map/ppermute | solution.py:650
  45.0 7.7 %collective-permute-start.8 = (f32[16,640]{1,0:T(8,128)S(1)}, f32[16,640]{1,0:T(8,128)S(1)}, u32[]{:S(2)}, u32[]{:S(2)}) collective-permute-start(f32[16,640]{1,0:T(8,128)S(1)} %shard_map.55.own), channel_id=1, source_target_pairs={{48,0},{49,1},{50,2},{51,3},{52,4},{53,5},{54,6},{55,7},{56,8},{57... | collective-permute-start | bytes 122888 | tf_op jit(solution)/shard_map/ppermute | solution.py:650
  49.2 6.3 %collective-permute-start.7 = (f32[16,640]{1,0:T(8,128)S(1)}, f32[16,640]{1,0:T(8,128)S(1)}, u32[]{:S(2)}, u32[]{:S(2)}) collective-permute-start(f32[16,640]{1,0:T(8,128)S(1)} %shard_map.55.own), channel_id=1, source_target_pairs={{448,0},{449,1},{450,2},{451,3},{452,4},{453,5},{454,6},{455,7},{4... | collective-permute-start | bytes 122888 | tf_op jit(solution)/shard_map/ppermute | solution.py:650
  58.1 12.1 %collective-permute-start.12 = (f32[16,512]{1,0:T(8,128)S(1)}, f32[16,512]{1,0:T(8,128)S(1)}, u32[]{:S(2)}, u32[]{:S(2)}) collective-permute-start(f32[16,512]{1,0:T(8,128)S(1)} %shard_map.56.own.second), channel_id=1, source_target_pairs={{80,0},{81,1},{82,2},{83,3},{84,4},{85,5},{86,6},{87,7},{88,8},{89... | collective-permute-start | bytes 98312 | tf_op jit(solution)/shard_map/ppermute | solution.py:650
  62.4 7.8 %collective-permute-start.11 = (f32[16,512]{1,0:T(8,128)S(1)}, f32[16,512]{1,0:T(8,128)S(1)}, u32[]{:S(2)}, u32[]{:S(2)}) collective-permute-start(f32[16,512]{1,0:T(8,128)S(1)} %shard_map.56.own.second), channel_id=1, source_target_pairs={{16,0},{17,1},{18,2},{19,3},{20,4},{21,5},{22,6},{23,7},{24,8},{25... | collective-permute-start | bytes 98312 | tf_op jit(solution)/shard_map/ppermute | solution.py:650
  66.1 5.0 %collective-permute-start.10 = (f32[16,512]{1,0:T(8,128)S(1)}, f32[16,512]{1,0:T(8,128)S(1)}, u32[]{:S(2)}, u32[]{:S(2)}) collective-permute-start(f32[16,512]{1,0:T(8,128)S(1)} %shard_map.56.own.second), channel_id=1, source_target_pairs={{64,0},{65,1},{66,2},{67,3},{68,4},{69,5},{70,6},{71,7},{72,8},{73... | collective-permute-start | bytes 98312 | tf_op jit(solution)/shard_map/ppermute | solution.py:650
  73.3 10.5 %collective-permute-start.15 = (f32[16,384]{1,0:T(8,128)S(1)}, f32[16,384]{1,0:T(8,128)S(1)}, u32[]{:S(2)}, u32[]{:S(2)}) collective-permute-start(f32[16,384]{1,0:T(8,128)S(1)} %shard_map.57.own), channel_id=1, source_target_pairs={{496,0},{497,1},{498,2},{499,3},{500,4},{501,5},{502,6},{503,7},{5... | collective-permute-start | bytes 73736 | tf_op jit(solution)/shard_map/ppermute | solution.py:650
  75.5 8.3 %collective-permute-start.14 = (f32[16,384]{1,0:T(8,128)S(1)}, f32[16,384]{1,0:T(8,128)S(1)}, u32[]{:S(2)}, u32[]{:S(2)}) collective-permute-start(f32[16,384]{1,0:T(8,128)S(1)} %shard_map.57.own), channel_id=1, source_target_pairs={{48,0},{49,1},{50,2},{51,3},{52,4},{53,5},{54,6},{55,7},{56,8},{57... | collective-permute-start | bytes 73736 | tf_op jit(solution)/shard_map/ppermute | solution.py:650
  80.1 5.8 %collective-permute-start.13 = (f32[16,384]{1,0:T(8,128)S(1)}, f32[16,384]{1,0:T(8,128)S(1)}, u32[]{:S(2)}, u32[]{:S(2)}) collective-permute-start(f32[16,384]{1,0:T(8,128)S(1)} %shard_map.57.own), channel_id=1, source_target_pairs={{448,0},{449,1},{450,2},{451,3},{452,4},{453,5},{454,6},{455,7},{4... | collective-permute-start | bytes 73736 | tf_op jit(solution)/shard_map/ppermute | solution.py:650

commit v8 on v7

--- a/solution.py
+++ b/solution.py
@@ -464,14 +464,17 @@
     return lax.rem(lax.axis_index("gz"), 2) == 0
 
 
-def spread_second_kernel(matrix, from_y, from_xy, from_x, start, out):
+def spread_early_kernel(matrix, out):
+    out[...] = jnp.where(is_even(), matrix[192:240], matrix[208:256])
+
+
+def spread_second_kernel(from_y, from_xy, from_x, start, out):
     even = is_even()
-    for q, (ref, row) in enumerate(far_columns(matrix, from_x, from_y, from_xy)):
-        up, down = ref[row + 16 : row + 64], ref[row : row + 48]
-        out[q * 48 : q * 48 + 48] = jnp.where(even, down, up)
+    for q, ref in enumerate((from_y, from_x, from_xy)):
+        out[q * 48 : q * 48 + 48] = jnp.where(even, ref[0:48], ref[16:64])
     bricks = [pack_bricks(start[...])] + [ref[64:72] for ref in (from_y, from_x, from_xy)]
     for q, brick in enumerate(bricks):
-        out[192 + q * 8 : 200 + q * 8] = brick
+        out[144 + q * 8 : 152 + q * 8] = brick
 
 
 def spread_first_kernel(from_y, from_xy, from_x, out):
@@ -508,10 +511,10 @@
     find_places(wide, range(24), atom, bricks_place, places)
 
 
-def join_slim_kernel(matrix, from_y, from_xy, from_x, second, slim, places):
+def join_slim_kernel(matrix, from_y, from_xy, from_x, second, early, slim, places):
     even = is_even()
     for q, (ref, row) in enumerate(far_columns(matrix, from_x, from_y, from_xy)):
-        other = second[q * 48 : q * 48 + 48]
+        other = second[q * 48 - 48 : q * 48] if q else early[...]
         below = jnp.concatenate([other, ref[row : row + 16]], axis=0)
         above = jnp.concatenate([ref[row + 48 : row + 64], other], axis=0)
         slim[q * 64 : q * 64 + 64] = jnp.where(even, below, above)
@@ -523,15 +526,15 @@
     find_places(slim, range(16), atom, bricks_place, places)
 
 
-def join_near_kernel(matrix, second, own_first, near_second, tall, places):
+def join_near_kernel(matrix, early, own_first, near_second, tall, places):
     even = is_even()
     for q in range(4):
         if q < 3:
             one, two = (ref[q * 32 : q * 32 + 32] for ref in (own_first, near_second))
             low, high = jnp.where(even, two, one), jnp.where(even, one, two)
         else:
-            low = jnp.where(even, second[16:48], own_first[112:144])
-            high = jnp.where(even, own_first[96:128], second[0:32])
+            low = jnp.where(even, early[16:48], own_first[112:144])
+            high = jnp.where(even, own_first[96:128], early[0:32])
         tall[q * 128 : q * 128 + 32] = low
         tall[q * 128 + 32 : q * 128 + 96] = matrix[q * 64 : q * 64 + 64]
         tall[q * 128 + 96 : q * 128 + 128] = high
@@ -549,9 +552,6 @@
     find_places(matrix, range(ATOMS), near_atom, THIRD_PLACE, fourth_places)
 
 
-WIDE_FLOPS = 1 << 28
-
-
 def first_tiles(rows, places, start, from_y, from_xy, from_x, bricks, field, gathered):
     pieces = [start[...]] + [unpack_bricks(ref[64:72]) for ref in (from_y, from_x, from_xy)]
     set_tiles(field, pieces + [unpack_bricks(brick) for brick in bricks])
@@ -568,7 +568,7 @@
 def first_slim_kernel(
     slim, places, start, from_y, from_xy, from_x, second, before, out, field, gathered
 ):
-    bricks = [second[192 + q * 8 : 200 + q * 8] for q in range(4)]
+    bricks = [second[144 + q * 8 : 152 + q * 8] for q in range(4)]
     out[:, 0 : 3 * LANES] = before[...]
     out[:, 3 * LANES : 5 * LANES] = first_tiles(
         slim, places, start, from_y, from_xy, from_x, bricks, field, gathered
@@ -612,7 +612,7 @@
     return jax.ShapeDtypeStruct((rows, LANES), jnp.int32)
 
 
-def call(kernel, shapes, *operands, scratch=(), place=VMEM, flops=0):
+def call(kernel, shapes, *operands, scratch=(), place=VMEM):
     shapes = [
         shape if isinstance(shape, jax.ShapeDtypeStruct) else jax.ShapeDtypeStruct(shape, jnp.float32)
         for shape in shapes
@@ -625,9 +625,6 @@
         ],
         out_specs=[VMEM] * len(shapes),
         scratch_shapes=list(scratch),
-        cost_estimate=pl.CostEstimate(flops=flops, bytes_accessed=flops // 64, transcendentals=0)
-        if flops
-        else None,
         compiler_params=pltpu.CompilerParams(vmem_limit_bytes=24 * 1024 * 1024),
     )(*operands)
 
@@ -655,10 +652,15 @@
 
 
 def swap_layers(to_first, to_second):
+    even = [(i, i ^ 1) for i in range(lax.axis_size("gz"))]
+    return lax.ppermute(to_first, "gz", even), swap_odd(to_second)
+
+
+def swap_odd(value):
     count = lax.axis_size("gz")
-    even = [(i, i ^ 1) for i in range(count)]
-    odd = [(i, (i + 1 if i % 2 else i - 1) % count) for i in range(count)]
-    return lax.ppermute(to_first, "gz", even), lax.ppermute(to_second, "gz", odd)
+    return lax.ppermute(
+        value, "gz", [(i, (i + 1 if i % 2 else i - 1) % count) for i in range(count)]
+    )
 
 
 def body(rhs, diagonal, blocks, neighbours):
@@ -678,8 +680,9 @@
         place=pl.BlockSpec(memory_space=pltpu.HBM),
     )
     from_x, from_y, from_xy = fetch_three(*out, 1)
-    sides = from_y, from_xy, from_x
-    (to_second,) = call(spread_second_kernel, [(224, WIDE)], matrix, *sides, start)
+    early = swap_odd(*call(spread_early_kernel, [(48, WIDE)], matrix))
+    *sides, early = lax.optimization_barrier((from_y, from_xy, from_x, early))
+    (to_second,) = call(spread_second_kernel, [(176, WIDE)], *sides, start)
     (to_first,) = call(spread_first_kernel, [(168, WIDE)], *sides)
     first_layers, second_layers = swap_layers(to_first, to_second)
     own_layers, near_layers = swap_layers(
@@ -693,11 +696,10 @@
         first_wide_kernel, [(SLOT_ROWS, 3 * LANES)],
         wide, wide_places, start, *sides, first_layers, own_layers,
         scratch=scratch_for(16, 3),
-        flops=WIDE_FLOPS,
     )
     first, second_layers = lax.optimization_barrier((first, second_layers))
     slim, slim_places = call(
-        join_slim_kernel, [(16 * SLOT_ROWS, WIDE), whole_numbers(16)], matrix, *sides, second_layers
+        join_slim_kernel, [(16 * SLOT_ROWS, WIDE), whole_numbers(16)], matrix, *sides, second_layers, early
     )
     (first,) = call(
         first_slim_kernel, [(SLOT_ROWS, 5 * LANES)],
@@ -706,7 +708,7 @@
     )
     tall, places = call(
         join_near_kernel, [(32 * SLOT_ROWS, WIDE), whole_numbers(32)],
-        matrix, second_layers, own_layers, near_layers,
+        matrix, early, own_layers, near_layers,
     )
     pieces = fetch_three(first, first, first, -1)
     (second,) = call(

time: 129 us -> 129 us (level)
  waiting for transfers between devices: 10.2 us -> 11.5 us
  blocking collectives: 38.4 us -> 37.1 us
    ppermute x12, starting transfers between devices: 52.5 us -> 47.6 us  [fetch(): return lax.ppermute(value, AXES, pairs)]
    ppermute x4 -> x5, starting transfers between devices: 12.1 us -> 17 us  [the longest x3 9.89 us: swap_odd(): lax.ppermute(value, 'gz', [(i, (i + 1 if i % 2 else i - 1) % count) for i...]
    ppermute x4 -> x5, waiting for transfers between devices: 0.66 us -> 2.47 us  [the longest x3 2.47 us: swap_odd(): lax.ppermute(value, 'gz', [(i, (i + 1 if i % 2 else i - 1) % count) for i...]
    pallas_call x16 -> x17, Pallas kernels: 14.5 us -> 14.5 us  [call(): pl.pallas_call(kernel, out_shape=shapes, in_specs=[SMEM if operand.dtype...]
  transfers between devices with their start and end apart: 16 -> 17, of which waited for: 6 -> 7; matrix products, arithmetic and copies ran while one was open for 0% -> 0% of each run, Pallas kernels for 4% -> 4%
where the time goes in v8:
time: 129 us; the launch traced here: 128 us
  starting transfers between devices  64.7 us (50%)
  blocking collectives  37.1 us (29%)
  Pallas kernels  14.5 us (11%)
  waiting for transfers between devices  11.5 us (9%)
    ppermute x12, starting transfers between devices, fetch(): return lax.ppermute(value, AXES, pairs)  47.6 us
    all_to_all x1, blocking collectives, body(): message = lax.all_to_all(message, ('gx', 'gy'), 0, 0, tiled=True)  18.7 us
    all_to_all x1, blocking collectives, body(): message = lax.all_to_all(message, 'gz', 0, 0, tiled=True)  18.4 us
    pallas_call x17, Pallas kernels, call(): pl.pallas_call(kernel, out_shape=shapes, in_specs=[SMEM if operand.dtype...  14.5 us
    ppermute x3, starting transfers between devices, swap_odd(): lax.ppermute(value, 'gz', [(i, (i + 1 if i % 2 else i - 1) % count) for i...  9.89 us
    ppermute x12, waiting for transfers between devices, fetch(): return lax.ppermute(value, AXES, pairs)  8.98 us
    ppermute x2, starting transfers between devices, swap_layers(): return (lax.ppermute(to_first, 'gz', even), swap_odd(to_second))  7.13 us
  transfers between devices with their start and end apart: 17, of which 7 were waited for; matrix products, arithmetic and copies ran while one was open for 0% of the time, Pallas kernels for 4%

profile of v8, /device:TPU:1, one launch (start us, length us, event | category | flops | bytes accessed | tf_op | source)
XLA Modules:
  0.0 128.0 jit_solution(7879604318844519046)
XLA Ops:
  1.2 11.5 %collective-permute-start = (f32[72,512]{1,0:T(8,128)S(1)}, f32[72,512]{1,0:T(8,128)S(1)}, u32[]{:S(2)}, u32[]{:S(2)}) collective-permute-start(f32[72,512]{1,0:T(8,128)S(1)} %get-tuple-element.32), channel_id=1, source_target_pairs={{16,0},{17,1},{18,2},{19,3},{20,4},{21,5},{22,6},{23,7},{24,8},{25... | collective-permute-start | bytes 442376 | tf_op jit(solution)/shard_map/ppermute | solution.py:647
  12.7 5.1 %collective-permute-start.1 = (f32[72,512]{1,0:T(8,128)S(1)}, f32[72,512]{1,0:T(8,128)S(1)}, u32[]{:S(2)}, u32[]{:S(2)}) collective-permute-start(f32[72,512]{1,0:T(8,128)S(1)} %get-tuple-element.33), channel_id=1, source_target_pairs={{80,0},{81,1},{82,2},{83,3},{84,4},{85,5},{86,6},{87,7},{88,8},{89... | collective-permute-start | bytes 442376 | tf_op jit(solution)/shard_map/ppermute | solution.py:647
  17.8 3.0 %collective-permute-start.2 = (f32[72,512]{1,0:T(8,128)S(1)}, f32[72,512]{1,0:T(8,128)S(1)}, u32[]{:S(2)}, u32[]{:S(2)}) collective-permute-start(f32[72,512]{1,0:T(8,128)S(1)} %get-tuple-element.34), channel_id=1, source_target_pairs={{64,0},{65,1},{66,2},{67,3},{68,4},{69,5},{70,6},{71,7},{72,8},{73... | collective-permute-start | bytes 442376 | tf_op jit(solution)/shard_map/ppermute | solution.py:647
  20.8 4.5 %collective-permute-start.3 = (f32[48,512]{1,0:T(8,128)S(1)}, f32[48,512]{1,0:T(8,128)S(1)}, u32[]{:S(2)}, u32[]{:S(2)}) collective-permute-start(f32[48,512]{1,0:T(8,128)S(1)} %shard_map.47), channel_id=1, source_target_pairs={{0,15},{1,2},{2,1},{3,4},{4,3},{5,6},{6,5},{7,8},{8,7},{9,10},{10,... | collective-permute-start | bytes 294920 | tf_op jit(solution)/shard_map/ppermute | solution.py:661
  25.3 2.5 %collective-permute-done.3.early = f32[48,512]{1,0:T(8,128)S(1)} collective-permute-done((f32[48,512]{1,0:T(8,128)S(1)}, f32[48,512]{1,0:T(8,128)S(1)}, u32[]{:S(2)}, u32[]{:S(2)}) %collective-permute-start.3) | collective-permute-done | bytes 98336 | tf_op jit(solution)/shard_map/ppermute | solution.py:661
  27.8 3.5 %collective-permute-start.6 = (f32[176,512]{1,0:T(8,128)S(1)}, f32[176,512]{1,0:T(8,128)S(1)}, u32[]{:S(2)}, u32[]{:S(2)}) collective-permute-start(f32[176,512]{1,0:T(8,128)S(1)} %shard_map.52), channel_id=1, source_target_pairs={{0,15},{1,2},{2,1},{3,4},{4,3},{5,6},{6,5},{7,8},{8,7},{9,10},{10,... | collective-permute-start | bytes 1081352 | tf_op jit(solution)/shard_map/ppermute | solution.py:661
  31.3 5.2 %collective-permute-start.4 = (f32[168,512]{1,0:T(8,128)S(1)}, f32[168,512]{1,0:T(8,128)S(1)}, u32[]{:S(2)}, u32[]{:S(2)}) collective-permute-start(f32[168,512]{1,0:T(8,128)S(1)} %shard_map.48), channel_id=1, source_target_pairs={{0,1},{1,0},{2,3},{3,2},{4,5},{5,4},{6,7},{7,6},{8,9},{9,8},{10,11... | collective-permute-start | bytes 1032200 | tf_op jit(solution)/shard_map/ppermute | solution.py:656
  36.6 1.9 %collective-permute-start.5 = (f32[152,512]{1,0:T(8,128)S(1)}, f32[152,512]{1,0:T(8,128)S(1)}, u32[]{:S(2)}, u32[]{:S(2)}) collective-permute-start(f32[152,512]{1,0:T(8,128)S(1)} %get-tuple-element.39), channel_id=1, source_target_pairs={{0,1},{1,0},{2,3},{3,2},{4,5},{5,4},{6,7},{7,6},{8,9},{9,8},{10,11... | collective-permute-start | bytes 933896 | tf_op jit(solution)/shard_map/ppermute | solution.py:656
  38.5 1.9 %collective-permute-start.7 = (f32[96,512]{1,0:T(8,128)S(1)}, f32[96,512]{1,0:T(8,128)S(1)}, u32[]{:S(2)}, u32[]{:S(2)}) collective-permute-start(f32[96,512]{1,0:T(8,128)S(1)} %get-tuple-element.48), channel_id=1, source_target_pairs={{0,15},{1,2},{2,1},{3,4},{4,3},{5,6},{6,5},{7,8},{8,7},{9,10},{10,... | collective-permute-start | bytes 589832 | tf_op jit(solution)/shard_map/ppermute | solution.py:661
  40.6 2.2 %shard_map.51.before = f32[16,384]{1,0:T(8,128)S(1)} custom-call(f32[384,512]{1,0:T(8,128)S(1)} %get-tuple-element.40.wide, s32[24,128]{1,0:T(8,128)S(1)} %get-tuple-element.41.places, f32[16,256]{1,0:T(8,128)S(1)} %get-tuple-element.38.start.refs_0_, f32[72,512]{1,0:T(8,128)S(1)} %collective-permute-done.from_y, ...), custom_call_target="tpu_custom_call" | custom-call | tf_op jit(solution)/shard_map/pallas_call | solution.py:620
  44.8 4.1 %collective-permute-start.10 = (f32[16,640]{1,0:T(8,128)S(1)}, f32[16,640]{1,0:T(8,128)S(1)}, u32[]{:S(2)}, u32[]{:S(2)}) collective-permute-start(f32[16,640]{1,0:T(8,128)S(1)} %shard_map.56.own), channel_id=1, source_target_pairs={{496,0},{497,1},{498,2},{499,3},{500,4},{501,5},{502,6},{503,7},{5... | collective-permute-start | bytes 122888 | tf_op jit(solution)/shard_map/ppermute | solution.py:647
  50.8 2.7 %collective-permute-start.8 = (f32[16,640]{1,0:T(8,128)S(1)}, f32[16,640]{1,0:T(8,128)S(1)}, u32[]{:S(2)}, u32[]{:S(2)}) collective-permute-start(f32[16,640]{1,0:T(8,128)S(1)} %shard_map.56.own), channel_id=1, source_target_pairs={{448,0},{449,1},{450,2},{451,3},{452,4},{453,5},{454,6},{455,7},{4... | collective-permute-start | bytes 122888 | tf_op jit(solution)/shard_map/ppermute | solution.py:647
  53.7 2.0 %collective-permute-done.9.from_y = f32[16,640]{1,0:T(8,128)S(1)} collective-permute-done((f32[16,640]{1,0:T(8,128)S(1)}, f32[16,640]{1,0:T(8,128)S(1)}, u32[]{:S(2)}, u32[]{:S(2)}) %collective-permute-start.9) | collective-permute-done | bytes 40992 | tf_op jit(solution)/shard_map/ppermute | solution.py:647
  57.1 2.7 %shard_map.57.own.second = f32[16,512]{1,0:T(8,128)S(1)} custom-call(f32[512,512]{1,0:T(8,128)S(1)} %get-tuple-element.49.tall, s32[32,128]{1,0:T(8,128)S(1)} %get-tuple-element.50.places, f32[16,640]{1,0:T(8,128)S(1)} %shard_map.56.own, f32[16,640]{1,0:T(8,128)S(1)} %collective-permute-done.8.from_x, f32[16,640]{1,0:T(8,128)S(1)} %collective-permute-done.9.from_y, ...), custom_call_target="tpu_custom_call" | custom-call | tf_op jit(solution)/shard_map/pallas_call | solution.py:620
  59.7 6.0 %collective-permute-start.13 = (f32[16,512]{1,0:T(8,128)S(1)}, f32[16,512]{1,0:T(8,128)S(1)}, u32[]{:S(2)}, u32[]{:S(2)}) collective-permute-start(f32[16,512]{1,0:T(8,128)S(1)} %shard_map.57.own.second), channel_id=1, source_target_pairs={{80,0},{81,1},{82,2},{83,3},{84,4},{85,5},{86,6},{87,7},{88,8},{89... | collective-permute-start | bytes 98312 | tf_op jit(solution)/shard_map/ppermute | solution.py:647
  65.7 2.2 %collective-permute-start.12 = (f32[16,512]{1,0:T(8,128)S(1)}, f32[16,512]{1,0:T(8,128)S(1)}, u32[]{:S(2)}, u32[]{:S(2)}) collective-permute-start(f32[16,512]{1,0:T(8,128)S(1)} %shard_map.57.own.second), channel_id=1, source_target_pairs={{16,0},{17,1},{18,2},{19,3},{20,4},{21,5},{22,6},{23,7},{24,8},{25... | collective-permute-start | bytes 98312 | tf_op jit(solution)/shard_map/ppermute | solution.py:647
  67.9 2.4 %collective-permute-start.11 = (f32[16,512]{1,0:T(8,128)S(1)}, f32[16,512]{1,0:T(8,128)S(1)}, u32[]{:S(2)}, u32[]{:S(2)}) collective-permute-start(f32[16,512]{1,0:T(8,128)S(1)} %shard_map.57.own.second), channel_id=1, source_target_pairs={{64,0},{65,1},{66,2},{67,3},{68,4},{69,5},{70,6},{71,7},{72,8},{73... | collective-permute-start | bytes 98312 | tf_op jit(solution)/shard_map/ppermute | solution.py:647
  72.9 2.2 %shard_map.58.own = f32[16,384]{1,0:T(8,128)S(1)} custom-call(f32[384,512]{1,0:T(8,128)S(1)} %get-tuple-element.46.wide, s32[24,128]{1,0:T(8,128)S(1)} %get-tuple-element.47.places, f32[16,512]{1,0:T(8,128)S(1)} %shard_map.57.own.second, f32[16,512]{1,0:T(8,128)S(1)} %collective-permute-done.11.from_x, f32[16,512]{1,0:T(8,128)S(1)} %collective-permute-done.12.from_y, ...), custom_call_target="tpu_custom_call" | custom-call | tf_op jit(solution)/shard_map/pallas_call | solution.py:620
  75.1 4.1 %collective-permute-start.16 = (f32[16,384]{1,0:T(8,128)S(1)}, f32[16,384]{1,0:T(8,128)S(1)}, u32[]{:S(2)}, u32[]{:S(2)}) collective-permute-start(f32[16,384]{1,0:T(8,128)S(1)} %shard_map.58.own), channel_id=1, source_target_pairs={{496,0},{497,1},{498,2},{499,3},{500,4},{501,5},{502,6},{503,7},{5... | collective-permute-start | bytes 73736 | tf_op jit(solution)/shard_map/ppermute | solution.py:647
  79.2 2.0 %collective-permute-start.15 = (f32[16,384]{1,0:T(8,128)S(1)}, f32[16,384]{1,0:T(8,128)S(1)}, u32[]{:S(2)}, u32[]{:S(2)}) collective-permute-start(f32[16,384]{1,0:T(8,128)S(1)} %shard_map.58.own), channel_id=1, source_target_pairs={{48,0},{49,1},{50,2},{51,3},{52,4},{53,5},{54,6},{55,7},{56,8},{57... | collective-permute-start | bytes 73736 | tf_op jit(solution)/shard_map/ppermute | solution.py:647
  81.2 2.7 %collective-permute-start.14 = (f32[16,384]{1,0:T(8,128)S(1)}, f32[16,384]{1,0:T(8,128)S(1)}, u32[]{:S(2)}, u32[]{:S(2)}) collective-permute-start(f32[16,384]{1,0:T(8,128)S(1)} %shard_map.58.own), channel_id=1, source_target_pairs={{448,0},{449,1},{450,2},{451,3},{452,4},{453,5},{454,6},{455,7},{4... | collective-permute-start | bytes 73736 | tf_op jit(solution)/shard_map/ppermute | solution.py:647
  87.2 2.1 %shard_map.60 = (f32[16,256]{1,0:T(8,128)S(1)}, f32[32,4,128]{2,1,0:T(4,128)S(1)}) custom-call(f32[256,512]{1,0:T(8,128)S(1)} %get-tuple-element.31.matrix, s32[16,128]{1,0:T(8,128)S(1)} %get-tuple-element.45.places, f32[16,384]{1,0:T(8,128)S(1)} %shard_map.58.own, f32[16,384]{1,0:T(8,128)S(1)} %collective-permute-done.14.from_x, ...), custom_call_target="tpu_custom_call" | custom-call | tf_op jit(solution)/shard_map/pallas_call | solution.py:620
  89.3 18.7 %all_to_all.10.ref = f32[32,4,128]{2,1,0:T(4,128)S(1)} all-to-all(f32[32,4,128]{2,1,0:T(4,128)S(1)} %get-tuple-element.55), channel_id=1, replica_groups=mesh['gx'=8,'gy'=4,'gz'=16] {'gx','gy'}, dimensions={0} | all-to-all | bytes 131072 | tf_op jit(solution)/shard_map/all_to_all | solution.py:736
  108.1 18.4 %all_to_all.11.ref = f32[16,4,128]{2,1,0:T(4,128)S(1)} all-to-all(f32[16,4,128]{2,1,0:T(4,128)S(1)} %shard_map.61), channel_id=1, replica_groups=mesh['gx'=8,'gy'=4,'gz'=16] {'gz'}, dimensions={0} | all-to-all | bytes 65536 | tf_op jit(solution)/shard_map/all_to_all | solution.py:738
  (29 shorter events, 14.2 us)
Async XLA Ops:
  1.2 26.6 %collective-permute-start = (f32[72,512]{1,0:T(8,128)S(1)}, f32[72,512]{1,0:T(8,128)S(1)}, u32[]{:S(2)}, u32[]{:S(2)}) collective-permute-start(f32[72,512]{1,0:T(8,128)S(1)} %get-tuple-element.32), channel_id=1, source_target_pairs={{16,0},{17,1},{18,2},{19,3},{20,4},{21,5},{22,6},{23,7},{24,8},{25... | collective-permute-start | bytes 442376 | tf_op jit(solution)/shard_map/ppermute | solution.py:647
  12.7 15.1 %collective-permute-start.1 = (f32[72,512]{1,0:T(8,128)S(1)}, f32[72,512]{1,0:T(8,128)S(1)}, u32[]{:S(2)}, u32[]{:S(2)}) collective-permute-start(f32[72,512]{1,0:T(8,128)S(1)} %get-tuple-element.33), channel_id=1, source_target_pairs={{80,0},{81,1},{82,2},{83,3},{84,4},{85,5},{86,6},{87,7},{88,8},{89... | collective-permute-start | bytes 442376 | tf_op jit(solution)/shard_map/ppermute | solution.py:647
  17.8 10.0 %collective-permute-start.2 = (f32[72,512]{1,0:T(8,128)S(1)}, f32[72,512]{1,0:T(8,128)S(1)}, u32[]{:S(2)}, u32[]{:S(2)}) collective-permute-start(f32[72,512]{1,0:T(8,128)S(1)} %get-tuple-element.34), channel_id=1, source_target_pairs={{64,0},{65,1},{66,2},{67,3},{68,4},{69,5},{70,6},{71,7},{72,8},{73... | collective-permute-start | bytes 442376 | tf_op jit(solution)/shard_map/ppermute | solution.py:647
  20.8 7.0 %collective-permute-start.3 = (f32[48,512]{1,0:T(8,128)S(1)}, f32[48,512]{1,0:T(8,128)S(1)}, u32[]{:S(2)}, u32[]{:S(2)}) collective-permute-start(f32[48,512]{1,0:T(8,128)S(1)} %shard_map.47), channel_id=1, source_target_pairs={{0,15},{1,2},{2,1},{3,4},{4,3},{5,6},{6,5},{7,8},{8,7},{9,10},{10,... | collective-permute-start | bytes 294920 | tf_op jit(solution)/shard_map/ppermute | solution.py:661
  27.8 15.0 %collective-permute-start.6 = (f32[176,512]{1,0:T(8,128)S(1)}, f32[176,512]{1,0:T(8,128)S(1)}, u32[]{:S(2)}, u32[]{:S(2)}) collective-permute-start(f32[176,512]{1,0:T(8,128)S(1)} %shard_map.52), channel_id=1, source_target_pairs={{0,15},{1,2},{2,1},{3,4},{4,3},{5,6},{6,5},{7,8},{8,7},{9,10},{10,... | collective-permute-start | bytes 1081352 | tf_op jit(solution)/shard_map/ppermute | solution.py:661
  31.3 9.1 %collective-permute-start.4 = (f32[168,512]{1,0:T(8,128)S(1)}, f32[168,512]{1,0:T(8,128)S(1)}, u32[]{:S(2)}, u32[]{:S(2)}) collective-permute-start(f32[168,512]{1,0:T(8,128)S(1)} %shard_map.48), channel_id=1, source_target_pairs={{0,1},{1,0},{2,3},{3,2},{4,5},{5,4},{6,7},{7,6},{8,9},{9,8},{10,11... | collective-permute-start | bytes 1032200 | tf_op jit(solution)/shard_map/ppermute | solution.py:656
  36.6 3.9 %collective-permute-start.5 = (f32[152,512]{1,0:T(8,128)S(1)}, f32[152,512]{1,0:T(8,128)S(1)}, u32[]{:S(2)}, u32[]{:S(2)}) collective-permute-start(f32[152,512]{1,0:T(8,128)S(1)} %get-tuple-element.39), channel_id=1, source_target_pairs={{0,1},{1,0},{2,3},{3,2},{4,5},{5,4},{6,7},{7,6},{8,9},{9,8},{10,11... | collective-permute-start | bytes 933896 | tf_op jit(solution)/shard_map/ppermute | solution.py:656
  38.5 15.0 %collective-permute-start.7 = (f32[96,512]{1,0:T(8,128)S(1)}, f32[96,512]{1,0:T(8,128)S(1)}, u32[]{:S(2)}, u32[]{:S(2)}) collective-permute-start(f32[96,512]{1,0:T(8,128)S(1)} %get-tuple-element.48), channel_id=1, source_target_pairs={{0,15},{1,2},{2,1},{3,4},{4,3},{5,6},{6,5},{7,8},{8,7},{9,10},{10,... | collective-permute-start | bytes 589832 | tf_op jit(solution)/shard_map/ppermute | solution.py:661
  44.8 9.0 %collective-permute-start.10 = (f32[16,640]{1,0:T(8,128)S(1)}, f32[16,640]{1,0:T(8,128)S(1)}, u32[]{:S(2)}, u32[]{:S(2)}) collective-permute-start(f32[16,640]{1,0:T(8,128)S(1)} %shard_map.56.own), channel_id=1, source_target_pairs={{496,0},{497,1},{498,2},{499,3},{500,4},{501,5},{502,6},{503,7},{5... | collective-permute-start | bytes 122888 | tf_op jit(solution)/shard_map/ppermute | solution.py:647
  48.9 6.9 %collective-permute-start.9 = (f32[16,640]{1,0:T(8,128)S(1)}, f32[16,640]{1,0:T(8,128)S(1)}, u32[]{:S(2)}, u32[]{:S(2)}) collective-permute-start(f32[16,640]{1,0:T(8,128)S(1)} %shard_map.56.own), channel_id=1, source_target_pairs={{48,0},{49,1},{50,2},{51,3},{52,4},{53,5},{54,6},{55,7},{56,8},{57... | collective-permute-start | bytes 122888 | tf_op jit(solution)/shard_map/ppermute | solution.py:647
  50.8 6.3 %collective-permute-start.8 = (f32[16,640]{1,0:T(8,128)S(1)}, f32[16,640]{1,0:T(8,128)S(1)}, u32[]{:S(2)}, u32[]{:S(2)}) collective-permute-start(f32[16,640]{1,0:T(8,128)S(1)} %shard_map.56.own), channel_id=1, source_target_pairs={{448,0},{449,1},{450,2},{451,3},{452,4},{453,5},{454,6},{455,7},{4... | collective-permute-start | bytes 122888 | tf_op jit(solution)/shard_map/ppermute | solution.py:647
  59.7 10.7 %collective-permute-start.13 = (f32[16,512]{1,0:T(8,128)S(1)}, f32[16,512]{1,0:T(8,128)S(1)}, u32[]{:S(2)}, u32[]{:S(2)}) collective-permute-start(f32[16,512]{1,0:T(8,128)S(1)} %shard_map.57.own.second), channel_id=1, source_target_pairs={{80,0},{81,1},{82,2},{83,3},{84,4},{85,5},{86,6},{87,7},{88,8},{89... | collective-permute-start | bytes 98312 | tf_op jit(solution)/shard_map/ppermute | solution.py:647
  65.7 6.0 %collective-permute-start.12 = (f32[16,512]{1,0:T(8,128)S(1)}, f32[16,512]{1,0:T(8,128)S(1)}, u32[]{:S(2)}, u32[]{:S(2)}) collective-permute-start(f32[16,512]{1,0:T(8,128)S(1)} %shard_map.57.own.second), channel_id=1, source_target_pairs={{16,0},{17,1},{18,2},{19,3},{20,4},{21,5},{22,6},{23,7},{24,8},{25... | collective-permute-start | bytes 98312 | tf_op jit(solution)/shard_map/ppermute | solution.py:647
  67.9 5.0 %collective-permute-start.11 = (f32[16,512]{1,0:T(8,128)S(1)}, f32[16,512]{1,0:T(8,128)S(1)}, u32[]{:S(2)}, u32[]{:S(2)}) collective-permute-start(f32[16,512]{1,0:T(8,128)S(1)} %shard_map.57.own.second), channel_id=1, source_target_pairs={{64,0},{65,1},{66,2},{67,3},{68,4},{69,5},{70,6},{71,7},{72,8},{73... | collective-permute-start | bytes 98312 | tf_op jit(solution)/shard_map/ppermute | solution.py:647
  75.1 8.9 %collective-permute-start.16 = (f32[16,384]{1,0:T(8,128)S(1)}, f32[16,384]{1,0:T(8,128)S(1)}, u32[]{:S(2)}, u32[]{:S(2)}) collective-permute-start(f32[16,384]{1,0:T(8,128)S(1)} %shard_map.58.own), channel_id=1, source_target_pairs={{496,0},{497,1},{498,2},{499,3},{500,4},{501,5},{502,6},{503,7},{5... | collective-permute-start | bytes 73736 | tf_op jit(solution)/shard_map/ppermute | solution.py:647
  79.2 6.7 %collective-permute-start.15 = (f32[16,384]{1,0:T(8,128)S(1)}, f32[16,384]{1,0:T(8,128)S(1)}, u32[]{:S(2)}, u32[]{:S(2)}) collective-permute-start(f32[16,384]{1,0:T(8,128)S(1)} %shard_map.58.own), channel_id=1, source_target_pairs={{48,0},{49,1},{50,2},{51,3},{52,4},{53,5},{54,6},{55,7},{56,8},{57... | collective-permute-start | bytes 73736 | tf_op jit(solution)/shard_map/ppermute | solution.py:647
  81.2 6.0 %collective-permute-start.14 = (f32[16,384]{1,0:T(8,128)S(1)}, f32[16,384]{1,0:T(8,128)S(1)}, u32[]{:S(2)}, u32[]{:S(2)}) collective-permute-start(f32[16,384]{1,0:T(8,128)S(1)} %shard_map.58.own), channel_id=1, source_target_pairs={{448,0},{449,1},{450,2},{451,3},{452,4},{453,5},{454,6},{455,7},{4... | collective-permute-start | bytes 73736 | tf_op jit(solution)/shard_map/ppermute | solution.py:647

commit v9 on v7

--- a/solution.py
+++ b/solution.py
@@ -8,6 +8,7 @@
 ITERS = 2
 DEGREE = 2 * ITERS
 SHIFT = 2.0
+RESOLUTION = 1e-14
 LANES = 128
 PAIRS = [(i, j) for i in range(DEGREE + 1) for j in range(i, DEGREE + 1)]
 VMEM = pl.BlockSpec(memory_space=pltpu.VMEM)
@@ -181,6 +182,7 @@
     zero = jnp.zeros(shape, jnp.float32)
     start = (jnp.where(row == 0, 1.0, 0.0), zero)
     inner = entry(0, 0, 0)
+    least = RESOLUTION * inner
     quasi_norm = jnp.sqrt(inner)
     image = apply(start)
     resid = search = start
@@ -190,14 +192,14 @@
         step = inner / with_start(image)
         resid = pair_add(resid, pair_scale(image, -step))
         direction = pair_add(search, pair_scale(direction, ratio * ratio * weight / step))
-        ratio = jnp.sqrt(square(resid, 2 * iteration + 1)) / quasi_norm
+        ratio = jnp.sqrt(jnp.maximum(square(resid, 2 * iteration + 1), least)) / quasi_norm
         quasi_norm, weight = shrink(quasi_norm, ratio, step)
         total = pair_add(total, pair_scale(direction, weight))
         search_odd = pair_add(search, pair_scale(image, -step))
         image_odd = apply(search_odd)
         resid = pair_add(resid, pair_scale(image_odd, -step))
         direction = pair_add(search_odd, pair_scale(direction, ratio * ratio * weight / step))
-        ratio = jnp.sqrt(square(resid, 2 * iteration + 2)) / quasi_norm
+        ratio = jnp.sqrt(jnp.maximum(square(resid, 2 * iteration + 2), least)) / quasi_norm
         quasi_norm, weight = shrink(quasi_norm, ratio, step)
         total = pair_add(total, pair_scale(direction, weight))
         if iteration + 1 < ITERS:
@@ -357,42 +359,35 @@
     return jnp.concatenate(tiles, axis=1)
 
 
-def spread_lanes(value):
-    for amount in (64, 32, 16):
-        value = value + pltpu.roll(value, amount, 1)
+def turn_blocks(value):
+    row, group = iota(value.shape, 0), iota(value.shape, 1) >> 4
+    for bit in (1, 2, 4):
+        lanes = bit * SLOT_ROWS
+        later = pltpu.roll(pltpu.roll(value, 8 - bit, 0), lanes, 1)
+        earlier = pltpu.roll(pltpu.roll(value, bit, 0), LANES - lanes, 1)
+        swapped = jnp.where((group & bit) != 0, later, earlier)
+        value = jnp.where((row & bit) == (group & bit), value, swapped)
     return value
 
 
-def to_tiles(rows):
-    shape = (8, LANES)
-    diagonal_mask = iota(shape, 0) == iota(shape, 1) >> 4
-    lane_slot = iota(shape, 1) >> 4
+def to_tiles(field):
     halves = []
     for half in range(2):
-        tiles = []
-        for x in range(2):
-            acc = jnp.zeros(shape, jnp.float32)
-            for slot in range(8):
-                row = rows(x, slot >> 2, slot & 3)[:, half * LANES : (half + 1) * LANES]
-                value = jnp.where(diagonal_mask, jnp.broadcast_to(row, shape), 0.0)
-                acc = jnp.where(lane_slot == slot, spread_lanes(value), acc)
-            tiles.append(acc)
+        lanes = slice(half * LANES, (half + 1) * LANES)
+        tiles = [
+            turn_blocks(jnp.concatenate([field[x, y, :, lanes] for y in range(2)], axis=0))
+            for x in range(2)
+        ]
         halves.append(jnp.concatenate(tiles, axis=1))
     return jnp.concatenate(halves, axis=0)
 
 
 def from_tiles(value, out):
-    shape = (8, LANES)
-    diagonal_mask = iota(shape, 0) == iota(shape, 1) >> 4
-    lane_slot = iota(shape, 1) >> 4
     for half in range(2):
         for x in range(2):
-            tile = value[half * 8 : half * 8 + 8, x * LANES : (x + 1) * LANES]
-            for slot in range(8):
-                own = spread_lanes(jnp.where(lane_slot == slot, tile, 0.0))
-                row = jnp.sum(jnp.where(diagonal_mask, own, 0.0), axis=0, keepdims=True)
-                z = slot & 3
-                out[x, slot >> 2, z : z + 1, half * LANES : (half + 1) * LANES] = row
+            rows = turn_blocks(value[half * 8 : half * 8 + 8, x * LANES : (x + 1) * LANES])
+            for y in range(2):
+                out[x, y, :, half * LANES : (half + 1) * LANES] = rows[y * 4 : y * 4 + 4]
 
 
 def pack_bricks(field):
@@ -442,7 +437,7 @@
                 own = SHIFT - jnp.broadcast_to(diagonal[x, y, z : z + 1], eye.shape)
                 matrix[row : row + SLOT_ROWS, 432:448] = jnp.where(eye, own, 0.0)
     copies[2].wait()
-    value = to_tiles(lambda x, y, z: rhs[x, y, z : z + 1])
+    value = to_tiles(rhs)
     start[...] = value
     bricks = pack_bricks(value)
     copies[3].wait()

time: 129 us -> 129 us (level)
  no operation moved by 1% of the time
where the time goes in v9:
time: 129 us; the launch traced here: 128 us
  starting transfers between devices  64.6 us (50%)
  blocking collectives  38.4 us (30%)
  Pallas kernels  14.4 us (11%)
  waiting for transfers between devices  10.2 us (8%)
    ppermute x12, starting transfers between devices, fetch(): return lax.ppermute(value, AXES, pairs)  52.5 us
    all_to_all x1, blocking collectives, body(): message = lax.all_to_all(message, ('gx', 'gy'), 0, 0, tiled=True)  19.7 us
    all_to_all x1, blocking collectives, body(): message = lax.all_to_all(message, 'gz', 0, 0, tiled=True)  18.7 us
    pallas_call x16, Pallas kernels, call(): pl.pallas_call(kernel, out_shape=shapes, in_specs=[SMEM if operand.dtype...  14.4 us
    ppermute x12, waiting for transfers between devices, fetch(): return lax.ppermute(value, AXES, pairs)  9.59 us
    ppermute x2, starting transfers between devices, swap_layers(): lax.ppermute(to_second, 'gz', odd)  7.41 us
    ppermute x2, starting transfers between devices, swap_layers(): lax.ppermute(to_first, 'gz', even)  4.73 us
  transfers between devices with their start and end apart: 16, of which 6 were waited for; matrix products, arithmetic and copies ran while one was open for 0% of the time, Pallas kernels for 4%

profile of v9, /device:TPU:1, one launch (start us, length us, event | category | flops | bytes accessed | tf_op | source)
XLA Modules:
  0.0 128.0 jit_solution(15178302671984183586)
XLA Ops:
  1.2 11.5 %collective-permute-start = (f32[72,512]{1,0:T(8,128)S(1)}, f32[72,512]{1,0:T(8,128)S(1)}, u32[]{:S(2)}, u32[]{:S(2)}) collective-permute-start(f32[72,512]{1,0:T(8,128)S(1)} %get-tuple-element.28), channel_id=1, source_target_pairs={{16,0},{17,1},{18,2},{19,3},{20,4},{21,5},{22,6},{23,7},{24,8},{25... | collective-permute-start | bytes 442376 | tf_op jit(solution)/shard_map/ppermute | solution.py:645
  12.7 5.1 %collective-permute-start.1 = (f32[72,512]{1,0:T(8,128)S(1)}, f32[72,512]{1,0:T(8,128)S(1)}, u32[]{:S(2)}, u32[]{:S(2)}) collective-permute-start(f32[72,512]{1,0:T(8,128)S(1)} %get-tuple-element.29), channel_id=1, source_target_pairs={{80,0},{81,1},{82,2},{83,3},{84,4},{85,5},{86,6},{87,7},{88,8},{89... | collective-permute-start | bytes 442376 | tf_op jit(solution)/shard_map/ppermute | solution.py:645
  17.8 3.0 %collective-permute-start.2 = (f32[72,512]{1,0:T(8,128)S(1)}, f32[72,512]{1,0:T(8,128)S(1)}, u32[]{:S(2)}, u32[]{:S(2)}) collective-permute-start(f32[72,512]{1,0:T(8,128)S(1)} %get-tuple-element.30), channel_id=1, source_target_pairs={{64,0},{65,1},{66,2},{67,3},{68,4},{69,5},{70,6},{71,7},{72,8},{73... | collective-permute-start | bytes 442376 | tf_op jit(solution)/shard_map/ppermute | solution.py:645
  20.8 3.3 %collective-permute-done.from_y = f32[72,512]{1,0:T(8,128)S(1)} collective-permute-done((f32[72,512]{1,0:T(8,128)S(1)}, f32[72,512]{1,0:T(8,128)S(1)}, u32[]{:S(2)}, u32[]{:S(2)}) %collective-permute-start) | collective-permute-done | bytes 147488 | tf_op jit(solution)/shard_map/ppermute | solution.py:645
  24.5 4.8 %collective-permute-start.5 = (f32[224,512]{1,0:T(8,128)S(1)}, f32[224,512]{1,0:T(8,128)S(1)}, u32[]{:S(2)}, u32[]{:S(2)}) collective-permute-start(f32[224,512]{1,0:T(8,128)S(1)} %shard_map.51), channel_id=1, source_target_pairs={{0,15},{1,2},{2,1},{3,4},{4,3},{5,6},{6,5},{7,8},{8,7},{9,10},{10,... | collective-permute-start | bytes 1376264 | tf_op jit(solution)/shard_map/ppermute | solution.py:656
  29.4 2.8 %collective-permute-start.3 = (f32[168,512]{1,0:T(8,128)S(1)}, f32[168,512]{1,0:T(8,128)S(1)}, u32[]{:S(2)}, u32[]{:S(2)}) collective-permute-start(f32[168,512]{1,0:T(8,128)S(1)} %shard_map.47), channel_id=1, source_target_pairs={{0,1},{1,0},{2,3},{3,2},{4,5},{5,4},{6,7},{7,6},{8,9},{9,8},{10,11... | collective-permute-start | bytes 1032200 | tf_op jit(solution)/shard_map/ppermute | solution.py:656
  34.2 2.6 %collective-permute-start.6 = (f32[96,512]{1,0:T(8,128)S(1)}, f32[96,512]{1,0:T(8,128)S(1)}, u32[]{:S(2)}, u32[]{:S(2)}) collective-permute-start(f32[96,512]{1,0:T(8,128)S(1)} %get-tuple-element.40), channel_id=1, source_target_pairs={{0,15},{1,2},{2,1},{3,4},{4,3},{5,6},{6,5},{7,8},{8,7},{9,10},{10,... | collective-permute-start | bytes 589832 | tf_op jit(solution)/shard_map/ppermute | solution.py:656
  36.9 2.2 %shard_map.50.before = f32[16,384]{1,0:T(8,128)S(1)} custom-call(f32[384,512]{1,0:T(8,128)S(1)} %get-tuple-element.33.wide, s32[24,128]{1,0:T(8,128)S(1)} %get-tuple-element.34.places, f32[16,256]{1,0:T(8,128)S(1)} %get-tuple-element.31.start.refs_0_, f32[72,512]{1,0:T(8,128)S(1)} %collective-permute-done.from_y, ...), custom_call_target="tpu_custom_call" | custom-call | flops 268435456 | bytes 4194304 | tf_op jit(solution)/shard_map/pallas_call | solution.py:615
  41.7 3.2 %collective-permute-start.9 = (f32[16,640]{1,0:T(8,128)S(1)}, f32[16,640]{1,0:T(8,128)S(1)}, u32[]{:S(2)}, u32[]{:S(2)}) collective-permute-start(f32[16,640]{1,0:T(8,128)S(1)} %shard_map.55.own), channel_id=1, source_target_pairs={{496,0},{497,1},{498,2},{499,3},{500,4},{501,5},{502,6},{503,7},{5... | collective-permute-start | bytes 122888 | tf_op jit(solution)/shard_map/ppermute | solution.py:645
  45.0 4.3 %collective-permute-start.8 = (f32[16,640]{1,0:T(8,128)S(1)}, f32[16,640]{1,0:T(8,128)S(1)}, u32[]{:S(2)}, u32[]{:S(2)}) collective-permute-start(f32[16,640]{1,0:T(8,128)S(1)} %shard_map.55.own), channel_id=1, source_target_pairs={{48,0},{49,1},{50,2},{51,3},{52,4},{53,5},{54,6},{55,7},{56,8},{57... | collective-permute-start | bytes 122888 | tf_op jit(solution)/shard_map/ppermute | solution.py:645
  49.2 3.2 %collective-permute-start.7 = (f32[16,640]{1,0:T(8,128)S(1)}, f32[16,640]{1,0:T(8,128)S(1)}, u32[]{:S(2)}, u32[]{:S(2)}) collective-permute-start(f32[16,640]{1,0:T(8,128)S(1)} %shard_map.55.own), channel_id=1, source_target_pairs={{448,0},{449,1},{450,2},{451,3},{452,4},{453,5},{454,6},{455,7},{4... | collective-permute-start | bytes 122888 | tf_op jit(solution)/shard_map/ppermute | solution.py:645
  52.7 2.8 %collective-permute-done.7.from_x = f32[16,640]{1,0:T(8,128)S(1)} collective-permute-done((f32[16,640]{1,0:T(8,128)S(1)}, f32[16,640]{1,0:T(8,128)S(1)}, u32[]{:S(2)}, u32[]{:S(2)}) %collective-permute-start.7) | collective-permute-done | bytes 40992 | tf_op jit(solution)/shard_map/ppermute | solution.py:645
  55.5 2.7 %shard_map.56.own.second = f32[16,512]{1,0:T(8,128)S(1)} custom-call(f32[512,512]{1,0:T(8,128)S(1)} %get-tuple-element.41.tall, s32[32,128]{1,0:T(8,128)S(1)} %get-tuple-element.42.places, f32[16,640]{1,0:T(8,128)S(1)} %shard_map.55.own, f32[16,640]{1,0:T(8,128)S(1)} %collective-permute-done.7.from_x, f32[16,640]{1,0:T(8,128)S(1)} %collective-permute-done.8.from_y, ...), custom_call_target="tpu_custom_call" | custom-call | tf_op jit(solution)/shard_map/pallas_call | solution.py:615
  58.1 4.3 %collective-permute-start.12 = (f32[16,512]{1,0:T(8,128)S(1)}, f32[16,512]{1,0:T(8,128)S(1)}, u32[]{:S(2)}, u32[]{:S(2)}) collective-permute-start(f32[16,512]{1,0:T(8,128)S(1)} %shard_map.56.own.second), channel_id=1, source_target_pairs={{80,0},{81,1},{82,2},{83,3},{84,4},{85,5},{86,6},{87,7},{88,8},{89... | collective-permute-start | bytes 98312 | tf_op jit(solution)/shard_map/ppermute | solution.py:645
  62.4 3.6 %collective-permute-start.11 = (f32[16,512]{1,0:T(8,128)S(1)}, f32[16,512]{1,0:T(8,128)S(1)}, u32[]{:S(2)}, u32[]{:S(2)}) collective-permute-start(f32[16,512]{1,0:T(8,128)S(1)} %shard_map.56.own.second), channel_id=1, source_target_pairs={{16,0},{17,1},{18,2},{19,3},{20,4},{21,5},{22,6},{23,7},{24,8},{25... | collective-permute-start | bytes 98312 | tf_op jit(solution)/shard_map/ppermute | solution.py:645
  66.1 4.0 %collective-permute-start.10 = (f32[16,512]{1,0:T(8,128)S(1)}, f32[16,512]{1,0:T(8,128)S(1)}, u32[]{:S(2)}, u32[]{:S(2)}) collective-permute-start(f32[16,512]{1,0:T(8,128)S(1)} %shard_map.56.own.second), channel_id=1, source_target_pairs={{64,0},{65,1},{66,2},{67,3},{68,4},{69,5},{70,6},{71,7},{72,8},{73... | collective-permute-start | bytes 98312 | tf_op jit(solution)/shard_map/ppermute | solution.py:645
  71.1 2.2 %shard_map.57.own = f32[16,384]{1,0:T(8,128)S(1)} custom-call(f32[384,512]{1,0:T(8,128)S(1)} %get-tuple-element.38.wide, s32[24,128]{1,0:T(8,128)S(1)} %get-tuple-element.39.places, f32[16,512]{1,0:T(8,128)S(1)} %shard_map.56.own.second, f32[16,512]{1,0:T(8,128)S(1)} %collective-permute-done.10.from_x, f32[16,512]{1,0:T(8,128)S(1)} %collective-permute-done.11.from_y, ...), custom_call_target="tpu_custom_call" | custom-call | tf_op jit(solution)/shard_map/pallas_call | solution.py:615
  73.3 2.2 %collective-permute-start.15 = (f32[16,384]{1,0:T(8,128)S(1)}, f32[16,384]{1,0:T(8,128)S(1)}, u32[]{:S(2)}, u32[]{:S(2)}) collective-permute-start(f32[16,384]{1,0:T(8,128)S(1)} %shard_map.57.own), channel_id=1, source_target_pairs={{496,0},{497,1},{498,2},{499,3},{500,4},{501,5},{502,6},{503,7},{5... | collective-permute-start | bytes 73736 | tf_op jit(solution)/shard_map/ppermute | solution.py:645
  75.5 4.6 %collective-permute-start.14 = (f32[16,384]{1,0:T(8,128)S(1)}, f32[16,384]{1,0:T(8,128)S(1)}, u32[]{:S(2)}, u32[]{:S(2)}) collective-permute-start(f32[16,384]{1,0:T(8,128)S(1)} %shard_map.57.own), channel_id=1, source_target_pairs={{48,0},{49,1},{50,2},{51,3},{52,4},{53,5},{54,6},{55,7},{56,8},{57... | collective-permute-start | bytes 73736 | tf_op jit(solution)/shard_map/ppermute | solution.py:645
  80.1 3.5 %collective-permute-start.13 = (f32[16,384]{1,0:T(8,128)S(1)}, f32[16,384]{1,0:T(8,128)S(1)}, u32[]{:S(2)}, u32[]{:S(2)}) collective-permute-start(f32[16,384]{1,0:T(8,128)S(1)} %shard_map.57.own), channel_id=1, source_target_pairs={{448,0},{449,1},{450,2},{451,3},{452,4},{453,5},{454,6},{455,7},{4... | collective-permute-start | bytes 73736 | tf_op jit(solution)/shard_map/ppermute | solution.py:645
  83.8 2.2 %collective-permute-done.13.from_x = f32[16,384]{1,0:T(8,128)S(1)} collective-permute-done((f32[16,384]{1,0:T(8,128)S(1)}, f32[16,384]{1,0:T(8,128)S(1)}, u32[]{:S(2)}, u32[]{:S(2)}) %collective-permute-start.13) | collective-permute-done | bytes 24608 | tf_op jit(solution)/shard_map/ppermute | solution.py:645
  85.9 2.1 %shard_map.59 = (f32[16,256]{1,0:T(8,128)S(1)}, f32[32,4,128]{2,1,0:T(4,128)S(1)}) custom-call(f32[256,512]{1,0:T(8,128)S(1)} %get-tuple-element.27.matrix, s32[16,128]{1,0:T(8,128)S(1)} %get-tuple-element.37.places, f32[16,384]{1,0:T(8,128)S(1)} %shard_map.57.own, f32[16,384]{1,0:T(8,128)S(1)} %collective-permute-done.13.from_x, ...), custom_call_target="tpu_custom_call" | custom-call | tf_op jit(solution)/shard_map/pallas_call | solution.py:615
  88.1 19.7 %all_to_all.10.ref = f32[32,4,128]{2,1,0:T(4,128)S(1)} all-to-all(f32[32,4,128]{2,1,0:T(4,128)S(1)} %get-tuple-element.47), channel_id=1, replica_groups=mesh['gx'=8,'gy'=4,'gz'=16] {'gx','gy'}, dimensions={0} | all-to-all | bytes 131072 | tf_op jit(solution)/shard_map/all_to_all | solution.py:729
  107.8 18.7 %all_to_all.11.ref = f32[16,4,128]{2,1,0:T(4,128)S(1)} all-to-all(f32[16,4,128]{2,1,0:T(4,128)S(1)} %shard_map.60), channel_id=1, replica_groups=mesh['gx'=8,'gy'=4,'gz'=16] {'gz'}, dimensions={0} | all-to-all | bytes 65536 | tf_op jit(solution)/shard_map/all_to_all | solution.py:731
  (26 shorter events, 9.1 us)
Async XLA Ops:
  1.2 22.9 %collective-permute-start = (f32[72,512]{1,0:T(8,128)S(1)}, f32[72,512]{1,0:T(8,128)S(1)}, u32[]{:S(2)}, u32[]{:S(2)}) collective-permute-start(f32[72,512]{1,0:T(8,128)S(1)} %get-tuple-element.28), channel_id=1, source_target_pairs={{16,0},{17,1},{18,2},{19,3},{20,4},{21,5},{22,6},{23,7},{24,8},{25... | collective-permute-start | bytes 442376 | tf_op jit(solution)/shard_map/ppermute | solution.py:645
  12.7 11.4 %collective-permute-start.1 = (f32[72,512]{1,0:T(8,128)S(1)}, f32[72,512]{1,0:T(8,128)S(1)}, u32[]{:S(2)}, u32[]{:S(2)}) collective-permute-start(f32[72,512]{1,0:T(8,128)S(1)} %get-tuple-element.29), channel_id=1, source_target_pairs={{80,0},{81,1},{82,2},{83,3},{84,4},{85,5},{86,6},{87,7},{88,8},{89... | collective-permute-start | bytes 442376 | tf_op jit(solution)/shard_map/ppermute | solution.py:645
  17.8 6.7 %collective-permute-start.2 = (f32[72,512]{1,0:T(8,128)S(1)}, f32[72,512]{1,0:T(8,128)S(1)}, u32[]{:S(2)}, u32[]{:S(2)}) collective-permute-start(f32[72,512]{1,0:T(8,128)S(1)} %get-tuple-element.30), channel_id=1, source_target_pairs={{64,0},{65,1},{66,2},{67,3},{68,4},{69,5},{70,6},{71,7},{72,8},{73... | collective-permute-start | bytes 442376 | tf_op jit(solution)/shard_map/ppermute | solution.py:645
  24.5 15.3 %collective-permute-start.5 = (f32[224,512]{1,0:T(8,128)S(1)}, f32[224,512]{1,0:T(8,128)S(1)}, u32[]{:S(2)}, u32[]{:S(2)}) collective-permute-start(f32[224,512]{1,0:T(8,128)S(1)} %shard_map.51), channel_id=1, source_target_pairs={{0,15},{1,2},{2,1},{3,4},{4,3},{5,6},{6,5},{7,8},{8,7},{9,10},{10,... | collective-permute-start | bytes 1376264 | tf_op jit(solution)/shard_map/ppermute | solution.py:656
  29.4 7.4 %collective-permute-start.3 = (f32[168,512]{1,0:T(8,128)S(1)}, f32[168,512]{1,0:T(8,128)S(1)}, u32[]{:S(2)}, u32[]{:S(2)}) collective-permute-start(f32[168,512]{1,0:T(8,128)S(1)} %shard_map.47), channel_id=1, source_target_pairs={{0,1},{1,0},{2,3},{3,2},{4,5},{5,4},{6,7},{7,6},{8,9},{9,8},{10,11... | collective-permute-start | bytes 1032200 | tf_op jit(solution)/shard_map/ppermute | solution.py:656
  32.2 4.6 %collective-permute-start.4 = (f32[152,512]{1,0:T(8,128)S(1)}, f32[152,512]{1,0:T(8,128)S(1)}, u32[]{:S(2)}, u32[]{:S(2)}) collective-permute-start(f32[152,512]{1,0:T(8,128)S(1)} %get-tuple-element.32), channel_id=1, source_target_pairs={{0,1},{1,0},{2,3},{3,2},{4,5},{5,4},{6,7},{7,6},{8,9},{9,8},{10,11... | collective-permute-start | bytes 933896 | tf_op jit(solution)/shard_map/ppermute | solution.py:656
  34.2 18.3 %collective-permute-start.6 = (f32[96,512]{1,0:T(8,128)S(1)}, f32[96,512]{1,0:T(8,128)S(1)}, u32[]{:S(2)}, u32[]{:S(2)}) collective-permute-start(f32[96,512]{1,0:T(8,128)S(1)} %get-tuple-element.40), channel_id=1, source_target_pairs={{0,15},{1,2},{2,1},{3,4},{4,3},{5,6},{6,5},{7,8},{8,7},{9,10},{10,... | collective-permute-start | bytes 589832 | tf_op jit(solution)/shard_map/ppermute | solution.py:656
  41.7 10.9 %collective-permute-start.9 = (f32[16,640]{1,0:T(8,128)S(1)}, f32[16,640]{1,0:T(8,128)S(1)}, u32[]{:S(2)}, u32[]{:S(2)}) collective-permute-start(f32[16,640]{1,0:T(8,128)S(1)} %shard_map.55.own), channel_id=1, source_target_pairs={{496,0},{497,1},{498,2},{499,3},{500,4},{501,5},{502,6},{503,7},{5... | collective-permute-start | bytes 122888 | tf_op jit(solution)/shard_map/ppermute | solution.py:645
  45.0 7.7 %collective-permute-start.8 = (f32[16,640]{1,0:T(8,128)S(1)}, f32[16,640]{1,0:T(8,128)S(1)}, u32[]{:S(2)}, u32[]{:S(2)}) collective-permute-start(f32[16,640]{1,0:T(8,128)S(1)} %shard_map.55.own), channel_id=1, source_target_pairs={{48,0},{49,1},{50,2},{51,3},{52,4},{53,5},{54,6},{55,7},{56,8},{57... | collective-permute-start | bytes 122888 | tf_op jit(solution)/shard_map/ppermute | solution.py:645
  49.2 6.3 %collective-permute-start.7 = (f32[16,640]{1,0:T(8,128)S(1)}, f32[16,640]{1,0:T(8,128)S(1)}, u32[]{:S(2)}, u32[]{:S(2)}) collective-permute-start(f32[16,640]{1,0:T(8,128)S(1)} %shard_map.55.own), channel_id=1, source_target_pairs={{448,0},{449,1},{450,2},{451,3},{452,4},{453,5},{454,6},{455,7},{4... | collective-permute-start | bytes 122888 | tf_op jit(solution)/shard_map/ppermute | solution.py:645
  58.1 12.1 %collective-permute-start.12 = (f32[16,512]{1,0:T(8,128)S(1)}, f32[16,512]{1,0:T(8,128)S(1)}, u32[]{:S(2)}, u32[]{:S(2)}) collective-permute-start(f32[16,512]{1,0:T(8,128)S(1)} %shard_map.56.own.second), channel_id=1, source_target_pairs={{80,0},{81,1},{82,2},{83,3},{84,4},{85,5},{86,6},{87,7},{88,8},{89... | collective-permute-start | bytes 98312 | tf_op jit(solution)/shard_map/ppermute | solution.py:645
  62.4 7.8 %collective-permute-start.11 = (f32[16,512]{1,0:T(8,128)S(1)}, f32[16,512]{1,0:T(8,128)S(1)}, u32[]{:S(2)}, u32[]{:S(2)}) collective-permute-start(f32[16,512]{1,0:T(8,128)S(1)} %shard_map.56.own.second), channel_id=1, source_target_pairs={{16,0},{17,1},{18,2},{19,3},{20,4},{21,5},{22,6},{23,7},{24,8},{25... | collective-permute-start | bytes 98312 | tf_op jit(solution)/shard_map/ppermute | solution.py:645
  66.1 5.0 %collective-permute-start.10 = (f32[16,512]{1,0:T(8,128)S(1)}, f32[16,512]{1,0:T(8,128)S(1)}, u32[]{:S(2)}, u32[]{:S(2)}) collective-permute-start(f32[16,512]{1,0:T(8,128)S(1)} %shard_map.56.own.second), channel_id=1, source_target_pairs={{64,0},{65,1},{66,2},{67,3},{68,4},{69,5},{70,6},{71,7},{72,8},{73... | collective-permute-start | bytes 98312 | tf_op jit(solution)/shard_map/ppermute | solution.py:645
  73.3 10.4 %collective-permute-start.15 = (f32[16,384]{1,0:T(8,128)S(1)}, f32[16,384]{1,0:T(8,128)S(1)}, u32[]{:S(2)}, u32[]{:S(2)}) collective-permute-start(f32[16,384]{1,0:T(8,128)S(1)} %shard_map.57.own), channel_id=1, source_target_pairs={{496,0},{497,1},{498,2},{499,3},{500,4},{501,5},{502,6},{503,7},{5... | collective-permute-start | bytes 73736 | tf_op jit(solution)/shard_map/ppermute | solution.py:645
  75.5 8.2 %collective-permute-start.14 = (f32[16,384]{1,0:T(8,128)S(1)}, f32[16,384]{1,0:T(8,128)S(1)}, u32[]{:S(2)}, u32[]{:S(2)}) collective-permute-start(f32[16,384]{1,0:T(8,128)S(1)} %shard_map.57.own), channel_id=1, source_target_pairs={{48,0},{49,1},{50,2},{51,3},{52,4},{53,5},{54,6},{55,7},{56,8},{57... | collective-permute-start | bytes 73736 | tf_op jit(solution)/shard_map/ppermute | solution.py:645
  80.1 5.8 %collective-permute-start.13 = (f32[16,384]{1,0:T(8,128)S(1)}, f32[16,384]{1,0:T(8,128)S(1)}, u32[]{:S(2)}, u32[]{:S(2)}) collective-permute-start(f32[16,384]{1,0:T(8,128)S(1)} %shard_map.57.own), channel_id=1, source_target_pairs={{448,0},{449,1},{450,2},{451,3},{452,4},{453,5},{454,6},{455,7},{4... | collective-permute-start | bytes 73736 | tf_op jit(solution)/shard_map/ppermute | solution.py:645

commit v10 on v9

--- a/solution.py
+++ b/solution.py
@@ -307,9 +307,31 @@
                 field[place] = pltpu.roll(tile, turn * SLOT_ROWS, 1) if turn else tile
 
 
-def couple(matrix, rows, field, places, gathered):
+def thirds(value):
+    head = value.astype(jnp.bfloat16)
+    rest = value - head.astype(jnp.float32)
+    middle = rest.astype(jnp.bfloat16)
+    return head, middle, (rest - middle.astype(jnp.float32)).astype(jnp.bfloat16)
+
+
+def multiply(matrix, rows, right):
+    right = right[0:CODE]
+    if not isinstance(matrix, tuple):
+        return jnp.dot(
+            matrix[rows, 0:CODE], right, precision=HIGH, preferred_element_type=jnp.float32
+        )
+    head, middle, tail = (part[rows, 0:CODE] for part in matrix)
+    right = jnp.concatenate(thirds(right), axis=1)
+    by_head = jnp.dot(head, right, preferred_element_type=jnp.float32)
+    by_middle = jnp.dot(middle, right[:, 0 : 2 * LANES], preferred_element_type=jnp.float32)
+    by_tail = jnp.dot(tail, right[:, 0:LANES], preferred_element_type=jnp.float32)
+    small = by_head[:, 2 * LANES : 3 * LANES] + by_middle[:, LANES : 2 * LANES] + by_tail
+    return small + (by_head[:, LANES : 2 * LANES] + by_middle[:, 0:LANES]) + by_head[:, 0:LANES]
+
+
+def couple(matrix, atoms, field, places, gathered):
     lane_slot = iota((SLOT_ROWS, LANES), 1) >> 4
-    groups = len(rows) // 8
+    groups = atoms // 8
 
     def gather(k, carry):
         for q in range(groups):
@@ -323,17 +345,7 @@
     lax.fori_loop(0, SELF + 1, gather, 0, unroll=SELF + 1)
     tiles = []
     for q in range(groups):
-        gathered[q, CODE:WIDE, :] = jnp.zeros((WIDE - CODE, LANES), jnp.float32)
-        group = rows[q * 8 : q * 8 + 8]
-        left, start = [], 0
-        for r in range(1, 9):
-            if r == 8 or group[r] != group[r - 1] + 1:
-                left.append(matrix[group[start] * SLOT_ROWS : (group[r - 1] + 1) * SLOT_ROWS, :])
-                start = r
-        left = left[0] if len(left) == 1 else jnp.concatenate(left, axis=0)
-        product = jnp.dot(
-            left, gathered[q], precision=HIGH, preferred_element_type=jnp.float32
-        )
+        product = multiply(matrix, slice(q * LANES, (q + 1) * LANES), gathered[q])
         acc = product[0:SLOT_ROWS]
         for slot in range(1, 8):
             piece = product[slot * SLOT_ROWS : (slot + 1) * SLOT_ROWS]
@@ -518,7 +530,7 @@
     find_places(slim, range(16), atom, bricks_place, places)
 
 
-def join_near_kernel(matrix, second, own_first, near_second, tall, places):
+def join_near_kernel(matrix, second, own_first, near_second, head, middle, tail, places, tall):
     even = is_even()
     for q in range(4):
         if q < 3:
@@ -531,9 +543,13 @@
         tall[q * 128 + 32 : q * 128 + 96] = matrix[q * 64 : q * 64 + 64]
         tall[q * 128 + 96 : q * 128 + 128] = high
     find_places(tall, range(32), tall_near_atom, first_place(even), places)
-
-
-def later_kernel(wide, slim, matrix, far, third_places, fourth_places):
+    head[...], middle[...], tail[...] = thirds(tall[...])
+
+
+def later_kernel(
+    wide, slim, matrix, far_head, far_middle, far_tail, head, middle, tail,
+    third_places, fourth_places, far,
+):
     even = is_even()
     for q in range(4):
         one, two = wide[q * 96 : q * 96 + 96], slim[q * 64 : q * 64 + 64]
@@ -542,6 +558,8 @@
         far[q * 96 : q * 96 + 96] = jnp.where(even, below, above)
     find_places(far, range(24), far_atom, SECOND_PLACE, third_places)
     find_places(matrix, range(ATOMS), near_atom, THIRD_PLACE, fourth_places)
+    far_head[...], far_middle[...], far_tail[...] = thirds(far[...])
+    head[...], middle[...], tail[...] = thirds(matrix[...])
 
 
 WIDE_FLOPS = 1 << 28
@@ -550,7 +568,7 @@
 def first_tiles(rows, places, start, from_y, from_xy, from_x, bricks, field, gathered):
     pieces = [start[...]] + [unpack_bricks(ref[64:72]) for ref in (from_y, from_x, from_xy)]
     set_tiles(field, pieces + [unpack_bricks(brick) for brick in bricks])
-    return couple(rows, range(rows.shape[0] // SLOT_ROWS), field, places, gathered)
+    return couple(rows, rows.shape[0] // SLOT_ROWS, field, places, gathered)
 
 
 def first_wide_kernel(
@@ -570,14 +588,18 @@
     )
 
 
-def second_kernel(tall, places, own, from_x, from_y, from_xy, out, field, gathered):
+def second_kernel(
+    head, middle, tail, places, own, from_x, from_y, from_xy, out, field, gathered
+):
     set_tiles(field, (from_xy, from_x, from_y, own))
-    out[...] = couple(tall, range(32), field, places, gathered)
-
-
-def third_kernel(wide, places, own, from_x, from_y, from_xy, out, field, gathered):
+    out[...] = couple((head, middle, tail), 32, field, places, gathered)
+
+
+def third_kernel(
+    head, middle, tail, places, own, from_x, from_y, from_xy, out, field, gathered
+):
     set_tiles(field, (own, from_y, from_x, from_xy))
-    out[...] = couple(wide, range(24), field, places, gathered)
+    out[...] = couple((head, middle, tail), 24, field, places, gathered)
 
 
 def pick_kernel(own, from_x, from_y, from_xy, second, first_own, second_own):
@@ -589,18 +611,23 @@
 
 
 def last_kernel(
-    matrix, places, own, from_x, from_y, from_xy, start, first, second, third_out, out,
+    head, middle, tail, places, own, from_x, from_y, from_xy, start, first, second,
+    third_out, out,
     field, gathered,
 ):
     pieces = from_xy, from_x, from_y, own
     set_tiles(field, pieces)
-    fourth = couple(matrix, range(ATOMS), field, places, gathered)
+    fourth = couple((head, middle, tail), ATOMS, field, places, gathered)
     third = pick_own(pieces, THIRD_PLACE)
     third_out[...] = third
     gram_kernel([start[...], first[...], second[...], third, fourth], out)
 
 
 SMEM = pl.BlockSpec(memory_space=pltpu.SMEM)
+
+
+def cut(atoms):
+    return jax.ShapeDtypeStruct((atoms * SLOT_ROWS, WIDE), jnp.bfloat16)
 
 
 def whole_numbers(rows):
@@ -630,7 +657,7 @@
 def scratch_for(tiles, groups):
     return (
         pltpu.VMEM((tiles * 8, SLOT_ROWS, LANES), jnp.float32),
-        pltpu.VMEM((groups, WIDE, LANES), jnp.float32),
+        pltpu.VMEM((groups, CODE, LANES), jnp.float32),
     )
 
 
@@ -699,30 +726,32 @@
         slim, slim_places, start, *sides, second_layers, first,
         scratch=scratch_for(16, 2),
     )
-    tall, places = call(
-        join_near_kernel, [(32 * SLOT_ROWS, WIDE), whole_numbers(32)],
+    *tall, places = call(
+        join_near_kernel, [cut(32)] * 3 + [whole_numbers(32)],
         matrix, second_layers, own_layers, near_layers,
+        scratch=[pltpu.VMEM((32 * SLOT_ROWS, WIDE), jnp.float32)],
     )
     pieces = fetch_three(first, first, first, -1)
     (second,) = call(
-        second_kernel, [(SLOT_ROWS, 4 * LANES)], tall, places, first, *pieces,
+        second_kernel, [(SLOT_ROWS, 4 * LANES)], *tall, places, first, *pieces,
         scratch=scratch_for(20, 4),
     )
     first_own, second_own = call(pick_kernel, [flat] * 2, first, *pieces, second)
-    far, third_places, fourth_places = call(
+    *parts, third_places, fourth_places = call(
         later_kernel,
-        [(24 * SLOT_ROWS, WIDE), whole_numbers(24), whole_numbers(ATOMS)],
+        [cut(24)] * 3 + [cut(ATOMS)] * 3 + [whole_numbers(24), whole_numbers(ATOMS)],
         wide, slim, matrix,
+        scratch=[pltpu.VMEM((24 * SLOT_ROWS, WIDE), jnp.float32)],
     )
     (third,) = call(
         third_kernel, [(SLOT_ROWS, 3 * LANES)],
-        far, third_places, second, *fetch_three(second, second, second, 1),
+        *parts[:3], third_places, second, *fetch_three(second, second, second, 1),
         scratch=scratch_for(16, 3),
     )
     third_own, message = call(
         last_kernel,
         [flat, (lax.axis_size("gx") * lax.axis_size("gy"), 4, LANES)],
-        matrix, fourth_places, third, *fetch_three(third, third, third, -1),
+        *parts[3:], fourth_places, third, *fetch_three(third, third, third, -1),
         start, first_own, second_own,
         scratch=scratch_for(12, 2),
     )

time: 129 us -> 128 us (level)
  no operation moved by 1% of the time
where the time goes in v10:
time: 128 us; the launch traced here: 127 us
  starting transfers between devices  64.6 us (50%)
  blocking collectives  38.4 us (30%)
  Pallas kernels  14.7 us (11%)
  waiting for transfers between devices  9.26 us (7%)
    ppermute x12, starting transfers between devices, fetch(): return lax.ppermute(value, AXES, pairs)  52.5 us
    all_to_all x1, blocking collectives, body(): message = lax.all_to_all(message, ('gx', 'gy'), 0, 0, tiled=True)  19.7 us
    all_to_all x1, blocking collectives, body(): message = lax.all_to_all(message, 'gz', 0, 0, tiled=True)  18.8 us
    pallas_call x16, Pallas kernels, call(): pl.pallas_call(kernel, out_shape=shapes, in_specs=[SMEM if operand.dtype...  14.7 us
    ppermute x12, waiting for transfers between devices, fetch(): return lax.ppermute(value, AXES, pairs)  8.59 us
    ppermute x2, starting transfers between devices, swap_layers(): lax.ppermute(to_second, 'gz', odd)  7.41 us
    ppermute x2, starting transfers between devices, swap_layers(): lax.ppermute(to_first, 'gz', even)  4.73 us
  transfers between devices with their start and end apart: 16, of which 6 were waited for; matrix products, arithmetic and copies ran while one was open for 0% of the time, Pallas kernels for 4%

profile of v10, /device:TPU:1, one launch (start us, length us, event | category | flops | bytes accessed | tf_op | source)
XLA Modules:
  0.0 127.3 jit_solution(2782376446918636738)
XLA Ops:
  1.2 11.5 %collective-permute-start = (f32[72,512]{1,0:T(8,128)S(1)}, f32[72,512]{1,0:T(8,128)S(1)}, u32[]{:S(2)}, u32[]{:S(2)}) collective-permute-start(f32[72,512]{1,0:T(8,128)S(1)} %get-tuple-element.35), channel_id=1, source_target_pairs={{16,0},{17,1},{18,2},{19,3},{20,4},{21,5},{22,6},{23,7},{24,8},{25... | collective-permute-start | bytes 442376 | tf_op jit(solution)/shard_map/ppermute | solution.py:672
  12.7 5.1 %collective-permute-start.1 = (f32[72,512]{1,0:T(8,128)S(1)}, f32[72,512]{1,0:T(8,128)S(1)}, u32[]{:S(2)}, u32[]{:S(2)}) collective-permute-start(f32[72,512]{1,0:T(8,128)S(1)} %get-tuple-element.36), channel_id=1, source_target_pairs={{80,0},{81,1},{82,2},{83,3},{84,4},{85,5},{86,6},{87,7},{88,8},{89... | collective-permute-start | bytes 442376 | tf_op jit(solution)/shard_map/ppermute | solution.py:672
  17.8 3.0 %collective-permute-start.2 = (f32[72,512]{1,0:T(8,128)S(1)}, f32[72,512]{1,0:T(8,128)S(1)}, u32[]{:S(2)}, u32[]{:S(2)}) collective-permute-start(f32[72,512]{1,0:T(8,128)S(1)} %get-tuple-element.37), channel_id=1, source_target_pairs={{64,0},{65,1},{66,2},{67,3},{68,4},{69,5},{70,6},{71,7},{72,8},{73... | collective-permute-start | bytes 442376 | tf_op jit(solution)/shard_map/ppermute | solution.py:672
  20.8 3.3 %collective-permute-done.from_y = f32[72,512]{1,0:T(8,128)S(1)} collective-permute-done((f32[72,512]{1,0:T(8,128)S(1)}, f32[72,512]{1,0:T(8,128)S(1)}, u32[]{:S(2)}, u32[]{:S(2)}) %collective-permute-start) | collective-permute-done | bytes 147488 | tf_op jit(solution)/shard_map/ppermute | solution.py:672
  24.5 4.8 %collective-permute-start.5 = (f32[224,512]{1,0:T(8,128)S(1)}, f32[224,512]{1,0:T(8,128)S(1)}, u32[]{:S(2)}, u32[]{:S(2)}) collective-permute-start(f32[224,512]{1,0:T(8,128)S(1)} %shard_map.51), channel_id=1, source_target_pairs={{0,15},{1,2},{2,1},{3,4},{4,3},{5,6},{6,5},{7,8},{8,7},{9,10},{10,... | collective-permute-start | bytes 1376264 | tf_op jit(solution)/shard_map/ppermute | solution.py:683
  29.4 2.8 %collective-permute-start.3 = (f32[168,512]{1,0:T(8,128)S(1)}, f32[168,512]{1,0:T(8,128)S(1)}, u32[]{:S(2)}, u32[]{:S(2)}) collective-permute-start(f32[168,512]{1,0:T(8,128)S(1)} %shard_map.47), channel_id=1, source_target_pairs={{0,1},{1,0},{2,3},{3,2},{4,5},{5,4},{6,7},{7,6},{8,9},{9,8},{10,11... | collective-permute-start | bytes 1032200 | tf_op jit(solution)/shard_map/ppermute | solution.py:683
  34.2 2.6 %collective-permute-start.6 = (f32[96,512]{1,0:T(8,128)S(1)}, f32[96,512]{1,0:T(8,128)S(1)}, u32[]{:S(2)}, u32[]{:S(2)}) collective-permute-start(f32[96,512]{1,0:T(8,128)S(1)} %get-tuple-element.52), channel_id=1, source_target_pairs={{0,15},{1,2},{2,1},{3,4},{4,3},{5,6},{6,5},{7,8},{8,7},{9,10},{10,... | collective-permute-start | bytes 589832 | tf_op jit(solution)/shard_map/ppermute | solution.py:683
  36.9 2.2 %shard_map.50.before = f32[16,384]{1,0:T(8,128)S(1)} custom-call(f32[384,512]{1,0:T(8,128)S(1)} %get-tuple-element.40.wide, s32[24,128]{1,0:T(8,128)S(1)} %get-tuple-element.41.places, f32[16,256]{1,0:T(8,128)S(1)} %get-tuple-element.38.start.refs_0_, f32[72,512]{1,0:T(8,128)S(1)} %collective-permute-done.from_y, ...), custom_call_target="tpu_custom_call" | custom-call | flops 268435456 | bytes 4194304 | tf_op jit(solution)/shard_map/pallas_call | solution.py:642
  41.7 3.2 %collective-permute-start.9 = (f32[16,640]{1,0:T(8,128)S(1)}, f32[16,640]{1,0:T(8,128)S(1)}, u32[]{:S(2)}, u32[]{:S(2)}) collective-permute-start(f32[16,640]{1,0:T(8,128)S(1)} %shard_map.55.own), channel_id=1, source_target_pairs={{496,0},{497,1},{498,2},{499,3},{500,4},{501,5},{502,6},{503,7},{5... | collective-permute-start | bytes 122888 | tf_op jit(solution)/shard_map/ppermute | solution.py:672
  44.9 4.3 %collective-permute-start.8 = (f32[16,640]{1,0:T(8,128)S(1)}, f32[16,640]{1,0:T(8,128)S(1)}, u32[]{:S(2)}, u32[]{:S(2)}) collective-permute-start(f32[16,640]{1,0:T(8,128)S(1)} %shard_map.55.own), channel_id=1, source_target_pairs={{48,0},{49,1},{50,2},{51,3},{52,4},{53,5},{54,6},{55,7},{56,8},{57... | collective-permute-start | bytes 122888 | tf_op jit(solution)/shard_map/ppermute | solution.py:672
  49.2 3.2 %collective-permute-start.7 = (f32[16,640]{1,0:T(8,128)S(1)}, f32[16,640]{1,0:T(8,128)S(1)}, u32[]{:S(2)}, u32[]{:S(2)}) collective-permute-start(f32[16,640]{1,0:T(8,128)S(1)} %shard_map.55.own), channel_id=1, source_target_pairs={{448,0},{449,1},{450,2},{451,3},{452,4},{453,5},{454,6},{455,7},{4... | collective-permute-start | bytes 122888 | tf_op jit(solution)/shard_map/ppermute | solution.py:672
  53.0 2.4 %collective-permute-done.7.from_x = f32[16,640]{1,0:T(8,128)S(1)} collective-permute-done((f32[16,640]{1,0:T(8,128)S(1)}, f32[16,640]{1,0:T(8,128)S(1)}, u32[]{:S(2)}, u32[]{:S(2)}) %collective-permute-start.7) | collective-permute-done | bytes 40992 | tf_op jit(solution)/shard_map/ppermute | solution.py:672
  55.5 2.3 %shard_map.56.own.second = f32[16,512]{1,0:T(8,128)S(1)} custom-call(bf16[512,512]{1,0:T(8,128)(2,1)S(1)} %get-tuple-element.53.head, bf16[512,512]{1,0:T(8,128)(2,1)S(1)} %get-tuple-element.54.middle, bf16[512,512]{1,0:T(8,128)(2,1)S(1)} %get-tuple-element.55.tail, s32[32,128]{1,0:T(8,128)S(1)} %get-tuple-element.56.places, f32[16,640]{1,0:T(8,128)S(1)} %shard_map.55.own, ...), custom_call_target="tpu_custom_call" | custom-call | tf_op jit(solution)/shard_map/pallas_call | solution.py:642
  57.8 4.3 %collective-permute-start.12 = (f32[16,512]{1,0:T(8,128)S(1)}, f32[16,512]{1,0:T(8,128)S(1)}, u32[]{:S(2)}, u32[]{:S(2)}) collective-permute-start(f32[16,512]{1,0:T(8,128)S(1)} %shard_map.56.own.second), channel_id=1, source_target_pairs={{80,0},{81,1},{82,2},{83,3},{84,4},{85,5},{86,6},{87,7},{88,8},{89... | collective-permute-start | bytes 98312 | tf_op jit(solution)/shard_map/ppermute | solution.py:672
  62.1 3.6 %collective-permute-start.11 = (f32[16,512]{1,0:T(8,128)S(1)}, f32[16,512]{1,0:T(8,128)S(1)}, u32[]{:S(2)}, u32[]{:S(2)}) collective-permute-start(f32[16,512]{1,0:T(8,128)S(1)} %shard_map.56.own.second), channel_id=1, source_target_pairs={{16,0},{17,1},{18,2},{19,3},{20,4},{21,5},{22,6},{23,7},{24,8},{25... | collective-permute-start | bytes 98312 | tf_op jit(solution)/shard_map/ppermute | solution.py:672
  65.7 4.0 %collective-permute-start.10 = (f32[16,512]{1,0:T(8,128)S(1)}, f32[16,512]{1,0:T(8,128)S(1)}, u32[]{:S(2)}, u32[]{:S(2)}) collective-permute-start(f32[16,512]{1,0:T(8,128)S(1)} %shard_map.56.own.second), channel_id=1, source_target_pairs={{64,0},{65,1},{66,2},{67,3},{68,4},{69,5},{70,6},{71,7},{72,8},{73... | collective-permute-start | bytes 98312 | tf_op jit(solution)/shard_map/ppermute | solution.py:672
  70.8 2.0 %shard_map.57.own = f32[16,384]{1,0:T(8,128)S(1)} custom-call(bf16[384,512]{1,0:T(8,128)(2,1)S(1)} %get-tuple-element.48.head, bf16[384,512]{1,0:T(8,128)(2,1)S(1)} %get-tuple-element.49.middle, bf16[384,512]{1,0:T(8,128)(2,1)S(1)} %get-tuple-element.50.tail, s32[24,128]{1,0:T(8,128)S(1)} %get-tuple-element.51.places, f32[16,512]{1,0:T(8,128)S(1)} %shard_map.56.own.second, ...), custom_call_target="tpu_custom_call" | custom-call | tf_op jit(solution)/shard_map/pallas_call | solution.py:642
  72.8 2.2 %collective-permute-start.15 = (f32[16,384]{1,0:T(8,128)S(1)}, f32[16,384]{1,0:T(8,128)S(1)}, u32[]{:S(2)}, u32[]{:S(2)}) collective-permute-start(f32[16,384]{1,0:T(8,128)S(1)} %shard_map.57.own), channel_id=1, source_target_pairs={{496,0},{497,1},{498,2},{499,3},{500,4},{501,5},{502,6},{503,7},{5... | collective-permute-start | bytes 73736 | tf_op jit(solution)/shard_map/ppermute | solution.py:672
  75.0 4.6 %collective-permute-start.14 = (f32[16,384]{1,0:T(8,128)S(1)}, f32[16,384]{1,0:T(8,128)S(1)}, u32[]{:S(2)}, u32[]{:S(2)}) collective-permute-start(f32[16,384]{1,0:T(8,128)S(1)} %shard_map.57.own), channel_id=1, source_target_pairs={{48,0},{49,1},{50,2},{51,3},{52,4},{53,5},{54,6},{55,7},{56,8},{57... | collective-permute-start | bytes 73736 | tf_op jit(solution)/shard_map/ppermute | solution.py:672
  79.6 3.5 %collective-permute-start.13 = (f32[16,384]{1,0:T(8,128)S(1)}, f32[16,384]{1,0:T(8,128)S(1)}, u32[]{:S(2)}, u32[]{:S(2)}) collective-permute-start(f32[16,384]{1,0:T(8,128)S(1)} %shard_map.57.own), channel_id=1, source_target_pairs={{448,0},{449,1},{450,2},{451,3},{452,4},{453,5},{454,6},{455,7},{4... | collective-permute-start | bytes 73736 | tf_op jit(solution)/shard_map/ppermute | solution.py:672
  83.2 2.2 %collective-permute-done.13.from_x = f32[16,384]{1,0:T(8,128)S(1)} collective-permute-done((f32[16,384]{1,0:T(8,128)S(1)}, f32[16,384]{1,0:T(8,128)S(1)}, u32[]{:S(2)}, u32[]{:S(2)}) %collective-permute-start.13) | collective-permute-done | bytes 24608 | tf_op jit(solution)/shard_map/ppermute | solution.py:672
  85.4 2.0 %shard_map.59 = (f32[16,256]{1,0:T(8,128)S(1)}, f32[32,4,128]{2,1,0:T(4,128)S(1)}) custom-call(bf16[256,512]{1,0:T(8,128)(2,1)S(1)} %get-tuple-element.44.head, bf16[256,512]{1,0:T(8,128)(2,1)S(1)} %get-tuple-element.45.middle, bf16[256,512]{1,0:T(8,128)(2,1)S(1)} %get-tuple-element.46.tail, s32[16,128]{1,0:T(8,128)S(1)} %get-tuple-element.47.places, ...), custom_call_target="tpu_custom_call" | custom-call | tf_op jit(solution)/shard_map/pallas_call | solution.py:642
  87.4 19.7 %all_to_all.10.ref = f32[32,4,128]{2,1,0:T(4,128)S(1)} all-to-all(f32[32,4,128]{2,1,0:T(4,128)S(1)} %get-tuple-element.61), channel_id=1, replica_groups=mesh['gx'=8,'gy'=4,'gz'=16] {'gx','gy'}, dimensions={0} | all-to-all | bytes 131072 | tf_op jit(solution)/shard_map/all_to_all | solution.py:758
  107.1 18.8 %all_to_all.11.ref = f32[16,4,128]{2,1,0:T(4,128)S(1)} all-to-all(f32[16,4,128]{2,1,0:T(4,128)S(1)} %shard_map.60), channel_id=1, replica_groups=mesh['gx'=8,'gy'=4,'gz'=16] {'gz'}, dimensions={0} | all-to-all | bytes 65536 | tf_op jit(solution)/shard_map/all_to_all | solution.py:760
  (26 shorter events, 9.5 us)
Async XLA Ops:
  1.2 22.9 %collective-permute-start = (f32[72,512]{1,0:T(8,128)S(1)}, f32[72,512]{1,0:T(8,128)S(1)}, u32[]{:S(2)}, u32[]{:S(2)}) collective-permute-start(f32[72,512]{1,0:T(8,128)S(1)} %get-tuple-element.35), channel_id=1, source_target_pairs={{16,0},{17,1},{18,2},{19,3},{20,4},{21,5},{22,6},{23,7},{24,8},{25... | collective-permute-start | bytes 442376 | tf_op jit(solution)/shard_map/ppermute | solution.py:672
  12.7 11.4 %collective-permute-start.1 = (f32[72,512]{1,0:T(8,128)S(1)}, f32[72,512]{1,0:T(8,128)S(1)}, u32[]{:S(2)}, u32[]{:S(2)}) collective-permute-start(f32[72,512]{1,0:T(8,128)S(1)} %get-tuple-element.36), channel_id=1, source_target_pairs={{80,0},{81,1},{82,2},{83,3},{84,4},{85,5},{86,6},{87,7},{88,8},{89... | collective-permute-start | bytes 442376 | tf_op jit(solution)/shard_map/ppermute | solution.py:672
  17.8 6.7 %collective-permute-start.2 = (f32[72,512]{1,0:T(8,128)S(1)}, f32[72,512]{1,0:T(8,128)S(1)}, u32[]{:S(2)}, u32[]{:S(2)}) collective-permute-start(f32[72,512]{1,0:T(8,128)S(1)} %get-tuple-element.37), channel_id=1, source_target_pairs={{64,0},{65,1},{66,2},{67,3},{68,4},{69,5},{70,6},{71,7},{72,8},{73... | collective-permute-start | bytes 442376 | tf_op jit(solution)/shard_map/ppermute | solution.py:672
  24.5 15.3 %collective-permute-start.5 = (f32[224,512]{1,0:T(8,128)S(1)}, f32[224,512]{1,0:T(8,128)S(1)}, u32[]{:S(2)}, u32[]{:S(2)}) collective-permute-start(f32[224,512]{1,0:T(8,128)S(1)} %shard_map.51), channel_id=1, source_target_pairs={{0,15},{1,2},{2,1},{3,4},{4,3},{5,6},{6,5},{7,8},{8,7},{9,10},{10,... | collective-permute-start | bytes 1376264 | tf_op jit(solution)/shard_map/ppermute | solution.py:683
  29.4 7.4 %collective-permute-start.3 = (f32[168,512]{1,0:T(8,128)S(1)}, f32[168,512]{1,0:T(8,128)S(1)}, u32[]{:S(2)}, u32[]{:S(2)}) collective-permute-start(f32[168,512]{1,0:T(8,128)S(1)} %shard_map.47), channel_id=1, source_target_pairs={{0,1},{1,0},{2,3},{3,2},{4,5},{5,4},{6,7},{7,6},{8,9},{9,8},{10,11... | collective-permute-start | bytes 1032200 | tf_op jit(solution)/shard_map/ppermute | solution.py:683
  32.2 4.6 %collective-permute-start.4 = (f32[152,512]{1,0:T(8,128)S(1)}, f32[152,512]{1,0:T(8,128)S(1)}, u32[]{:S(2)}, u32[]{:S(2)}) collective-permute-start(f32[152,512]{1,0:T(8,128)S(1)} %get-tuple-element.39), channel_id=1, source_target_pairs={{0,1},{1,0},{2,3},{3,2},{4,5},{5,4},{6,7},{7,6},{8,9},{9,8},{10,11... | collective-permute-start | bytes 933896 | tf_op jit(solution)/shard_map/ppermute | solution.py:683
  34.2 18.3 %collective-permute-start.6 = (f32[96,512]{1,0:T(8,128)S(1)}, f32[96,512]{1,0:T(8,128)S(1)}, u32[]{:S(2)}, u32[]{:S(2)}) collective-permute-start(f32[96,512]{1,0:T(8,128)S(1)} %get-tuple-element.52), channel_id=1, source_target_pairs={{0,15},{1,2},{2,1},{3,4},{4,3},{5,6},{6,5},{7,8},{8,7},{9,10},{10,... | collective-permute-start | bytes 589832 | tf_op jit(solution)/shard_map/ppermute | solution.py:683
  41.7 11.3 %collective-permute-start.9 = (f32[16,640]{1,0:T(8,128)S(1)}, f32[16,640]{1,0:T(8,128)S(1)}, u32[]{:S(2)}, u32[]{:S(2)}) collective-permute-start(f32[16,640]{1,0:T(8,128)S(1)} %shard_map.55.own), channel_id=1, source_target_pairs={{496,0},{497,1},{498,2},{499,3},{500,4},{501,5},{502,6},{503,7},{5... | collective-permute-start | bytes 122888 | tf_op jit(solution)/shard_map/ppermute | solution.py:672
  44.9 8.1 %collective-permute-start.8 = (f32[16,640]{1,0:T(8,128)S(1)}, f32[16,640]{1,0:T(8,128)S(1)}, u32[]{:S(2)}, u32[]{:S(2)}) collective-permute-start(f32[16,640]{1,0:T(8,128)S(1)} %shard_map.55.own), channel_id=1, source_target_pairs={{48,0},{49,1},{50,2},{51,3},{52,4},{53,5},{54,6},{55,7},{56,8},{57... | collective-permute-start | bytes 122888 | tf_op jit(solution)/shard_map/ppermute | solution.py:672
  49.2 6.3 %collective-permute-start.7 = (f32[16,640]{1,0:T(8,128)S(1)}, f32[16,640]{1,0:T(8,128)S(1)}, u32[]{:S(2)}, u32[]{:S(2)}) collective-permute-start(f32[16,640]{1,0:T(8,128)S(1)} %shard_map.55.own), channel_id=1, source_target_pairs={{448,0},{449,1},{450,2},{451,3},{452,4},{453,5},{454,6},{455,7},{4... | collective-permute-start | bytes 122888 | tf_op jit(solution)/shard_map/ppermute | solution.py:672
  57.8 12.7 %collective-permute-start.12 = (f32[16,512]{1,0:T(8,128)S(1)}, f32[16,512]{1,0:T(8,128)S(1)}, u32[]{:S(2)}, u32[]{:S(2)}) collective-permute-start(f32[16,512]{1,0:T(8,128)S(1)} %shard_map.56.own.second), channel_id=1, source_target_pairs={{80,0},{81,1},{82,2},{83,3},{84,4},{85,5},{86,6},{87,7},{88,8},{89... | collective-permute-start | bytes 98312 | tf_op jit(solution)/shard_map/ppermute | solution.py:672
  62.1 8.4 %collective-permute-start.11 = (f32[16,512]{1,0:T(8,128)S(1)}, f32[16,512]{1,0:T(8,128)S(1)}, u32[]{:S(2)}, u32[]{:S(2)}) collective-permute-start(f32[16,512]{1,0:T(8,128)S(1)} %shard_map.56.own.second), channel_id=1, source_target_pairs={{16,0},{17,1},{18,2},{19,3},{20,4},{21,5},{22,6},{23,7},{24,8},{25... | collective-permute-start | bytes 98312 | tf_op jit(solution)/shard_map/ppermute | solution.py:672
  65.7 5.0 %collective-permute-start.10 = (f32[16,512]{1,0:T(8,128)S(1)}, f32[16,512]{1,0:T(8,128)S(1)}, u32[]{:S(2)}, u32[]{:S(2)}) collective-permute-start(f32[16,512]{1,0:T(8,128)S(1)} %shard_map.56.own.second), channel_id=1, source_target_pairs={{64,0},{65,1},{66,2},{67,3},{68,4},{69,5},{70,6},{71,7},{72,8},{73... | collective-permute-start | bytes 98312 | tf_op jit(solution)/shard_map/ppermute | solution.py:672
  72.8 10.4 %collective-permute-start.15 = (f32[16,384]{1,0:T(8,128)S(1)}, f32[16,384]{1,0:T(8,128)S(1)}, u32[]{:S(2)}, u32[]{:S(2)}) collective-permute-start(f32[16,384]{1,0:T(8,128)S(1)} %shard_map.57.own), channel_id=1, source_target_pairs={{496,0},{497,1},{498,2},{499,3},{500,4},{501,5},{502,6},{503,7},{5... | collective-permute-start | bytes 73736 | tf_op jit(solution)/shard_map/ppermute | solution.py:672
  75.0 8.2 %collective-permute-start.14 = (f32[16,384]{1,0:T(8,128)S(1)}, f32[16,384]{1,0:T(8,128)S(1)}, u32[]{:S(2)}, u32[]{:S(2)}) collective-permute-start(f32[16,384]{1,0:T(8,128)S(1)} %shard_map.57.own), channel_id=1, source_target_pairs={{48,0},{49,1},{50,2},{51,3},{52,4},{53,5},{54,6},{55,7},{56,8},{57... | collective-permute-start | bytes 73736 | tf_op jit(solution)/shard_map/ppermute | solution.py:672
  79.6 5.8 %collective-permute-start.13 = (f32[16,384]{1,0:T(8,128)S(1)}, f32[16,384]{1,0:T(8,128)S(1)}, u32[]{:S(2)}, u32[]{:S(2)}) collective-permute-start(f32[16,384]{1,0:T(8,128)S(1)} %shard_map.57.own), channel_id=1, source_target_pairs={{448,0},{449,1},{450,2},{451,3},{452,4},{453,5},{454,6},{455,7},{4... | collective-permute-start | bytes 73736 | tf_op jit(solution)/shard_map/ppermute | solution.py:672

commit v11 on v10

--- a/solution.py
+++ b/solution.py
@@ -589,20 +589,20 @@
 
 
 def second_kernel(
-    head, middle, tail, places, own, from_x, from_y, from_xy, out, field, gathered
+    head, middle, tail, places, own, from_x, from_xy, from_y, out, field, gathered
 ):
     set_tiles(field, (from_xy, from_x, from_y, own))
     out[...] = couple((head, middle, tail), 32, field, places, gathered)
 
 
 def third_kernel(
-    head, middle, tail, places, own, from_x, from_y, from_xy, out, field, gathered
+    head, middle, tail, places, own, from_x, from_xy, from_y, out, field, gathered
 ):
     set_tiles(field, (own, from_y, from_x, from_xy))
     out[...] = couple((head, middle, tail), 24, field, places, gathered)
 
 
-def pick_kernel(own, from_x, from_y, from_xy, second, first_own, second_own):
+def pick_kernel(own, from_x, from_xy, from_y, second, first_own, second_own):
     pieces = from_xy, from_x, from_y, own
     first_own[...] = jnp.where(
         is_even(), pick_own(pieces, first_place(True)), pick_own(pieces, first_place(False))
@@ -611,7 +611,7 @@
 
 
 def last_kernel(
-    head, middle, tail, places, own, from_x, from_y, from_xy, start, first, second,
+    head, middle, tail, places, own, from_x, from_xy, from_y, start, first, second,
     third_out, out,
     field, gathered,
 ):
@@ -673,7 +673,7 @@
 
 
 def fetch_three(to_x, to_y, to_xy, sign):
-    return fetch(to_x, sign, 0), fetch(to_y, 0, sign), fetch(to_xy, sign, sign)
+    return fetch(to_x, sign, 0), fetch(to_xy, sign, sign), fetch(to_y, 0, sign)
 
 
 def swap_layers(to_first, to_second):
@@ -699,7 +699,7 @@
         ],
         place=pl.BlockSpec(memory_space=pltpu.HBM),
     )
-    from_x, from_y, from_xy = fetch_three(*out, 1)
+    from_x, from_xy, from_y = fetch_three(*out, 1)
     sides = from_y, from_xy, from_x
     (to_second,) = call(spread_second_kernel, [(224, WIDE)], matrix, *sides, start)
     (to_first,) = call(spread_first_kernel, [(168, WIDE)], *sides)

time: 128 us -> 128 us (level)
  transfers between devices with their start and end apart: 16 -> 16, of which waited for: 6 -> 8; matrix products, arithmetic and copies ran while one was open for 0% -> 0% of each run, Pallas kernels for 4% -> 4%
where the time goes in v11:
time: 128 us
  starting transfers between devices  64 us (50%)
  blocking collectives  38.5 us (30%)
  Pallas kernels  14.7 us (11%)
  waiting for transfers between devices  10.2 us (8%)
    ppermute x12, starting transfers between devices, fetch(): return lax.ppermute(value, AXES, pairs)  51.8 us
    all_to_all x1, blocking collectives, body(): message = lax.all_to_all(message, ('gx', 'gy'), 0, 0, tiled=True)  20 us
    all_to_all x1, blocking collectives, body(): message = lax.all_to_all(message, 'gz', 0, 0, tiled=True)  18.5 us
    pallas_call x16, Pallas kernels, call(): pl.pallas_call(kernel, out_shape=shapes, in_specs=[SMEM if operand.dtype...  14.7 us
    ppermute x12, waiting for transfers between devices, fetch(): return lax.ppermute(value, AXES, pairs)  9.56 us
    ppermute x2, starting transfers between devices, swap_layers(): lax.ppermute(to_second, 'gz', odd)  7.41 us
    ppermute x2, starting transfers between devices, swap_layers(): lax.ppermute(to_first, 'gz', even)  4.73 us
  transfers between devices with their start and end apart: 16, of which 8 were waited for; matrix products, arithmetic and copies ran while one was open for 0% of the time, Pallas kernels for 4%

profile of v11, /device:TPU:1, one launch (start us, length us, event | category | flops | bytes accessed | tf_op | source)
XLA Modules:
  0.0 127.7 jit_solution(13472989188033491125)
XLA Ops:
  1.2 11.5 %collective-permute-start = (f32[72,512]{1,0:T(8,128)S(1)}, f32[72,512]{1,0:T(8,128)S(1)}, u32[]{:S(2)}, u32[]{:S(2)}) collective-permute-start(f32[72,512]{1,0:T(8,128)S(1)} %get-tuple-element.35), channel_id=1, source_target_pairs={{16,0},{17,1},{18,2},{19,3},{20,4},{21,5},{22,6},{23,7},{24,8},{25... | collective-permute-start | bytes 442376 | tf_op jit(solution)/shard_map/ppermute | solution.py:672
  12.7 5.1 %collective-permute-start.1 = (f32[72,512]{1,0:T(8,128)S(1)}, f32[72,512]{1,0:T(8,128)S(1)}, u32[]{:S(2)}, u32[]{:S(2)}) collective-permute-start(f32[72,512]{1,0:T(8,128)S(1)} %get-tuple-element.36), channel_id=1, source_target_pairs={{80,0},{81,1},{82,2},{83,3},{84,4},{85,5},{86,6},{87,7},{88,8},{89... | collective-permute-start | bytes 442376 | tf_op jit(solution)/shard_map/ppermute | solution.py:672
  17.8 3.0 %collective-permute-start.2 = (f32[72,512]{1,0:T(8,128)S(1)}, f32[72,512]{1,0:T(8,128)S(1)}, u32[]{:S(2)}, u32[]{:S(2)}) collective-permute-start(f32[72,512]{1,0:T(8,128)S(1)} %get-tuple-element.37), channel_id=1, source_target_pairs={{64,0},{65,1},{66,2},{67,3},{68,4},{69,5},{70,6},{71,7},{72,8},{73... | collective-permute-start | bytes 442376 | tf_op jit(solution)/shard_map/ppermute | solution.py:672
  20.8 3.3 %collective-permute-done.from_y = f32[72,512]{1,0:T(8,128)S(1)} collective-permute-done((f32[72,512]{1,0:T(8,128)S(1)}, f32[72,512]{1,0:T(8,128)S(1)}, u32[]{:S(2)}, u32[]{:S(2)}) %collective-permute-start) | collective-permute-done | bytes 147488 | tf_op jit(solution)/shard_map/ppermute | solution.py:672
  24.5 4.8 %collective-permute-start.5 = (f32[224,512]{1,0:T(8,128)S(1)}, f32[224,512]{1,0:T(8,128)S(1)}, u32[]{:S(2)}, u32[]{:S(2)}) collective-permute-start(f32[224,512]{1,0:T(8,128)S(1)} %shard_map.51), channel_id=1, source_target_pairs={{0,15},{1,2},{2,1},{3,4},{4,3},{5,6},{6,5},{7,8},{8,7},{9,10},{10,... | collective-permute-start | bytes 1376264 | tf_op jit(solution)/shard_map/ppermute | solution.py:683
  29.4 2.8 %collective-permute-start.3 = (f32[168,512]{1,0:T(8,128)S(1)}, f32[168,512]{1,0:T(8,128)S(1)}, u32[]{:S(2)}, u32[]{:S(2)}) collective-permute-start(f32[168,512]{1,0:T(8,128)S(1)} %shard_map.47), channel_id=1, source_target_pairs={{0,1},{1,0},{2,3},{3,2},{4,5},{5,4},{6,7},{7,6},{8,9},{9,8},{10,11... | collective-permute-start | bytes 1032200 | tf_op jit(solution)/shard_map/ppermute | solution.py:683
  32.2 1.9 %collective-permute-start.4 = (f32[152,512]{1,0:T(8,128)S(1)}, f32[152,512]{1,0:T(8,128)S(1)}, u32[]{:S(2)}, u32[]{:S(2)}) collective-permute-start(f32[152,512]{1,0:T(8,128)S(1)} %get-tuple-element.39), channel_id=1, source_target_pairs={{0,1},{1,0},{2,3},{3,2},{4,5},{5,4},{6,7},{7,6},{8,9},{9,8},{10,11... | collective-permute-start | bytes 933896 | tf_op jit(solution)/shard_map/ppermute | solution.py:683
  34.2 2.6 %collective-permute-start.6 = (f32[96,512]{1,0:T(8,128)S(1)}, f32[96,512]{1,0:T(8,128)S(1)}, u32[]{:S(2)}, u32[]{:S(2)}) collective-permute-start(f32[96,512]{1,0:T(8,128)S(1)} %get-tuple-element.52), channel_id=1, source_target_pairs={{0,15},{1,2},{2,1},{3,4},{4,3},{5,6},{6,5},{7,8},{8,7},{9,10},{10,... | collective-permute-start | bytes 589832 | tf_op jit(solution)/shard_map/ppermute | solution.py:683
  36.9 2.2 %shard_map.50.before = f32[16,384]{1,0:T(8,128)S(1)} custom-call(f32[384,512]{1,0:T(8,128)S(1)} %get-tuple-element.40.wide, s32[24,128]{1,0:T(8,128)S(1)} %get-tuple-element.41.places, f32[16,256]{1,0:T(8,128)S(1)} %get-tuple-element.38.start.refs_0_, f32[72,512]{1,0:T(8,128)S(1)} %collective-permute-done.from_y, ...), custom_call_target="tpu_custom_call" | custom-call | flops 268435456 | bytes 4194304 | tf_op jit(solution)/shard_map/pallas_call | solution.py:642
  39.9 1.8 %shard_map.55.own = f32[16,640]{1,0:T(8,128)S(1)} custom-call(f32[256,512]{1,0:T(8,128)S(1)} %get-tuple-element.43.slim, s32[16,128]{1,0:T(8,128)S(1)} %get-tuple-element.57.places, f32[16,256]{1,0:T(8,128)S(1)} %get-tuple-element.38.start.refs_0_, f32[72,512]{1,0:T(8,128)S(1)} %collective-permute-done.from_y, f32[72,512]{1,0:T(8,128)S(1)} %collective-permute-done.1.from_xy, ...), custom_call_target="tpu_custom_call" | custom-call | tf_op jit(solution)/shard_map/pallas_call | solution.py:642
  41.7 3.8 %collective-permute-start.9 = (f32[16,640]{1,0:T(8,128)S(1)}, f32[16,640]{1,0:T(8,128)S(1)}, u32[]{:S(2)}, u32[]{:S(2)}) collective-permute-start(f32[16,640]{1,0:T(8,128)S(1)} %shard_map.55.own), channel_id=1, source_target_pairs={{48,0},{49,1},{50,2},{51,3},{52,4},{53,5},{54,6},{55,7},{56,8},{57... | collective-permute-start | bytes 122888 | tf_op jit(solution)/shard_map/ppermute | solution.py:672
  45.5 3.7 %collective-permute-start.8 = (f32[16,640]{1,0:T(8,128)S(1)}, f32[16,640]{1,0:T(8,128)S(1)}, u32[]{:S(2)}, u32[]{:S(2)}) collective-permute-start(f32[16,640]{1,0:T(8,128)S(1)} %shard_map.55.own), channel_id=1, source_target_pairs={{496,0},{497,1},{498,2},{499,3},{500,4},{501,5},{502,6},{503,7},{5... | collective-permute-start | bytes 122888 | tf_op jit(solution)/shard_map/ppermute | solution.py:672
  49.2 3.2 %collective-permute-start.7 = (f32[16,640]{1,0:T(8,128)S(1)}, f32[16,640]{1,0:T(8,128)S(1)}, u32[]{:S(2)}, u32[]{:S(2)}) collective-permute-start(f32[16,640]{1,0:T(8,128)S(1)} %shard_map.55.own), channel_id=1, source_target_pairs={{448,0},{449,1},{450,2},{451,3},{452,4},{453,5},{454,6},{455,7},{4... | collective-permute-start | bytes 122888 | tf_op jit(solution)/shard_map/ppermute | solution.py:672
  55.2 2.3 %shard_map.56.own.second = f32[16,512]{1,0:T(8,128)S(1)} custom-call(bf16[512,512]{1,0:T(8,128)(2,1)S(1)} %get-tuple-element.53.head, bf16[512,512]{1,0:T(8,128)(2,1)S(1)} %get-tuple-element.54.middle, bf16[512,512]{1,0:T(8,128)(2,1)S(1)} %get-tuple-element.55.tail, s32[32,128]{1,0:T(8,128)S(1)} %get-tuple-element.56.places, f32[16,640]{1,0:T(8,128)S(1)} %shard_map.55.own, ...), custom_call_target="tpu_custom_call" | custom-call | tf_op jit(solution)/shard_map/pallas_call | solution.py:642
  57.5 3.4 %collective-permute-start.12 = (f32[16,512]{1,0:T(8,128)S(1)}, f32[16,512]{1,0:T(8,128)S(1)}, u32[]{:S(2)}, u32[]{:S(2)}) collective-permute-start(f32[16,512]{1,0:T(8,128)S(1)} %shard_map.56.own.second), channel_id=1, source_target_pairs={{16,0},{17,1},{18,2},{19,3},{20,4},{21,5},{22,6},{23,7},{24,8},{25... | collective-permute-start | bytes 98312 | tf_op jit(solution)/shard_map/ppermute | solution.py:672
  60.9 5.9 %collective-permute-start.11 = (f32[16,512]{1,0:T(8,128)S(1)}, f32[16,512]{1,0:T(8,128)S(1)}, u32[]{:S(2)}, u32[]{:S(2)}) collective-permute-start(f32[16,512]{1,0:T(8,128)S(1)} %shard_map.56.own.second), channel_id=1, source_target_pairs={{80,0},{81,1},{82,2},{83,3},{84,4},{85,5},{86,6},{87,7},{88,8},{89... | collective-permute-start | bytes 98312 | tf_op jit(solution)/shard_map/ppermute | solution.py:672
  66.8 2.8 %collective-permute-start.10 = (f32[16,512]{1,0:T(8,128)S(1)}, f32[16,512]{1,0:T(8,128)S(1)}, u32[]{:S(2)}, u32[]{:S(2)}) collective-permute-start(f32[16,512]{1,0:T(8,128)S(1)} %shard_map.56.own.second), channel_id=1, source_target_pairs={{64,0},{65,1},{66,2},{67,3},{68,4},{69,5},{70,6},{71,7},{72,8},{73... | collective-permute-start | bytes 98312 | tf_op jit(solution)/shard_map/ppermute | solution.py:672
  71.5 2.0 %shard_map.57.own = f32[16,384]{1,0:T(8,128)S(1)} custom-call(bf16[384,512]{1,0:T(8,128)(2,1)S(1)} %get-tuple-element.48.head, bf16[384,512]{1,0:T(8,128)(2,1)S(1)} %get-tuple-element.49.middle, bf16[384,512]{1,0:T(8,128)(2,1)S(1)} %get-tuple-element.50.tail, s32[24,128]{1,0:T(8,128)S(1)} %get-tuple-element.51.places, f32[16,512]{1,0:T(8,128)S(1)} %shard_map.56.own.second, ...), custom_call_target="tpu_custom_call" | custom-call | tf_op jit(solution)/shard_map/pallas_call | solution.py:642
  73.4 1.9 %collective-permute-start.15 = (f32[16,384]{1,0:T(8,128)S(1)}, f32[16,384]{1,0:T(8,128)S(1)}, u32[]{:S(2)}, u32[]{:S(2)}) collective-permute-start(f32[16,384]{1,0:T(8,128)S(1)} %shard_map.57.own), channel_id=1, source_target_pairs={{48,0},{49,1},{50,2},{51,3},{52,4},{53,5},{54,6},{55,7},{56,8},{57... | collective-permute-start | bytes 73736 | tf_op jit(solution)/shard_map/ppermute | solution.py:672
  75.4 4.5 %collective-permute-start.14 = (f32[16,384]{1,0:T(8,128)S(1)}, f32[16,384]{1,0:T(8,128)S(1)}, u32[]{:S(2)}, u32[]{:S(2)}) collective-permute-start(f32[16,384]{1,0:T(8,128)S(1)} %shard_map.57.own), channel_id=1, source_target_pairs={{496,0},{497,1},{498,2},{499,3},{500,4},{501,5},{502,6},{503,7},{5... | collective-permute-start | bytes 73736 | tf_op jit(solution)/shard_map/ppermute | solution.py:672
  79.9 3.0 %collective-permute-start.13 = (f32[16,384]{1,0:T(8,128)S(1)}, f32[16,384]{1,0:T(8,128)S(1)}, u32[]{:S(2)}, u32[]{:S(2)}) collective-permute-start(f32[16,384]{1,0:T(8,128)S(1)} %shard_map.57.own), channel_id=1, source_target_pairs={{448,0},{449,1},{450,2},{451,3},{452,4},{453,5},{454,6},{455,7},{4... | collective-permute-start | bytes 73736 | tf_op jit(solution)/shard_map/ppermute | solution.py:672
  85.7 2.0 %shard_map.59 = (f32[16,256]{1,0:T(8,128)S(1)}, f32[32,4,128]{2,1,0:T(4,128)S(1)}) custom-call(bf16[256,512]{1,0:T(8,128)(2,1)S(1)} %get-tuple-element.44.head, bf16[256,512]{1,0:T(8,128)(2,1)S(1)} %get-tuple-element.45.middle, bf16[256,512]{1,0:T(8,128)(2,1)S(1)} %get-tuple-element.46.tail, s32[16,128]{1,0:T(8,128)S(1)} %get-tuple-element.47.places, ...), custom_call_target="tpu_custom_call" | custom-call | tf_op jit(solution)/shard_map/pallas_call | solution.py:642
  87.7 20.0 %all_to_all.10.ref = f32[32,4,128]{2,1,0:T(4,128)S(1)} all-to-all(f32[32,4,128]{2,1,0:T(4,128)S(1)} %get-tuple-element.61), channel_id=1, replica_groups=mesh['gx'=8,'gy'=4,'gz'=16] {'gx','gy'}, dimensions={0} | all-to-all | bytes 131072 | tf_op jit(solution)/shard_map/all_to_all | solution.py:758
  107.8 18.5 %all_to_all.11.ref = f32[16,4,128]{2,1,0:T(4,128)S(1)} all-to-all(f32[16,4,128]{2,1,0:T(4,128)S(1)} %shard_map.60), channel_id=1, replica_groups=mesh['gx'=8,'gy'=4,'gz'=16] {'gz'}, dimensions={0} | all-to-all | bytes 65536 | tf_op jit(solution)/shard_map/all_to_all | solution.py:760
  (26 shorter events, 11.4 us)
Async XLA Ops:
  1.2 22.9 %collective-permute-start = (f32[72,512]{1,0:T(8,128)S(1)}, f32[72,512]{1,0:T(8,128)S(1)}, u32[]{:S(2)}, u32[]{:S(2)}) collective-permute-start(f32[72,512]{1,0:T(8,128)S(1)} %get-tuple-element.35), channel_id=1, source_target_pairs={{16,0},{17,1},{18,2},{19,3},{20,4},{21,5},{22,6},{23,7},{24,8},{25... | collective-permute-start | bytes 442376 | tf_op jit(solution)/shard_map/ppermute | solution.py:672
  12.7 11.4 %collective-permute-start.1 = (f32[72,512]{1,0:T(8,128)S(1)}, f32[72,512]{1,0:T(8,128)S(1)}, u32[]{:S(2)}, u32[]{:S(2)}) collective-permute-start(f32[72,512]{1,0:T(8,128)S(1)} %get-tuple-element.36), channel_id=1, source_target_pairs={{80,0},{81,1},{82,2},{83,3},{84,4},{85,5},{86,6},{87,7},{88,8},{89... | collective-permute-start | bytes 442376 | tf_op jit(solution)/shard_map/ppermute | solution.py:672
  17.8 6.7 %collective-permute-start.2 = (f32[72,512]{1,0:T(8,128)S(1)}, f32[72,512]{1,0:T(8,128)S(1)}, u32[]{:S(2)}, u32[]{:S(2)}) collective-permute-start(f32[72,512]{1,0:T(8,128)S(1)} %get-tuple-element.37), channel_id=1, source_target_pairs={{64,0},{65,1},{66,2},{67,3},{68,4},{69,5},{70,6},{71,7},{72,8},{73... | collective-permute-start | bytes 442376 | tf_op jit(solution)/shard_map/ppermute | solution.py:672
  24.5 15.3 %collective-permute-start.5 = (f32[224,512]{1,0:T(8,128)S(1)}, f32[224,512]{1,0:T(8,128)S(1)}, u32[]{:S(2)}, u32[]{:S(2)}) collective-permute-start(f32[224,512]{1,0:T(8,128)S(1)} %shard_map.51), channel_id=1, source_target_pairs={{0,15},{1,2},{2,1},{3,4},{4,3},{5,6},{6,5},{7,8},{8,7},{9,10},{10,... | collective-permute-start | bytes 1376264 | tf_op jit(solution)/shard_map/ppermute | solution.py:683
  29.4 7.4 %collective-permute-start.3 = (f32[168,512]{1,0:T(8,128)S(1)}, f32[168,512]{1,0:T(8,128)S(1)}, u32[]{:S(2)}, u32[]{:S(2)}) collective-permute-start(f32[168,512]{1,0:T(8,128)S(1)} %shard_map.47), channel_id=1, source_target_pairs={{0,1},{1,0},{2,3},{3,2},{4,5},{5,4},{6,7},{7,6},{8,9},{9,8},{10,11... | collective-permute-start | bytes 1032200 | tf_op jit(solution)/shard_map/ppermute | solution.py:683
  32.2 4.6 %collective-permute-start.4 = (f32[152,512]{1,0:T(8,128)S(1)}, f32[152,512]{1,0:T(8,128)S(1)}, u32[]{:S(2)}, u32[]{:S(2)}) collective-permute-start(f32[152,512]{1,0:T(8,128)S(1)} %get-tuple-element.39), channel_id=1, source_target_pairs={{0,1},{1,0},{2,3},{3,2},{4,5},{5,4},{6,7},{7,6},{8,9},{9,8},{10,11... | collective-permute-start | bytes 933896 | tf_op jit(solution)/shard_map/ppermute | solution.py:683
  34.2 18.3 %collective-permute-start.6 = (f32[96,512]{1,0:T(8,128)S(1)}, f32[96,512]{1,0:T(8,128)S(1)}, u32[]{:S(2)}, u32[]{:S(2)}) collective-permute-start(f32[96,512]{1,0:T(8,128)S(1)} %get-tuple-element.52), channel_id=1, source_target_pairs={{0,15},{1,2},{2,1},{3,4},{4,3},{5,6},{6,5},{7,8},{8,7},{9,10},{10,... | collective-permute-start | bytes 589832 | tf_op jit(solution)/shard_map/ppermute | solution.py:683
  41.7 11.3 %collective-permute-start.9 = (f32[16,640]{1,0:T(8,128)S(1)}, f32[16,640]{1,0:T(8,128)S(1)}, u32[]{:S(2)}, u32[]{:S(2)}) collective-permute-start(f32[16,640]{1,0:T(8,128)S(1)} %shard_map.55.own), channel_id=1, source_target_pairs={{48,0},{49,1},{50,2},{51,3},{52,4},{53,5},{54,6},{55,7},{56,8},{57... | collective-permute-start | bytes 122888 | tf_op jit(solution)/shard_map/ppermute | solution.py:672
  45.5 9.2 %collective-permute-start.8 = (f32[16,640]{1,0:T(8,128)S(1)}, f32[16,640]{1,0:T(8,128)S(1)}, u32[]{:S(2)}, u32[]{:S(2)}) collective-permute-start(f32[16,640]{1,0:T(8,128)S(1)} %shard_map.55.own), channel_id=1, source_target_pairs={{496,0},{497,1},{498,2},{499,3},{500,4},{501,5},{502,6},{503,7},{5... | collective-permute-start | bytes 122888 | tf_op jit(solution)/shard_map/ppermute | solution.py:672
  49.2 6.0 %collective-permute-start.7 = (f32[16,640]{1,0:T(8,128)S(1)}, f32[16,640]{1,0:T(8,128)S(1)}, u32[]{:S(2)}, u32[]{:S(2)}) collective-permute-start(f32[16,640]{1,0:T(8,128)S(1)} %shard_map.55.own), channel_id=1, source_target_pairs={{448,0},{449,1},{450,2},{451,3},{452,4},{453,5},{454,6},{455,7},{4... | collective-permute-start | bytes 122888 | tf_op jit(solution)/shard_map/ppermute | solution.py:672
  57.5 12.8 %collective-permute-start.12 = (f32[16,512]{1,0:T(8,128)S(1)}, f32[16,512]{1,0:T(8,128)S(1)}, u32[]{:S(2)}, u32[]{:S(2)}) collective-permute-start(f32[16,512]{1,0:T(8,128)S(1)} %shard_map.56.own.second), channel_id=1, source_target_pairs={{16,0},{17,1},{18,2},{19,3},{20,4},{21,5},{22,6},{23,7},{24,8},{25... | collective-permute-start | bytes 98312 | tf_op jit(solution)/shard_map/ppermute | solution.py:672
  60.9 9.4 %collective-permute-start.11 = (f32[16,512]{1,0:T(8,128)S(1)}, f32[16,512]{1,0:T(8,128)S(1)}, u32[]{:S(2)}, u32[]{:S(2)}) collective-permute-start(f32[16,512]{1,0:T(8,128)S(1)} %shard_map.56.own.second), channel_id=1, source_target_pairs={{80,0},{81,1},{82,2},{83,3},{84,4},{85,5},{86,6},{87,7},{88,8},{89... | collective-permute-start | bytes 98312 | tf_op jit(solution)/shard_map/ppermute | solution.py:672
  66.8 4.7 %collective-permute-start.10 = (f32[16,512]{1,0:T(8,128)S(1)}, f32[16,512]{1,0:T(8,128)S(1)}, u32[]{:S(2)}, u32[]{:S(2)}) collective-permute-start(f32[16,512]{1,0:T(8,128)S(1)} %shard_map.56.own.second), channel_id=1, source_target_pairs={{64,0},{65,1},{66,2},{67,3},{68,4},{69,5},{70,6},{71,7},{72,8},{73... | collective-permute-start | bytes 98312 | tf_op jit(solution)/shard_map/ppermute | solution.py:672
  73.4 9.6 %collective-permute-start.15 = (f32[16,384]{1,0:T(8,128)S(1)}, f32[16,384]{1,0:T(8,128)S(1)}, u32[]{:S(2)}, u32[]{:S(2)}) collective-permute-start(f32[16,384]{1,0:T(8,128)S(1)} %shard_map.57.own), channel_id=1, source_target_pairs={{48,0},{49,1},{50,2},{51,3},{52,4},{53,5},{54,6},{55,7},{56,8},{57... | collective-permute-start | bytes 73736 | tf_op jit(solution)/shard_map/ppermute | solution.py:672
  75.4 8.8 %collective-permute-start.14 = (f32[16,384]{1,0:T(8,128)S(1)}, f32[16,384]{1,0:T(8,128)S(1)}, u32[]{:S(2)}, u32[]{:S(2)}) collective-permute-start(f32[16,384]{1,0:T(8,128)S(1)} %shard_map.57.own), channel_id=1, source_target_pairs={{496,0},{497,1},{498,2},{499,3},{500,4},{501,5},{502,6},{503,7},{5... | collective-permute-start | bytes 73736 | tf_op jit(solution)/shard_map/ppermute | solution.py:672
  79.9 5.8 %collective-permute-start.13 = (f32[16,384]{1,0:T(8,128)S(1)}, f32[16,384]{1,0:T(8,128)S(1)}, u32[]{:S(2)}, u32[]{:S(2)}) collective-permute-start(f32[16,384]{1,0:T(8,128)S(1)} %shard_map.57.own), channel_id=1, source_target_pairs={{448,0},{449,1},{450,2},{451,3},{452,4},{453,5},{454,6},{455,7},{4... | collective-permute-start | bytes 73736 | tf_op jit(solution)/shard_map/ppermute | solution.py:672

commit v12 on v10

--- a/solution.py
+++ b/solution.py
@@ -755,7 +755,7 @@
         start, first_own, second_own,
         scratch=scratch_for(12, 2),
     )
-    message = lax.all_to_all(message, ("gx", "gy"), 0, 0, tiled=True)
+    message = lax.all_to_all(message, ("gy", "gx"), 0, 0, tiled=True)
     (message,) = call(relay_kernel, [(lax.axis_size("gz"), 4, LANES)], message)
     message = lax.all_to_all(message, "gz", 0, 0, tiled=True)
     (result,) = call(finish_kernel, [rhs.shape], message, start, first_own, second_own, third_own)

time: 128 us -> 128 us (level)
  no operation moved by 1% of the time
where the time goes in v12:
time: 128 us; the launch traced here: 127 us
  starting transfers between devices  64.6 us (50%)
  blocking collectives  38.5 us (30%)
  Pallas kernels  14.7 us (11%)
  waiting for transfers between devices  9.28 us (7%)
    ppermute x12, starting transfers between devices, fetch(): return lax.ppermute(value, AXES, pairs)  52.5 us
    all_to_all x1, blocking collectives, body(): message = lax.all_to_all(message, ('gy', 'gx'), 0, 0, tiled=True)  19.7 us
    all_to_all x1, blocking collectives, body(): message = lax.all_to_all(message, 'gz', 0, 0, tiled=True)  18.8 us
    pallas_call x16, Pallas kernels, call(): pl.pallas_call(kernel, out_shape=shapes, in_specs=[SMEM if operand.dtype...  14.7 us
    ppermute x12, waiting for transfers between devices, fetch(): return lax.ppermute(value, AXES, pairs)  8.61 us
    ppermute x2, starting transfers between devices, swap_layers(): lax.ppermute(to_second, 'gz', odd)  7.41 us
    ppermute x2, starting transfers between devices, swap_layers(): lax.ppermute(to_first, 'gz', even)  4.73 us
  transfers between devices with their start and end apart: 16, of which 6 were waited for; matrix products, arithmetic and copies ran while one was open for 0% of the time, Pallas kernels for 4%

profile of v12, /device:TPU:1, one launch (start us, length us, event | category | flops | bytes accessed | tf_op | source)
XLA Modules:
  0.0 127.4 jit_solution(14295071173237700994)
XLA Ops:
  1.2 11.5 %collective-permute-start = (f32[72,512]{1,0:T(8,128)S(1)}, f32[72,512]{1,0:T(8,128)S(1)}, u32[]{:S(2)}, u32[]{:S(2)}) collective-permute-start(f32[72,512]{1,0:T(8,128)S(1)} %get-tuple-element.35), channel_id=1, source_target_pairs={{16,0},{17,1},{18,2},{19,3},{20,4},{21,5},{22,6},{23,7},{24,8},{25... | collective-permute-start | bytes 442376 | tf_op jit(solution)/shard_map/ppermute | solution.py:672
  12.7 5.1 %collective-permute-start.1 = (f32[72,512]{1,0:T(8,128)S(1)}, f32[72,512]{1,0:T(8,128)S(1)}, u32[]{:S(2)}, u32[]{:S(2)}) collective-permute-start(f32[72,512]{1,0:T(8,128)S(1)} %get-tuple-element.36), channel_id=1, source_target_pairs={{80,0},{81,1},{82,2},{83,3},{84,4},{85,5},{86,6},{87,7},{88,8},{89... | collective-permute-start | bytes 442376 | tf_op jit(solution)/shard_map/ppermute | solution.py:672
  17.8 3.0 %collective-permute-start.2 = (f32[72,512]{1,0:T(8,128)S(1)}, f32[72,512]{1,0:T(8,128)S(1)}, u32[]{:S(2)}, u32[]{:S(2)}) collective-permute-start(f32[72,512]{1,0:T(8,128)S(1)} %get-tuple-element.37), channel_id=1, source_target_pairs={{64,0},{65,1},{66,2},{67,3},{68,4},{69,5},{70,6},{71,7},{72,8},{73... | collective-permute-start | bytes 442376 | tf_op jit(solution)/shard_map/ppermute | solution.py:672
  20.8 3.3 %collective-permute-done.from_y = f32[72,512]{1,0:T(8,128)S(1)} collective-permute-done((f32[72,512]{1,0:T(8,128)S(1)}, f32[72,512]{1,0:T(8,128)S(1)}, u32[]{:S(2)}, u32[]{:S(2)}) %collective-permute-start) | collective-permute-done | bytes 147488 | tf_op jit(solution)/shard_map/ppermute | solution.py:672
  24.5 4.8 %collective-permute-start.5 = (f32[224,512]{1,0:T(8,128)S(1)}, f32[224,512]{1,0:T(8,128)S(1)}, u32[]{:S(2)}, u32[]{:S(2)}) collective-permute-start(f32[224,512]{1,0:T(8,128)S(1)} %shard_map.51), channel_id=1, source_target_pairs={{0,15},{1,2},{2,1},{3,4},{4,3},{5,6},{6,5},{7,8},{8,7},{9,10},{10,... | collective-permute-start | bytes 1376264 | tf_op jit(solution)/shard_map/ppermute | solution.py:683
  29.4 2.8 %collective-permute-start.3 = (f32[168,512]{1,0:T(8,128)S(1)}, f32[168,512]{1,0:T(8,128)S(1)}, u32[]{:S(2)}, u32[]{:S(2)}) collective-permute-start(f32[168,512]{1,0:T(8,128)S(1)} %shard_map.47), channel_id=1, source_target_pairs={{0,1},{1,0},{2,3},{3,2},{4,5},{5,4},{6,7},{7,6},{8,9},{9,8},{10,11... | collective-permute-start | bytes 1032200 | tf_op jit(solution)/shard_map/ppermute | solution.py:683
  34.2 2.6 %collective-permute-start.6 = (f32[96,512]{1,0:T(8,128)S(1)}, f32[96,512]{1,0:T(8,128)S(1)}, u32[]{:S(2)}, u32[]{:S(2)}) collective-permute-start(f32[96,512]{1,0:T(8,128)S(1)} %get-tuple-element.52), channel_id=1, source_target_pairs={{0,15},{1,2},{2,1},{3,4},{4,3},{5,6},{6,5},{7,8},{8,7},{9,10},{10,... | collective-permute-start | bytes 589832 | tf_op jit(solution)/shard_map/ppermute | solution.py:683
  36.9 2.2 %shard_map.50.before = f32[16,384]{1,0:T(8,128)S(1)} custom-call(f32[384,512]{1,0:T(8,128)S(1)} %get-tuple-element.40.wide, s32[24,128]{1,0:T(8,128)S(1)} %get-tuple-element.41.places, f32[16,256]{1,0:T(8,128)S(1)} %get-tuple-element.38.start.refs_0_, f32[72,512]{1,0:T(8,128)S(1)} %collective-permute-done.from_y, ...), custom_call_target="tpu_custom_call" | custom-call | flops 268435456 | bytes 4194304 | tf_op jit(solution)/shard_map/pallas_call | solution.py:642
  41.7 3.2 %collective-permute-start.9 = (f32[16,640]{1,0:T(8,128)S(1)}, f32[16,640]{1,0:T(8,128)S(1)}, u32[]{:S(2)}, u32[]{:S(2)}) collective-permute-start(f32[16,640]{1,0:T(8,128)S(1)} %shard_map.55.own), channel_id=1, source_target_pairs={{496,0},{497,1},{498,2},{499,3},{500,4},{501,5},{502,6},{503,7},{5... | collective-permute-start | bytes 122888 | tf_op jit(solution)/shard_map/ppermute | solution.py:672
  44.9 4.3 %collective-permute-start.8 = (f32[16,640]{1,0:T(8,128)S(1)}, f32[16,640]{1,0:T(8,128)S(1)}, u32[]{:S(2)}, u32[]{:S(2)}) collective-permute-start(f32[16,640]{1,0:T(8,128)S(1)} %shard_map.55.own), channel_id=1, source_target_pairs={{48,0},{49,1},{50,2},{51,3},{52,4},{53,5},{54,6},{55,7},{56,8},{57... | collective-permute-start | bytes 122888 | tf_op jit(solution)/shard_map/ppermute | solution.py:672
  49.2 3.2 %collective-permute-start.7 = (f32[16,640]{1,0:T(8,128)S(1)}, f32[16,640]{1,0:T(8,128)S(1)}, u32[]{:S(2)}, u32[]{:S(2)}) collective-permute-start(f32[16,640]{1,0:T(8,128)S(1)} %shard_map.55.own), channel_id=1, source_target_pairs={{448,0},{449,1},{450,2},{451,3},{452,4},{453,5},{454,6},{455,7},{4... | collective-permute-start | bytes 122888 | tf_op jit(solution)/shard_map/ppermute | solution.py:672
  53.0 2.4 %collective-permute-done.7.from_x = f32[16,640]{1,0:T(8,128)S(1)} collective-permute-done((f32[16,640]{1,0:T(8,128)S(1)}, f32[16,640]{1,0:T(8,128)S(1)}, u32[]{:S(2)}, u32[]{:S(2)}) %collective-permute-start.7) | collective-permute-done | bytes 40992 | tf_op jit(solution)/shard_map/ppermute | solution.py:672
  55.5 2.3 %shard_map.56.own.second = f32[16,512]{1,0:T(8,128)S(1)} custom-call(bf16[512,512]{1,0:T(8,128)(2,1)S(1)} %get-tuple-element.53.head, bf16[512,512]{1,0:T(8,128)(2,1)S(1)} %get-tuple-element.54.middle, bf16[512,512]{1,0:T(8,128)(2,1)S(1)} %get-tuple-element.55.tail, s32[32,128]{1,0:T(8,128)S(1)} %get-tuple-element.56.places, f32[16,640]{1,0:T(8,128)S(1)} %shard_map.55.own, ...), custom_call_target="tpu_custom_call" | custom-call | tf_op jit(solution)/shard_map/pallas_call | solution.py:642
  57.8 4.3 %collective-permute-start.12 = (f32[16,512]{1,0:T(8,128)S(1)}, f32[16,512]{1,0:T(8,128)S(1)}, u32[]{:S(2)}, u32[]{:S(2)}) collective-permute-start(f32[16,512]{1,0:T(8,128)S(1)} %shard_map.56.own.second), channel_id=1, source_target_pairs={{80,0},{81,1},{82,2},{83,3},{84,4},{85,5},{86,6},{87,7},{88,8},{89... | collective-permute-start | bytes 98312 | tf_op jit(solution)/shard_map/ppermute | solution.py:672
  62.1 3.6 %collective-permute-start.11 = (f32[16,512]{1,0:T(8,128)S(1)}, f32[16,512]{1,0:T(8,128)S(1)}, u32[]{:S(2)}, u32[]{:S(2)}) collective-permute-start(f32[16,512]{1,0:T(8,128)S(1)} %shard_map.56.own.second), channel_id=1, source_target_pairs={{16,0},{17,1},{18,2},{19,3},{20,4},{21,5},{22,6},{23,7},{24,8},{25... | collective-permute-start | bytes 98312 | tf_op jit(solution)/shard_map/ppermute | solution.py:672
  65.7 4.0 %collective-permute-start.10 = (f32[16,512]{1,0:T(8,128)S(1)}, f32[16,512]{1,0:T(8,128)S(1)}, u32[]{:S(2)}, u32[]{:S(2)}) collective-permute-start(f32[16,512]{1,0:T(8,128)S(1)} %shard_map.56.own.second), channel_id=1, source_target_pairs={{64,0},{65,1},{66,2},{67,3},{68,4},{69,5},{70,6},{71,7},{72,8},{73... | collective-permute-start | bytes 98312 | tf_op jit(solution)/shard_map/ppermute | solution.py:672
  70.8 2.0 %shard_map.57.own = f32[16,384]{1,0:T(8,128)S(1)} custom-call(bf16[384,512]{1,0:T(8,128)(2,1)S(1)} %get-tuple-element.48.head, bf16[384,512]{1,0:T(8,128)(2,1)S(1)} %get-tuple-element.49.middle, bf16[384,512]{1,0:T(8,128)(2,1)S(1)} %get-tuple-element.50.tail, s32[24,128]{1,0:T(8,128)S(1)} %get-tuple-element.51.places, f32[16,512]{1,0:T(8,128)S(1)} %shard_map.56.own.second, ...), custom_call_target="tpu_custom_call" | custom-call | tf_op jit(solution)/shard_map/pallas_call | solution.py:642
  72.8 2.2 %collective-permute-start.15 = (f32[16,384]{1,0:T(8,128)S(1)}, f32[16,384]{1,0:T(8,128)S(1)}, u32[]{:S(2)}, u32[]{:S(2)}) collective-permute-start(f32[16,384]{1,0:T(8,128)S(1)} %shard_map.57.own), channel_id=1, source_target_pairs={{496,0},{497,1},{498,2},{499,3},{500,4},{501,5},{502,6},{503,7},{5... | collective-permute-start | bytes 73736 | tf_op jit(solution)/shard_map/ppermute | solution.py:672
  75.0 4.6 %collective-permute-start.14 = (f32[16,384]{1,0:T(8,128)S(1)}, f32[16,384]{1,0:T(8,128)S(1)}, u32[]{:S(2)}, u32[]{:S(2)}) collective-permute-start(f32[16,384]{1,0:T(8,128)S(1)} %shard_map.57.own), channel_id=1, source_target_pairs={{48,0},{49,1},{50,2},{51,3},{52,4},{53,5},{54,6},{55,7},{56,8},{57... | collective-permute-start | bytes 73736 | tf_op jit(solution)/shard_map/ppermute | solution.py:672
  79.6 3.5 %collective-permute-start.13 = (f32[16,384]{1,0:T(8,128)S(1)}, f32[16,384]{1,0:T(8,128)S(1)}, u32[]{:S(2)}, u32[]{:S(2)}) collective-permute-start(f32[16,384]{1,0:T(8,128)S(1)} %shard_map.57.own), channel_id=1, source_target_pairs={{448,0},{449,1},{450,2},{451,3},{452,4},{453,5},{454,6},{455,7},{4... | collective-permute-start | bytes 73736 | tf_op jit(solution)/shard_map/ppermute | solution.py:672
  83.2 2.2 %collective-permute-done.13.from_x = f32[16,384]{1,0:T(8,128)S(1)} collective-permute-done((f32[16,384]{1,0:T(8,128)S(1)}, f32[16,384]{1,0:T(8,128)S(1)}, u32[]{:S(2)}, u32[]{:S(2)}) %collective-permute-start.13) | collective-permute-done | bytes 24608 | tf_op jit(solution)/shard_map/ppermute | solution.py:672
  85.4 2.0 %shard_map.59 = (f32[16,256]{1,0:T(8,128)S(1)}, f32[32,4,128]{2,1,0:T(4,128)S(1)}) custom-call(bf16[256,512]{1,0:T(8,128)(2,1)S(1)} %get-tuple-element.44.head, bf16[256,512]{1,0:T(8,128)(2,1)S(1)} %get-tuple-element.45.middle, bf16[256,512]{1,0:T(8,128)(2,1)S(1)} %get-tuple-element.46.tail, s32[16,128]{1,0:T(8,128)S(1)} %get-tuple-element.47.places, ...), custom_call_target="tpu_custom_call" | custom-call | tf_op jit(solution)/shard_map/pallas_call | solution.py:642
  87.4 19.7 %all_to_all.10.ref = f32[32,4,128]{2,1,0:T(4,128)S(1)} all-to-all(f32[32,4,128]{2,1,0:T(4,128)S(1)} %get-tuple-element.61), channel_id=1, replica_groups=mesh['gx'=8,'gy'=4,'gz'=16] {'gy','gx'}, dimensions={0} | all-to-all | bytes 131072 | tf_op jit(solution)/shard_map/all_to_all | solution.py:758
  107.2 18.8 %all_to_all.11.ref = f32[16,4,128]{2,1,0:T(4,128)S(1)} all-to-all(f32[16,4,128]{2,1,0:T(4,128)S(1)} %shard_map.60), channel_id=1, replica_groups=mesh['gx'=8,'gy'=4,'gz'=16] {'gz'}, dimensions={0} | all-to-all | bytes 65536 | tf_op jit(solution)/shard_map/all_to_all | solution.py:760
  (26 shorter events, 9.5 us)
Async XLA Ops:
  1.2 22.9 %collective-permute-start = (f32[72,512]{1,0:T(8,128)S(1)}, f32[72,512]{1,0:T(8,128)S(1)}, u32[]{:S(2)}, u32[]{:S(2)}) collective-permute-start(f32[72,512]{1,0:T(8,128)S(1)} %get-tuple-element.35), channel_id=1, source_target_pairs={{16,0},{17,1},{18,2},{19,3},{20,4},{21,5},{22,6},{23,7},{24,8},{25... | collective-permute-start | bytes 442376 | tf_op jit(solution)/shard_map/ppermute | solution.py:672
  12.7 11.4 %collective-permute-start.1 = (f32[72,512]{1,0:T(8,128)S(1)}, f32[72,512]{1,0:T(8,128)S(1)}, u32[]{:S(2)}, u32[]{:S(2)}) collective-permute-start(f32[72,512]{1,0:T(8,128)S(1)} %get-tuple-element.36), channel_id=1, source_target_pairs={{80,0},{81,1},{82,2},{83,3},{84,4},{85,5},{86,6},{87,7},{88,8},{89... | collective-permute-start | bytes 442376 | tf_op jit(solution)/shard_map/ppermute | solution.py:672
  17.8 6.7 %collective-permute-start.2 = (f32[72,512]{1,0:T(8,128)S(1)}, f32[72,512]{1,0:T(8,128)S(1)}, u32[]{:S(2)}, u32[]{:S(2)}) collective-permute-start(f32[72,512]{1,0:T(8,128)S(1)} %get-tuple-element.37), channel_id=1, source_target_pairs={{64,0},{65,1},{66,2},{67,3},{68,4},{69,5},{70,6},{71,7},{72,8},{73... | collective-permute-start | bytes 442376 | tf_op jit(solution)/shard_map/ppermute | solution.py:672
  24.5 15.3 %collective-permute-start.5 = (f32[224,512]{1,0:T(8,128)S(1)}, f32[224,512]{1,0:T(8,128)S(1)}, u32[]{:S(2)}, u32[]{:S(2)}) collective-permute-start(f32[224,512]{1,0:T(8,128)S(1)} %shard_map.51), channel_id=1, source_target_pairs={{0,15},{1,2},{2,1},{3,4},{4,3},{5,6},{6,5},{7,8},{8,7},{9,10},{10,... | collective-permute-start | bytes 1376264 | tf_op jit(solution)/shard_map/ppermute | solution.py:683
  29.4 7.4 %collective-permute-start.3 = (f32[168,512]{1,0:T(8,128)S(1)}, f32[168,512]{1,0:T(8,128)S(1)}, u32[]{:S(2)}, u32[]{:S(2)}) collective-permute-start(f32[168,512]{1,0:T(8,128)S(1)} %shard_map.47), channel_id=1, source_target_pairs={{0,1},{1,0},{2,3},{3,2},{4,5},{5,4},{6,7},{7,6},{8,9},{9,8},{10,11... | collective-permute-start | bytes 1032200 | tf_op jit(solution)/shard_map/ppermute | solution.py:683
  32.2 4.6 %collective-permute-start.4 = (f32[152,512]{1,0:T(8,128)S(1)}, f32[152,512]{1,0:T(8,128)S(1)}, u32[]{:S(2)}, u32[]{:S(2)}) collective-permute-start(f32[152,512]{1,0:T(8,128)S(1)} %get-tuple-element.39), channel_id=1, source_target_pairs={{0,1},{1,0},{2,3},{3,2},{4,5},{5,4},{6,7},{7,6},{8,9},{9,8},{10,11... | collective-permute-start | bytes 933896 | tf_op jit(solution)/shard_map/ppermute | solution.py:683
  34.2 18.3 %collective-permute-start.6 = (f32[96,512]{1,0:T(8,128)S(1)}, f32[96,512]{1,0:T(8,128)S(1)}, u32[]{:S(2)}, u32[]{:S(2)}) collective-permute-start(f32[96,512]{1,0:T(8,128)S(1)} %get-tuple-element.52), channel_id=1, source_target_pairs={{0,15},{1,2},{2,1},{3,4},{4,3},{5,6},{6,5},{7,8},{8,7},{9,10},{10,... | collective-permute-start | bytes 589832 | tf_op jit(solution)/shard_map/ppermute | solution.py:683
  41.7 11.3 %collective-permute-start.9 = (f32[16,640]{1,0:T(8,128)S(1)}, f32[16,640]{1,0:T(8,128)S(1)}, u32[]{:S(2)}, u32[]{:S(2)}) collective-permute-start(f32[16,640]{1,0:T(8,128)S(1)} %shard_map.55.own), channel_id=1, source_target_pairs={{496,0},{497,1},{498,2},{499,3},{500,4},{501,5},{502,6},{503,7},{5... | collective-permute-start | bytes 122888 | tf_op jit(solution)/shard_map/ppermute | solution.py:672
  44.9 8.1 %collective-permute-start.8 = (f32[16,640]{1,0:T(8,128)S(1)}, f32[16,640]{1,0:T(8,128)S(1)}, u32[]{:S(2)}, u32[]{:S(2)}) collective-permute-start(f32[16,640]{1,0:T(8,128)S(1)} %shard_map.55.own), channel_id=1, source_target_pairs={{48,0},{49,1},{50,2},{51,3},{52,4},{53,5},{54,6},{55,7},{56,8},{57... | collective-permute-start | bytes 122888 | tf_op jit(solution)/shard_map/ppermute | solution.py:672
  49.2 6.3 %collective-permute-start.7 = (f32[16,640]{1,0:T(8,128)S(1)}, f32[16,640]{1,0:T(8,128)S(1)}, u32[]{:S(2)}, u32[]{:S(2)}) collective-permute-start(f32[16,640]{1,0:T(8,128)S(1)} %shard_map.55.own), channel_id=1, source_target_pairs={{448,0},{449,1},{450,2},{451,3},{452,4},{453,5},{454,6},{455,7},{4... | collective-permute-start | bytes 122888 | tf_op jit(solution)/shard_map/ppermute | solution.py:672
  57.8 12.7 %collective-permute-start.12 = (f32[16,512]{1,0:T(8,128)S(1)}, f32[16,512]{1,0:T(8,128)S(1)}, u32[]{:S(2)}, u32[]{:S(2)}) collective-permute-start(f32[16,512]{1,0:T(8,128)S(1)} %shard_map.56.own.second), channel_id=1, source_target_pairs={{80,0},{81,1},{82,2},{83,3},{84,4},{85,5},{86,6},{87,7},{88,8},{89... | collective-permute-start | bytes 98312 | tf_op jit(solution)/shard_map/ppermute | solution.py:672
  62.1 8.4 %collective-permute-start.11 = (f32[16,512]{1,0:T(8,128)S(1)}, f32[16,512]{1,0:T(8,128)S(1)}, u32[]{:S(2)}, u32[]{:S(2)}) collective-permute-start(f32[16,512]{1,0:T(8,128)S(1)} %shard_map.56.own.second), channel_id=1, source_target_pairs={{16,0},{17,1},{18,2},{19,3},{20,4},{21,5},{22,6},{23,7},{24,8},{25... | collective-permute-start | bytes 98312 | tf_op jit(solution)/shard_map/ppermute | solution.py:672
  65.7 5.0 %collective-permute-start.10 = (f32[16,512]{1,0:T(8,128)S(1)}, f32[16,512]{1,0:T(8,128)S(1)}, u32[]{:S(2)}, u32[]{:S(2)}) collective-permute-start(f32[16,512]{1,0:T(8,128)S(1)} %shard_map.56.own.second), channel_id=1, source_target_pairs={{64,0},{65,1},{66,2},{67,3},{68,4},{69,5},{70,6},{71,7},{72,8},{73... | collective-permute-start | bytes 98312 | tf_op jit(solution)/shard_map/ppermute | solution.py:672
  72.8 10.4 %collective-permute-start.15 = (f32[16,384]{1,0:T(8,128)S(1)}, f32[16,384]{1,0:T(8,128)S(1)}, u32[]{:S(2)}, u32[]{:S(2)}) collective-permute-start(f32[16,384]{1,0:T(8,128)S(1)} %shard_map.57.own), channel_id=1, source_target_pairs={{496,0},{497,1},{498,2},{499,3},{500,4},{501,5},{502,6},{503,7},{5... | collective-permute-start | bytes 73736 | tf_op jit(solution)/shard_map/ppermute | solution.py:672
  75.0 8.2 %collective-permute-start.14 = (f32[16,384]{1,0:T(8,128)S(1)}, f32[16,384]{1,0:T(8,128)S(1)}, u32[]{:S(2)}, u32[]{:S(2)}) collective-permute-start(f32[16,384]{1,0:T(8,128)S(1)} %shard_map.57.own), channel_id=1, source_target_pairs={{48,0},{49,1},{50,2},{51,3},{52,4},{53,5},{54,6},{55,7},{56,8},{57... | collective-permute-start | bytes 73736 | tf_op jit(solution)/shard_map/ppermute | solution.py:672
  79.6 5.8 %collective-permute-start.13 = (f32[16,384]{1,0:T(8,128)S(1)}, f32[16,384]{1,0:T(8,128)S(1)}, u32[]{:S(2)}, u32[]{:S(2)}) collective-permute-start(f32[16,384]{1,0:T(8,128)S(1)} %shard_map.57.own), channel_id=1, source_target_pairs={{448,0},{449,1},{450,2},{451,3},{452,4},{453,5},{454,6},{455,7},{4... | collective-permute-start | bytes 73736 | tf_op jit(solution)/shard_map/ppermute | solution.py:672

commit v13 on v10

--- a/solution.py
+++ b/solution.py
@@ -62,12 +62,13 @@
     return lax.broadcasted_iota(jnp.int32, shape, axis)
 
 
-def gram_kernel(fields, out):
-    columns = 16
-    diagonal_mask = iota((8, LANES), 0) == iota((8, LANES), 1) // columns
-    rows = []
+EARLY = [pair for pair in PAIRS if pair[1] <= 2]
+
+
+def gram_rows(fields, pairs):
+    rows = {}
     parts = [split(field) for field in fields]
-    for i, j in PAIRS:
+    for i, j in pairs:
         product = fields[i] * fields[j]
         (a_head, a_tail), (b_head, b_tail) = parts[i], parts[j]
         rest = ((a_head * b_head - product) + a_head * b_tail + a_tail * b_head) + a_tail * b_tail
@@ -81,7 +82,17 @@
         total = pieces[0]
         for amount in (4, 2, 1):
             total = pair_add(total, roll_pair(total, amount, 0))
-        rows.append((total[0][0:1], total[1][0:1]))
+        rows[i, j] = total[0][0:1], total[1][0:1]
+    return rows
+
+
+def gram_kernel(fields, early, out):
+    columns = 16
+    diagonal_mask = iota((8, LANES), 0) == iota((8, LANES), 1) // columns
+    found = gram_rows(fields, [pair for pair in PAIRS if pair not in EARLY])
+    for q, pair in enumerate(EARLY):
+        found[pair] = early[q : q + 1], early[8 + q : 9 + q]
+    rows = [found[pair] for pair in PAIRS]
     rows += [(jnp.zeros((1, LANES), jnp.float32),) * 2] * (16 - len(rows))
     packed = [[], []]
     for start in (0, 8):
@@ -602,16 +613,20 @@
     out[...] = couple((head, middle, tail), 24, field, places, gathered)
 
 
-def pick_kernel(own, from_x, from_y, from_xy, second, first_own, second_own):
+def pick_kernel(own, from_x, from_y, from_xy, second, start, first_own, second_own, early):
     pieces = from_xy, from_x, from_y, own
     first_own[...] = jnp.where(
         is_even(), pick_own(pieces, first_place(True)), pick_own(pieces, first_place(False))
     )
     second_own[...] = pick_own((second,), SECOND_PLACE)
+    early[...] = jnp.zeros_like(early)
+    rows = gram_rows([start[...], first_own[...], second_own[...]], EARLY)
+    for q, pair in enumerate(EARLY):
+        early[q : q + 1], early[8 + q : 9 + q] = rows[pair]
 
 
 def last_kernel(
-    head, middle, tail, places, own, from_x, from_y, from_xy, start, first, second,
+    head, middle, tail, places, own, from_x, from_y, from_xy, start, first, second, early,
     third_out, out,
     field, gathered,
 ):
@@ -620,7 +635,7 @@
     fourth = couple((head, middle, tail), ATOMS, field, places, gathered)
     third = pick_own(pieces, THIRD_PLACE)
     third_out[...] = third
-    gram_kernel([start[...], first[...], second[...], third, fourth], out)
+    gram_kernel([start[...], first[...], second[...], third, fourth], early, out)
 
 
 SMEM = pl.BlockSpec(memory_space=pltpu.SMEM)
@@ -736,7 +751,9 @@
         second_kernel, [(SLOT_ROWS, 4 * LANES)], *tall, places, first, *pieces,
         scratch=scratch_for(20, 4),
     )
-    first_own, second_own = call(pick_kernel, [flat] * 2, first, *pieces, second)
+    first_own, second_own, early = call(
+        pick_kernel, [flat] * 2 + [(16, LANES)], first, *pieces, second, start
+    )
     *parts, third_places, fourth_places = call(
         later_kernel,
         [cut(24)] * 3 + [cut(ATOMS)] * 3 + [whole_numbers(24), whole_numbers(ATOMS)],
@@ -752,7 +769,7 @@
         last_kernel,
         [flat, (lax.axis_size("gx") * lax.axis_size("gy"), 4, LANES)],
         *parts[3:], fourth_places, third, *fetch_three(third, third, third, -1),
-        start, first_own, second_own,
+        start, first_own, second_own, early,
         scratch=scratch_for(12, 2),
     )
     message = lax.all_to_all(message, ("gx", "gy"), 0, 0, tiled=True)

time: 128 us -> 128 us (level)
  transfers between devices with their start and end apart: 16 -> 16, of which waited for: 6 -> 6; matrix products, arithmetic and copies ran while one was open for 0% -> 0% of each run, Pallas kernels for 4% -> 5%
where the time goes in v13:
time: 128 us; the launch traced here: 127 us
  starting transfers between devices  64.6 us (50%)
  blocking collectives  38.4 us (30%)
  Pallas kernels  14.7 us (11%)
  waiting for transfers between devices  9.18 us (7%)
    ppermute x12, starting transfers between devices, fetch(): return lax.ppermute(value, AXES, pairs)  52.5 us
    all_to_all x1, blocking collectives, body(): message = lax.all_to_all(message, ('gx', 'gy'), 0, 0, tiled=True)  19.7 us
    all_to_all x1, blocking collectives, body(): message = lax.all_to_all(message, 'gz', 0, 0, tiled=True)  18.8 us
    pallas_call x16, Pallas kernels, call(): pl.pallas_call(kernel, out_shape=shapes, in_specs=[SMEM if operand.dtype...  14.7 us
    ppermute x12, waiting for transfers between devices, fetch(): return lax.ppermute(value, AXES, pairs)  8.51 us
    ppermute x2, starting transfers between devices, swap_layers(): lax.ppermute(to_second, 'gz', odd)  7.41 us
    ppermute x2, starting transfers between devices, swap_layers(): lax.ppermute(to_first, 'gz', even)  4.73 us
  transfers between devices with their start and end apart: 16, of which 6 were waited for; matrix products, arithmetic and copies ran while one was open for 0% of the time, Pallas kernels for 5%

profile of v13, /device:TPU:1, one launch (start us, length us, event | category | flops | bytes accessed | tf_op | source)
XLA Modules:
  0.0 127.2 jit_solution(5406577377608042977)
XLA Ops:
  1.2 11.5 %collective-permute-start = (f32[72,512]{1,0:T(8,128)S(1)}, f32[72,512]{1,0:T(8,128)S(1)}, u32[]{:S(2)}, u32[]{:S(2)}) collective-permute-start(f32[72,512]{1,0:T(8,128)S(1)} %get-tuple-element.36), channel_id=1, source_target_pairs={{16,0},{17,1},{18,2},{19,3},{20,4},{21,5},{22,6},{23,7},{24,8},{25... | collective-permute-start | bytes 442376 | tf_op jit(solution)/shard_map/ppermute | solution.py:687
  12.7 5.1 %collective-permute-start.1 = (f32[72,512]{1,0:T(8,128)S(1)}, f32[72,512]{1,0:T(8,128)S(1)}, u32[]{:S(2)}, u32[]{:S(2)}) collective-permute-start(f32[72,512]{1,0:T(8,128)S(1)} %get-tuple-element.37), channel_id=1, source_target_pairs={{80,0},{81,1},{82,2},{83,3},{84,4},{85,5},{86,6},{87,7},{88,8},{89... | collective-permute-start | bytes 442376 | tf_op jit(solution)/shard_map/ppermute | solution.py:687
  17.8 3.0 %collective-permute-start.2 = (f32[72,512]{1,0:T(8,128)S(1)}, f32[72,512]{1,0:T(8,128)S(1)}, u32[]{:S(2)}, u32[]{:S(2)}) collective-permute-start(f32[72,512]{1,0:T(8,128)S(1)} %get-tuple-element.38), channel_id=1, source_target_pairs={{64,0},{65,1},{66,2},{67,3},{68,4},{69,5},{70,6},{71,7},{72,8},{73... | collective-permute-start | bytes 442376 | tf_op jit(solution)/shard_map/ppermute | solution.py:687
  20.8 3.3 %collective-permute-done.from_y = f32[72,512]{1,0:T(8,128)S(1)} collective-permute-done((f32[72,512]{1,0:T(8,128)S(1)}, f32[72,512]{1,0:T(8,128)S(1)}, u32[]{:S(2)}, u32[]{:S(2)}) %collective-permute-start) | collective-permute-done | bytes 147488 | tf_op jit(solution)/shard_map/ppermute | solution.py:687
  24.5 4.8 %collective-permute-start.5 = (f32[224,512]{1,0:T(8,128)S(1)}, f32[224,512]{1,0:T(8,128)S(1)}, u32[]{:S(2)}, u32[]{:S(2)}) collective-permute-start(f32[224,512]{1,0:T(8,128)S(1)} %shard_map.51), channel_id=1, source_target_pairs={{0,15},{1,2},{2,1},{3,4},{4,3},{5,6},{6,5},{7,8},{8,7},{9,10},{10,... | collective-permute-start | bytes 1376264 | tf_op jit(solution)/shard_map/ppermute | solution.py:698
  29.4 2.8 %collective-permute-start.3 = (f32[168,512]{1,0:T(8,128)S(1)}, f32[168,512]{1,0:T(8,128)S(1)}, u32[]{:S(2)}, u32[]{:S(2)}) collective-permute-start(f32[168,512]{1,0:T(8,128)S(1)} %shard_map.47), channel_id=1, source_target_pairs={{0,1},{1,0},{2,3},{3,2},{4,5},{5,4},{6,7},{7,6},{8,9},{9,8},{10,11... | collective-permute-start | bytes 1032200 | tf_op jit(solution)/shard_map/ppermute | solution.py:698
  34.2 2.6 %collective-permute-start.6 = (f32[96,512]{1,0:T(8,128)S(1)}, f32[96,512]{1,0:T(8,128)S(1)}, u32[]{:S(2)}, u32[]{:S(2)}) collective-permute-start(f32[96,512]{1,0:T(8,128)S(1)} %get-tuple-element.53), channel_id=1, source_target_pairs={{0,15},{1,2},{2,1},{3,4},{4,3},{5,6},{6,5},{7,8},{8,7},{9,10},{10,... | collective-permute-start | bytes 589832 | tf_op jit(solution)/shard_map/ppermute | solution.py:698
  36.9 2.2 %shard_map.50.before = f32[16,384]{1,0:T(8,128)S(1)} custom-call(f32[384,512]{1,0:T(8,128)S(1)} %get-tuple-element.41.wide, s32[24,128]{1,0:T(8,128)S(1)} %get-tuple-element.42.places, f32[16,256]{1,0:T(8,128)S(1)} %get-tuple-element.39.start.refs_0_, f32[72,512]{1,0:T(8,128)S(1)} %collective-permute-done.from_y, ...), custom_call_target="tpu_custom_call" | custom-call | flops 268435456 | bytes 4194304 | tf_op jit(solution)/shard_map/pallas_call | solution.py:657
  41.7 3.2 %collective-permute-start.9 = (f32[16,640]{1,0:T(8,128)S(1)}, f32[16,640]{1,0:T(8,128)S(1)}, u32[]{:S(2)}, u32[]{:S(2)}) collective-permute-start(f32[16,640]{1,0:T(8,128)S(1)} %shard_map.55.own), channel_id=1, source_target_pairs={{496,0},{497,1},{498,2},{499,3},{500,4},{501,5},{502,6},{503,7},{5... | collective-permute-start | bytes 122888 | tf_op jit(solution)/shard_map/ppermute | solution.py:687
  44.9 4.3 %collective-permute-start.8 = (f32[16,640]{1,0:T(8,128)S(1)}, f32[16,640]{1,0:T(8,128)S(1)}, u32[]{:S(2)}, u32[]{:S(2)}) collective-permute-start(f32[16,640]{1,0:T(8,128)S(1)} %shard_map.55.own), channel_id=1, source_target_pairs={{48,0},{49,1},{50,2},{51,3},{52,4},{53,5},{54,6},{55,7},{56,8},{57... | collective-permute-start | bytes 122888 | tf_op jit(solution)/shard_map/ppermute | solution.py:687
  49.2 3.2 %collective-permute-start.7 = (f32[16,640]{1,0:T(8,128)S(1)}, f32[16,640]{1,0:T(8,128)S(1)}, u32[]{:S(2)}, u32[]{:S(2)}) collective-permute-start(f32[16,640]{1,0:T(8,128)S(1)} %shard_map.55.own), channel_id=1, source_target_pairs={{448,0},{449,1},{450,2},{451,3},{452,4},{453,5},{454,6},{455,7},{4... | collective-permute-start | bytes 122888 | tf_op jit(solution)/shard_map/ppermute | solution.py:687
  53.0 2.4 %collective-permute-done.7.from_x = f32[16,640]{1,0:T(8,128)S(1)} collective-permute-done((f32[16,640]{1,0:T(8,128)S(1)}, f32[16,640]{1,0:T(8,128)S(1)}, u32[]{:S(2)}, u32[]{:S(2)}) %collective-permute-start.7) | collective-permute-done | bytes 40992 | tf_op jit(solution)/shard_map/ppermute | solution.py:687
  55.5 2.3 %shard_map.56.own.second = f32[16,512]{1,0:T(8,128)S(1)} custom-call(bf16[512,512]{1,0:T(8,128)(2,1)S(1)} %get-tuple-element.54.head, bf16[512,512]{1,0:T(8,128)(2,1)S(1)} %get-tuple-element.55.middle, bf16[512,512]{1,0:T(8,128)(2,1)S(1)} %get-tuple-element.56.tail, s32[32,128]{1,0:T(8,128)S(1)} %get-tuple-element.57.places, f32[16,640]{1,0:T(8,128)S(1)} %shard_map.55.own, ...), custom_call_target="tpu_custom_call" | custom-call | tf_op jit(solution)/shard_map/pallas_call | solution.py:657
  57.8 4.3 %collective-permute-start.12 = (f32[16,512]{1,0:T(8,128)S(1)}, f32[16,512]{1,0:T(8,128)S(1)}, u32[]{:S(2)}, u32[]{:S(2)}) collective-permute-start(f32[16,512]{1,0:T(8,128)S(1)} %shard_map.56.own.second), channel_id=1, source_target_pairs={{80,0},{81,1},{82,2},{83,3},{84,4},{85,5},{86,6},{87,7},{88,8},{89... | collective-permute-start | bytes 98312 | tf_op jit(solution)/shard_map/ppermute | solution.py:687
  62.1 3.6 %collective-permute-start.11 = (f32[16,512]{1,0:T(8,128)S(1)}, f32[16,512]{1,0:T(8,128)S(1)}, u32[]{:S(2)}, u32[]{:S(2)}) collective-permute-start(f32[16,512]{1,0:T(8,128)S(1)} %shard_map.56.own.second), channel_id=1, source_target_pairs={{16,0},{17,1},{18,2},{19,3},{20,4},{21,5},{22,6},{23,7},{24,8},{25... | collective-permute-start | bytes 98312 | tf_op jit(solution)/shard_map/ppermute | solution.py:687
  65.7 4.0 %collective-permute-start.10 = (f32[16,512]{1,0:T(8,128)S(1)}, f32[16,512]{1,0:T(8,128)S(1)}, u32[]{:S(2)}, u32[]{:S(2)}) collective-permute-start(f32[16,512]{1,0:T(8,128)S(1)} %shard_map.56.own.second), channel_id=1, source_target_pairs={{64,0},{65,1},{66,2},{67,3},{68,4},{69,5},{70,6},{71,7},{72,8},{73... | collective-permute-start | bytes 98312 | tf_op jit(solution)/shard_map/ppermute | solution.py:687
  70.8 2.0 %shard_map.57.own = f32[16,384]{1,0:T(8,128)S(1)} custom-call(bf16[384,512]{1,0:T(8,128)(2,1)S(1)} %get-tuple-element.49.head, bf16[384,512]{1,0:T(8,128)(2,1)S(1)} %get-tuple-element.50.middle, bf16[384,512]{1,0:T(8,128)(2,1)S(1)} %get-tuple-element.51.tail, s32[24,128]{1,0:T(8,128)S(1)} %get-tuple-element.52.places, f32[16,512]{1,0:T(8,128)S(1)} %shard_map.56.own.second, ...), custom_call_target="tpu_custom_call" | custom-call | tf_op jit(solution)/shard_map/pallas_call | solution.py:657
  72.7 2.2 %collective-permute-start.15 = (f32[16,384]{1,0:T(8,128)S(1)}, f32[16,384]{1,0:T(8,128)S(1)}, u32[]{:S(2)}, u32[]{:S(2)}) collective-permute-start(f32[16,384]{1,0:T(8,128)S(1)} %shard_map.57.own), channel_id=1, source_target_pairs={{496,0},{497,1},{498,2},{499,3},{500,4},{501,5},{502,6},{503,7},{5... | collective-permute-start | bytes 73736 | tf_op jit(solution)/shard_map/ppermute | solution.py:687
  75.0 4.6 %collective-permute-start.14 = (f32[16,384]{1,0:T(8,128)S(1)}, f32[16,384]{1,0:T(8,128)S(1)}, u32[]{:S(2)}, u32[]{:S(2)}) collective-permute-start(f32[16,384]{1,0:T(8,128)S(1)} %shard_map.57.own), channel_id=1, source_target_pairs={{48,0},{49,1},{50,2},{51,3},{52,4},{53,5},{54,6},{55,7},{56,8},{57... | collective-permute-start | bytes 73736 | tf_op jit(solution)/shard_map/ppermute | solution.py:687
  79.6 3.5 %collective-permute-start.13 = (f32[16,384]{1,0:T(8,128)S(1)}, f32[16,384]{1,0:T(8,128)S(1)}, u32[]{:S(2)}, u32[]{:S(2)}) collective-permute-start(f32[16,384]{1,0:T(8,128)S(1)} %shard_map.57.own), channel_id=1, source_target_pairs={{448,0},{449,1},{450,2},{451,3},{452,4},{453,5},{454,6},{455,7},{4... | collective-permute-start | bytes 73736 | tf_op jit(solution)/shard_map/ppermute | solution.py:687
  83.3 2.1 %collective-permute-done.13.from_x = f32[16,384]{1,0:T(8,128)S(1)} collective-permute-done((f32[16,384]{1,0:T(8,128)S(1)}, f32[16,384]{1,0:T(8,128)S(1)}, u32[]{:S(2)}, u32[]{:S(2)}) %collective-permute-start.13) | collective-permute-done | bytes 24608 | tf_op jit(solution)/shard_map/ppermute | solution.py:687
  85.4 2.0 %shard_map.59 = (f32[16,256]{1,0:T(8,128)S(1)}, f32[32,4,128]{2,1,0:T(4,128)S(1)}) custom-call(bf16[256,512]{1,0:T(8,128)(2,1)S(1)} %get-tuple-element.45.head, bf16[256,512]{1,0:T(8,128)(2,1)S(1)} %get-tuple-element.46.middle, bf16[256,512]{1,0:T(8,128)(2,1)S(1)} %get-tuple-element.47.tail, s32[16,128]{1,0:T(8,128)S(1)} %get-tuple-element.48.places, ...), custom_call_target="tpu_custom_call" | custom-call | tf_op jit(solution)/shard_map/pallas_call | solution.py:657
  87.4 19.7 %all_to_all.10.ref = f32[32,4,128]{2,1,0:T(4,128)S(1)} all-to-all(f32[32,4,128]{2,1,0:T(4,128)S(1)} %get-tuple-element.63), channel_id=1, replica_groups=mesh['gx'=8,'gy'=4,'gz'=16] {'gx','gy'}, dimensions={0} | all-to-all | bytes 131072 | tf_op jit(solution)/shard_map/all_to_all | solution.py:775
  107.1 18.8 %all_to_all.11.ref = f32[16,4,128]{2,1,0:T(4,128)S(1)} all-to-all(f32[16,4,128]{2,1,0:T(4,128)S(1)} %shard_map.60), channel_id=1, replica_groups=mesh['gx'=8,'gy'=4,'gz'=16] {'gz'}, dimensions={0} | all-to-all | bytes 65536 | tf_op jit(solution)/shard_map/all_to_all | solution.py:777
  (26 shorter events, 9.6 us)
Async XLA Ops:
  1.2 22.9 %collective-permute-start = (f32[72,512]{1,0:T(8,128)S(1)}, f32[72,512]{1,0:T(8,128)S(1)}, u32[]{:S(2)}, u32[]{:S(2)}) collective-permute-start(f32[72,512]{1,0:T(8,128)S(1)} %get-tuple-element.36), channel_id=1, source_target_pairs={{16,0},{17,1},{18,2},{19,3},{20,4},{21,5},{22,6},{23,7},{24,8},{25... | collective-permute-start | bytes 442376 | tf_op jit(solution)/shard_map/ppermute | solution.py:687
  12.7 11.4 %collective-permute-start.1 = (f32[72,512]{1,0:T(8,128)S(1)}, f32[72,512]{1,0:T(8,128)S(1)}, u32[]{:S(2)}, u32[]{:S(2)}) collective-permute-start(f32[72,512]{1,0:T(8,128)S(1)} %get-tuple-element.37), channel_id=1, source_target_pairs={{80,0},{81,1},{82,2},{83,3},{84,4},{85,5},{86,6},{87,7},{88,8},{89... | collective-permute-start | bytes 442376 | tf_op jit(solution)/shard_map/ppermute | solution.py:687
  17.8 6.7 %collective-permute-start.2 = (f32[72,512]{1,0:T(8,128)S(1)}, f32[72,512]{1,0:T(8,128)S(1)}, u32[]{:S(2)}, u32[]{:S(2)}) collective-permute-start(f32[72,512]{1,0:T(8,128)S(1)} %get-tuple-element.38), channel_id=1, source_target_pairs={{64,0},{65,1},{66,2},{67,3},{68,4},{69,5},{70,6},{71,7},{72,8},{73... | collective-permute-start | bytes 442376 | tf_op jit(solution)/shard_map/ppermute | solution.py:687
  24.5 15.3 %collective-permute-start.5 = (f32[224,512]{1,0:T(8,128)S(1)}, f32[224,512]{1,0:T(8,128)S(1)}, u32[]{:S(2)}, u32[]{:S(2)}) collective-permute-start(f32[224,512]{1,0:T(8,128)S(1)} %shard_map.51), channel_id=1, source_target_pairs={{0,15},{1,2},{2,1},{3,4},{4,3},{5,6},{6,5},{7,8},{8,7},{9,10},{10,... | collective-permute-start | bytes 1376264 | tf_op jit(solution)/shard_map/ppermute | solution.py:698
  29.4 7.4 %collective-permute-start.3 = (f32[168,512]{1,0:T(8,128)S(1)}, f32[168,512]{1,0:T(8,128)S(1)}, u32[]{:S(2)}, u32[]{:S(2)}) collective-permute-start(f32[168,512]{1,0:T(8,128)S(1)} %shard_map.47), channel_id=1, source_target_pairs={{0,1},{1,0},{2,3},{3,2},{4,5},{5,4},{6,7},{7,6},{8,9},{9,8},{10,11... | collective-permute-start | bytes 1032200 | tf_op jit(solution)/shard_map/ppermute | solution.py:698
  32.2 4.6 %collective-permute-start.4 = (f32[152,512]{1,0:T(8,128)S(1)}, f32[152,512]{1,0:T(8,128)S(1)}, u32[]{:S(2)}, u32[]{:S(2)}) collective-permute-start(f32[152,512]{1,0:T(8,128)S(1)} %get-tuple-element.40), channel_id=1, source_target_pairs={{0,1},{1,0},{2,3},{3,2},{4,5},{5,4},{6,7},{7,6},{8,9},{9,8},{10,11... | collective-permute-start | bytes 933896 | tf_op jit(solution)/shard_map/ppermute | solution.py:698
  34.2 18.3 %collective-permute-start.6 = (f32[96,512]{1,0:T(8,128)S(1)}, f32[96,512]{1,0:T(8,128)S(1)}, u32[]{:S(2)}, u32[]{:S(2)}) collective-permute-start(f32[96,512]{1,0:T(8,128)S(1)} %get-tuple-element.53), channel_id=1, source_target_pairs={{0,15},{1,2},{2,1},{3,4},{4,3},{5,6},{6,5},{7,8},{8,7},{9,10},{10,... | collective-permute-start | bytes 589832 | tf_op jit(solution)/shard_map/ppermute | solution.py:698
  41.7 11.3 %collective-permute-start.9 = (f32[16,640]{1,0:T(8,128)S(1)}, f32[16,640]{1,0:T(8,128)S(1)}, u32[]{:S(2)}, u32[]{:S(2)}) collective-permute-start(f32[16,640]{1,0:T(8,128)S(1)} %shard_map.55.own), channel_id=1, source_target_pairs={{496,0},{497,1},{498,2},{499,3},{500,4},{501,5},{502,6},{503,7},{5... | collective-permute-start | bytes 122888 | tf_op jit(solution)/shard_map/ppermute | solution.py:687
  44.9 8.1 %collective-permute-start.8 = (f32[16,640]{1,0:T(8,128)S(1)}, f32[16,640]{1,0:T(8,128)S(1)}, u32[]{:S(2)}, u32[]{:S(2)}) collective-permute-start(f32[16,640]{1,0:T(8,128)S(1)} %shard_map.55.own), channel_id=1, source_target_pairs={{48,0},{49,1},{50,2},{51,3},{52,4},{53,5},{54,6},{55,7},{56,8},{57... | collective-permute-start | bytes 122888 | tf_op jit(solution)/shard_map/ppermute | solution.py:687
  49.2 6.3 %collective-permute-start.7 = (f32[16,640]{1,0:T(8,128)S(1)}, f32[16,640]{1,0:T(8,128)S(1)}, u32[]{:S(2)}, u32[]{:S(2)}) collective-permute-start(f32[16,640]{1,0:T(8,128)S(1)} %shard_map.55.own), channel_id=1, source_target_pairs={{448,0},{449,1},{450,2},{451,3},{452,4},{453,5},{454,6},{455,7},{4... | collective-permute-start | bytes 122888 | tf_op jit(solution)/shard_map/ppermute | solution.py:687
  57.8 12.7 %collective-permute-start.12 = (f32[16,512]{1,0:T(8,128)S(1)}, f32[16,512]{1,0:T(8,128)S(1)}, u32[]{:S(2)}, u32[]{:S(2)}) collective-permute-start(f32[16,512]{1,0:T(8,128)S(1)} %shard_map.56.own.second), channel_id=1, source_target_pairs={{80,0},{81,1},{82,2},{83,3},{84,4},{85,5},{86,6},{87,7},{88,8},{89... | collective-permute-start | bytes 98312 | tf_op jit(solution)/shard_map/ppermute | solution.py:687
  62.1 8.4 %collective-permute-start.11 = (f32[16,512]{1,0:T(8,128)S(1)}, f32[16,512]{1,0:T(8,128)S(1)}, u32[]{:S(2)}, u32[]{:S(2)}) collective-permute-start(f32[16,512]{1,0:T(8,128)S(1)} %shard_map.56.own.second), channel_id=1, source_target_pairs={{16,0},{17,1},{18,2},{19,3},{20,4},{21,5},{22,6},{23,7},{24,8},{25... | collective-permute-start | bytes 98312 | tf_op jit(solution)/shard_map/ppermute | solution.py:687
  65.7 5.0 %collective-permute-start.10 = (f32[16,512]{1,0:T(8,128)S(1)}, f32[16,512]{1,0:T(8,128)S(1)}, u32[]{:S(2)}, u32[]{:S(2)}) collective-permute-start(f32[16,512]{1,0:T(8,128)S(1)} %shard_map.56.own.second), channel_id=1, source_target_pairs={{64,0},{65,1},{66,2},{67,3},{68,4},{69,5},{70,6},{71,7},{72,8},{73... | collective-permute-start | bytes 98312 | tf_op jit(solution)/shard_map/ppermute | solution.py:687
  72.7 10.5 %collective-permute-start.15 = (f32[16,384]{1,0:T(8,128)S(1)}, f32[16,384]{1,0:T(8,128)S(1)}, u32[]{:S(2)}, u32[]{:S(2)}) collective-permute-start(f32[16,384]{1,0:T(8,128)S(1)} %shard_map.57.own), channel_id=1, source_target_pairs={{496,0},{497,1},{498,2},{499,3},{500,4},{501,5},{502,6},{503,7},{5... | collective-permute-start | bytes 73736 | tf_op jit(solution)/shard_map/ppermute | solution.py:687
  75.0 8.3 %collective-permute-start.14 = (f32[16,384]{1,0:T(8,128)S(1)}, f32[16,384]{1,0:T(8,128)S(1)}, u32[]{:S(2)}, u32[]{:S(2)}) collective-permute-start(f32[16,384]{1,0:T(8,128)S(1)} %shard_map.57.own), channel_id=1, source_target_pairs={{48,0},{49,1},{50,2},{51,3},{52,4},{53,5},{54,6},{55,7},{56,8},{57... | collective-permute-start | bytes 73736 | tf_op jit(solution)/shard_map/ppermute | solution.py:687
  79.6 5.8 %collective-permute-start.13 = (f32[16,384]{1,0:T(8,128)S(1)}, f32[16,384]{1,0:T(8,128)S(1)}, u32[]{:S(2)}, u32[]{:S(2)}) collective-permute-start(f32[16,384]{1,0:T(8,128)S(1)} %shard_map.57.own), channel_id=1, source_target_pairs={{448,0},{449,1},{450,2},{451,3},{452,4},{453,5},{454,6},{455,7},{4... | collective-permute-start | bytes 73736 | tf_op jit(solution)/shard_map/ppermute | solution.py:687

commit v14 on v13

--- a/solution.py
+++ b/solution.py
@@ -576,41 +576,50 @@
 WIDE_FLOPS = 1 << 28
 
 
-def first_tiles(rows, places, start, from_y, from_xy, from_x, bricks, field, gathered):
+def first_tiles(rows, places, start, from_y, from_xy, from_x, bricks, field, gathered, listed, sem):
     pieces = [start[...]] + [unpack_bricks(ref[64:72]) for ref in (from_y, from_x, from_xy)]
+    copy = pltpu.make_async_copy(places, listed, sem)
+    copy.start()
     set_tiles(field, pieces + [unpack_bricks(brick) for brick in bricks])
-    return couple(rows, rows.shape[0] // SLOT_ROWS, field, places, gathered)
+    copy.wait()
+    return couple(rows, rows.shape[0] // SLOT_ROWS, field, listed, gathered)
 
 
 def first_wide_kernel(
-    wide, places, start, from_y, from_xy, from_x, first, own_first, out, field, gathered
+    wide, places, start, from_y, from_xy, from_x, first, own_first, out, field, gathered, listed, sem
 ):
     bricks = [own_first[144:152]] + [first[144 + q * 8 : 152 + q * 8] for q in range(3)]
-    out[...] = first_tiles(wide, places, start, from_y, from_xy, from_x, bricks, field, gathered)
+    out[...] = first_tiles(wide, places, start, from_y, from_xy, from_x, bricks, field, gathered, listed, sem)
 
 
 def first_slim_kernel(
-    slim, places, start, from_y, from_xy, from_x, second, before, out, field, gathered
+    slim, places, start, from_y, from_xy, from_x, second, before, out, field, gathered, listed, sem
 ):
     bricks = [second[192 + q * 8 : 200 + q * 8] for q in range(4)]
     out[:, 0 : 3 * LANES] = before[...]
     out[:, 3 * LANES : 5 * LANES] = first_tiles(
-        slim, places, start, from_y, from_xy, from_x, bricks, field, gathered
+        slim, places, start, from_y, from_xy, from_x, bricks, field, gathered, listed, sem
     )
 
 
 def second_kernel(
-    head, middle, tail, places, own, from_x, from_y, from_xy, out, field, gathered
+    head, middle, tail, places, own, from_x, from_y, from_xy, out, field, gathered, listed, sem
 ):
+    copy = pltpu.make_async_copy(places, listed, sem)
+    copy.start()
     set_tiles(field, (from_xy, from_x, from_y, own))
-    out[...] = couple((head, middle, tail), 32, field, places, gathered)
+    copy.wait()
+    out[...] = couple((head, middle, tail), 32, field, listed, gathered)
 
 
 def third_kernel(
-    head, middle, tail, places, own, from_x, from_y, from_xy, out, field, gathered
+    head, middle, tail, places, own, from_x, from_y, from_xy, out, field, gathered, listed, sem
 ):
+    copy = pltpu.make_async_copy(places, listed, sem)
+    copy.start()
     set_tiles(field, (own, from_y, from_x, from_xy))
-    out[...] = couple((head, middle, tail), 24, field, places, gathered)
+    copy.wait()
+    out[...] = couple((head, middle, tail), 24, field, listed, gathered)
 
 
 def pick_kernel(own, from_x, from_y, from_xy, second, start, first_own, second_own, early):
@@ -628,17 +637,17 @@
 def last_kernel(
     head, middle, tail, places, own, from_x, from_y, from_xy, start, first, second, early,
     third_out, out,
-    field, gathered,
+    field, gathered, listed, sem,
 ):
     pieces = from_xy, from_x, from_y, own
+    copy = pltpu.make_async_copy(places, listed, sem)
+    copy.start()
     set_tiles(field, pieces)
-    fourth = couple((head, middle, tail), ATOMS, field, places, gathered)
+    copy.wait()
+    fourth = couple((head, middle, tail), ATOMS, field, listed, gathered)
     third = pick_own(pieces, THIRD_PLACE)
     third_out[...] = third
     gram_kernel([start[...], first[...], second[...], third, fourth], early, out)
-
-
-SMEM = pl.BlockSpec(memory_space=pltpu.SMEM)
 
 
 def cut(atoms):
@@ -657,9 +666,7 @@
     return pl.pallas_call(
         kernel,
         out_shape=shapes,
-        in_specs=[
-            SMEM if operand.dtype == jnp.int32 and place is VMEM else place for operand in operands
-        ],
+        in_specs=[place] * len(operands),
         out_specs=[VMEM] * len(shapes),
         scratch_shapes=list(scratch),
         cost_estimate=pl.CostEstimate(flops=flops, bytes_accessed=flops // 64, transcendentals=0)
@@ -673,6 +680,8 @@
     return (
         pltpu.VMEM((tiles * 8, SLOT_ROWS, LANES), jnp.float32),
         pltpu.VMEM((groups, CODE, LANES), jnp.float32),
+        pltpu.SMEM((groups * 8, LANES), jnp.int32),
+        pltpu.SemaphoreType.DMA,
     )
 
 

time: 128 us -> 128 us (level)
  no operation moved by 1% of the time
where the time goes in v14:
time: 128 us; the launch traced here: 127 us
  starting transfers between devices  64.6 us (50%)
  blocking collectives  38.4 us (30%)
  Pallas kernels  14.3 us (11%)
  waiting for transfers between devices  9.19 us (7%)
    ppermute x12, starting transfers between devices, fetch(): return lax.ppermute(value, AXES, pairs)  52.5 us
    all_to_all x1, blocking collectives, body(): message = lax.all_to_all(message, ('gx', 'gy'), 0, 0, tiled=True)  19.6 us
    all_to_all x1, blocking collectives, body(): message = lax.all_to_all(message, 'gz', 0, 0, tiled=True)  18.8 us
    pallas_call x16, Pallas kernels, call(): pl.pallas_call(kernel, out_shape=shapes, in_specs=[place] * len(operands)...  14.3 us
    ppermute x12, waiting for transfers between devices, fetch(): return lax.ppermute(value, AXES, pairs)  8.49 us
    ppermute x2, starting transfers between devices, swap_layers(): lax.ppermute(to_second, 'gz', odd)  7.41 us
    ppermute x2, starting transfers between devices, swap_layers(): lax.ppermute(to_first, 'gz', even)  4.73 us
  transfers between devices with their start and end apart: 16, of which 6 were waited for; matrix products, arithmetic and copies ran while one was open for 0% of the time, Pallas kernels for 5%

profile of v14, /device:TPU:1, one launch (start us, length us, event | category | flops | bytes accessed | tf_op | source)
XLA Modules:
  0.0 126.8 jit_solution(9213659583377605590)
XLA Ops:
  1.2 11.5 %collective-permute-start = (f32[72,512]{1,0:T(8,128)S(1)}, f32[72,512]{1,0:T(8,128)S(1)}, u32[]{:S(2)}, u32[]{:S(2)}) collective-permute-start(f32[72,512]{1,0:T(8,128)S(1)} %get-tuple-element.36), channel_id=1, source_target_pairs={{16,0},{17,1},{18,2},{19,3},{20,4},{21,5},{22,6},{23,7},{24,8},{25... | collective-permute-start | bytes 442376 | tf_op jit(solution)/shard_map/ppermute | solution.py:696
  12.7 5.1 %collective-permute-start.1 = (f32[72,512]{1,0:T(8,128)S(1)}, f32[72,512]{1,0:T(8,128)S(1)}, u32[]{:S(2)}, u32[]{:S(2)}) collective-permute-start(f32[72,512]{1,0:T(8,128)S(1)} %get-tuple-element.37), channel_id=1, source_target_pairs={{80,0},{81,1},{82,2},{83,3},{84,4},{85,5},{86,6},{87,7},{88,8},{89... | collective-permute-start | bytes 442376 | tf_op jit(solution)/shard_map/ppermute | solution.py:696
  17.8 3.0 %collective-permute-start.2 = (f32[72,512]{1,0:T(8,128)S(1)}, f32[72,512]{1,0:T(8,128)S(1)}, u32[]{:S(2)}, u32[]{:S(2)}) collective-permute-start(f32[72,512]{1,0:T(8,128)S(1)} %get-tuple-element.38), channel_id=1, source_target_pairs={{64,0},{65,1},{66,2},{67,3},{68,4},{69,5},{70,6},{71,7},{72,8},{73... | collective-permute-start | bytes 442376 | tf_op jit(solution)/shard_map/ppermute | solution.py:696
  20.8 3.3 %collective-permute-done.from_y = f32[72,512]{1,0:T(8,128)S(1)} collective-permute-done((f32[72,512]{1,0:T(8,128)S(1)}, f32[72,512]{1,0:T(8,128)S(1)}, u32[]{:S(2)}, u32[]{:S(2)}) %collective-permute-start) | collective-permute-done | bytes 147488 | tf_op jit(solution)/shard_map/ppermute | solution.py:696
  24.5 4.8 %collective-permute-start.5 = (f32[224,512]{1,0:T(8,128)S(1)}, f32[224,512]{1,0:T(8,128)S(1)}, u32[]{:S(2)}, u32[]{:S(2)}) collective-permute-start(f32[224,512]{1,0:T(8,128)S(1)} %shard_map.51), channel_id=1, source_target_pairs={{0,15},{1,2},{2,1},{3,4},{4,3},{5,6},{6,5},{7,8},{8,7},{9,10},{10,... | collective-permute-start | bytes 1376264 | tf_op jit(solution)/shard_map/ppermute | solution.py:707
  29.4 2.8 %collective-permute-start.3 = (f32[168,512]{1,0:T(8,128)S(1)}, f32[168,512]{1,0:T(8,128)S(1)}, u32[]{:S(2)}, u32[]{:S(2)}) collective-permute-start(f32[168,512]{1,0:T(8,128)S(1)} %shard_map.47), channel_id=1, source_target_pairs={{0,1},{1,0},{2,3},{3,2},{4,5},{5,4},{6,7},{7,6},{8,9},{9,8},{10,11... | collective-permute-start | bytes 1032200 | tf_op jit(solution)/shard_map/ppermute | solution.py:707
  32.2 1.9 %collective-permute-start.4 = (f32[152,512]{1,0:T(8,128)S(1)}, f32[152,512]{1,0:T(8,128)S(1)}, u32[]{:S(2)}, u32[]{:S(2)}) collective-permute-start(f32[152,512]{1,0:T(8,128)S(1)} %get-tuple-element.40), channel_id=1, source_target_pairs={{0,1},{1,0},{2,3},{3,2},{4,5},{5,4},{6,7},{7,6},{8,9},{9,8},{10,11... | collective-permute-start | bytes 933896 | tf_op jit(solution)/shard_map/ppermute | solution.py:707
  34.2 2.6 %collective-permute-start.6 = (f32[96,512]{1,0:T(8,128)S(1)}, f32[96,512]{1,0:T(8,128)S(1)}, u32[]{:S(2)}, u32[]{:S(2)}) collective-permute-start(f32[96,512]{1,0:T(8,128)S(1)} %get-tuple-element.53), channel_id=1, source_target_pairs={{0,15},{1,2},{2,1},{3,4},{4,3},{5,6},{6,5},{7,8},{8,7},{9,10},{10,... | collective-permute-start | bytes 589832 | tf_op jit(solution)/shard_map/ppermute | solution.py:707
  36.9 2.2 %shard_map.50.before = f32[16,384]{1,0:T(8,128)S(1)} custom-call(f32[384,512]{1,0:T(8,128)S(1)} %get-tuple-element.41.wide, s32[24,128]{1,0:T(8,128)S(1)} %get-tuple-element.42.places, f32[16,256]{1,0:T(8,128)S(1)} %get-tuple-element.39.start.refs_0_, f32[72,512]{1,0:T(8,128)S(1)} %collective-permute-done.from_y, ...), custom_call_target="tpu_custom_call" | custom-call | flops 268435456 | bytes 4194304 | tf_op jit(solution)/shard_map/pallas_call | solution.py:666
  41.7 3.2 %collective-permute-start.9 = (f32[16,640]{1,0:T(8,128)S(1)}, f32[16,640]{1,0:T(8,128)S(1)}, u32[]{:S(2)}, u32[]{:S(2)}) collective-permute-start(f32[16,640]{1,0:T(8,128)S(1)} %shard_map.55.own), channel_id=1, source_target_pairs={{496,0},{497,1},{498,2},{499,3},{500,4},{501,5},{502,6},{503,7},{5... | collective-permute-start | bytes 122888 | tf_op jit(solution)/shard_map/ppermute | solution.py:696
  44.9 4.3 %collective-permute-start.8 = (f32[16,640]{1,0:T(8,128)S(1)}, f32[16,640]{1,0:T(8,128)S(1)}, u32[]{:S(2)}, u32[]{:S(2)}) collective-permute-start(f32[16,640]{1,0:T(8,128)S(1)} %shard_map.55.own), channel_id=1, source_target_pairs={{48,0},{49,1},{50,2},{51,3},{52,4},{53,5},{54,6},{55,7},{56,8},{57... | collective-permute-start | bytes 122888 | tf_op jit(solution)/shard_map/ppermute | solution.py:696
  49.2 3.2 %collective-permute-start.7 = (f32[16,640]{1,0:T(8,128)S(1)}, f32[16,640]{1,0:T(8,128)S(1)}, u32[]{:S(2)}, u32[]{:S(2)}) collective-permute-start(f32[16,640]{1,0:T(8,128)S(1)} %shard_map.55.own), channel_id=1, source_target_pairs={{448,0},{449,1},{450,2},{451,3},{452,4},{453,5},{454,6},{455,7},{4... | collective-permute-start | bytes 122888 | tf_op jit(solution)/shard_map/ppermute | solution.py:696
  53.0 2.4 %collective-permute-done.7.from_x = f32[16,640]{1,0:T(8,128)S(1)} collective-permute-done((f32[16,640]{1,0:T(8,128)S(1)}, f32[16,640]{1,0:T(8,128)S(1)}, u32[]{:S(2)}, u32[]{:S(2)}) %collective-permute-start.7) | collective-permute-done | bytes 40992 | tf_op jit(solution)/shard_map/ppermute | solution.py:696
  55.4 2.3 %shard_map.56.own.second = f32[16,512]{1,0:T(8,128)S(1)} custom-call(bf16[512,512]{1,0:T(8,128)(2,1)S(1)} %get-tuple-element.54.head, bf16[512,512]{1,0:T(8,128)(2,1)S(1)} %get-tuple-element.55.middle, bf16[512,512]{1,0:T(8,128)(2,1)S(1)} %get-tuple-element.56.tail, s32[32,128]{1,0:T(8,128)S(1)} %get-tuple-element.57.places, f32[16,640]{1,0:T(8,128)S(1)} %shard_map.55.own, ...), custom_call_target="tpu_custom_call" | custom-call | tf_op jit(solution)/shard_map/pallas_call | solution.py:666
  57.7 4.3 %collective-permute-start.12 = (f32[16,512]{1,0:T(8,128)S(1)}, f32[16,512]{1,0:T(8,128)S(1)}, u32[]{:S(2)}, u32[]{:S(2)}) collective-permute-start(f32[16,512]{1,0:T(8,128)S(1)} %shard_map.56.own.second), channel_id=1, source_target_pairs={{80,0},{81,1},{82,2},{83,3},{84,4},{85,5},{86,6},{87,7},{88,8},{89... | collective-permute-start | bytes 98312 | tf_op jit(solution)/shard_map/ppermute | solution.py:696
  62.0 3.6 %collective-permute-start.11 = (f32[16,512]{1,0:T(8,128)S(1)}, f32[16,512]{1,0:T(8,128)S(1)}, u32[]{:S(2)}, u32[]{:S(2)}) collective-permute-start(f32[16,512]{1,0:T(8,128)S(1)} %shard_map.56.own.second), channel_id=1, source_target_pairs={{16,0},{17,1},{18,2},{19,3},{20,4},{21,5},{22,6},{23,7},{24,8},{25... | collective-permute-start | bytes 98312 | tf_op jit(solution)/shard_map/ppermute | solution.py:696
  65.6 4.0 %collective-permute-start.10 = (f32[16,512]{1,0:T(8,128)S(1)}, f32[16,512]{1,0:T(8,128)S(1)}, u32[]{:S(2)}, u32[]{:S(2)}) collective-permute-start(f32[16,512]{1,0:T(8,128)S(1)} %shard_map.56.own.second), channel_id=1, source_target_pairs={{64,0},{65,1},{66,2},{67,3},{68,4},{69,5},{70,6},{71,7},{72,8},{73... | collective-permute-start | bytes 98312 | tf_op jit(solution)/shard_map/ppermute | solution.py:696
  70.7 1.9 %shard_map.57.own = f32[16,384]{1,0:T(8,128)S(1)} custom-call(bf16[384,512]{1,0:T(8,128)(2,1)S(1)} %get-tuple-element.49.head, bf16[384,512]{1,0:T(8,128)(2,1)S(1)} %get-tuple-element.50.middle, bf16[384,512]{1,0:T(8,128)(2,1)S(1)} %get-tuple-element.51.tail, s32[24,128]{1,0:T(8,128)S(1)} %get-tuple-element.52.places, f32[16,512]{1,0:T(8,128)S(1)} %shard_map.56.own.second, ...), custom_call_target="tpu_custom_call" | custom-call | tf_op jit(solution)/shard_map/pallas_call | solution.py:666
  72.6 2.2 %collective-permute-start.15 = (f32[16,384]{1,0:T(8,128)S(1)}, f32[16,384]{1,0:T(8,128)S(1)}, u32[]{:S(2)}, u32[]{:S(2)}) collective-permute-start(f32[16,384]{1,0:T(8,128)S(1)} %shard_map.57.own), channel_id=1, source_target_pairs={{496,0},{497,1},{498,2},{499,3},{500,4},{501,5},{502,6},{503,7},{5... | collective-permute-start | bytes 73736 | tf_op jit(solution)/shard_map/ppermute | solution.py:696
  74.8 4.6 %collective-permute-start.14 = (f32[16,384]{1,0:T(8,128)S(1)}, f32[16,384]{1,0:T(8,128)S(1)}, u32[]{:S(2)}, u32[]{:S(2)}) collective-permute-start(f32[16,384]{1,0:T(8,128)S(1)} %shard_map.57.own), channel_id=1, source_target_pairs={{48,0},{49,1},{50,2},{51,3},{52,4},{53,5},{54,6},{55,7},{56,8},{57... | collective-permute-start | bytes 73736 | tf_op jit(solution)/shard_map/ppermute | solution.py:696
  79.4 3.5 %collective-permute-start.13 = (f32[16,384]{1,0:T(8,128)S(1)}, f32[16,384]{1,0:T(8,128)S(1)}, u32[]{:S(2)}, u32[]{:S(2)}) collective-permute-start(f32[16,384]{1,0:T(8,128)S(1)} %shard_map.57.own), channel_id=1, source_target_pairs={{448,0},{449,1},{450,2},{451,3},{452,4},{453,5},{454,6},{455,7},{4... | collective-permute-start | bytes 73736 | tf_op jit(solution)/shard_map/ppermute | solution.py:696
  83.1 2.1 %collective-permute-done.13.from_x = f32[16,384]{1,0:T(8,128)S(1)} collective-permute-done((f32[16,384]{1,0:T(8,128)S(1)}, f32[16,384]{1,0:T(8,128)S(1)}, u32[]{:S(2)}, u32[]{:S(2)}) %collective-permute-start.13) | collective-permute-done | bytes 24608 | tf_op jit(solution)/shard_map/ppermute | solution.py:696
  86.9 19.6 %all_to_all.10.ref = f32[32,4,128]{2,1,0:T(4,128)S(1)} all-to-all(f32[32,4,128]{2,1,0:T(4,128)S(1)} %get-tuple-element.63), channel_id=1, replica_groups=mesh['gx'=8,'gy'=4,'gz'=16] {'gx','gy'}, dimensions={0} | all-to-all | bytes 131072 | tf_op jit(solution)/shard_map/all_to_all | solution.py:784
  106.6 18.8 %all_to_all.11.ref = f32[16,4,128]{2,1,0:T(4,128)S(1)} all-to-all(f32[16,4,128]{2,1,0:T(4,128)S(1)} %shard_map.60), channel_id=1, replica_groups=mesh['gx'=8,'gy'=4,'gz'=16] {'gz'}, dimensions={0} | all-to-all | bytes 65536 | tf_op jit(solution)/shard_map/all_to_all | solution.py:786
  (26 shorter events, 9.4 us)
Async XLA Ops:
  1.2 22.9 %collective-permute-start = (f32[72,512]{1,0:T(8,128)S(1)}, f32[72,512]{1,0:T(8,128)S(1)}, u32[]{:S(2)}, u32[]{:S(2)}) collective-permute-start(f32[72,512]{1,0:T(8,128)S(1)} %get-tuple-element.36), channel_id=1, source_target_pairs={{16,0},{17,1},{18,2},{19,3},{20,4},{21,5},{22,6},{23,7},{24,8},{25... | collective-permute-start | bytes 442376 | tf_op jit(solution)/shard_map/ppermute | solution.py:696
  12.7 11.4 %collective-permute-start.1 = (f32[72,512]{1,0:T(8,128)S(1)}, f32[72,512]{1,0:T(8,128)S(1)}, u32[]{:S(2)}, u32[]{:S(2)}) collective-permute-start(f32[72,512]{1,0:T(8,128)S(1)} %get-tuple-element.37), channel_id=1, source_target_pairs={{80,0},{81,1},{82,2},{83,3},{84,4},{85,5},{86,6},{87,7},{88,8},{89... | collective-permute-start | bytes 442376 | tf_op jit(solution)/shard_map/ppermute | solution.py:696
  17.8 6.7 %collective-permute-start.2 = (f32[72,512]{1,0:T(8,128)S(1)}, f32[72,512]{1,0:T(8,128)S(1)}, u32[]{:S(2)}, u32[]{:S(2)}) collective-permute-start(f32[72,512]{1,0:T(8,128)S(1)} %get-tuple-element.38), channel_id=1, source_target_pairs={{64,0},{65,1},{66,2},{67,3},{68,4},{69,5},{70,6},{71,7},{72,8},{73... | collective-permute-start | bytes 442376 | tf_op jit(solution)/shard_map/ppermute | solution.py:696
  24.5 15.3 %collective-permute-start.5 = (f32[224,512]{1,0:T(8,128)S(1)}, f32[224,512]{1,0:T(8,128)S(1)}, u32[]{:S(2)}, u32[]{:S(2)}) collective-permute-start(f32[224,512]{1,0:T(8,128)S(1)} %shard_map.51), channel_id=1, source_target_pairs={{0,15},{1,2},{2,1},{3,4},{4,3},{5,6},{6,5},{7,8},{8,7},{9,10},{10,... | collective-permute-start | bytes 1376264 | tf_op jit(solution)/shard_map/ppermute | solution.py:707
  29.4 7.4 %collective-permute-start.3 = (f32[168,512]{1,0:T(8,128)S(1)}, f32[168,512]{1,0:T(8,128)S(1)}, u32[]{:S(2)}, u32[]{:S(2)}) collective-permute-start(f32[168,512]{1,0:T(8,128)S(1)} %shard_map.47), channel_id=1, source_target_pairs={{0,1},{1,0},{2,3},{3,2},{4,5},{5,4},{6,7},{7,6},{8,9},{9,8},{10,11... | collective-permute-start | bytes 1032200 | tf_op jit(solution)/shard_map/ppermute | solution.py:707
  32.2 4.6 %collective-permute-start.4 = (f32[152,512]{1,0:T(8,128)S(1)}, f32[152,512]{1,0:T(8,128)S(1)}, u32[]{:S(2)}, u32[]{:S(2)}) collective-permute-start(f32[152,512]{1,0:T(8,128)S(1)} %get-tuple-element.40), channel_id=1, source_target_pairs={{0,1},{1,0},{2,3},{3,2},{4,5},{5,4},{6,7},{7,6},{8,9},{9,8},{10,11... | collective-permute-start | bytes 933896 | tf_op jit(solution)/shard_map/ppermute | solution.py:707
  34.2 18.2 %collective-permute-start.6 = (f32[96,512]{1,0:T(8,128)S(1)}, f32[96,512]{1,0:T(8,128)S(1)}, u32[]{:S(2)}, u32[]{:S(2)}) collective-permute-start(f32[96,512]{1,0:T(8,128)S(1)} %get-tuple-element.53), channel_id=1, source_target_pairs={{0,15},{1,2},{2,1},{3,4},{4,3},{5,6},{6,5},{7,8},{8,7},{9,10},{10,... | collective-permute-start | bytes 589832 | tf_op jit(solution)/shard_map/ppermute | solution.py:707
  41.7 11.3 %collective-permute-start.9 = (f32[16,640]{1,0:T(8,128)S(1)}, f32[16,640]{1,0:T(8,128)S(1)}, u32[]{:S(2)}, u32[]{:S(2)}) collective-permute-start(f32[16,640]{1,0:T(8,128)S(1)} %shard_map.55.own), channel_id=1, source_target_pairs={{496,0},{497,1},{498,2},{499,3},{500,4},{501,5},{502,6},{503,7},{5... | collective-permute-start | bytes 122888 | tf_op jit(solution)/shard_map/ppermute | solution.py:696
  44.9 8.1 %collective-permute-start.8 = (f32[16,640]{1,0:T(8,128)S(1)}, f32[16,640]{1,0:T(8,128)S(1)}, u32[]{:S(2)}, u32[]{:S(2)}) collective-permute-start(f32[16,640]{1,0:T(8,128)S(1)} %shard_map.55.own), channel_id=1, source_target_pairs={{48,0},{49,1},{50,2},{51,3},{52,4},{53,5},{54,6},{55,7},{56,8},{57... | collective-permute-start | bytes 122888 | tf_op jit(solution)/shard_map/ppermute | solution.py:696
  49.2 6.3 %collective-permute-start.7 = (f32[16,640]{1,0:T(8,128)S(1)}, f32[16,640]{1,0:T(8,128)S(1)}, u32[]{:S(2)}, u32[]{:S(2)}) collective-permute-start(f32[16,640]{1,0:T(8,128)S(1)} %shard_map.55.own), channel_id=1, source_target_pairs={{448,0},{449,1},{450,2},{451,3},{452,4},{453,5},{454,6},{455,7},{4... | collective-permute-start | bytes 122888 | tf_op jit(solution)/shard_map/ppermute | solution.py:696
  57.7 12.7 %collective-permute-start.12 = (f32[16,512]{1,0:T(8,128)S(1)}, f32[16,512]{1,0:T(8,128)S(1)}, u32[]{:S(2)}, u32[]{:S(2)}) collective-permute-start(f32[16,512]{1,0:T(8,128)S(1)} %shard_map.56.own.second), channel_id=1, source_target_pairs={{80,0},{81,1},{82,2},{83,3},{84,4},{85,5},{86,6},{87,7},{88,8},{89... | collective-permute-start | bytes 98312 | tf_op jit(solution)/shard_map/ppermute | solution.py:696
  62.0 8.4 %collective-permute-start.11 = (f32[16,512]{1,0:T(8,128)S(1)}, f32[16,512]{1,0:T(8,128)S(1)}, u32[]{:S(2)}, u32[]{:S(2)}) collective-permute-start(f32[16,512]{1,0:T(8,128)S(1)} %shard_map.56.own.second), channel_id=1, source_target_pairs={{16,0},{17,1},{18,2},{19,3},{20,4},{21,5},{22,6},{23,7},{24,8},{25... | collective-permute-start | bytes 98312 | tf_op jit(solution)/shard_map/ppermute | solution.py:696
  65.6 5.1 %collective-permute-start.10 = (f32[16,512]{1,0:T(8,128)S(1)}, f32[16,512]{1,0:T(8,128)S(1)}, u32[]{:S(2)}, u32[]{:S(2)}) collective-permute-start(f32[16,512]{1,0:T(8,128)S(1)} %shard_map.56.own.second), channel_id=1, source_target_pairs={{64,0},{65,1},{66,2},{67,3},{68,4},{69,5},{70,6},{71,7},{72,8},{73... | collective-permute-start | bytes 98312 | tf_op jit(solution)/shard_map/ppermute | solution.py:696
  72.6 10.5 %collective-permute-start.15 = (f32[16,384]{1,0:T(8,128)S(1)}, f32[16,384]{1,0:T(8,128)S(1)}, u32[]{:S(2)}, u32[]{:S(2)}) collective-permute-start(f32[16,384]{1,0:T(8,128)S(1)} %shard_map.57.own), channel_id=1, source_target_pairs={{496,0},{497,1},{498,2},{499,3},{500,4},{501,5},{502,6},{503,7},{5... | collective-permute-start | bytes 73736 | tf_op jit(solution)/shard_map/ppermute | solution.py:696
  74.8 8.3 %collective-permute-start.14 = (f32[16,384]{1,0:T(8,128)S(1)}, f32[16,384]{1,0:T(8,128)S(1)}, u32[]{:S(2)}, u32[]{:S(2)}) collective-permute-start(f32[16,384]{1,0:T(8,128)S(1)} %shard_map.57.own), channel_id=1, source_target_pairs={{48,0},{49,1},{50,2},{51,3},{52,4},{53,5},{54,6},{55,7},{56,8},{57... | collective-permute-start | bytes 73736 | tf_op jit(solution)/shard_map/ppermute | solution.py:696
  79.4 5.8 %collective-permute-start.13 = (f32[16,384]{1,0:T(8,128)S(1)}, f32[16,384]{1,0:T(8,128)S(1)}, u32[]{:S(2)}, u32[]{:S(2)}) collective-permute-start(f32[16,384]{1,0:T(8,128)S(1)} %shard_map.57.own), channel_id=1, source_target_pairs={{448,0},{449,1},{450,2},{451,3},{452,4},{453,5},{454,6},{455,7},{4... | collective-permute-start | bytes 73736 | tf_op jit(solution)/shard_map/ppermute | solution.py:696
